TPU v7x, 32 devices: a whole 2x2x4 slice. The times are simulated.
32 devices in a mesh: expert: 8 (over z, y), dp: 4 (over x, core).
Axes of the slice: x: 2, y: 2, z: 4, core: 2. Of those that a mesh axis runs over, the one named last changes fastest.
Arguments:
- tokens: bfloat16 [2048, 2048], P(('expert', 'dp')), may hold values from -6 to 6
- grad_out: bfloat16 [2048, 2048], P(('expert', 'dp')), may hold values from -6 to 6
- route_expert: int32 [2048, 4], P(('expert', 'dp')), may hold values from 0 to 7, all different within a row; in each aligned block of 64 rows (0 to 63, 64 to 127, ...) at most 33 rows name the same one
- route_weight: bfloat16 [2048, 4], P(('expert', 'dp')), may hold values from 0.019897461 to 0.5
- gate_up_weight: bfloat16 [8, 2048, 768], P('expert', 'dp'), may hold values from -0.125 to 0.125
- down_weight: bfloat16 [8, 2048, 384], P('expert', 'dp'), may hold values from -0.3125 to 0.3125
Outputs:
- grad_tokens: bfloat16 [2048, 2048], P(('expert', 'dp'))
- grad_route: bfloat16 [2048, 4], P(('expert', 'dp'))
- grad_gate_up: float32 [8, 2048, 768], P('expert', 'dp')
- grad_down: float32 [8, 2048, 384], P('expert', 'dp')
Inputs may be any that keep to these rules, and one draw needn't show every extreme that they name: `route_expert`: each row names 4 different experts. In the 64 rows of one device (aligned blocks) no expert is named by more than 33 rows, a bound that some block reaches.
All inputs are finite; a program needn't handle non-finite values.
Results may differ from a plain program's by a relative error of at most 0.01.
Values may be sent and summed in bfloat16 or wider, within the bound.
No kernel may reach another device: no remote copies, remote signals or barrier semaphores. Data moves between devices by JAX's collectives and lax.ppermute only.
A program may use at most 64 MiB of HBM per device.

v0:
```python
import jax
import jax.numpy as jnp
from jax import lax
from jax.sharding import PartitionSpec as P


def swish(value):
    return value * jax.nn.sigmoid(value)


def to_local(rows, group_count, local_count, capacity):
    tail = rows.shape[2:]
    shaped = rows.reshape((group_count, local_count, capacity) + tail)
    shaped = jnp.swapaxes(shaped, 0, 1)
    return shaped.reshape((local_count, group_count * capacity) + tail)


def to_groups(rows, group_count, local_count, capacity):
    tail = rows.shape[2:]
    shaped = rows.reshape((local_count, group_count, capacity) + tail)
    shaped = jnp.swapaxes(shaped, 0, 1)
    return shaped.reshape((group_count, local_count * capacity) + tail)


def on_device(tokens, grad_out, route_expert, route_weight, gate_up_weight, down_weight):
    token_count, model_width = tokens.shape
    route_count = route_expert.shape[1]
    group_count = lax.axis_size("expert")
    local_count = gate_up_weight.shape[0]
    hidden_width = down_weight.shape[2]
    expert_total = local_count * group_count
    capacity = min(token_count, (token_count * route_count + expert_total - 1) // expert_total + 1)
    slot_total = expert_total * capacity
    flat_expert = route_expert.reshape(-1)
    expert_ids = jnp.arange(expert_total, dtype=jnp.int32)
    onehot = (flat_expert[:, None] == expert_ids[None, :]).astype(jnp.int32)
    before = jnp.cumsum(onehot, axis=0) - onehot
    rank = jnp.sum(before * onehot, axis=1)
    slot_of = flat_expert * capacity + rank
    slot_ids = jnp.arange(slot_total, dtype=jnp.int32)
    placed = slot_ids[:, None] == slot_of[None, :]
    by_token = jnp.any(placed.reshape(slot_total, token_count, route_count), axis=2).astype(
        jnp.bfloat16
    )
    send_x = jnp.dot(by_token, tokens, preferred_element_type=jnp.float32).astype(jnp.bfloat16)
    send_dy = jnp.dot(by_token, grad_out, preferred_element_type=jnp.float32).astype(jnp.bfloat16)
    flat_weight = route_weight.reshape(-1).astype(jnp.float32)
    send_w = jnp.sum(jnp.where(placed, flat_weight[None, :], 0.0), axis=1).astype(jnp.bfloat16)
    recv_x, recv_dy, recv_w = (
        lax.all_to_all(
            send_x.reshape(group_count, local_count * capacity, model_width),
            "expert",
            split_axis=0,
            concat_axis=0,
            tiled=True,
        ),
        lax.all_to_all(
            send_dy.reshape(group_count, local_count * capacity, model_width),
            "expert",
            split_axis=0,
            concat_axis=0,
            tiled=True,
        ),
        lax.all_to_all(
            send_w.reshape(group_count, local_count * capacity),
            "expert",
            split_axis=0,
            concat_axis=0,
            tiled=True,
        ),
    )
    rows_x = to_local(recv_x, group_count, local_count, capacity)
    rows_dy = to_local(recv_dy, group_count, local_count, capacity)
    rows_w = to_local(recv_w, group_count, local_count, capacity)
    full_in, full_out = (
        lax.all_gather(gate_up_weight, "dp", axis=1, tiled=True),
        lax.all_gather(down_weight, "dp", axis=1, tiled=True),
    )
    pre = jnp.einsum("erd,edf->erf", rows_x, full_in, preferred_element_type=jnp.float32)
    gate_pre = pre[:, :, :hidden_width]
    up_pre = pre[:, :, hidden_width:]
    act = swish(gate_pre)
    hidden = (act * up_pre).astype(jnp.bfloat16)
    expert_out = jnp.einsum("erf,edf->erd", hidden, full_out, preferred_element_type=jnp.float32)
    route_grad = jnp.sum(rows_dy.astype(jnp.float32) * expert_out, axis=2).astype(jnp.bfloat16)
    scaled = (rows_w.astype(jnp.float32)[:, :, None] * rows_dy).astype(jnp.bfloat16)
    grad_hidden = jnp.einsum("erd,edf->erf", scaled, full_out, preferred_element_type=jnp.float32)
    sig = jax.nn.sigmoid(gate_pre)
    grad_gate = grad_hidden * up_pre * sig * (1.0 + gate_pre * (1.0 - sig))
    grad_up = grad_hidden * act
    grad_pre = jnp.concatenate([grad_gate, grad_up], axis=2).astype(jnp.bfloat16)
    rows_grad = jnp.einsum(
        "erf,edf->erd", grad_pre, full_in, preferred_element_type=jnp.float32
    ).astype(jnp.bfloat16)
    back_x, back_w = (
        lax.all_to_all(
            to_groups(rows_grad, group_count, local_count, capacity),
            "expert",
            split_axis=0,
            concat_axis=0,
            tiled=True,
        ),
        lax.all_to_all(
            to_groups(route_grad, group_count, local_count, capacity),
            "expert",
            split_axis=0,
            concat_axis=0,
            tiled=True,
        ),
    )
    back_x = back_x.reshape(slot_total, model_width)
    back_w = back_w.reshape(slot_total).astype(jnp.float32)
    grad_tokens = jnp.einsum(
        "st,sd->td", by_token, back_x, preferred_element_type=jnp.float32
    ).astype(jnp.bfloat16)
    grad_route = jnp.sum(jnp.where(placed, back_w[:, None], 0.0), axis=0)
    grad_route = grad_route.reshape(token_count, route_count).astype(jnp.bfloat16)
    all_x = lax.all_to_all(rows_x, "dp", split_axis=2, concat_axis=1, tiled=True)
    grad_gate_up = jnp.einsum(
        "erd,erf->edf",
        all_x,
        lax.all_gather(grad_pre, "dp", axis=1, tiled=True),
        preferred_element_type=jnp.float32,
    )
    summed = lax.psum_scatter(
        jnp.einsum("erd,erf->def", scaled, hidden, preferred_element_type=jnp.float32),
        "dp",
        scatter_dimension=0,
        tiled=True,
    )
    grad_down = jnp.swapaxes(summed, 0, 1)
    return (grad_tokens, grad_route, grad_gate_up, grad_down)


def solution(mesh):
    return jax.shard_map(
        on_device,
        mesh=mesh,
        in_specs=(
            P(("expert", "dp"), None),
            P(("expert", "dp"), None),
            P(("expert", "dp"), None),
            P(("expert", "dp"), None),
            P("expert", "dp", None),
            P("expert", "dp", None),
        ),
        out_specs=(
            P(("expert", "dp"), None),
            P(("expert", "dp"), None),
            P("expert", "dp", None),
            P("expert", "dp", None),
        ),
        check_vma=False,
    )
```

profile of v0, /device:TPU:1, one launch (start us, length us, event | category | flops | bytes accessed | tf_op | source)
XLA Modules:
  0.0 243.6 jit_solution(13650692119365666340)
XLA Ops:
  7.2 0.7 all-gather.6.cloned.1.call-update
  7.9 0.8 copy.55
  8.7 0.1 eq.50
  8.8 0.1 eq.46
  8.9 0.6 reduce-window.6
  9.5 0.2 slice_reduce_fusion
  9.8 0.1 fusion.32
  9.9 0.1 reduce_sum.39
  10.0 0.1 copy.57
  10.0 0.7 multiply_add_fusion
  10.7 0.1 fusion.29
  10.9 0.5 convolution_convert_fusion
  11.4 1.4 reshape.255
  12.8 6.5 %all-to-all-start.2 = ((bf16[8,33,2048]{2,1,0:T(8,128)(2,1)}), bf16[8,33,2048]{2,1,0:T(8,128)(2,1)S(1)}, u32[]{:S(2)}, u32[]{:S(2)}) async-start(bf16[8,33,2048]{2,1,0:T(8,128)(2,1)} %reshape.255), calls=%async_computation.2 | async-start | bytes 2621440 | tf_op jit(solution)/shard_map/all_to_all | solution.py:50
  19.3 0.5 convolution_convert_fusion.1
  19.8 1.4 reshape.253
  21.2 28.6 %all-to-all-done.2 = bf16[8,33,2048]{2,1,0:T(8,128)(2,1)S(1)} async-done(((bf16[8,33,2048]{2,1,0:T(8,128)(2,1)}), bf16[8,33,2048]{2,1,0:T(8,128)(2,1)S(1)}, u32[]{:S(2)}, u32[]{:S(2)}) %all-to-all-start.2) | async-done | bytes 1081376 | tf_op jit(solution)/shard_map/all_to_all | solution.py:50
  49.8 4.7 %all-to-all-start.1 = ((bf16[8,33,2048]{2,1,0:T(8,128)(2,1)}), bf16[8,33,2048]{2,1,0:T(8,128)(2,1)S(1)}, u32[]{:S(2)}, u32[]{:S(2)}) async-start(bf16[8,33,2048]{2,1,0:T(8,128)(2,1)} %reshape.253), calls=%async_computation.1 | async-start | bytes 2621440 | tf_op jit(solution)/shard_map/all_to_all | solution.py:57
  54.5 0.7 all-gather.4.cloned.1.call-update
  55.2 1.3 reshape.256
  56.6 28.6 %all-to-all-done.1 = bf16[8,33,2048]{2,1,0:T(8,128)(2,1)S(1)} async-done(((bf16[8,33,2048]{2,1,0:T(8,128)(2,1)}), bf16[8,33,2048]{2,1,0:T(8,128)(2,1)S(1)}, u32[]{:S(2)}, u32[]{:S(2)}) %all-to-all-start.1) | async-done | bytes 1081376 | tf_op jit(solution)/shard_map/all_to_all | solution.py:57
  85.2 1.7 reshape.265
  86.9 3.2 %fusion.18 = f32[1,264,768]{2,1,0:T(8,128)S(1)} fusion(bf16[264,2048]{1,0:T(8,128)(2,1)} %reshape.256, bf16[1,2048,768]{2,1,0:T(8,128)(2,1)} %all-gather.6.cloned.1.call-done), kind=kOutput, calls=%fused_computation.18 | convolution fusion | flops 830472192 | bytes 5038080 | tf_op jit(solution)/shard_map/erd,edf->erf/dot_general | solution.py:79
  90.1 0.9 copy-done.2
  91.0 0.1 fusion.30
  91.2 3.0 %fusion.15 = bf16[264]{0:T(512)(128)(2,1)S(1)} fusion(f32[264,2048]{1,0:T(8,128)} %reshape.265, bf16[264,384]{1,0:T(8,128)(2,1)S(1)} %fusion.30, bf16[1,2048,384]{2,1,0:T(8,128)(2,1)} %all-gather.4.cloned.1.call-done), kind=kOutput, calls=%fused_computation.17 | convolution fusion | flops 416317184 | bytes 3938832 | tf_op jit(solution)/shard_map/erf,edf->erd/dot_general | solution.py:84
  94.1 0.7 convert_element_type.192
  94.8 4.5 %all-to-all-start.4 = ((bf16[8,1,33]{2,1,0:T(2,128)(2,1)}), bf16[8,1,33]{2,1,0:T(2,128)(2,1)S(1)}, u32[]{:S(2)}, u32[]{:S(2)}) async-start(bf16[8,1,33]{2,1,0:T(2,128)(2,1)} %convert_element_type.192), calls=%async_computation.4 | async-start | bytes 8192 | tf_op jit(solution)/shard_map/all_to_all | solution.py:103
  99.3 0.1 copy.58
  99.4 0.1 reshape.262
  99.5 5.0 %all-to-all-done.4 = bf16[8,1,33]{2,1,0:T(2,128)(2,1)S(1)} async-done(((bf16[8,1,33]{2,1,0:T(2,128)(2,1)}), bf16[8,1,33]{2,1,0:T(2,128)(2,1)S(1)}, u32[]{:S(2)}, u32[]{:S(2)}) %all-to-all-start.4) | async-done | bytes 560 | tf_op jit(solution)/shard_map/all_to_all | solution.py:103
  104.6 0.1 reshape.266
  104.6 0.2 select_reduce_fusion
  104.9 0.7 convert_element_type.191
  105.5 3.3 %all-to-all-start = ((bf16[8,1,33]{2,1,0:T(2,128)(2,1)}), bf16[8,1,33]{2,1,0:T(2,128)(2,1)S(1)}, u32[]{:S(2)}, u32[]{:S(2)}) async-start(bf16[8,1,33]{2,1,0:T(2,128)(2,1)} %convert_element_type.191), calls=%async_computation | async-start | bytes 8192 | tf_op jit(solution)/shard_map/all_to_all | solution.py:64
  108.9 1.7 reshape.264
  110.6 3.5 %all-to-all-done = bf16[8,1,33]{2,1,0:T(2,128)(2,1)S(1)} async-done(((bf16[8,1,33]{2,1,0:T(2,128)(2,1)}), bf16[8,1,33]{2,1,0:T(2,128)(2,1)S(1)}, u32[]{:S(2)}, u32[]{:S(2)}) %all-to-all-start) | async-done | bytes 560 | tf_op jit(solution)/shard_map/all_to_all | solution.py:64
  114.1 0.1 reshape.263
  114.1 3.1 %multiply_convert_fusion.3 = (bf16[1,264,384]{2,1,0:T(8,128)(2,1)S(1)}, bf16[1,264,384]{2,1,0:T(8,128)(2,1)S(1)}) fusion(f32[1,264,768]{2,1,0:T(8,128)} %copy-done.2, bf16[1,2048,384]{2,1,0:T(8,128)(2,1)} %all-gather.4.cloned.1.call-done, f32[1,264,1,1,1,1,2048]{6,1,5,4,3,2,0:T(8,128)} %reshape.264, f32[264]{0:T(512)S(1)} %reshape.263), kind=kOutput, calls=%fused_computation.27 | convolution fusion | flops 417635328 | bytes 4953120 | tf_op jit(solution)/shard_map/erd,edf->erf/dot_general | solution.py:87
  117.3 0.9 pad_maximum_fusion
  118.1 0.2 reduce-scatter.2.cloned.1.call-start
  118.4 4.4 %convolution_bitcast_fusion = f32[2048,1,384]{0,2,1:T(8,128)} fusion(bf16[264,384]{1,0:T(8,128)(2,1)S(1)} %fusion.30, f32[1,264,1,1,1,1,2048]{6,1,5,4,3,2,0:T(8,128)} %reshape.264, f32[264]{0:T(512)S(1)} %reshape.263), kind=kOutput, calls=%fused_computation.4 | convolution fusion | flops 416317440 | bytes 5512224 | tf_op jit(solution)/shard_map/erd,erf->def/dot_general | solution.py:126
  122.8 1.3 reshape_transpose_reshape.10
  124.1 7.5 %copy.61 = bf16[1,264,2048]{1,0,2:T(2,128)(2,1)S(1)} copy(bf16[1,264,2048]{2,1,0:T(8,128)(2,1)} %reshape_transpose_reshape.10) | data formatting | bytes 2162688 | tf_op jit(solution)/shard_map/reshape;transpose;reshape | solution.py:15
  131.7 0.5 broadcast.64
  132.2 34.5 %reduce.12 = bf16[2048,264]{1,0:T(8,128)(2,1)} reduce(bf16[2048,1,264]{2,1,0:T(2,128)(2,1)S(1)} %bitcast.68, bf16[]{:T(256)} %broadcast.64), dimensions={1}, to_apply=%bitcast.52.reduce_sub_computation | reduce | bytes 2162690
  166.7 5.0 %reshape.280 = bf16[4,2,67584]{2,1,0:T(2,128)(2,1)} reshape(bf16[2048,264]{1,0:T(8,128)(2,1)} %reduce.12) | data formatting | bytes 2162688
  171.7 6.7 %all-to-all-start.5 = ((bf16[4,2,67584]{2,1,0:T(2,128)(2,1)}), bf16[4,2,67584]{2,1,0:T(2,128)(2,1)S(1)}, u32[]{:S(2)}, u32[]{:S(2)}) async-start(bf16[4,2,67584]{2,1,0:T(2,128)(2,1)} %reshape.280), calls=%async_computation.5 | async-start | bytes 2162688 | tf_op jit(solution)/shard_map/all_to_all | solution.py:118
  178.4 2.9 %fusion.4 = bf16[264,2048]{1,0:T(8,128)(2,1)S(1)} fusion(bf16[1,2048,768]{2,1,0:T(8,128)(2,1)} %all-gather.6.cloned.1.call-done, bf16[264,384]{1,0:T(8,128)(2,1)S(1)} %bitcast.74, bf16[264,384]{1,0:T(8,128)(2,1)S(1)} %bitcast.73), kind=kOutput, calls=%fused_computation.6 | convolution fusion | flops 831823872 | bytes 4632576 | tf_op jit(solution)/shard_map/erf,edf->erd/dot_general | solution.py:92
  181.3 1.4 reshape_transpose_reshape.4
  182.7 9.6 %all-to-all-done.5 = bf16[4,2,67584]{2,1,0:T(2,128)(2,1)S(1)} async-done(((bf16[4,2,67584]{2,1,0:T(2,128)(2,1)}), bf16[4,2,67584]{2,1,0:T(2,128)(2,1)S(1)}, u32[]{:S(2)}, u32[]{:S(2)}) %all-to-all-start.5) | async-done | bytes 1081376 | tf_op jit(solution)/shard_map/all_to_all | solution.py:118
  192.3 1.0 copy-done.1
  193.3 4.5 %all-to-all-start.3 = ((bf16[8,33,2048]{2,1,0:T(8,128)(2,1)}), bf16[8,33,2048]{2,1,0:T(8,128)(2,1)}, u32[]{:S(2)}, u32[]{:S(2)}) async-start(bf16[8,33,2048]{2,1,0:T(8,128)(2,1)} %reshape_transpose_reshape.4), calls=%async_computation.3 | async-start | bytes 2621440 | tf_op jit(solution)/shard_map/all_to_all | solution.py:96
  197.8 4.6 %reshape.281 = bf16[2048,1,264]{2,1,0:T(2,128)(2,1)S(1)} reshape(bf16[4,2,67584]{2,1,0:T(2,128)(2,1)} %copy-done.1) | data formatting | bytes 2162688
  202.3 6.1 %copy.62 = bf16[1,264,2048]{2,1,0:T(8,128)(2,1)} copy(bf16[1,264,2048]{1,0,2:T(2,128)(2,1)S(1)} %bitcast.69) | data formatting | bytes 2162688 | tf_op jit(solution)/shard_map/all_to_all | solution.py:118
  208.5 3.0 %all_to_all.34 = bf16[1,264,4,512]{3,2,1,0:T(4,128)(2,1)S(1)} reshape(bf16[1,264,2048]{2,1,0:T(8,128)(2,1)} %copy.62) | data formatting | bytes 2162688 | tf_op jit(solution)/shard_map/all_to_all | solution.py:118
  211.5 0.2 copy.63
  211.7 0.1 convert_element_type.185
  211.8 0.7 copy.64
  212.5 15.7 %all-to-all-done.3 = bf16[8,33,2048]{2,1,0:T(8,128)(2,1)} async-done(((bf16[8,33,2048]{2,1,0:T(8,128)(2,1)}), bf16[8,33,2048]{2,1,0:T(8,128)(2,1)}, u32[]{:S(2)}, u32[]{:S(2)}) %all-to-all-start.3) | async-done | bytes 1081376 | tf_op jit(solution)/shard_map/all_to_all | solution.py:96
  228.2 1.7 reshape.258
  229.9 1.1 convolution_convert_fusion.2
  231.0 3.8 %fusion.12 = f32[1,512,768]{2,1,0:T(8,128)} fusion(bf16[1056,512]{1,0:T(8,128)(2,1)S(1)} %bitcast.71, bf16[1,1056,768]{2,1,0:T(8,128)(2,1)} %all-gather.8.cloned.1.call-done), kind=kOutput, calls=%fused_computation.16 | convolution fusion | flops 830472192 | bytes 4276224 | tf_op jit(solution)/shard_map/erd,erf->edf/dot_general | solution.py:119
  234.8 2.3 copy.65
  (31 shorter events, 0.3 us)
Async XLA Ops:
  7.2 3.7 %copy-start = (bf16[64,2048]{1,0:T(8,128)(2,1)S(1)}, bf16[64,2048]{1,0:T(8,128)(2,1)}, u32[]{:S(2)}) copy-start(bf16[64,2048]{1,0:T(8,128)(2,1)} %param.6) | copy-start | bytes 786436
  7.2 79.7 %all-gather.6.cloned.1.call-start = ((), (), s32[]{:S(2)}) async-start(), calls=%async_computation.8 | async-start | bytes 3932160 | tf_op jit(solution)/shard_map/all_gather | solution.py:76
  12.8 6.5 %copy-start.3 = (bf16[64,2048]{1,0:T(8,128)(2,1)S(1)}, bf16[64,2048]{1,0:T(8,128)(2,1)}, u32[]{:S(2)}) copy-start(bf16[64,2048]{1,0:T(8,128)(2,1)} %param.7) | copy-start | bytes 786436
  12.8 37.0 %all-to-all-start.2 = ((bf16[8,33,2048]{2,1,0:T(8,128)(2,1)}), bf16[8,33,2048]{2,1,0:T(8,128)(2,1)S(1)}, u32[]{:S(2)}, u32[]{:S(2)}) async-start(bf16[8,33,2048]{2,1,0:T(8,128)(2,1)} %reshape.255), calls=%async_computation.2 | async-start | bytes 2621440 | tf_op jit(solution)/shard_map/all_to_all | solution.py:50
  49.8 35.4 %all-to-all-start.1 = ((bf16[8,33,2048]{2,1,0:T(8,128)(2,1)}), bf16[8,33,2048]{2,1,0:T(8,128)(2,1)S(1)}, u32[]{:S(2)}, u32[]{:S(2)}) async-start(bf16[8,33,2048]{2,1,0:T(8,128)(2,1)} %reshape.253), calls=%async_computation.1 | async-start | bytes 2621440 | tf_op jit(solution)/shard_map/all_to_all | solution.py:57
  54.5 36.7 %all-gather.4.cloned.1.call-start = ((), (), s32[]{:S(2)}) async-start(), calls=%async_computation.7 | async-start | bytes 1966080 | tf_op jit(solution)/shard_map/all_gather | solution.py:77
  90.1 0.9 copy-start.2
  91.1 8.2 %copy-start.8 = (bf16[64,4]{0,1:T(4,128)(2,1)S(1)}, bf16[64,4]{0,1:T(4,128)(2,1)}, u32[]{:S(2)}) copy-start(bf16[64,4]{0,1:T(4,128)(2,1)} %param.9) | copy-start | bytes 1540
  94.8 9.7 %all-to-all-start.4 = ((bf16[8,1,33]{2,1,0:T(2,128)(2,1)}), bf16[8,1,33]{2,1,0:T(2,128)(2,1)S(1)}, u32[]{:S(2)}, u32[]{:S(2)}) async-start(bf16[8,1,33]{2,1,0:T(2,128)(2,1)} %convert_element_type.192), calls=%async_computation.4 | async-start | bytes 8192 | tf_op jit(solution)/shard_map/all_to_all | solution.py:103
  105.5 8.5 %all-to-all-start = ((bf16[8,1,33]{2,1,0:T(2,128)(2,1)}), bf16[8,1,33]{2,1,0:T(2,128)(2,1)S(1)}, u32[]{:S(2)}, u32[]{:S(2)}) async-start(bf16[8,1,33]{2,1,0:T(2,128)(2,1)} %convert_element_type.191), calls=%async_computation | async-start | bytes 8192 | tf_op jit(solution)/shard_map/all_to_all | solution.py:64
  108.9 122.1 %all-gather.8.cloned.1.call-start = ((), (), s32[]{:S(2)}) async-start(), calls=%async_computation.9 | async-start | bytes 2027520 | tf_op jit(solution)/shard_map/all_gather | solution.py:122
  117.2 5.5 %copy-start.4 = (bf16[1,264,384]{2,1,0:T(8,128)(2,1)}, bf16[1,264,384]{2,1,0:T(8,128)(2,1)S(1)}, u32[]{:S(2)}) copy-start(bf16[1,264,384]{2,1,0:T(8,128)(2,1)S(1)} %get-tuple-element.30) | copy-start | bytes 608260
  117.2 5.5 %copy-start.6 = (bf16[1,264,384]{2,1,0:T(8,128)(2,1)}, bf16[1,264,384]{2,1,0:T(8,128)(2,1)S(1)}, u32[]{:S(2)}) copy-start(bf16[1,264,384]{2,1,0:T(8,128)(2,1)S(1)} %get-tuple-element.31) | copy-start | bytes 608260
  118.1 116.6 %reduce-scatter.2.cloned.1.call-start = ((), (), s32[]{:S(2)}) async-start(), calls=%async_computation.10 | async-start | bytes 3932160 | tf_op jit(solution)/shard_map/reduce_scatter | solution.py:125
  171.7 6.7 %copy-start.5 = (bf16[1,264,384]{2,1,0:T(8,128)(2,1)S(1)}, bf16[1,264,384]{2,1,0:T(8,128)(2,1)}, u32[]{:S(2)}) copy-start(bf16[1,264,384]{2,1,0:T(8,128)(2,1)} %copy-done.4) | copy-start | bytes 608260
  171.7 6.7 %copy-start.7 = (bf16[1,264,384]{2,1,0:T(8,128)(2,1)S(1)}, bf16[1,264,384]{2,1,0:T(8,128)(2,1)}, u32[]{:S(2)}) copy-start(bf16[1,264,384]{2,1,0:T(8,128)(2,1)} %copy-done.6) | copy-start | bytes 608260
  171.7 20.6 %all-to-all-start.5 = ((bf16[4,2,67584]{2,1,0:T(2,128)(2,1)}), bf16[4,2,67584]{2,1,0:T(2,128)(2,1)S(1)}, u32[]{:S(2)}, u32[]{:S(2)}) async-start(bf16[4,2,67584]{2,1,0:T(2,128)(2,1)} %reshape.280), calls=%async_computation.5 | async-start | bytes 2162688 | tf_op jit(solution)/shard_map/all_to_all | solution.py:118
  192.3 1.0 copy-start.1
  193.3 34.9 %all-to-all-start.3 = ((bf16[8,33,2048]{2,1,0:T(8,128)(2,1)}), bf16[8,33,2048]{2,1,0:T(8,128)(2,1)}, u32[]{:S(2)}, u32[]{:S(2)}) async-start(bf16[8,33,2048]{2,1,0:T(8,128)(2,1)} %reshape_transpose_reshape.4), calls=%async_computation.3 | async-start | bytes 2621440 | tf_op jit(solution)/shard_map/all_to_all | solution.py:96
Sparse Core Ops, SparseCore 0:
  9.6 31.0 all-gather.5
  56.9 21.5 all-gather.3
  118.3 19.9 all-gather.7
  140.7 37.5 reduce-scatter.1
where the time goes:
time: 246 us; the launch traced here: 244 us
  waiting for transfers between devices  92.4 us (38%)
  local copies, waits for them, and re-layouts  47 us (19%)
  other arithmetic  37.2 us (15%)
  starting transfers between devices  30.5 us (12%)
  matrix products  22.5 us (9%)
  between operations  14 us (6%)
    unnamed x1, other arithmetic  34.5 us
    all_to_all x1, waiting for transfers between devices, on_device(): lax.all_to_all(send_dy.reshape(group_count, local_count * capacity, model...  28.6 us
    all_to_all x1, waiting for transfers between devices, on_device(): lax.all_to_all(send_x.reshape(group_count, local_count * capacity, model_...  28.6 us
    all_to_all x1, waiting for transfers between devices, on_device(): lax.all_to_all(to_groups(rows_grad, group_count, local_count, capacity),...  15.7 us
    unnamed x24, local copies, waits for them, and re-layouts  15.7 us
    all_to_all x1, waiting for transfers between devices, on_device(): lax.all_to_all(rows_x, 'dp', split_axis=2, concat_axis=1, tiled=True)  9.59 us
    all_to_all x3, local copies, waits for them, and re-layouts, on_device(): lax.all_to_all(rows_x, 'dp', split_axis=2, concat_axis=1, tiled=True)  9.31 us
    another operation x2, local copies, waits for them, and re-layouts, to_local(): return shaped.reshape((local_count, group_count * capacity) + tail)  8.88 us
  transfers between devices with their start and end apart: 10, of which 6 were waited for; matrix products, arithmetic and copies ran while one was open for 37% of the time, Pallas kernels for 0%

commit v1 on v0

--- a/solution.py
+++ b/solution.py
@@ -1,12 +1,205 @@
+import functools
+
 import jax
 import jax.numpy as jnp
 from jax import lax
+from jax.experimental import pallas as pl
+from jax.experimental.pallas import tpu as pltpu
 from jax.sharding import PartitionSpec as P
+
+BF16 = jnp.bfloat16
+F32 = jnp.float32
 
 
 def swish(value):
     return value * jax.nn.sigmoid(value)
 
+
+def dot(a, b):
+    return jnp.dot(a, b, preferred_element_type=F32)
+
+
+def dot_nt(a, b):
+    return lax.dot_general(a, b, (((1,), (1,)), ((), ())), preferred_element_type=F32)
+
+
+def dot_tn(a, b):
+    return lax.dot_general(a, b, (((0,), (0,)), ((), ())), preferred_element_type=F32)
+
+
+def select_matrix(weight_row, row_total):
+    token_total = weight_row.shape[1]
+    routed = weight_row != 0.0
+    earlier = lax.broadcasted_iota(jnp.int32, (token_total, token_total), 0)
+    later = lax.broadcasted_iota(jnp.int32, (token_total, token_total), 1)
+    upper = (earlier < later).astype(F32).astype(BF16)
+    ones = jnp.broadcast_to(routed.astype(F32), (8, token_total)).astype(BF16)
+    rank = dot(ones, upper)[0:1, :]
+    rank = jnp.where(routed, rank, -1.0).astype(jnp.int32)
+    slots = lax.broadcasted_iota(jnp.int32, (row_total, token_total), 0)
+    return (slots == rank).astype(F32).astype(BF16)
+
+
+def x_kernel(place_ref, w_ref, x_ref, *refs):
+    parts = (len(refs) - 2) // 2
+    in_refs, slice_refs = refs[:parts], refs[parts : 2 * parts]
+    pre_ref, pick_ref = refs[2 * parts :]
+    rows, depth = slice_refs[0].shape
+    pick_ref[...] = select_matrix(w_ref[...], rows)
+    for j in range(parts):
+        columns = pl.ds(pl.multiple_of(place_ref[j] * depth, depth), depth)
+        slice_refs[j][...] = dot(pick_ref[...], x_ref[:, columns]).astype(BF16)
+        term = dot(slice_refs[j][...], in_refs[j][...])
+        if j == 0:
+            pre_ref[...] = term
+        else:
+            pre_ref[...] += term
+
+
+def dy_kernel(place_ref, w_ref, dy_ref, pre_ref, pick_ref, *refs):
+    parts = (len(refs) - 3) // 3
+    in_refs, out_refs, slice_refs = refs[:parts], refs[parts : 2 * parts], refs[2 * parts : 3 * parts]
+    mid_ref, grad_ref, route_ref = refs[3 * parts :]
+    rows, depth = slice_refs[0].shape
+    hidden_width = out_refs[0].shape[1]
+    pick = pick_ref[...]
+    back = jnp.zeros((rows, hidden_width), F32)
+    for j in range(parts):
+        columns = pl.ds(pl.multiple_of(place_ref[j] * depth, depth), depth)
+        slice_refs[j][...] = dot(pick, dy_ref[:, columns]).astype(BF16)
+        back += dot(slice_refs[j][...], out_refs[j][...])
+    weight = jnp.sum(pick.astype(F32) * w_ref[...], axis=1, keepdims=True)
+    gate_pre = pre_ref[:, :hidden_width]
+    up_pre = pre_ref[:, hidden_width:]
+    sig = jax.nn.sigmoid(gate_pre)
+    act = gate_pre * sig
+    hidden = (act * up_pre).astype(BF16).astype(F32)
+    route = jnp.sum(hidden * back, axis=1, keepdims=True)
+    grad_hidden = weight * back
+    grad_gate = grad_hidden * up_pre * sig * (1.0 + gate_pre * (1.0 - sig))
+    mid_ref[:, :hidden_width] = grad_gate.astype(BF16)
+    mid_ref[:, hidden_width : 2 * hidden_width] = (grad_hidden * act).astype(BF16)
+    mid_ref[:, 2 * hidden_width :] = (weight * hidden).astype(BF16)
+    route_ref[...] = jnp.sum(pick.astype(F32) * route, axis=0, keepdims=True)
+    spread = dot_tn(pick, mid_ref[:, : 2 * hidden_width]).astype(BF16)
+    for j in range(parts):
+        columns = pl.ds(pl.multiple_of(place_ref[j] * depth, depth), depth)
+        grad_ref[:, columns] = dot_nt(spread, in_refs[j][...]).astype(BF16)
+
+
+def weight_kernel(*refs):
+    parts = (len(refs) - 2) // 3
+    x_refs, dy_refs, mid_refs = refs[:parts], refs[parts : 2 * parts], refs[2 * parts : 3 * parts]
+    in_ref, out_ref = refs[3 * parts :]
+    hidden_width = out_ref.shape[1]
+    for j in range(parts):
+        in_term = dot_tn(x_refs[j][...], mid_refs[j][:, : 2 * hidden_width])
+        out_term = dot_tn(dy_refs[j][...], mid_refs[j][:, 2 * hidden_width :])
+        if j == 0:
+            in_ref[...] = in_term
+            out_ref[...] = out_term
+        else:
+            in_ref[...] += in_term
+            out_ref[...] += out_term
+
+
+def call(kernel, out_shapes, smem, arrays, flops):
+    vmem = pl.BlockSpec(memory_space=pltpu.VMEM)
+    specs = [pl.BlockSpec(memory_space=pltpu.SMEM)] * len(smem) + [vmem] * len(arrays)
+    moved = sum(a.size * a.dtype.itemsize for a in list(arrays) + list(out_shapes))
+    return pl.pallas_call(
+        kernel,
+        out_shape=tuple(out_shapes),
+        in_specs=specs,
+        out_specs=tuple([vmem] * len(out_shapes)),
+        compiler_params=pltpu.CompilerParams(vmem_limit_bytes=40 * 1024 * 1024),
+        cost_estimate=pl.CostEstimate(flops=flops, bytes_accessed=moved, transcendentals=0),
+    )(*smem, *arrays)
+
+
+def swap(value, axis, size, mask):
+    return lax.ppermute(value, axis, [(i, i ^ mask) for i in range(size)])
+
+
+def gather_four(value):
+    near = swap(value, "dp", 4, 1)
+    far = swap(value, "dp", 4, 2)
+    return [value, near, far, swap(far, "dp", 4, 1)]
+
+
+def spread_four(values):
+    return [values[0]] + [swap(values[j], "dp", 4, j) for j in range(1, 4)]
+
+
+def on_device_gathered(tokens, grad_out, route_expert, route_weight, gate_up_weight, down_weight):
+    token_count, model_width = tokens.shape
+    route_count = route_expert.shape[1]
+    group_count = lax.axis_size("expert")
+    part_count = lax.axis_size("dp")
+    hidden_width = down_weight.shape[2]
+    depth = model_width // part_count
+    capacity = min(token_count, (token_count * route_count + group_count - 1) // group_count + 1)
+    rows = (group_count * capacity + 15) // 16 * 16
+    everyone = group_count * token_count
+
+    places = lax.axis_index("dp") ^ jnp.arange(part_count, dtype=jnp.int32)
+    names = route_expert.T[None, :, :] == jnp.arange(group_count, dtype=jnp.int32)[:, None, None]
+    dense = jnp.sum(jnp.where(names, route_weight.T[None, :, :], 0), axis=1).astype(BF16)
+    weight_row = lax.all_to_all(dense, "expert", split_axis=0, concat_axis=0, tiled=True)
+    weight_row = weight_row.reshape(1, everyone).astype(F32)
+
+    all_tokens = lax.all_gather(tokens, "expert", axis=0, tiled=True)
+    all_grad = lax.all_gather(grad_out, "expert", axis=0, tiled=True)
+    in_parts = gather_four(gate_up_weight[0])
+    out_parts = gather_four(down_weight[0])
+
+    sliced = [jax.ShapeDtypeStruct((rows, depth), BF16)] * part_count
+    *x_slices, pre, pick = call(
+        x_kernel,
+        sliced
+        + [
+            jax.ShapeDtypeStruct((rows, 2 * hidden_width), F32),
+            jax.ShapeDtypeStruct((rows, everyone), BF16),
+        ],
+        [places],
+        [weight_row, all_tokens, *in_parts],
+        2 * rows * model_width * (everyone + 2 * hidden_width),
+    )
+    x_slices = spread_four(x_slices)
+    *dy_slices, mid, grad_rows, route_row = call(
+        dy_kernel,
+        sliced
+        + [
+            jax.ShapeDtypeStruct((rows, 3 * hidden_width), BF16),
+            jax.ShapeDtypeStruct((everyone, model_width), BF16),
+            jax.ShapeDtypeStruct((1, everyone), F32),
+        ],
+        [places],
+        [weight_row, all_grad, pre, pick, *in_parts, *out_parts],
+        2 * rows * model_width * (everyone + hidden_width) + 4 * everyone * hidden_width * model_width,
+    )
+    dy_slices = spread_four(dy_slices)
+    mids = gather_four(mid)
+    grad_tokens = lax.psum_scatter(grad_rows, "expert", scatter_dimension=0, tiled=True)
+    route_back = lax.all_to_all(
+        route_row.reshape(group_count, token_count).astype(BF16),
+        "expert",
+        split_axis=0,
+        concat_axis=0,
+        tiled=True,
+    )
+    grad_route = jnp.sum(jnp.where(names, route_back[:, None, :], 0), axis=0).astype(BF16).T
+    grad_gate_up, grad_down = call(
+        weight_kernel,
+        [
+            jax.ShapeDtypeStruct((depth, 2 * hidden_width), F32),
+            jax.ShapeDtypeStruct((depth, hidden_width), F32),
+        ],
+        [],
+        [*x_slices, *dy_slices, *mids],
+        2 * part_count * rows * depth * 3 * hidden_width,
+    )
+    return (grad_tokens, grad_route, grad_gate_up[None], grad_down[None])
 
 def to_local(rows, group_count, local_count, capacity):
     tail = rows.shape[2:]
@@ -22,7 +215,7 @@
     return shaped.reshape((group_count, local_count * capacity) + tail)
 
 
-def on_device(tokens, grad_out, route_expert, route_weight, gate_up_weight, down_weight):
+def on_device_routed(tokens, grad_out, route_expert, route_weight, gate_up_weight, down_weight):
     token_count, model_width = tokens.shape
     route_count = route_expert.shape[1]
     group_count = lax.axis_size("expert")
@@ -133,6 +326,15 @@
 
 
 def solution(mesh):
+    def on_device(*arrays):
+        route_expert, down_weight = arrays[2], arrays[5]
+        gathers = (
+            down_weight.shape[0] == 1
+            and lax.axis_size("dp") == 4
+            and lax.axis_size("expert") <= 2 * route_expert.shape[1]
+        )
+        return (on_device_gathered if gathers else on_device_routed)(*arrays)
+
     return jax.shard_map(
         on_device,
         mesh=mesh,

time: 246 us -> 200 us (0.81)
  other arithmetic: 37.2 us -> 1.33 us
  local copies, waits for them, and re-layouts: 47 us -> 23.4 us
  matrix products: 22.5 us -> 0 us
  waiting for transfers between devices: 92.4 us -> 112 us
  Pallas kernels: 0 us -> 14.4 us
  blocking collectives: 0 us -> 9.27 us
  starting transfers between devices: 30.5 us -> 21.9 us
    all_to_all x6 -> x1, waiting for transfers between devices: 91 us -> 5.18 us  [on_device_gathered(): lax.all_to_all(dense, 'expert', split_axis=0, concat_axis=0, tiled=True)]
    ppermute x0 -> x15, waiting for transfers between devices: none -> 47.9 us  [swap(): return lax.ppermute(value, axis, [(i, i ^ mask) for i in range(size)])]
    all_gather x3 -> x2, waiting for transfers between devices: 0.02 us -> 46.7 us  [the longest x1 40 us: on_device_gathered(): all_grad = lax.all_gather(grad_out, 'expert', axis=0, tiled=True)]
    unnamed x1 -> x0, other arithmetic: 34.5 us -> none
    all_to_all x6 -> x1, starting transfers between devices: 30.1 us -> 5.8 us  [on_device_gathered(): lax.all_to_all(dense, 'expert', split_axis=0, concat_axis=0, tiled=True)]
    dot_general x9 -> x0, matrix products: 22.5 us -> none  [the longest x1 4.38 us: on_device(): jnp.einsum('erd,erf->def', scaled, hidden, preferred_element_type=jnp.flo...]
    ppermute x0 -> x15, starting transfers between devices: none -> 16 us  [swap(): return lax.ppermute(value, axis, [(i, i ^ mask) for i in range(size)])]
    pallas_call x0 -> x3, Pallas kernels: none -> 14.4 us  [call(): pl.pallas_call(kernel, out_shape=tuple(out_shapes), in_specs=specs, out_s...]
  transfers between devices with their start and end apart: 10 -> 19, of which waited for: 6 -> 10; matrix products, arithmetic and copies ran while one was open for 37% -> 1% of each run, Pallas kernels for 0% -> 4%
where the time goes in v1:
time: 200 us; the launch traced here: 196 us
  waiting for transfers between devices  112 us (56%)
  local copies, waits for them, and re-layouts  23.4 us (12%)
  starting transfers between devices  21.9 us (11%)
  Pallas kernels  14.4 us (7%)
  between operations  13.8 us (7%)
  blocking collectives  9.27 us (5%)
    ppermute x15, waiting for transfers between devices, swap(): return lax.ppermute(value, axis, [(i, i ^ mask) for i in range(size)])  47.9 us
    all_gather x1, waiting for transfers between devices, on_device_gathered(): all_grad = lax.all_gather(grad_out, 'expert', axis=0, tiled=True)  40 us
    unnamed x63, local copies, waits for them, and re-layouts  22.6 us
    ppermute x15, starting transfers between devices, swap(): return lax.ppermute(value, axis, [(i, i ^ mask) for i in range(size)])  16 us
    pallas_call x3, Pallas kernels, call(): pl.pallas_call(kernel, out_shape=tuple(out_shapes), in_specs=specs, out_s...  14.4 us
    reduce_scatter x1, waiting for transfers between devices, on_device_gathered(): lax.psum_scatter(grad_rows, 'expert', scatter_dimension=0, tiled=True)  11.1 us
    all_to_all x1, blocking collectives, on_device_gathered(): lax.all_to_all(route_row.reshape(group_count, token_count).astype(BF16),...  9.27 us
    all_gather x1, waiting for transfers between devices, on_device_gathered(): all_tokens = lax.all_gather(tokens, 'expert', axis=0, tiled=True)  6.69 us
  transfers between devices with their start and end apart: 19, of which 10 were waited for; matrix products, arithmetic and copies ran while one was open for 1% of the time, Pallas kernels for 4%

profile of v1, /device:TPU:1, one launch (start us, length us, event | category | flops | bytes accessed | tf_op | source)
XLA Modules:
  0.0 196.4 jit_solution(4533589870223889987)
XLA Ops:
  7.2 0.0 all-gather.5.cloned.1.call-start
  7.2 0.7 all-gather.5.cloned.1.call-update
  7.9 0.0 all-gather.3.cloned.1.call-start
  7.9 0.7 all-gather.3.cloned.1.call-update
  8.6 2.1 %collective-permute-start.1 = (bf16[512,768]{1,0:T(8,128)(2,1)}, bf16[512,768]{1,0:T(8,128)(2,1)S(1)}, u32[]{:S(2)}, u32[]{:S(2)}) collective-permute-start(bf16[512,768]{1,0:T(8,128)(2,1)} %bitcast.11), channel_id=1, source_target_pairs={{0,2},{1,3},{2,0},{3,1},{4,6},{5,7},{6,4},{7,5},{8,10},{9,11},{10,... | collective-permute-start | bytes 2359304 | tf_op jit(solution)/shard_map/ppermute | solution.py:121
  10.8 1.0 collective-permute-start
  11.7 16.6 %collective-permute-done.1.refs_2_ = bf16[512,768]{1,0:T(8,128)(2,1)S(1)} collective-permute-done((bf16[512,768]{1,0:T(8,128)(2,1)}, bf16[512,768]{1,0:T(8,128)(2,1)S(1)}, u32[]{:S(2)}, u32[]{:S(2)}) %collective-permute-start.1) | collective-permute-done | bytes 786464 | tf_op jit(solution)/shard_map/ppermute | solution.py:121
  28.3 1.1 collective-permute-start.2
  29.5 1.5 collective-permute-start.4
  30.9 0.3 collective-permute-start.3
  31.2 9.3 %collective-permute-done.4.refs_6_ = bf16[512,384]{1,0:T(8,128)(2,1)} collective-permute-done((bf16[512,384]{1,0:T(8,128)(2,1)}, bf16[512,384]{1,0:T(8,128)(2,1)}, u32[]{:S(2)}, u32[]{:S(2)}) %collective-permute-start.4) | collective-permute-done | bytes 393248 | tf_op jit(solution)/shard_map/ppermute | solution.py:121
  40.5 0.8 collective-permute-start.5
  41.3 0.7 fusion.2
  42.0 0.6 copy.13
  42.6 5.8 %all-to-all-start = ((bf16[8,1,64]{2,1,0:T(2,128)(2,1)}), bf16[8,1,64]{2,1,0:T(2,128)(2,1)S(1)}, u32[]{:S(2)}, u32[]{:S(2)}) async-start(bf16[8,1,64]{2,1,0:T(2,128)(2,1)} %copy.13), calls=%async_computation | async-start | bytes 8192 | tf_op jit(solution)/shard_map/all_to_all | solution.py:148
  48.4 0.0 reduce-scatter.2.cloned.1.call-start
  48.5 5.2 %all-to-all-done = bf16[8,1,64]{2,1,0:T(2,128)(2,1)S(1)} async-done(((bf16[8,1,64]{2,1,0:T(2,128)(2,1)}), bf16[8,1,64]{2,1,0:T(2,128)(2,1)S(1)}, u32[]{:S(2)}, u32[]{:S(2)}) %all-to-all-start) | async-done | bytes 1056 | tf_op jit(solution)/shard_map/all_to_all | solution.py:148
  53.7 0.1 reshape.44.w_ref
  53.8 6.7 %all-gather.5.cloned.1.call-done.x_ref = bf16[512,2048]{1,0:T(8,128)(2,1)} async-done(((bf16[64,2048]{1,0:T(8,128)(2,1)}), bf16[512,2048]{1,0:T(8,128)(2,1)}) %all-gather.5.cloned.1.call-update) | async-done | bytes 2097168 | tf_op jit(solution)/shard_map/all_gather | solution.py:151
  60.5 1.6 copy-done.1
  62.0 1.1 copy-done.2
  63.2 2.7 %shard_map.93 = (bf16[272,512]{1,0:T(8,128)(2,1)S(1)}, bf16[272,512]{1,0:T(8,128)(2,1)S(1)}, bf16[272,512]{1,0:T(8,128)(2,1)S(1)}, bf16[272,512]{1,0:T(8,128)(2,...) custom-call(s32[4]{0:T(128)S(1)} %iota_xor_fusion.place_ref, f32[1,512]{1,0:T(1,128)S(1)} %reshape.44.w_ref, ...), custom_call_target="tpu_custom_call" | custom-call | flops 1426063360 | bytes 7473152 | tf_op jit(solution)/shard_map/pallas_call | solution.py:110
  65.9 0.7 copy-done.7
  66.6 0.7 copy-done.9
  67.3 0.7 copy-done.11
  68.0 0.7 copy-done.22
  68.7 0.9 copy-done.26
  69.6 0.7 copy-done.28
  70.3 40.0 %all-gather.3.cloned.1.call-done.dy_ref = bf16[512,2048]{1,0:T(8,128)(2,1)} async-done(((bf16[64,2048]{1,0:T(8,128)(2,1)}), bf16[512,2048]{1,0:T(8,128)(2,1)}) %all-gather.3.cloned.1.call-update) | async-done | bytes 2097168 | tf_op jit(solution)/shard_map/all_gather | solution.py:152
  110.4 1.6 copy-done
  112.0 1.1 copy-done.27
  113.1 1.0 copy-done.29
  114.1 6.5 %shard_map.94 = (bf16[272,512]{1,0:T(8,128)(2,1)S(1)}, bf16[272,512]{1,0:T(8,128)(2,1)S(1)}, bf16[272,512]{1,0:T(8,128)(2,1)S(1)}, bf16[272,512]{1,0:T(8,128)(2,...) custom-call(s32[4]{0:T(128)S(1)} %iota_xor_fusion.place_ref, ...), custom_call_target="tpu_custom_call" | custom-call | flops 2608857088 | bytes 11771904 | tf_op jit(solution)/shard_map/pallas_call | solution.py:110
  120.6 0.8 copy-done.4
  121.4 0.7 copy-done.17
  122.1 0.7 copy-done.20
  122.8 0.7 copy-done.21
  123.6 0.7 copy-done.24
  124.3 0.0 reduce-scatter.2.cloned.1.call-update
  124.3 1.1 copy-done.5
  125.4 1.2 collective-permute-start.13
  126.6 2.1 %collective-permute-start.12 = (bf16[272,1152]{1,0:T(8,128)(2,1)S(1)}, bf16[272,1152]{1,0:T(8,128)(2,1)S(1)}, u32[]{:S(2)}, u32[]{:S(2)}) collective-permute-start(bf16[272,1152]{1,0:T(8,128)(2,1)S(1)} %copy-done.5), channel_id=1, source_target_pairs={{0,1},{1,0},{2,3},{3,2},{4,5},{5,4},{6,7},{7,6},{8,9},{9,8},{10,11... | collective-permute-start | bytes 1880072 | tf_op jit(solution)/shard_map/ppermute | solution.py:121
  128.7 10.7 %collective-permute-done.13.refs_10_ = bf16[272,1152]{1,0:T(8,128)(2,1)S(1)} collective-permute-done((bf16[272,1152]{1,0:T(8,128)(2,1)S(1)}, bf16[272,1152]{1,0:T(8,128)(2,1)S(1)}, u32[]{:S(2)}, u32[]{:S(2)}) %collective-permute-start.13) | collective-permute-done | bytes 626720 | tf_op jit(solution)/shard_map/ppermute | solution.py:121
  139.4 2.6 %collective-permute-start.14 = (bf16[272,1152]{1,0:T(8,128)(2,1)S(1)}, bf16[272,1152]{1,0:T(8,128)(2,1)S(1)}, u32[]{:S(2)}, u32[]{:S(2)}) collective-permute-start(bf16[272,1152]{1,0:T(8,128)(2,1)S(1)} %collective-permute-done.13.refs_10_), channel_id=1, source_target_pairs={{0,1},{1,0},{2,3},{3,2},{4,5},{5,4},{6,7},{7,6},{8,9},{9,8},{10,11... | collective-permute-start | bytes 1880072 | tf_op jit(solution)/shard_map/ppermute | solution.py:121
  142.0 1.2 collective-permute-start.10
  143.2 0.9 collective-permute-start.11
  144.1 0.7 copy-done.13
  144.9 0.1 collective-permute-start.6
  145.0 4.9 %collective-permute-done.10.refs_6_ = bf16[272,512]{1,0:T(8,128)(2,1)S(1)} collective-permute-done((bf16[272,512]{1,0:T(8,128)(2,1)}, bf16[272,512]{1,0:T(8,128)(2,1)S(1)}, u32[]{:S(2)}, u32[]{:S(2)}) %collective-permute-start.10) | collective-permute-done | bytes 278560 | tf_op jit(solution)/shard_map/ppermute | solution.py:121
  149.9 0.7 copy-done.15
  150.6 1.2 collective-permute-start.7
  151.8 5.7 %collective-permute-done.11.refs_7_ = bf16[272,512]{1,0:T(8,128)(2,1)S(1)} collective-permute-done((bf16[272,512]{1,0:T(8,128)(2,1)}, bf16[272,512]{1,0:T(8,128)(2,1)S(1)}, u32[]{:S(2)}, u32[]{:S(2)}) %collective-permute-start.11) | collective-permute-done | bytes 278560 | tf_op jit(solution)/shard_map/ppermute | solution.py:121
  157.5 0.7 copy-done.18
  158.2 0.1 convert_element_type.31
  158.3 9.3 %all_to_all.15 = bf16[8,1,64]{2,1,0:T(2,128)(2,1)S(1)} all-to-all(bf16[8,1,64]{2,1,0:T(2,128)(2,1)S(1)} %convert_element_type.31), channel_id=1, replica_groups=mesh['expert'=8,'dp'=4] {'expert'}, dimensions={0} | all-to-all | bytes 2048 | tf_op jit(solution)/shard_map/all_to_all | solution.py:184
  167.6 0.6 fusion.3
  168.2 0.6 collective-permute-done.8.refs_3_
  168.8 1.0 copy-done.14
  169.7 1.0 copy-done.16
  170.7 1.0 copy-done.19
  171.7 1.0 copy-done.23
  172.6 1.0 copy-done.25
  173.6 5.3 %shard_map.95 = (f32[512,768]{1,0:T(8,128)}, f32[512,384]{1,0:T(8,128)}) custom-call(bf16[272,512]{1,0:T(8,128)(2,1)S(1)} %copy-done.23, bf16[272,512]{1,0:T(8,128)(2,1)} %collective-permute-done.6.refs_1_, bf16[272,512]{1,0:T(8,128)(2,1)} %collective-permute-done.7.refs_2_, bf16[272,512]{1,0:T(8,128)(2,1)} %collective-permute-done.8.refs_3_, ...), custom_call_target="tpu_custom_call" | custom-call | flops 1283457024 | bytes 7094272 | tf_op jit(solution)/shard_map/pallas_call | solution.py:110
  178.8 11.1 %reduce-scatter.2.cloned.1.call-done = bf16[64,2048]{1,0:T(8,128)(2,1)} async-done(((bf16[512,2048]{1,0:T(8,128)(2,1)}), bf16[64,2048]{1,0:T(8,128)(2,1)}) %reduce-scatter.2.cloned.1.call-update) | async-done | bytes 262160 | tf_op jit(solution)/shard_map/reduce_scatter | solution.py:183
  (52 shorter events, 0.2 us)
Async XLA Ops:
  7.2 53.3 %all-gather.5.cloned.1.call-start = ((), (), s32[]{:S(2)}) async-start(), calls=%async_computation.4 | async-start | bytes 2359296 | tf_op jit(solution)/shard_map/all_gather | solution.py:151
  7.9 102.5 %all-gather.3.cloned.1.call-start = ((), (), s32[]{:S(2)}) async-start(), calls=%async_computation.3 | async-start | bytes 2359296 | tf_op jit(solution)/shard_map/all_gather | solution.py:152
  8.6 19.7 %collective-permute-start.1 = (bf16[512,768]{1,0:T(8,128)(2,1)}, bf16[512,768]{1,0:T(8,128)(2,1)S(1)}, u32[]{:S(2)}, u32[]{:S(2)}) collective-permute-start(bf16[512,768]{1,0:T(8,128)(2,1)} %bitcast.11), channel_id=1, source_target_pairs={{0,2},{1,3},{2,0},{3,1},{4,6},{5,7},{6,4},{7,5},{8,10},{9,11},{10,... | collective-permute-start | bytes 2359304 | tf_op jit(solution)/shard_map/ppermute | solution.py:121
  10.8 43.0 %collective-permute-start = (bf16[512,768]{1,0:T(8,128)(2,1)}, bf16[512,768]{1,0:T(8,128)(2,1)S(1)}, u32[]{:S(2)}, u32[]{:S(2)}) collective-permute-start(bf16[512,768]{1,0:T(8,128)(2,1)} %bitcast.12), channel_id=1, source_target_pairs={{0,1},{1,0},{2,3},{3,2},{4,5},{5,4},{6,7},{7,6},{8,9},{9,8},{10,11... | collective-permute-start | bytes 2359304 | tf_op jit(solution)/shard_map/ppermute | solution.py:121
  28.3 25.4 %collective-permute-start.2 = (bf16[512,768]{1,0:T(8,128)(2,1)S(1)}, bf16[512,768]{1,0:T(8,128)(2,1)S(1)}, u32[]{:S(2)}, u32[]{:S(2)}) collective-permute-start(bf16[512,768]{1,0:T(8,128)(2,1)S(1)} %collective-permute-done.1.refs_2_), channel_id=1, source_target_pairs={{0,1},{1,0},{2,3},{3,2},{4,5},{5,4},{6,7},{7,6},{8,9},{9,8},{10,11... | collective-permute-start | bytes 2359304 | tf_op jit(solution)/shard_map/ppermute | solution.py:121
  29.5 11.1 %collective-permute-start.4 = (bf16[512,384]{1,0:T(8,128)(2,1)}, bf16[512,384]{1,0:T(8,128)(2,1)}, u32[]{:S(2)}, u32[]{:S(2)}) collective-permute-start(bf16[512,384]{1,0:T(8,128)(2,1)} %bitcast.15), channel_id=1, source_target_pairs={{0,2},{1,3},{2,0},{3,1},{4,6},{5,7},{6,4},{7,5},{8,10},{9,11},{10,... | collective-permute-start | bytes 1179656 | tf_op jit(solution)/shard_map/ppermute | solution.py:121
  30.9 39.4 %collective-permute-start.3 = (bf16[512,384]{1,0:T(8,128)(2,1)}, bf16[512,384]{1,0:T(8,128)(2,1)}, u32[]{:S(2)}, u32[]{:S(2)}) collective-permute-start(bf16[512,384]{1,0:T(8,128)(2,1)} %bitcast.16), channel_id=1, source_target_pairs={{0,1},{1,0},{2,3},{3,2},{4,5},{5,4},{6,7},{7,6},{8,9},{9,8},{10,11... | collective-permute-start | bytes 1179656 | tf_op jit(solution)/shard_map/ppermute | solution.py:121
  40.5 29.8 %collective-permute-start.5 = (bf16[512,384]{1,0:T(8,128)(2,1)}, bf16[512,384]{1,0:T(8,128)(2,1)}, u32[]{:S(2)}, u32[]{:S(2)}) collective-permute-start(bf16[512,384]{1,0:T(8,128)(2,1)} %collective-permute-done.4.refs_6_), channel_id=1, source_target_pairs={{0,1},{1,0},{2,3},{3,2},{4,5},{5,4},{6,7},{7,6},{8,9},{9,8},{10,11... | collective-permute-start | bytes 1179656 | tf_op jit(solution)/shard_map/ppermute | solution.py:121
  42.6 11.0 %all-to-all-start = ((bf16[8,1,64]{2,1,0:T(2,128)(2,1)}), bf16[8,1,64]{2,1,0:T(2,128)(2,1)S(1)}, u32[]{:S(2)}, u32[]{:S(2)}) async-start(bf16[8,1,64]{2,1,0:T(2,128)(2,1)} %copy.13), calls=%async_computation | async-start | bytes 8192 | tf_op jit(solution)/shard_map/all_to_all | solution.py:148
  48.4 141.5 %reduce-scatter.2.cloned.1.call-start = ((), (), s32[]{:S(2)}) async-start(), calls=%async_computation.5 | async-start | bytes 2359296 | tf_op jit(solution)/shard_map/reduce_scatter | solution.py:183
  60.4 1.6 copy-start.1
  62.0 1.1 copy-start.2
  63.2 47.2 %copy-start.3 = (bf16[1,512,768]{2,1,0:T(8,128)(2,1)S(1)}, bf16[1,512,768]{2,1,0:T(8,128)(2,1)}, u32[]{:S(2)}) copy-start(bf16[1,512,768]{2,1,0:T(8,128)(2,1)} %param.10) | copy-start | bytes 2359300
  63.2 47.2 %copy-start.6 = (bf16[1,512,384]{2,1,0:T(8,128)(2,1)S(1)}, bf16[1,512,384]{2,1,0:T(8,128)(2,1)}, u32[]{:S(2)}) copy-start(bf16[1,512,384]{2,1,0:T(8,128)(2,1)} %param.11) | copy-start | bytes 1179652
  65.9 0.7 copy-start.7
  66.6 0.7 copy-start.9
  67.3 0.7 copy-start.11
  68.0 0.7 copy-start.22
  68.7 0.9 copy-start.26
  69.6 0.7 copy-start.28
  110.4 1.6 copy-start
  112.0 1.1 copy-start.27
  113.1 1.0 copy-start.29
  120.6 0.8 copy-start.4
  121.4 0.7 copy-start.17
  122.1 0.7 copy-start.20
  122.8 0.7 copy-start.21
  123.6 0.7 copy-start.24
  124.3 20.6 %copy-start.12 = (bf16[272,512]{1,0:T(8,128)(2,1)S(1)}, bf16[272,512]{1,0:T(8,128)(2,1)}, u32[]{:S(2)}) copy-start(bf16[272,512]{1,0:T(8,128)(2,1)} %copy-done.11) | copy-start | bytes 835588
  124.3 26.3 %copy-start.10 = (bf16[272,512]{1,0:T(8,128)(2,1)S(1)}, bf16[272,512]{1,0:T(8,128)(2,1)}, u32[]{:S(2)}) copy-start(bf16[272,512]{1,0:T(8,128)(2,1)} %copy-done.9) | copy-start | bytes 835588
  124.3 33.9 %copy-start.8 = (bf16[272,512]{1,0:T(8,128)(2,1)S(1)}, bf16[272,512]{1,0:T(8,128)(2,1)}, u32[]{:S(2)}) copy-start(bf16[272,512]{1,0:T(8,128)(2,1)} %copy-done.7) | copy-start | bytes 835588
  124.3 43.3 %copy-start.30 = (s32[64,4]{0,1:T(4,128)S(1)}, s32[64,4]{0,1:T(4,128)}, u32[]{:S(2)}) copy-start(s32[64,4]{0,1:T(4,128)} %param.8) | copy-start | bytes 3076
  124.3 1.2 copy-start.5
  125.4 13.9 %collective-permute-start.13 = (bf16[272,1152]{1,0:T(8,128)(2,1)S(1)}, bf16[272,1152]{1,0:T(8,128)(2,1)S(1)}, u32[]{:S(2)}, u32[]{:S(2)}) collective-permute-start(bf16[272,1152]{1,0:T(8,128)(2,1)S(1)} %copy-done.5), channel_id=1, source_target_pairs={{0,2},{1,3},{2,0},{3,1},{4,6},{5,7},{6,4},{7,5},{8,10},{9,11},{10,... | collective-permute-start | bytes 1880072 | tf_op jit(solution)/shard_map/ppermute | solution.py:121
  126.6 42.1 %collective-permute-start.12 = (bf16[272,1152]{1,0:T(8,128)(2,1)S(1)}, bf16[272,1152]{1,0:T(8,128)(2,1)S(1)}, u32[]{:S(2)}, u32[]{:S(2)}) collective-permute-start(bf16[272,1152]{1,0:T(8,128)(2,1)S(1)} %copy-done.5), channel_id=1, source_target_pairs={{0,1},{1,0},{2,3},{3,2},{4,5},{5,4},{6,7},{7,6},{8,9},{9,8},{10,11... | collective-permute-start | bytes 1880072 | tf_op jit(solution)/shard_map/ppermute | solution.py:121
  139.4 29.4 %collective-permute-start.14 = (bf16[272,1152]{1,0:T(8,128)(2,1)S(1)}, bf16[272,1152]{1,0:T(8,128)(2,1)S(1)}, u32[]{:S(2)}, u32[]{:S(2)}) collective-permute-start(bf16[272,1152]{1,0:T(8,128)(2,1)S(1)} %collective-permute-done.13.refs_10_), channel_id=1, source_target_pairs={{0,1},{1,0},{2,3},{3,2},{4,5},{5,4},{6,7},{7,6},{8,9},{9,8},{10,11... | collective-permute-start | bytes 1880072 | tf_op jit(solution)/shard_map/ppermute | solution.py:121
  142.0 2.2 %collective-permute-start.9 = (bf16[272,512]{1,0:T(8,128)(2,1)}, bf16[272,512]{1,0:T(8,128)(2,1)S(1)}, u32[]{:S(2)}, u32[]{:S(2)}) collective-permute-start(bf16[272,512]{1,0:T(8,128)(2,1)} %copy-done.21), channel_id=1, source_target_pairs={{0,1},{1,0},{2,3},{3,2},{4,5},{5,4},{6,7},{7,6},{8,9},{9,8},{10,11... | collective-permute-start | bytes 835592 | tf_op jit(solution)/shard_map/ppermute | solution.py:121
  142.0 7.9 %collective-permute-start.10 = (bf16[272,512]{1,0:T(8,128)(2,1)}, bf16[272,512]{1,0:T(8,128)(2,1)S(1)}, u32[]{:S(2)}, u32[]{:S(2)}) collective-permute-start(bf16[272,512]{1,0:T(8,128)(2,1)} %copy-done.20), channel_id=1, source_target_pairs={{0,2},{1,3},{2,0},{3,1},{4,6},{5,7},{6,4},{7,5},{8,10},{9,11},{10,... | collective-permute-start | bytes 835592 | tf_op jit(solution)/shard_map/ppermute | solution.py:121
  143.2 14.3 %collective-permute-start.11 = (bf16[272,512]{1,0:T(8,128)(2,1)}, bf16[272,512]{1,0:T(8,128)(2,1)S(1)}, u32[]{:S(2)}, u32[]{:S(2)}) collective-permute-start(bf16[272,512]{1,0:T(8,128)(2,1)} %copy-done.17), channel_id=1, source_target_pairs={{0,3},{1,2},{2,1},{3,0},{4,7},{5,6},{6,5},{7,4},{8,11},{9,10},{10,... | collective-permute-start | bytes 835592 | tf_op jit(solution)/shard_map/ppermute | solution.py:121
  144.1 0.7 copy-start.13
  144.9 23.3 %collective-permute-start.6 = (bf16[272,512]{1,0:T(8,128)(2,1)S(1)}, bf16[272,512]{1,0:T(8,128)(2,1)}, u32[]{:S(2)}, u32[]{:S(2)}) collective-permute-start(bf16[272,512]{1,0:T(8,128)(2,1)S(1)} %copy-done.12), channel_id=1, source_target_pairs={{0,1},{1,0},{2,3},{3,2},{4,5},{5,4},{6,7},{7,6},{8,9},{9,8},{10,11... | collective-permute-start | bytes 835592 | tf_op jit(solution)/shard_map/ppermute | solution.py:121
  149.9 0.7 copy-start.15
  150.6 17.6 %collective-permute-start.7 = (bf16[272,512]{1,0:T(8,128)(2,1)S(1)}, bf16[272,512]{1,0:T(8,128)(2,1)}, u32[]{:S(2)}, u32[]{:S(2)}) collective-permute-start(bf16[272,512]{1,0:T(8,128)(2,1)S(1)} %copy-done.10), channel_id=1, source_target_pairs={{0,2},{1,3},{2,0},{3,1},{4,6},{5,7},{6,4},{7,5},{8,10},{9,11},{10,... | collective-permute-start | bytes 835592 | tf_op jit(solution)/shard_map/ppermute | solution.py:121
  157.5 0.7 copy-start.18
  158.2 10.6 %collective-permute-start.8 = (bf16[272,512]{1,0:T(8,128)(2,1)S(1)}, bf16[272,512]{1,0:T(8,128)(2,1)}, u32[]{:S(2)}, u32[]{:S(2)}) collective-permute-start(bf16[272,512]{1,0:T(8,128)(2,1)S(1)} %copy-done.8), channel_id=1, source_target_pairs={{0,3},{1,2},{2,1},{3,0},{4,7},{5,6},{6,5},{7,4},{8,11},{9,10},{10,... | collective-permute-start | bytes 835592 | tf_op jit(solution)/shard_map/ppermute | solution.py:121
  168.8 1.0 copy-start.14
  169.7 1.0 copy-start.16
  170.7 1.0 copy-start.19
  171.7 1.0 copy-start.23
  172.6 1.0 copy-start.25
Sparse Core Ops, SparseCore 0:
  10.1 50.2 all-gather.4
  62.6 47.7 all-gather.2
  124.4 65.4 reduce-scatter.1

commit v2 on v0

--- a/solution.py
+++ b/solution.py
@@ -1,11 +1,549 @@
+import functools
+
 import jax
 import jax.numpy as jnp
 from jax import lax
+from jax.experimental import pallas as pl
+from jax.experimental.pallas import tpu as pltpu
 from jax.sharding import PartitionSpec as P
+
+BF16 = jnp.bfloat16
+F32 = jnp.float32
+LANES = 128
 
 
 def swish(value):
     return value * jax.nn.sigmoid(value)
+
+
+def dot(a, b):
+    return jnp.dot(a, b, preferred_element_type=F32)
+
+
+def dot_nt(a, b):
+    return lax.dot_general(a, b, (((1,), (1,)), ((), ())), preferred_element_type=F32)
+
+
+def dot_tn(a, b):
+    return lax.dot_general(a, b, (((0,), (0,)), ((), ())), preferred_element_type=F32)
+
+
+def start(source, target, sem):
+    copy = pltpu.make_async_copy(source, target, sem)
+    copy.start()
+    return copy
+
+
+def picks(weight, main):
+    token_count = weight.shape[1]
+    routed = weight != 0.0
+    first = lax.broadcasted_iota(jnp.int32, (token_count, token_count), 0)
+    second = lax.broadcasted_iota(jnp.int32, (token_count, token_count), 1)
+    upper = (first < second).astype(F32).astype(BF16)
+    rank = dot(routed.astype(F32).astype(BF16), upper)
+    rank = jnp.where(routed, rank, -1.0).astype(jnp.int32)
+    slots = lax.broadcasted_iota(jnp.int32, (main, token_count), 0)
+    mains = [(slots == rank[i : i + 1, :]).astype(F32) for i in range(weight.shape[0])]
+    tails = (rank == main).astype(F32)
+    return mains, tails
+
+
+def bounce(pairs, held, target, sems):
+    copies = [start(source, place, sems.at[i]) for i, (source, place) in enumerate(pairs)]
+    for copy in copies:
+        copy.wait()
+    start(held, target, sems.at[0]).wait()
+
+
+def route_kernel(peer_ref, named_ref, given_ref, dy_ref, joint_ref, dense_ref, held, sems):
+    count = dy_ref.shape[0]
+    copy = start(dy_ref, held.at[pl.ds(0, count)], sems.at[0])
+    named = named_ref[...]
+    given = given_ref[...].astype(F32)
+    experts = dense_ref.shape[0]
+    lines = [
+        jnp.sum(jnp.where(named == peer_ref[i], given, 0.0), axis=0, keepdims=True) for i in range(experts)
+    ]
+    dense = jnp.concatenate(lines, axis=0)
+    dense_ref[...] = dense
+    turned = jnp.concatenate(lines[experts // 2 :] + lines[: experts // 2] + [jnp.zeros_like(dense)], axis=0)
+    held[count:, :] = jnp.zeros((held.shape[0] - count, held.shape[1]), BF16)
+    held[count:, :count] = turned.astype(BF16)
+    copy.wait()
+    start(held, joint_ref, sems.at[1]).wait()
+
+
+def join_kernel(in_ref, out_ref, joint_ref, again_ref, held, sems):
+    width = in_ref.shape[1]
+    pairs = [
+        (in_ref, held.at[:, pl.ds(0, width)]),
+        (out_ref, held.at[:, pl.ds(width, out_ref.shape[1])]),
+    ]
+    copies = [start(source, place, sems.at[i]) for i, (source, place) in enumerate(pairs)]
+    for copy in copies:
+        copy.wait()
+    copies = [start(held, joint_ref, sems.at[0]), start(held, again_ref, sems.at[1])]
+    for copy in copies:
+        copy.wait()
+
+
+def after_kernel(*refs):
+    pass
+
+
+def stack_kernel(own_ref, far_ref, after_ref, joint_ref, held, sems):
+    count = own_ref.shape[0]
+    pairs = [(own_ref, held.at[pl.ds(0, count)]), (far_ref, held.at[pl.ds(count, count)])]
+    bounce(pairs, held, joint_ref, sems)
+
+
+def relay_kernel(near_a, far_a, near_b, far_b, after_ref, mid_ref, joint_ref, mid_out_ref, held, sems):
+    count, width = near_a.shape
+    pairs = []
+    for at, near, far in ((0, near_a, far_a), (count, near_b, far_b)):
+        pairs.append((near, held.at[pl.ds(at, count), pl.ds(0, width)]))
+        pairs.append((far.at[:, pl.ds(width, width)], held.at[pl.ds(at, count), pl.ds(width, width)]))
+    bounce(pairs, held, joint_ref, sems)
+
+
+def pack_kernel(first, x_ref, joint_ref, *refs):
+    count = 4
+    x, joint, block, fold, sems = refs[-5:]
+    out_refs = refs[-5 - count : -5]
+    tokens, width = x.shape
+    chunks = width // LANES
+    main = block.shape[1] // 2
+    copies = [
+        start(joint_ref.at[pl.ds(tokens, 16)], joint.at[pl.ds(tokens, 16)], sems.at[count]),
+        start(x_ref, x, sems.at[count + 1]),
+        start(joint_ref.at[pl.ds(0, tokens)], joint.at[pl.ds(0, tokens)], sems.at[count + 2]),
+    ]
+    copies.pop(0).wait()
+    weight = joint[tokens:, :LANES].astype(F32)[0:8, :tokens]
+    mains, tails = picks(weight, main)
+    mains = mains[first : first + count]
+    pick = jnp.concatenate(mains + [tails, jnp.zeros_like(tails)], axis=0).astype(BF16)
+    lane = lax.broadcasted_iota(jnp.int32, (main, LANES), 1)
+    for source, base in ((x, 0), (joint, main)):
+        copies.pop(0).wait()
+        rows = dot(pick, source[0:tokens])
+        for j in range(count):
+            block[j, base : base + main, :width] = rows[main * j : main * (j + 1)].astype(BF16)
+            line = main * count + first + j
+            for c in range(chunks):
+                fold[c : c + 1, :] = rows[line : line + 1, LANES * c : LANES * (c + 1)]
+            low = 0 if base == 0 else chunks
+            block[j, low : low + chunks, width:] = fold[...].astype(BF16)
+    copies = []
+    for j in range(count):
+        mine = weight[first + j : first + j + 1, :]
+        column = jnp.sum(mains[j] * mine, axis=1, keepdims=True)
+        last = jnp.sum(tails[first + j : first + j + 1, :] * mine, axis=1, keepdims=True)
+        block[j, main:, width:] = jnp.where(lane < LANES // 2, column, last).astype(BF16)
+        copies.append(start(block.at[j], out_refs[j], sems.at[j]))
+    for copy in copies:
+        copy.wait()
+
+
+def slice_kernel(place_ref, *refs):
+    blocks, parts = 4, 4
+    in_refs, (keep_ref, near_ref, far_ref, weight_ref) = refs[:blocks], refs[blocks : blocks + 4]
+    held, sliced, fold, sems, out_sems = refs[blocks + 4 :]
+    main = held.shape[1] // 2
+    depth = sliced.shape[2] // 2
+    width = parts * depth
+    chunks = width // LANES
+    copies = [start(in_refs[i], held.at[i], sems.at[i]) for i in range(blocks)]
+    lane = lax.broadcasted_iota(jnp.int32, (1, LANES), 1)
+    lasts = []
+    for i in range(blocks):
+        copies[i].wait()
+        for j in range(parts):
+            columns = pl.ds(pl.multiple_of(place_ref[j] * depth, depth), depth)
+            for side in range(2):
+                sliced[j, main * i : main * (i + 1), side * depth : (side + 1) * depth] = held[
+                    i, side * main : (side + 1) * main, columns
+                ]
+        for side in range(2):
+            fold[side, chunks * i : chunks * (i + 1), :] = held[
+                i, side * chunks : (side + 1) * chunks, width:
+            ].astype(F32)
+        weights = held[i, main:, width:].astype(F32)
+        weight_ref[main * i : main * (i + 1), :] = weights
+        last = jnp.sum(jnp.where(lane == LANES - 1, weights[0:1, :], 0.0), axis=1, keepdims=True)
+        lasts.append(jnp.broadcast_to(last, (1, LANES)))
+    weight_ref[main * blocks :, :] = jnp.concatenate(lasts + [jnp.zeros((16 - blocks, LANES), F32)], axis=0)
+    each = chunks // parts
+    for j in range(parts):
+        for side in range(2):
+            for q in range(each):
+                tail = fold[side, pl.ds(place_ref[j] * each + q, blocks, stride=chunks), :]
+                tail = jnp.concatenate([tail, jnp.zeros((16 - blocks, LANES), F32)], axis=0).astype(BF16)
+                at = side * depth + q * LANES
+                sliced[j, main * blocks :, at : at + LANES] = tail
+    targets = [keep_ref, near_ref, far_ref.at[:, pl.ds(0, 2 * depth)], far_ref.at[:, pl.ds(2 * depth, 2 * depth)]]
+    copies = [start(sliced.at[j], targets[j], out_sems.at[j]) for j in range(parts)]
+    for copy in copies:
+        copy.wait()
+
+
+def main_kernel(early, place_ref, w_ref, *refs):
+    blocks, parts = 4, 4
+    weights = refs[:parts]
+    keep_ref, near_ref, far_ref = refs[parts : parts + 3]
+    x, dy, mid, back, tail, fold, sems, out_sems = refs[-8:]
+    mid_ref, back_refs = refs[-9 - blocks], refs[-8 - blocks : -8]
+    width = x.shape[1]
+    depth = width // parts
+    row_refs = [keep_ref, near_ref, far_ref.at[:, pl.ds(0, 2 * depth)], far_ref.at[:, pl.ds(2 * depth, 2 * depth)]]
+    hidden_width = mid.shape[1] // 3
+    main = back.shape[1]
+    chunks = width // LANES
+    total = x.shape[0]
+    loads = []
+    for j in range(parts):
+        at = pl.ds(j * depth, depth)
+        loads.append(start(row_refs[j].at[:, pl.ds(0, depth)], x.at[:, at], sems.at[0, j]))
+        loads.append(start(row_refs[j].at[:, pl.ds(depth, depth)], dy.at[:, at], sems.at[1, j]))
+    if early:
+        start(refs[parts + 3], mid.at[pl.ds(0, early)], sems.at[2, 0]).wait()
+    pre = jnp.zeros((total, 2 * hidden_width), F32)
+    grad = jnp.zeros((total, hidden_width), F32)
+    for j in range(parts):
+        at = slice(j * depth, (j + 1) * depth)
+        loads.pop(0).wait()
+        pre += dot(x[:, at], weights[j][:, : 2 * hidden_width])
+        loads.pop(0).wait()
+        grad += dot(dy[:, at], weights[j][:, 2 * hidden_width :])
+    weight = w_ref[:, 0:1]
+    gate_pre = pre[:, :hidden_width]
+    up_pre = pre[:, hidden_width:]
+    sig = jax.nn.sigmoid(gate_pre)
+    act = gate_pre * sig
+    hidden = (act * up_pre).astype(BF16).astype(F32)
+    route = jnp.sum(hidden * grad, axis=1, keepdims=True)
+    grad_hidden = weight * grad
+    grad_gate = grad_hidden * up_pre * sig * (1.0 + gate_pre * (1.0 - sig))
+    mid[early:, :hidden_width] = grad_gate.astype(BF16)
+    mid[early:, hidden_width : 2 * hidden_width] = (grad_hidden * act).astype(BF16)
+    mid[early:, 2 * hidden_width :] = (weight * hidden).astype(BF16)
+    copies = [start(mid, mid_ref, out_sems.at[blocks])]
+    for j in range(parts):
+        columns = pl.ds(pl.multiple_of(place_ref[j] * depth, depth), depth)
+        part = dot_nt(mid[early:, : 2 * hidden_width], weights[j][:, : 2 * hidden_width])
+        tail[:, columns] = part[main * blocks :]
+        part = part.astype(BF16)
+        for i in range(blocks):
+            back[i, :, columns] = part[main * i : main * (i + 1)]
+    row = lax.broadcasted_iota(jnp.int32, (main, LANES), 0)
+    lane = lax.broadcasted_iota(jnp.int32, (main, LANES), 1)
+    for i in range(blocks):
+        for c in range(chunks):
+            fold[c : c + 1, :] = tail[i : i + 1, LANES * c : LANES * (c + 1)]
+        back[i, :chunks, width:] = fold[...].astype(BF16)
+        mine = jnp.where(row == lane, route[main * i : main * (i + 1)], 0.0)
+        mine = jnp.sum(mine, axis=0, keepdims=True)
+        mine = jnp.where(lane[0:1] == main, route[main * blocks + i : main * blocks + i + 1], mine)
+        back[i, chunks:, width:] = jnp.broadcast_to(mine, (main - chunks, LANES)).astype(BF16)
+        copies.append(start(back.at[i], back_refs[i], out_sems.at[i]))
+    for copy in copies:
+        copy.wait()
+
+
+def unpack_sum(weight, block_refs, held, rows, fold, sems):
+    count = len(block_refs)
+    main = held.shape[1]
+    width = rows.shape[1]
+    chunks = width // LANES
+    copies = [start(block_refs[j], held.at[j], sems.at[j]) for j in range(count)]
+    mains, tails = picks(weight, main)
+    mains = mains[:count]
+    pick = jnp.concatenate(mains + [tails, jnp.zeros_like(tails)], axis=0).astype(BF16)
+    lane = lax.broadcasted_iota(jnp.int32, (1, LANES), 1)
+    routes = []
+    for j in range(count):
+        copies[j].wait()
+        rows[main * j : main * (j + 1), :] = held[j, :, :width]
+        fold[chunks * j : chunks * (j + 1), :] = held[j, :chunks, width:].astype(F32)
+        mine = held[j, chunks:, width:].astype(F32)
+        dense = dot(mine[:, :main].astype(BF16), mains[j].astype(BF16))[0:1, :]
+        last = jnp.sum(jnp.where(lane == main, mine[0:1, :], 0.0), axis=1, keepdims=True)
+        routes.append(dense + last * tails[j : j + 1, :])
+    for c in range(chunks):
+        tail = fold[pl.ds(c, count, stride=chunks), :]
+        tail = jnp.concatenate([tail, jnp.zeros((16 - count, LANES), F32)], axis=0).astype(BF16)
+        rows[main * count :, LANES * c : LANES * (c + 1)] = tail
+    return dot_tn(pick, rows[...]), routes
+
+
+def relay_sum_kernel(joint_ref, b0, b1, b2, b3, out_ref, given, held, rows, fold, total, sems):
+    tokens, width = total.shape[0], rows.shape[1]
+    start(joint_ref.at[pl.ds(tokens, 16), pl.ds(0, LANES)], given, sems.at[4]).wait()
+    weight = given[...].astype(F32)[0:8, :tokens]
+    summed, routes = unpack_sum(weight, (b0, b1, b2, b3), held, rows, fold, sems)
+    total[:, :width] = summed.astype(BF16)
+    total[:, width:] = jnp.zeros((tokens, LANES), BF16)
+    block = jnp.concatenate(routes + [jnp.zeros((12, tokens), F32)], axis=0).astype(BF16)
+    total[0:16, width : width + tokens] = block
+    start(total, out_ref, sems.at[4]).wait()
+
+
+def combine_kernel(peer_ref, w_ref, named_ref, b0, b1, b2, b3, far_ref, grad_ref, route_ref, far, held, rows, fold, sems):
+    width = grad_ref.shape[1]
+    tokens = grad_ref.shape[0]
+    copy = start(far_ref, far, sems.at[4])
+    summed, routes = unpack_sum(w_ref[...], (b0, b1, b2, b3), held, rows, fold, sems)
+    copy.wait()
+    grad_ref[...] = (summed + far[:, :width].astype(F32)).astype(BF16)
+    others = far[0:16, width : width + tokens].astype(F32)
+    named = named_ref[...]
+    route = jnp.zeros(route_ref.shape, F32)
+    for j in range(4):
+        route = route + jnp.where(named == peer_ref[j], routes[j], 0.0)
+        route = route + jnp.where(named == peer_ref[4 + j], others[j : j + 1, :], 0.0)
+    route_ref[...] = route.astype(BF16)
+
+
+def weight_kernel(keep_a, keep_b, near_ref, far_a, far_b, mid_ref, mid_near_ref, mid_far_ref, in_ref, out_ref, rows, mids, sems):
+    depth, hidden_width = out_ref.shape
+    count = keep_a.shape[0]
+    span, other = pl.ds(0, 2 * depth), pl.ds(2 * depth, 2 * depth)
+    copies = []
+    row_refs = [keep_a, keep_b, near_ref.at[:, span], far_a.at[:, span], far_b.at[:, span], near_ref.at[:, other]]
+    at = 0
+    for i, ref in enumerate(row_refs):
+        copies.append(start(ref, rows.at[pl.ds(at, ref.shape[0])], sems.at[0, i]))
+        at += ref.shape[0]
+    both = 2 * count
+    mid_refs = [mid_ref, mid_near_ref.at[pl.ds(0, both)], mid_far_ref, mid_near_ref.at[pl.ds(both, both)]]
+    for j, ref in enumerate(mid_refs):
+        copies.append(start(ref, mids.at[pl.ds(both * j, both)], sems.at[1, j]))
+    for copy in copies:
+        copy.wait()
+    in_ref[...] = dot_tn(rows[:, :depth], mids[:, : 2 * hidden_width])
+    out_ref[...] = dot_tn(rows[:, depth:], mids[:, 2 * hidden_width :])
+
+
+def call(kernel, outs, smem, vmem, hbm, scratch, flops, hbm_outs, mib=20, aliases=None):
+    on_vmem = pl.BlockSpec(memory_space=pltpu.VMEM)
+    on_hbm = pl.BlockSpec(memory_space=pltpu.HBM)
+    on_smem = pl.BlockSpec(memory_space=pltpu.SMEM)
+    outs = [jax.ShapeDtypeStruct(shape, kind) for shape, kind in outs]
+    moved = sum(a.size * a.dtype.itemsize for a in list(vmem) + list(hbm) + outs)
+    return pl.pallas_call(
+        kernel,
+        out_shape=tuple(outs),
+        in_specs=[on_smem] * len(smem) + [on_vmem] * len(vmem) + [on_hbm] * len(hbm),
+        out_specs=tuple([on_hbm] * hbm_outs + [on_vmem] * (len(outs) - hbm_outs)),
+        scratch_shapes=scratch,
+        compiler_params=pltpu.CompilerParams(vmem_limit_bytes=mib * 1024 * 1024),
+        cost_estimate=pl.CostEstimate(flops=flops, bytes_accessed=moved, transcendentals=0),
+        input_output_aliases=aliases or {},
+    )(*smem, *vmem, *hbm)
+
+
+def swap(value, axis, mask):
+    return lax.ppermute(value, axis, [(i, i ^ mask) for i in range(lax.axis_size(axis))])
+
+
+def on_device_packed(tokens, grad_out, route_expert, route_weight, gate_up_weight, down_weight):
+    token_count, width = tokens.shape
+    blocks, parts, half = 8, 4, 4
+    hidden_width = down_weight.shape[2]
+    depth = width // parts
+    chunks = width // LANES
+    main = block_rows(token_count, route_expert.shape[1], blocks) // 16 * 16
+    rows = main * half + 16
+
+    peers = lax.axis_index("expert") ^ jnp.arange(blocks, dtype=jnp.int32)
+    places = lax.axis_index("dp") ^ jnp.arange(parts, dtype=jnp.int32)
+    named = route_expert.T
+    far_tokens = swap(tokens, "expert", half)
+    joint, dense = call(
+        route_kernel,
+        [((token_count + 16, width), BF16), ((blocks, token_count), F32)],
+        [peers],
+        [named, route_weight.T],
+        [grad_out],
+        [pltpu.VMEM((token_count + 16, width), BF16), pltpu.SemaphoreType.DMA((2,))],
+        0,
+        1,
+    )
+    far_joint = swap(joint, "expert", half)
+
+    def stack(own, far, after):
+        (joined,) = call(
+            stack_kernel,
+            [((2 * own.shape[0], own.shape[1]), BF16)],
+            [],
+            [],
+            [own, far, after],
+            [pltpu.VMEM((2 * own.shape[0], own.shape[1]), BF16), pltpu.SemaphoreType.DMA((2,))],
+            0,
+            1,
+        )
+        return joined
+
+    def pack(first, x, value, after):
+        packed = call(
+            functools.partial(pack_kernel, first),
+            [((2 * main, width + LANES), BF16)] * half,
+            [],
+            [],
+            [x, value, *after],
+            [
+                pltpu.VMEM((token_count, width), BF16),
+                pltpu.VMEM((token_count + 16, width), BF16),
+                pltpu.VMEM((half, 2 * main, width + LANES), BF16),
+                pltpu.VMEM((chunks, LANES), F32),
+                pltpu.SemaphoreType.DMA((half + 3,)),
+            ],
+            4 * (half * main + 16) * token_count * width,
+            half,
+        )
+        return [packed[0]] + [swap(packed[j], "expert", j) for j in range(1, half)]
+
+    own = pack(half, tokens, joint, [])
+    weights, again = call(
+        join_kernel,
+        [((depth, 3 * hidden_width), BF16)] * 2,
+        [],
+        [],
+        [gate_up_weight[0], down_weight[0]],
+        [pltpu.VMEM((depth, 3 * hidden_width), BF16), pltpu.SemaphoreType.DMA((2,))],
+        0,
+        2,
+    )
+    far_weights = swap(weights, "dp", 2)
+    far = pack(0, far_tokens, far_joint, own[1:])
+
+    again, far_weights = call(
+        after_kernel,
+        [(again.shape, BF16), (far_weights.shape, BF16)],
+        [],
+        [],
+        [again, far_weights, far[0]],
+        [],
+        0,
+        2,
+        aliases={0: 0, 1: 1},
+    )
+    weight_parts = [again, swap(again, "dp", 1), far_weights, swap(far_weights, "dp", 1)]
+
+    def sliced(packed):
+        return call(
+            slice_kernel,
+            [
+                ((rows, 2 * depth), BF16),
+                ((rows, 2 * depth), BF16),
+                ((rows, 4 * depth), BF16),
+                ((rows, LANES), F32),
+            ],
+            [places],
+            [],
+            packed,
+            [
+                pltpu.VMEM((half, 2 * main, width + LANES), BF16),
+                pltpu.VMEM((parts, rows, 2 * depth), BF16),
+                pltpu.VMEM((2, half * chunks, LANES), F32),
+                pltpu.SemaphoreType.DMA((half,)),
+                pltpu.SemaphoreType.DMA((parts,)),
+            ],
+            0,
+            3,
+        )
+
+    def middle(slices, weight, before):
+        early = before[0].shape[0] if before else 0
+        return call(
+            functools.partial(main_kernel, early),
+            [((early + rows, 3 * hidden_width), BF16)] + [((main, width + LANES), BF16)] * half,
+            [places],
+            [weight, *weight_parts],
+            [*slices, *before],
+            [
+                pltpu.VMEM((rows, width), BF16),
+                pltpu.VMEM((rows, width), BF16),
+                pltpu.VMEM((early + rows, 3 * hidden_width), BF16),
+                pltpu.VMEM((half, main, width + LANES), BF16),
+                pltpu.VMEM((16, width), F32),
+                pltpu.VMEM((chunks, LANES), F32),
+                pltpu.SemaphoreType.DMA((3, parts)),
+                pltpu.SemaphoreType.DMA((half + 1,)),
+            ],
+            2 * rows * width * 5 * hidden_width,
+            1 + half,
+        )
+
+    *own_slices, own_weight = sliced(own)
+    own_far = swap(own_slices[2], "dp", 2)
+    own_mid, *near_back = middle(own_slices, own_weight, [])
+    *far_slices, far_weight = sliced(far)
+    far_far = swap(far_slices[2], "dp", 2)
+    mid, *far_back = middle(far_slices, far_weight, [own_mid])
+    sum_scratch = [
+        pltpu.VMEM((half, main, width + LANES), BF16),
+        pltpu.VMEM((half * main + 16, width), BF16),
+        pltpu.VMEM((half * chunks, LANES), F32),
+    ]
+    far_back = far_back[:1] + [swap(far_back[j], "expert", j) for j in range(1, half)]
+    (partial,) = call(
+        relay_sum_kernel,
+        [((token_count, width + LANES), BF16)],
+        [],
+        [],
+        [far_joint, *far_back],
+        [pltpu.VMEM((16, LANES), BF16)]
+        + sum_scratch
+        + [pltpu.VMEM((token_count, width + LANES), BF16), pltpu.SemaphoreType.DMA((half + 1,))],
+        2 * (half * main + 16) * width * token_count,
+        1,
+    )
+    far_partial = swap(partial, "expert", half)
+    near_back = near_back[:1] + [swap(near_back[j], "expert", j) for j in range(1, half)]
+    near_rows, mid = call(
+        relay_kernel,
+        [((2 * rows, 4 * depth), BF16), (mid.shape, BF16)],
+        [],
+        [],
+        [own_slices[1], own_far, far_slices[1], far_far, partial, mid],
+        [pltpu.VMEM((2 * rows, 4 * depth), BF16), pltpu.SemaphoreType.DMA((4,))],
+        0,
+        2,
+        aliases={5: 1},
+    )
+    mid_far = swap(mid, "dp", 2)
+    near_rows = swap(near_rows, "dp", 1)
+    grad_tokens, grad_route = call(
+        combine_kernel,
+        [((token_count, width), BF16), (named.shape, BF16)],
+        [peers],
+        [dense, named],
+        [*near_back, far_partial],
+        [pltpu.VMEM((token_count, width + LANES), BF16)] + sum_scratch + [pltpu.SemaphoreType.DMA((half + 1,))],
+        2 * (half * main + 16) * width * token_count,
+        0,
+    )
+    mid_near = swap(stack(mid, mid_far, grad_route), "dp", 1)
+    grad_gate_up, grad_down = call(
+        weight_kernel,
+        [((depth, 2 * hidden_width), F32), ((depth, hidden_width), F32)],
+        [],
+        [],
+        [own_slices[0], far_slices[0], near_rows, own_far, far_far, mid, mid_near, mid_far],
+        [
+            pltpu.VMEM((2 * parts * rows, 2 * depth), BF16),
+            pltpu.VMEM((2 * parts * rows, 3 * hidden_width), BF16),
+            pltpu.SemaphoreType.DMA((2, 6)),
+        ],
+        4 * parts * rows * depth * 3 * hidden_width,
+        0,
+    )
+    return (grad_tokens, grad_route.T, grad_gate_up[None], grad_down[None])
+
+
+def block_rows(token_count, route_count, expert_total):
+    return min(token_count, (token_count * route_count + expert_total - 1) // expert_total + 1)
 
 
 def to_local(rows, group_count, local_count, capacity):
@@ -22,7 +560,7 @@
     return shaped.reshape((group_count, local_count * capacity) + tail)
 
 
-def on_device(tokens, grad_out, route_expert, route_weight, gate_up_weight, down_weight):
+def on_device_routed(tokens, grad_out, route_expert, route_weight, gate_up_weight, down_weight):
     token_count, model_width = tokens.shape
     route_count = route_expert.shape[1]
     group_count = lax.axis_size("expert")
@@ -132,7 +670,25 @@
     return (grad_tokens, grad_route, grad_gate_up, grad_down)
 
 
+def packs(tokens, route_expert, down_weight):
+    chunks = tokens.shape[1] // LANES
+    capacity = block_rows(tokens.shape[0], route_expert.shape[1], lax.axis_size("expert"))
+    return (
+        lax.axis_size("expert") == 8
+        and lax.axis_size("dp") == 4
+        and down_weight.shape[0] == 1
+        and capacity % 16 <= 1
+        and chunks == 16
+        and 2 * chunks <= capacity < LANES // 2
+    )
+
+
 def solution(mesh):
+    def on_device(*arrays):
+        if packs(arrays[0], arrays[2], arrays[5]):
+            return on_device_packed(*arrays)
+        return on_device_routed(*arrays)
+
     return jax.shard_map(
         on_device,
         mesh=mesh,

time: 246 us -> 116 us (0.47)
  waiting for transfers between devices: 92.4 us -> 50.5 us
  local copies, waits for them, and re-layouts: 47 us -> 8.08 us
  other arithmetic: 37.2 us -> 0.01 us
  Pallas kernels: 0 us -> 29.3 us
  matrix products: 22.5 us -> 0 us
  between operations: 14 us -> 0.91 us
  starting transfers between devices: 30.5 us -> 26.5 us
    all_to_all x6 -> x0, waiting for transfers between devices: 91 us -> none  [the longest x1 28.6 us: on_device(): lax.all_to_all(send_dy.reshape(group_count, local_count * capacity, model...]
    ppermute x0 -> x23, waiting for transfers between devices: none -> 50.5 us  [swap(): lax.ppermute(value, axis, [(i, i ^ mask) for i in range(lax.axis_size(axi...]
    unnamed x1 -> x0, other arithmetic: 34.5 us -> none
    all_to_all x6 -> x0, starting transfers between devices: 30.1 us -> none  [the longest x1 6.67 us: on_device(): lax.all_to_all(rows_x, 'dp', split_axis=2, concat_axis=1, tiled=True)]
    pallas_call x0 -> x14, Pallas kernels: none -> 29.3 us  [call(): pl.pallas_call(kernel, out_shape=tuple(outs), in_specs=[on_smem] * len(sm...]
    ppermute x0 -> x23, starting transfers between devices: none -> 26.5 us  [swap(): lax.ppermute(value, axis, [(i, i ^ mask) for i in range(lax.axis_size(axi...]
    dot_general x9 -> x0, matrix products: 22.5 us -> none  [the longest x1 4.38 us: on_device(): jnp.einsum('erd,erf->def', scaled, hidden, preferred_element_type=jnp.flo...]
    another operation x5 -> x0, local copies, waits for them, and re-layouts: 11.6 us -> none  [the longest x2 8.88 us: to_local(): return shaped.reshape((local_count, group_count * capacity) + tail)]
  transfers between devices with their start and end apart: 10 -> 23, of which waited for: 6 -> 12; matrix products, arithmetic and copies ran while one was open for 37% -> 0% of each run, Pallas kernels for 0% -> 20%
where the time goes in v2:
time: 116 us; the launch traced here: 115 us
  waiting for transfers between devices  50.5 us (44%)
  Pallas kernels  29.3 us (25%)
  starting transfers between devices  26.5 us (23%)
  local copies, waits for them, and re-layouts  8.08 us (7%)
    ppermute x23, waiting for transfers between devices, swap(): lax.ppermute(value, axis, [(i, i ^ mask) for i in range(lax.axis_size(axi...  50.5 us
    pallas_call x14, Pallas kernels, call(): pl.pallas_call(kernel, out_shape=tuple(outs), in_specs=[on_smem] * len(sm...  29.3 us
    ppermute x23, starting transfers between devices, swap(): lax.ppermute(value, axis, [(i, i ^ mask) for i in range(lax.axis_size(axi...  26.5 us
    unnamed x38, local copies, waits for them, and re-layouts  8.08 us
  transfers between devices with their start and end apart: 23, of which 12 were waited for; matrix products, arithmetic and copies ran while one was open for 0% of the time, Pallas kernels for 20%

profile of v2, /device:TPU:1, one launch (start us, length us, event | category | flops | bytes accessed | tf_op | source)
XLA Modules:
  0.0 115.4 jit_solution(4385921997977734954)
XLA Ops:
  0.7 1.1 copy-done.10
  1.8 1.0 copy-done.11
  2.8 1.1 shard_map.96
  3.9 2.1 %collective-permute-start.3 = (bf16[512,1152]{1,0:T(8,128)(2,1)}, bf16[512,1152]{1,0:T(8,128)(2,1)S(1)}, u32[]{:S(2)}, u32[]{:S(2)}) collective-permute-start(bf16[512,1152]{1,0:T(8,128)(2,1)} %get-tuple-element.50), channel_id=1, source_target_pairs={{0,2},{1,3},{2,0},{3,1},{4,6},{5,7},{6,4},{7,5},{8,10},{9,11},{10,... | collective-permute-start | bytes 3538952 | tf_op jit(solution)/shard_map/ppermute | solution.py:346
  6.0 2.3 %collective-permute-start.4 = (bf16[64,2048]{1,0:T(8,128)(2,1)S(1)}, bf16[64,2048]{1,0:T(8,128)(2,1)S(1)}, u32[]{:S(2)}, u32[]{:S(2)}) collective-permute-start(bf16[64,2048]{1,0:T(8,128)(2,1)S(1)} %copy-done.15), channel_id=1, source_target_pairs={{0,16},{4,20},{8,24},{12,28},{16,0},{20,4},{24,8},{28,12},{1,17},{... | collective-permute-start | bytes 786440 | tf_op jit(solution)/shard_map/ppermute | solution.py:346
  8.4 0.7 shard_map.93
  9.1 0.1 collective-permute-start.5
  9.2 1.3 %shard_map.94 = (bf16[64,2176]{1,0:T(8,128)(2,1)S(1)}, bf16[64,2176]{1,0:T(8,128)(2,1)S(1)}, bf16[64,2176]{1,0:T(8,128)(2,1)S(1)}, bf16[64,2176]{1,0:T(8,128)(2,1)S(1)}) custom-call(bf16[64,2048]{1,0:T(8,128)(2,1)S(1)} %copy-done.15, bf16[80,2048]{1,0:T(8,128)(2,1)S(1)} %get-tuple-element.43.joint_ref), custom_call_target="tpu_custom_call" | custom-call | flops 75497472 | bytes 1703936 | tf_op jit(solution)/shard_map/pallas_call | solution.py:333
  10.6 0.7 copy-done.12
  11.3 1.2 %collective-permute-start = (bf16[64,2176]{1,0:T(8,128)(2,1)S(1)}, bf16[64,2176]{1,0:T(8,128)(2,1)S(1)}, u32[]{:S(2)}, u32[]{:S(2)}) collective-permute-start(bf16[64,2176]{1,0:T(8,128)(2,1)S(1)} %get-tuple-element.45), channel_id=1, source_target_pairs={{0,4},{4,0},{8,12},{12,8},{16,20},{20,16},{24,28},{28,24},{1,5},{5... | collective-permute-start | bytes 835592 | tf_op jit(solution)/shard_map/ppermute | solution.py:346
  12.5 1.3 %collective-permute-start.1 = (bf16[64,2176]{1,0:T(8,128)(2,1)S(1)}, bf16[64,2176]{1,0:T(8,128)(2,1)S(1)}, u32[]{:S(2)}, u32[]{:S(2)}) collective-permute-start(bf16[64,2176]{1,0:T(8,128)(2,1)S(1)} %get-tuple-element.46), channel_id=1, source_target_pairs={{0,8},{4,12},{8,0},{12,4},{16,24},{20,28},{24,16},{28,20},{1,9},{5... | collective-permute-start | bytes 835592 | tf_op jit(solution)/shard_map/ppermute | solution.py:346
  13.8 12.9 %collective-permute-done.4.x_ref = bf16[64,2048]{1,0:T(8,128)(2,1)S(1)} collective-permute-done((bf16[64,2048]{1,0:T(8,128)(2,1)S(1)}, bf16[64,2048]{1,0:T(8,128)(2,1)S(1)}, u32[]{:S(2)}, u32[]{:S(2)}) %collective-permute-start.4) | collective-permute-done | bytes 262176 | tf_op jit(solution)/shard_map/ppermute | solution.py:346
  26.7 2.4 %collective-permute-start.2 = (bf16[64,2176]{1,0:T(8,128)(2,1)S(1)}, bf16[64,2176]{1,0:T(8,128)(2,1)S(1)}, u32[]{:S(2)}, u32[]{:S(2)}) collective-permute-start(bf16[64,2176]{1,0:T(8,128)(2,1)S(1)} %get-tuple-element.47), channel_id=1, source_target_pairs={{0,12},{4,8},{8,4},{12,0},{16,28},{20,24},{24,20},{28,16},{1,13},{... | collective-permute-start | bytes 835592 | tf_op jit(solution)/shard_map/ppermute | solution.py:346
  29.2 0.0 collective-permute-done.refs_1_.refs_0_
  29.2 0.0 collective-permute-done.1.refs_2_.refs_1_
  29.2 12.6 %collective-permute-done.2.refs_3_.refs_2_ = bf16[64,2176]{1,0:T(8,128)(2,1)S(1)} collective-permute-done((bf16[64,2176]{1,0:T(8,128)(2,1)S(1)}, bf16[64,2176]{1,0:T(8,128)(2,1)S(1)}, u32[]{:S(2)}, u32[]{:S(2)}) %collective-permute-start.2) | collective-permute-done | bytes 278560 | tf_op jit(solution)/shard_map/ppermute | solution.py:346
  41.8 0.0 collective-permute-done.5.joint_ref
  41.8 2.0 %shard_map.97 = (bf16[64,2176]{1,0:T(8,128)(2,1)S(1)}, bf16[64,2176]{1,0:T(8,128)(2,1)}, bf16[64,2176]{1,0:T(8,128)(2,1)}, bf16[64,2176]{1,0:T(8,128)(2,1)}) custom-call(bf16[64,2048]{1,0:T(8,128)(2,1)S(1)} %collective-permute-done.4.x_ref, bf16[80,2048]{1,0:T(8,128)(2,1)S(1)} %collective-permute-done.5.joint_ref, ...), custom_call_target="tpu_custom_call" | custom-call | flops 75497472 | bytes 2539520 | tf_op jit(solution)/shard_map/pallas_call | solution.py:333
  43.8 0.6 copy-done.2
  44.5 0.5 collective-permute-start.6
  45.0 0.0 collective-permute-start.7
  45.0 0.2 collective-permute-start.11
  45.2 0.0 collective-permute-start.12
  45.2 2.4 %collective-permute-start.13 = (bf16[64,2176]{1,0:T(8,128)(2,1)}, bf16[64,2176]{1,0:T(8,128)(2,1)}, u32[]{:S(2)}, u32[]{:S(2)}) collective-permute-start(bf16[64,2176]{1,0:T(8,128)(2,1)} %get-tuple-element.63), channel_id=1, source_target_pairs={{0,12},{4,8},{8,4},{12,0},{16,28},{20,24},{24,20},{28,16},{1,13},{... | collective-permute-start | bytes 835592 | tf_op jit(solution)/shard_map/ppermute | solution.py:346
  47.6 1.0 copy-done.5
  48.6 1.0 copy-done.7
  49.6 1.0 copy-done.9
  50.6 1.0 copy-done.13
  51.5 1.3 %shard_map.95 = (bf16[144,1024]{1,0:T(8,128)(2,1)S(1)}, bf16[144,1024]{1,0:T(8,128)(2,1)S(1)}, bf16[144,2048]{1,0:T(8,128)(2,1)S(1)}, f32[144,128]{1,0:T(8,128)S(1)}) custom-call(s32[4]{0:T(128)S(1)} %iota_xor_fusion.place_ref, bf16[64,2176]{1,0:T(8,128)(2,1)S(1)} %copy-done.13, bf16[64,2176]{1,0:T(8,128)(2,1)S(1)} %copy-done.5, ...), custom_call_target="tpu_custom_call" | custom-call | bytes 2367488 | tf_op jit(solution)/shard_map/pallas_call | solution.py:333
  52.8 0.3 collective-permute-done.11.refs_1_
  53.0 0.2 collective-permute-start.18
  53.3 6.6 %collective-permute-done.13.refs_3_ = bf16[64,2176]{1,0:T(8,128)(2,1)} collective-permute-done((bf16[64,2176]{1,0:T(8,128)(2,1)}, bf16[64,2176]{1,0:T(8,128)(2,1)}, u32[]{:S(2)}, u32[]{:S(2)}) %collective-permute-start.13) | collective-permute-done | bytes 278560 | tf_op jit(solution)/shard_map/ppermute | solution.py:346
  59.9 2.0 %shard_map.100 = (bf16[144,1024]{1,0:T(8,128)(2,1)S(1)}, bf16[144,1024]{1,0:T(8,128)(2,1)S(1)}, bf16[144,2048]{1,0:T(8,128)(2,1)S(1)}, f32[144,128]{1,0:T(8,128)S(1)}) custom-call(s32[4]{0:T(128)S(1)} %iota_xor_fusion.place_ref, bf16[64,2176]{1,0:T(8,128)(2,1)S(1)} %copy-done.3, bf16[64,2176]{1,0:T(8,128)(2,1)} %collective-permute-done.11.refs_1_, ...), custom_call_target="tpu_custom_call" | custom-call | bytes 2367488 | tf_op jit(solution)/shard_map/pallas_call | solution.py:333
  61.9 0.3 collective-permute-start.19
  62.2 5.6 %shard_map.99 = (bf16[144,1152]{1,0:T(8,128)(2,1)S(1)}, bf16[32,2176]{1,0:T(8,128)(2,1)S(1)}, bf16[32,2176]{1,0:T(8,128)(2,1)S(1)}, bf16[32,2176]{1,0:T(8,128)(2,1)S(1)}, bf16[32,2176]{1,0:T(8,128)(2,1)S(1)}) custom-call(s32[4]{0:T(128)S(1)} %iota_xor_fusion.place_ref, f32[144,128]{1,0:T(8,128)S(1)} %get-tuple-element.48.w_ref, ...), custom_call_target="tpu_custom_call" | custom-call | flops 1132462080 | bytes 6860800 | tf_op jit(solution)/shard_map/pallas_call | solution.py:333
  67.8 0.0 copy-start.1
  67.8 5.8 %shard_map.101 = (bf16[288,1152]{1,0:T(8,128)(2,1)S(1)}, bf16[32,2176]{1,0:T(8,128)(2,1)S(1)}, bf16[32,2176]{1,0:T(8,128)(2,1)S(1)}, bf16[32,2176]{1,0:T(8,128)(2,1)S(1)}, bf16[32,2176]{1,0:T(8,128)(2,1)S(1)}) custom-call(s32[4]{0:T(128)S(1)} %iota_xor_fusion.place_ref, f32[144,128]{1,0:T(8,128)S(1)} %get-tuple-element.64.w_ref, ...), custom_call_target="tpu_custom_call" | custom-call | flops 1132462080 | bytes 7524352 | tf_op jit(solution)/shard_map/pallas_call | solution.py:333
  73.7 0.3 collective-permute-start.14
  73.9 0.3 collective-permute-start.15
  74.2 2.1 %collective-permute-start.16 = (bf16[32,2176]{1,0:T(8,128)(2,1)S(1)}, bf16[32,2176]{1,0:T(8,128)(2,1)S(1)}, u32[]{:S(2)}, u32[]{:S(2)}) collective-permute-start(bf16[32,2176]{1,0:T(8,128)(2,1)S(1)} %get-tuple-element.72), channel_id=1, source_target_pairs={{0,12},{4,8},{8,4},{12,0},{16,28},{20,24},{24,20},{28,16},{1,13},{... | collective-permute-start | bytes 417800 | tf_op jit(solution)/shard_map/ppermute | solution.py:346
  76.4 1.6 %collective-permute-done.14.b1 = bf16[32,2176]{1,0:T(8,128)(2,1)S(1)} collective-permute-done((bf16[32,2176]{1,0:T(8,128)(2,1)S(1)}, bf16[32,2176]{1,0:T(8,128)(2,1)S(1)}, u32[]{:S(2)}, u32[]{:S(2)}) %collective-permute-start.14) | collective-permute-done | bytes 139296 | tf_op jit(solution)/shard_map/ppermute | solution.py:346
  77.9 0.2 collective-permute-done.15.b2
  78.1 2.5 %collective-permute-done.16.b3 = bf16[32,2176]{1,0:T(8,128)(2,1)S(1)} collective-permute-done((bf16[32,2176]{1,0:T(8,128)(2,1)S(1)}, bf16[32,2176]{1,0:T(8,128)(2,1)S(1)}, u32[]{:S(2)}, u32[]{:S(2)}) %collective-permute-start.16) | collective-permute-done | bytes 139296 | tf_op jit(solution)/shard_map/ppermute | solution.py:346
  80.6 1.6 %shard_map.102.after_ref = bf16[64,2176]{1,0:T(8,128)(2,1)S(1)} custom-call(bf16[80,2048]{1,0:T(8,128)(2,1)S(1)} %copy-done.1, bf16[32,2176]{1,0:T(8,128)(2,1)S(1)} %get-tuple-element.69.b0, bf16[32,2176]{1,0:T(8,128)(2,1)S(1)} %collective-permute-done.14.b1, bf16[32,2176]{1,0:T(8,128)(2,1)S(1)} %collective-permute-done.15.b2, ...), custom_call_target="tpu_custom_call" | custom-call | flops 37748736 | bytes 1163264 | tf_op jit(solution)/shard_map/pallas_call | solution.py:333
  82.2 0.0 collective-permute-done.18.far_a
  82.2 0.4 shard_map.104
  82.6 1.3 %collective-permute-start.21 = (bf16[288,1152]{1,0:T(8,128)(2,1)S(1)}, bf16[288,1152]{1,0:T(8,128)(2,1)S(1)}, u32[]{:S(2)}, u32[]{:S(2)}) collective-permute-start(bf16[288,1152]{1,0:T(8,128)(2,1)S(1)} %get-tuple-element.77.own_ref.mid_ref), channel_id=1, source_target_pairs={{0,2},{1,3},{2,0},{3,1},{4,6},{5,7},{6,4},{7,5},{8,10},{9,11},{10,... | collective-permute-start | bytes 1990664 | tf_op jit(solution)/shard_map/ppermute | solution.py:346
  83.9 2.6 %collective-permute-start.17 = (bf16[64,2176]{1,0:T(8,128)(2,1)S(1)}, bf16[64,2176]{1,0:T(8,128)(2,1)S(1)}, u32[]{:S(2)}, u32[]{:S(2)}) collective-permute-start(bf16[64,2176]{1,0:T(8,128)(2,1)S(1)} %shard_map.102.after_ref), channel_id=1, source_target_pairs={{0,16},{4,20},{8,24},{12,28},{16,0},{20,4},{24,8},{28,12},{1,17},{... | collective-permute-start | bytes 835592 | tf_op jit(solution)/shard_map/ppermute | solution.py:346
  86.5 1.5 %collective-permute-start.8 = (bf16[32,2176]{1,0:T(8,128)(2,1)S(1)}, bf16[32,2176]{1,0:T(8,128)(2,1)S(1)}, u32[]{:S(2)}, u32[]{:S(2)}) collective-permute-start(bf16[32,2176]{1,0:T(8,128)(2,1)S(1)} %get-tuple-element.58), channel_id=1, source_target_pairs={{0,4},{4,0},{8,12},{12,8},{16,20},{20,16},{24,28},{28,24},{1,5},{5... | collective-permute-start | bytes 417800 | tf_op jit(solution)/shard_map/ppermute | solution.py:346
  88.0 0.0 collective-permute-start.9
  88.1 1.2 %collective-permute-start.10 = (bf16[32,2176]{1,0:T(8,128)(2,1)S(1)}, bf16[32,2176]{1,0:T(8,128)(2,1)S(1)}, u32[]{:S(2)}, u32[]{:S(2)}) collective-permute-start(bf16[32,2176]{1,0:T(8,128)(2,1)S(1)} %get-tuple-element.60), channel_id=1, source_target_pairs={{0,12},{4,8},{8,4},{12,0},{16,28},{20,24},{24,20},{28,16},{1,13},{... | collective-permute-start | bytes 417800 | tf_op jit(solution)/shard_map/ppermute | solution.py:346
  89.2 1.6 %collective-permute-done.8.b1 = bf16[32,2176]{1,0:T(8,128)(2,1)S(1)} collective-permute-done((bf16[32,2176]{1,0:T(8,128)(2,1)S(1)}, bf16[32,2176]{1,0:T(8,128)(2,1)S(1)}, u32[]{:S(2)}, u32[]{:S(2)}) %collective-permute-start.8) | collective-permute-done | bytes 139296 | tf_op jit(solution)/shard_map/ppermute | solution.py:346
  90.8 3.0 %collective-permute-done.9.b2 = bf16[32,2176]{1,0:T(8,128)(2,1)S(1)} collective-permute-done((bf16[32,2176]{1,0:T(8,128)(2,1)S(1)}, bf16[32,2176]{1,0:T(8,128)(2,1)S(1)}, u32[]{:S(2)}, u32[]{:S(2)}) %collective-permute-start.9) | collective-permute-done | bytes 139296 | tf_op jit(solution)/shard_map/ppermute | solution.py:346
  93.8 1.3 %collective-permute-done.10.b3 = bf16[32,2176]{1,0:T(8,128)(2,1)S(1)} collective-permute-done((bf16[32,2176]{1,0:T(8,128)(2,1)S(1)}, bf16[32,2176]{1,0:T(8,128)(2,1)S(1)}, u32[]{:S(2)}, u32[]{:S(2)}) %collective-permute-start.10) | collective-permute-done | bytes 139296 | tf_op jit(solution)/shard_map/ppermute | solution.py:346
  95.2 3.6 %collective-permute-done.17.far_ref = bf16[64,2176]{1,0:T(8,128)(2,1)S(1)} collective-permute-done((bf16[64,2176]{1,0:T(8,128)(2,1)S(1)}, bf16[64,2176]{1,0:T(8,128)(2,1)S(1)}, u32[]{:S(2)}, u32[]{:S(2)}) %collective-permute-start.17) | collective-permute-done | bytes 278560 | tf_op jit(solution)/shard_map/ppermute | solution.py:346
  98.8 3.0 %shard_map.103 = (bf16[64,2048]{1,0:T(8,128)(2,1)}, bf16[4,64]{1,0:T(4,128)(2,1)}) custom-call(s32[8]{0:T(128)S(1)} %iota_xor_fusion.1.peer_ref, f32[8,64]{1,0:T(8,128)S(1)} %get-tuple-element.42.w_ref, s32[4,64]{1,0:T(4,128)S(1)} %bitcast.10, bf16[32,2176]{1,0:T(8,128)(2,1)S(1)} %get-tuple-element.57.b0, bf16[32,2176]{1,0:T(8,128)(2,1)S(1)} %collective-permute-done.8.b1, ...), custom_call_target="tpu_custom_call" | custom-call | flops 37748736 | bytes 1101312 | tf_op jit(solution)/shard_map/pallas_call | solution.py:333
  101.8 0.0 collective-permute-done.21.far_ref.mid_far_ref
  101.8 0.0 copy-start.17
  101.8 0.7 copy-done.17
  102.5 0.6 shard_map.105
  103.0 4.0 %collective-permute-start.22 = (bf16[576,1152]{1,0:T(8,128)(2,1)S(1)}, bf16[576,1152]{1,0:T(8,128)(2,1)S(1)}, u32[]{:S(2)}, u32[]{:S(2)}) collective-permute-start(bf16[576,1152]{1,0:T(8,128)(2,1)S(1)} %shard_map.105), channel_id=1, source_target_pairs={{0,1},{1,0},{2,3},{3,2},{4,5},{5,4},{6,7},{7,6},{8,9},{9,8},{10,11... | collective-permute-start | bytes 3981320 | tf_op jit(solution)/shard_map/ppermute | solution.py:346
  107.0 0.1 collective-permute-start.20
  107.1 4.3 %collective-permute-done.20.near_ref = bf16[288,2048]{1,0:T(8,128)(2,1)S(1)} collective-permute-done((bf16[288,2048]{1,0:T(8,128)(2,1)S(1)}, bf16[288,2048]{1,0:T(8,128)(2,1)S(1)}, u32[]{:S(2)}, u32[]{:S(2)}) %collective-permute-start.20) | collective-permute-done | bytes 1179680 | tf_op jit(solution)/shard_map/ppermute | solution.py:346
  111.4 4.0 %shard_map.106 = (f32[512,768]{1,0:T(8,128)}, f32[512,384]{1,0:T(8,128)}) custom-call(bf16[144,1024]{1,0:T(8,128)(2,1)S(1)} %get-tuple-element.54.refs_4_.keep_a, bf16[144,1024]{1,0:T(8,128)(2,1)S(1)} %get-tuple-element.65.refs_4_.keep_b, bf16[288,2048]{1,0:T(8,128)(2,1)S(1)} %collective-permute-done.20.near_ref, ...), custom_call_target="tpu_custom_call" | custom-call | flops 1358954496 | bytes 7962624 | tf_op jit(solution)/shard_map/pallas_call | solution.py:333
  (36 shorter events, 0.1 us)
Async XLA Ops:
  0.6 7.7 %copy-start.16 = (s32[64,4]{0,1:T(4,128)S(1)}, s32[64,4]{0,1:T(4,128)}, u32[]{:S(2)}) copy-start(s32[64,4]{0,1:T(4,128)} %param.8) | copy-start | bytes 3076
  0.6 7.7 %copy-start.18 = (bf16[64,4]{0,1:T(4,128)(2,1)S(1)}, bf16[64,4]{0,1:T(4,128)(2,1)}, u32[]{:S(2)}) copy-start(bf16[64,4]{0,1:T(4,128)(2,1)} %param.9) | copy-start | bytes 1540
  0.7 1.1 copy-start.10
  1.8 1.0 copy-start.11
  2.8 3.2 %copy-start.15 = (bf16[64,2048]{1,0:T(8,128)(2,1)S(1)}, bf16[64,2048]{1,0:T(8,128)(2,1)}, u32[]{:S(2)}) copy-start(bf16[64,2048]{1,0:T(8,128)(2,1)} %x_ref.1) | copy-start | bytes 786436
  2.8 5.6 %copy-start.14 = (bf16[64,2048]{1,0:T(8,128)(2,1)S(1)}, bf16[64,2048]{1,0:T(8,128)(2,1)}, u32[]{:S(2)}) copy-start(bf16[64,2048]{1,0:T(8,128)(2,1)} %dy_ref.1) | copy-start | bytes 786436
  3.9 39.8 %collective-permute-start.3 = (bf16[512,1152]{1,0:T(8,128)(2,1)}, bf16[512,1152]{1,0:T(8,128)(2,1)S(1)}, u32[]{:S(2)}, u32[]{:S(2)}) collective-permute-start(bf16[512,1152]{1,0:T(8,128)(2,1)} %get-tuple-element.50), channel_id=1, source_target_pairs={{0,2},{1,3},{2,0},{3,1},{4,6},{5,7},{6,4},{7,5},{8,10},{9,11},{10,... | collective-permute-start | bytes 3538952 | tf_op jit(solution)/shard_map/ppermute | solution.py:346
  6.0 20.7 %collective-permute-start.4 = (bf16[64,2048]{1,0:T(8,128)(2,1)S(1)}, bf16[64,2048]{1,0:T(8,128)(2,1)S(1)}, u32[]{:S(2)}, u32[]{:S(2)}) collective-permute-start(bf16[64,2048]{1,0:T(8,128)(2,1)S(1)} %copy-done.15), channel_id=1, source_target_pairs={{0,16},{4,20},{8,24},{12,28},{16,0},{20,4},{24,8},{28,12},{1,17},{... | collective-permute-start | bytes 786440 | tf_op jit(solution)/shard_map/ppermute | solution.py:346
  9.1 32.7 %collective-permute-start.5 = (bf16[80,2048]{1,0:T(8,128)(2,1)S(1)}, bf16[80,2048]{1,0:T(8,128)(2,1)S(1)}, u32[]{:S(2)}, u32[]{:S(2)}) collective-permute-start(bf16[80,2048]{1,0:T(8,128)(2,1)S(1)} %get-tuple-element.43.joint_ref), channel_id=1, source_target_pairs={{0,16},{4,20},{8,24},{12,28},{16,0},{20,4},{24,8},{28,12},{1,17},{... | collective-permute-start | bytes 983048 | tf_op jit(solution)/shard_map/ppermute | solution.py:346
  10.6 0.7 copy-start.12
  11.3 17.9 %collective-permute-start = (bf16[64,2176]{1,0:T(8,128)(2,1)S(1)}, bf16[64,2176]{1,0:T(8,128)(2,1)S(1)}, u32[]{:S(2)}, u32[]{:S(2)}) collective-permute-start(bf16[64,2176]{1,0:T(8,128)(2,1)S(1)} %get-tuple-element.45), channel_id=1, source_target_pairs={{0,4},{4,0},{8,12},{12,8},{16,20},{20,16},{24,28},{28,24},{1,5},{5... | collective-permute-start | bytes 835592 | tf_op jit(solution)/shard_map/ppermute | solution.py:346
  12.5 16.7 %collective-permute-start.1 = (bf16[64,2176]{1,0:T(8,128)(2,1)S(1)}, bf16[64,2176]{1,0:T(8,128)(2,1)S(1)}, u32[]{:S(2)}, u32[]{:S(2)}) collective-permute-start(bf16[64,2176]{1,0:T(8,128)(2,1)S(1)} %get-tuple-element.46), channel_id=1, source_target_pairs={{0,8},{4,12},{8,0},{12,4},{16,24},{20,28},{24,16},{28,20},{1,9},{5... | collective-permute-start | bytes 835592 | tf_op jit(solution)/shard_map/ppermute | solution.py:346
  26.7 15.0 %collective-permute-start.2 = (bf16[64,2176]{1,0:T(8,128)(2,1)S(1)}, bf16[64,2176]{1,0:T(8,128)(2,1)S(1)}, u32[]{:S(2)}, u32[]{:S(2)}) collective-permute-start(bf16[64,2176]{1,0:T(8,128)(2,1)S(1)} %get-tuple-element.47), channel_id=1, source_target_pairs={{0,12},{4,8},{8,4},{12,0},{16,28},{20,24},{24,20},{28,16},{1,13},{... | collective-permute-start | bytes 835592 | tf_op jit(solution)/shard_map/ppermute | solution.py:346
  29.2 14.6 %copy-start.4 = (bf16[64,2176]{1,0:T(8,128)(2,1)}, bf16[64,2176]{1,0:T(8,128)(2,1)S(1)}, u32[]{:S(2)}) copy-start(bf16[64,2176]{1,0:T(8,128)(2,1)S(1)} %collective-permute-done.refs_1_.refs_0_) | copy-start | bytes 835588
  29.2 14.6 %copy-start.6 = (bf16[64,2176]{1,0:T(8,128)(2,1)}, bf16[64,2176]{1,0:T(8,128)(2,1)S(1)}, u32[]{:S(2)}) copy-start(bf16[64,2176]{1,0:T(8,128)(2,1)S(1)} %collective-permute-done.1.refs_2_.refs_1_) | copy-start | bytes 835588
  41.8 2.1 %copy-start.8 = (bf16[64,2176]{1,0:T(8,128)(2,1)}, bf16[64,2176]{1,0:T(8,128)(2,1)S(1)}, u32[]{:S(2)}) copy-start(bf16[64,2176]{1,0:T(8,128)(2,1)S(1)} %collective-permute-done.2.refs_3_.refs_2_) | copy-start | bytes 835588
  41.8 2.1 %copy-start = (bf16[80,2048]{1,0:T(8,128)(2,1)}, bf16[80,2048]{1,0:T(8,128)(2,1)S(1)}, u32[]{:S(2)}) copy-start(bf16[80,2048]{1,0:T(8,128)(2,1)S(1)} %collective-permute-done.5.joint_ref) | copy-start | bytes 983044
  43.8 0.7 copy-start.2
  44.5 17.7 %collective-permute-start.6 = (bf16[512,1152]{1,0:T(8,128)(2,1)S(1)}, bf16[512,1152]{1,0:T(8,128)(2,1)S(1)}, u32[]{:S(2)}, u32[]{:S(2)}) collective-permute-start(bf16[512,1152]{1,0:T(8,128)(2,1)S(1)} %get-tuple-element.52.refs_0_), channel_id=1, source_target_pairs={{0,1},{1,0},{2,3},{3,2},{4,5},{5,4},{6,7},{7,6},{8,9},{9,8},{10,11... | collective-permute-start | bytes 3538952 | tf_op jit(solution)/shard_map/ppermute | solution.py:346
  45.0 17.2 %collective-permute-start.7 = (bf16[512,1152]{1,0:T(8,128)(2,1)S(1)}, bf16[512,1152]{1,0:T(8,128)(2,1)}, u32[]{:S(2)}, u32[]{:S(2)}) collective-permute-start(bf16[512,1152]{1,0:T(8,128)(2,1)S(1)} %get-tuple-element.53.refs_2_), channel_id=1, source_target_pairs={{0,1},{1,0},{2,3},{3,2},{4,5},{5,4},{6,7},{7,6},{8,9},{9,8},{10,11... | collective-permute-start | bytes 3538952 | tf_op jit(solution)/shard_map/ppermute | solution.py:346
  45.0 8.1 %collective-permute-start.11 = (bf16[64,2176]{1,0:T(8,128)(2,1)}, bf16[64,2176]{1,0:T(8,128)(2,1)}, u32[]{:S(2)}, u32[]{:S(2)}) collective-permute-start(bf16[64,2176]{1,0:T(8,128)(2,1)} %get-tuple-element.61), channel_id=1, source_target_pairs={{0,4},{4,0},{8,12},{12,8},{16,20},{20,16},{24,28},{28,24},{1,5},{5... | collective-permute-start | bytes 835592 | tf_op jit(solution)/shard_map/ppermute | solution.py:346
  45.2 8.1 %collective-permute-start.12 = (bf16[64,2176]{1,0:T(8,128)(2,1)}, bf16[64,2176]{1,0:T(8,128)(2,1)}, u32[]{:S(2)}, u32[]{:S(2)}) collective-permute-start(bf16[64,2176]{1,0:T(8,128)(2,1)} %get-tuple-element.62), channel_id=1, source_target_pairs={{0,8},{4,12},{8,0},{12,4},{16,24},{20,28},{24,16},{28,20},{1,9},{5... | collective-permute-start | bytes 835592 | tf_op jit(solution)/shard_map/ppermute | solution.py:346
  45.2 14.7 %collective-permute-start.13 = (bf16[64,2176]{1,0:T(8,128)(2,1)}, bf16[64,2176]{1,0:T(8,128)(2,1)}, u32[]{:S(2)}, u32[]{:S(2)}) collective-permute-start(bf16[64,2176]{1,0:T(8,128)(2,1)} %get-tuple-element.63), channel_id=1, source_target_pairs={{0,12},{4,8},{8,4},{12,0},{16,28},{20,24},{24,20},{28,16},{1,13},{... | collective-permute-start | bytes 835592 | tf_op jit(solution)/shard_map/ppermute | solution.py:346
  47.6 12.2 %copy-start.3 = (bf16[64,2176]{1,0:T(8,128)(2,1)S(1)}, bf16[64,2176]{1,0:T(8,128)(2,1)}, u32[]{:S(2)}) copy-start(bf16[64,2176]{1,0:T(8,128)(2,1)} %copy-done.2) | copy-start | bytes 835588
  47.6 1.0 copy-start.5
  48.6 1.0 copy-start.7
  49.6 1.0 copy-start.9
  50.6 1.0 copy-start.13
  53.0 29.2 %collective-permute-start.18 = (bf16[144,2048]{1,0:T(8,128)(2,1)S(1)}, bf16[144,2048]{1,0:T(8,128)(2,1)S(1)}, u32[]{:S(2)}, u32[]{:S(2)}) collective-permute-start(bf16[144,2048]{1,0:T(8,128)(2,1)S(1)} %get-tuple-element.56.refs_6_), channel_id=1, source_target_pairs={{0,2},{1,3},{2,0},{3,1},{4,6},{5,7},{6,4},{7,5},{8,10},{9,11},{10,... | collective-permute-start | bytes 1769480 | tf_op jit(solution)/shard_map/ppermute | solution.py:346
  61.9 20.3 %collective-permute-start.19 = (bf16[144,2048]{1,0:T(8,128)(2,1)S(1)}, bf16[144,2048]{1,0:T(8,128)(2,1)S(1)}, u32[]{:S(2)}, u32[]{:S(2)}) collective-permute-start(bf16[144,2048]{1,0:T(8,128)(2,1)S(1)} %get-tuple-element.67.refs_6_), channel_id=1, source_target_pairs={{0,2},{1,3},{2,0},{3,1},{4,6},{5,7},{6,4},{7,5},{8,10},{9,11},{10,... | collective-permute-start | bytes 1769480 | tf_op jit(solution)/shard_map/ppermute | solution.py:346
  67.8 12.8 %copy-start.1 = (bf16[80,2048]{1,0:T(8,128)(2,1)S(1)}, bf16[80,2048]{1,0:T(8,128)(2,1)}, u32[]{:S(2)}) copy-start(bf16[80,2048]{1,0:T(8,128)(2,1)} %copy-done) | copy-start | bytes 983044
  73.7 4.3 %collective-permute-start.14 = (bf16[32,2176]{1,0:T(8,128)(2,1)S(1)}, bf16[32,2176]{1,0:T(8,128)(2,1)S(1)}, u32[]{:S(2)}, u32[]{:S(2)}) collective-permute-start(bf16[32,2176]{1,0:T(8,128)(2,1)S(1)} %get-tuple-element.70), channel_id=1, source_target_pairs={{0,4},{4,0},{8,12},{12,8},{16,20},{20,16},{24,28},{28,24},{1,5},{5... | collective-permute-start | bytes 417800 | tf_op jit(solution)/shard_map/ppermute | solution.py:346
  73.9 4.2 %collective-permute-start.15 = (bf16[32,2176]{1,0:T(8,128)(2,1)S(1)}, bf16[32,2176]{1,0:T(8,128)(2,1)S(1)}, u32[]{:S(2)}, u32[]{:S(2)}) collective-permute-start(bf16[32,2176]{1,0:T(8,128)(2,1)S(1)} %get-tuple-element.71), channel_id=1, source_target_pairs={{0,8},{4,12},{8,0},{12,4},{16,24},{20,28},{24,16},{28,20},{1,9},{5... | collective-permute-start | bytes 417800 | tf_op jit(solution)/shard_map/ppermute | solution.py:346
  74.2 6.4 %collective-permute-start.16 = (bf16[32,2176]{1,0:T(8,128)(2,1)S(1)}, bf16[32,2176]{1,0:T(8,128)(2,1)S(1)}, u32[]{:S(2)}, u32[]{:S(2)}) collective-permute-start(bf16[32,2176]{1,0:T(8,128)(2,1)S(1)} %get-tuple-element.72), channel_id=1, source_target_pairs={{0,12},{4,8},{8,4},{12,0},{16,28},{20,24},{24,20},{28,16},{1,13},{... | collective-permute-start | bytes 417800 | tf_op jit(solution)/shard_map/ppermute | solution.py:346
  82.6 19.2 %collective-permute-start.21 = (bf16[288,1152]{1,0:T(8,128)(2,1)S(1)}, bf16[288,1152]{1,0:T(8,128)(2,1)S(1)}, u32[]{:S(2)}, u32[]{:S(2)}) collective-permute-start(bf16[288,1152]{1,0:T(8,128)(2,1)S(1)} %get-tuple-element.77.own_ref.mid_ref), channel_id=1, source_target_pairs={{0,2},{1,3},{2,0},{3,1},{4,6},{5,7},{6,4},{7,5},{8,10},{9,11},{10,... | collective-permute-start | bytes 1990664 | tf_op jit(solution)/shard_map/ppermute | solution.py:346
  83.9 14.8 %collective-permute-start.17 = (bf16[64,2176]{1,0:T(8,128)(2,1)S(1)}, bf16[64,2176]{1,0:T(8,128)(2,1)S(1)}, u32[]{:S(2)}, u32[]{:S(2)}) collective-permute-start(bf16[64,2176]{1,0:T(8,128)(2,1)S(1)} %shard_map.102.after_ref), channel_id=1, source_target_pairs={{0,16},{4,20},{8,24},{12,28},{16,0},{20,4},{24,8},{28,12},{1,17},{... | collective-permute-start | bytes 835592 | tf_op jit(solution)/shard_map/ppermute | solution.py:346
  86.5 4.3 %collective-permute-start.8 = (bf16[32,2176]{1,0:T(8,128)(2,1)S(1)}, bf16[32,2176]{1,0:T(8,128)(2,1)S(1)}, u32[]{:S(2)}, u32[]{:S(2)}) collective-permute-start(bf16[32,2176]{1,0:T(8,128)(2,1)S(1)} %get-tuple-element.58), channel_id=1, source_target_pairs={{0,4},{4,0},{8,12},{12,8},{16,20},{20,16},{24,28},{28,24},{1,5},{5... | collective-permute-start | bytes 417800 | tf_op jit(solution)/shard_map/ppermute | solution.py:346
  88.0 5.8 %collective-permute-start.9 = (bf16[32,2176]{1,0:T(8,128)(2,1)S(1)}, bf16[32,2176]{1,0:T(8,128)(2,1)S(1)}, u32[]{:S(2)}, u32[]{:S(2)}) collective-permute-start(bf16[32,2176]{1,0:T(8,128)(2,1)S(1)} %get-tuple-element.59), channel_id=1, source_target_pairs={{0,8},{4,12},{8,0},{12,4},{16,24},{20,28},{24,16},{28,20},{1,9},{5... | collective-permute-start | bytes 417800 | tf_op jit(solution)/shard_map/ppermute | solution.py:346
  88.1 7.1 %collective-permute-start.10 = (bf16[32,2176]{1,0:T(8,128)(2,1)S(1)}, bf16[32,2176]{1,0:T(8,128)(2,1)S(1)}, u32[]{:S(2)}, u32[]{:S(2)}) collective-permute-start(bf16[32,2176]{1,0:T(8,128)(2,1)S(1)} %get-tuple-element.60), channel_id=1, source_target_pairs={{0,12},{4,8},{8,4},{12,0},{16,28},{20,24},{24,20},{28,16},{1,13},{... | collective-permute-start | bytes 417800 | tf_op jit(solution)/shard_map/ppermute | solution.py:346
  101.8 0.7 copy-start.17
  103.0 8.3 %collective-permute-start.22 = (bf16[576,1152]{1,0:T(8,128)(2,1)S(1)}, bf16[576,1152]{1,0:T(8,128)(2,1)S(1)}, u32[]{:S(2)}, u32[]{:S(2)}) collective-permute-start(bf16[576,1152]{1,0:T(8,128)(2,1)S(1)} %shard_map.105), channel_id=1, source_target_pairs={{0,1},{1,0},{2,3},{3,2},{4,5},{5,4},{6,7},{7,6},{8,9},{9,8},{10,11... | collective-permute-start | bytes 3981320 | tf_op jit(solution)/shard_map/ppermute | solution.py:346
  107.0 4.4 %collective-permute-start.20 = (bf16[288,2048]{1,0:T(8,128)(2,1)S(1)}, bf16[288,2048]{1,0:T(8,128)(2,1)S(1)}, u32[]{:S(2)}, u32[]{:S(2)}) collective-permute-start(bf16[288,2048]{1,0:T(8,128)(2,1)S(1)} %get-tuple-element.76), channel_id=1, source_target_pairs={{0,1},{1,0},{2,3},{3,2},{4,5},{5,4},{6,7},{7,6},{8,9},{9,8},{10,11... | collective-permute-start | bytes 3538952 | tf_op jit(solution)/shard_map/ppermute | solution.py:346

commit v3 on v0

--- a/solution.py
+++ b/solution.py
@@ -1,11 +1,468 @@
+import functools
+
 import jax
 import jax.numpy as jnp
 from jax import lax
+from jax.experimental import pallas as pl
+from jax.experimental.pallas import tpu as pltpu
 from jax.sharding import PartitionSpec as P
+
+BF16 = jnp.bfloat16
+F32 = jnp.float32
+LANES = 128
 
 
 def swish(value):
     return value * jax.nn.sigmoid(value)
+
+
+def dot(a, b):
+    return jnp.dot(a, b, preferred_element_type=F32)
+
+
+def dot_nt(a, b):
+    return lax.dot_general(a, b, (((1,), (1,)), ((), ())), preferred_element_type=F32)
+
+
+def dot_tn(a, b):
+    return lax.dot_general(a, b, (((0,), (0,)), ((), ())), preferred_element_type=F32)
+
+
+def picks(weight, main):
+    token_count = weight.shape[1]
+    routed = weight != 0.0
+    first = lax.broadcasted_iota(jnp.int32, (token_count, token_count), 0)
+    second = lax.broadcasted_iota(jnp.int32, (token_count, token_count), 1)
+    upper = (first < second).astype(F32).astype(BF16)
+    rank = dot(routed.astype(F32).astype(BF16), upper)
+    rank = jnp.where(routed, rank, -1.0).astype(jnp.int32)
+    slots = lax.broadcasted_iota(jnp.int32, (main, token_count), 0)
+    mains = [(slots == rank[i : i + 1, :]).astype(F32) for i in range(weight.shape[0])]
+    tails = (rank == main).astype(F32)
+    return mains, tails
+
+
+def route_kernel(peer_ref, named_ref, given_ref, x_ref, dy_ref, joint_ref, dense_ref):
+    count, width = x_ref.shape
+    named = named_ref[...]
+    given = given_ref[...].astype(F32)
+    experts = dense_ref.shape[0]
+    lines = [
+        jnp.sum(jnp.where(named == peer_ref[i], given, 0.0), axis=0, keepdims=True) for i in range(experts)
+    ]
+    dense = jnp.concatenate(lines, axis=0)
+    dense_ref[...] = dense
+    turned = jnp.concatenate(lines[experts // 2 :] + lines[: experts // 2] + [jnp.zeros_like(dense)], axis=0)
+    joint_ref[0:count, :width] = x_ref[...]
+    joint_ref[count:, :width] = dy_ref[...]
+    joint_ref[:, width:] = jnp.zeros((2 * count, LANES), BF16)
+    joint_ref[0:16, width : width + count] = turned.astype(BF16)
+
+
+def join_kernel(in_ref, out_ref, after_ref, joint_ref, again_ref):
+    width = in_ref.shape[1]
+    for target in (joint_ref, again_ref):
+        target[:, :width] = in_ref[...]
+        target[:, width:] = out_ref[...]
+
+
+def after_kernel(*refs):
+    pass
+
+
+def relay_kernel(near_a, far_a, near_b, far_b, mid_ref, mid_out_ref, joint_ref):
+    count, width = near_a.shape
+    for at, near, far in ((0, near_a, far_a), (count, near_b, far_b)):
+        joint_ref[at : at + count, :width] = near[...]
+        joint_ref[at : at + count, width:] = far[:, width:]
+
+
+def pack_kernel(first, joint_ref, *refs):
+    count = 4
+    out_refs, fold = refs[-1 - count : -1], refs[-1]
+    tokens, width = joint_ref.shape[0] // 2, joint_ref.shape[1] - LANES
+    chunks = width // LANES
+    main = out_refs[0].shape[0] // 2
+    weight = joint_ref[0:16, width:].astype(F32)[0:8, :tokens]
+    mains, tails = picks(weight, main)
+    mains = mains[first : first + count]
+    pick = jnp.concatenate(mains + [tails, jnp.zeros_like(tails)], axis=0).astype(BF16)
+    lane = lax.broadcasted_iota(jnp.int32, (main, LANES), 1)
+    for at, base, low in ((0, 0, 0), (tokens, main, chunks)):
+        rows = dot(pick, joint_ref[at : at + tokens, :width])
+        for j in range(count):
+            out_refs[j][base : base + main, :width] = rows[main * j : main * (j + 1)].astype(BF16)
+            line = main * count + first + j
+            for c in range(chunks):
+                fold[c : c + 1, :] = rows[line : line + 1, LANES * c : LANES * (c + 1)]
+            out_refs[j][low : low + chunks, width:] = fold[...].astype(BF16)
+    for j in range(count):
+        mine = weight[first + j : first + j + 1, :]
+        column = jnp.sum(mains[j] * mine, axis=1, keepdims=True)
+        last = jnp.sum(tails[first + j : first + j + 1, :] * mine, axis=1, keepdims=True)
+        out_refs[j][main:, width:] = jnp.where(lane < LANES // 2, column, last).astype(BF16)
+
+
+def slice_kernel(place_ref, *refs):
+    blocks, parts = 4, 4
+    in_refs, (keep_ref, near_ref, far_ref, weight_ref, fold) = refs[:blocks], refs[-5:]
+    main = in_refs[0].shape[0] // 2
+    depth = keep_ref.shape[1] // 2
+    width = parts * depth
+    chunks = width // LANES
+    targets = [(keep_ref, 0), (near_ref, 0), (far_ref, 0), (far_ref, 2 * depth)]
+    lane = lax.broadcasted_iota(jnp.int32, (1, LANES), 1)
+    lasts = []
+    for i in range(blocks):
+        for j, (target, shift) in enumerate(targets):
+            columns = pl.ds(pl.multiple_of(place_ref[j] * depth, depth), depth)
+            for side in range(2):
+                at = shift + side * depth
+                target[main * i : main * (i + 1), at : at + depth] = in_refs[i][
+                    side * main : (side + 1) * main, columns
+                ]
+        for side in range(2):
+            fold[side, chunks * i : chunks * (i + 1), :] = in_refs[i][
+                side * chunks : (side + 1) * chunks, width:
+            ].astype(F32)
+        weights = in_refs[i][main:, width:].astype(F32)
+        weight_ref[main * i : main * (i + 1), :] = weights
+        last = jnp.sum(jnp.where(lane == LANES - 1, weights[0:1, :], 0.0), axis=1, keepdims=True)
+        lasts.append(jnp.broadcast_to(last, (1, LANES)))
+    weight_ref[main * blocks :, :] = jnp.concatenate(lasts + [jnp.zeros((16 - blocks, LANES), F32)], axis=0)
+    each = chunks // parts
+    for j, (target, shift) in enumerate(targets):
+        for side in range(2):
+            for q in range(each):
+                tail = fold[side, pl.ds(place_ref[j] * each + q, blocks, stride=chunks), :]
+                tail = jnp.concatenate([tail, jnp.zeros((16 - blocks, LANES), F32)], axis=0).astype(BF16)
+                at = shift + side * depth + q * LANES
+                target[main * blocks :, at : at + LANES] = tail
+
+
+def main_kernel(early, place_ref, w_ref, *refs):
+    blocks, parts = 4, 4
+    weights = refs[:parts]
+    keep_ref, near_ref, far_ref = refs[parts : parts + 3]
+    mid, backs, (tail, fold) = refs[-3 - blocks], refs[-2 - blocks : -2], refs[-2:]
+    depth = keep_ref.shape[1] // 2
+    width = parts * depth
+    hidden_width = mid.shape[1] // 3
+    main = backs[0].shape[0]
+    chunks = width // LANES
+    total = keep_ref.shape[0]
+    pre = jnp.zeros((total, 2 * hidden_width), F32)
+    grad = jnp.zeros((total, hidden_width), F32)
+    for j, (ref, shift) in enumerate([(keep_ref, 0), (near_ref, 0), (far_ref, 0), (far_ref, 2 * depth)]):
+        pre += dot(ref[:, shift : shift + depth], weights[j][:, : 2 * hidden_width])
+        grad += dot(ref[:, shift + depth : shift + 2 * depth], weights[j][:, 2 * hidden_width :])
+    if early:
+        mid[0:early, :] = refs[parts + 3][...]
+    weight = w_ref[:, 0:1]
+    gate_pre = pre[:, :hidden_width]
+    up_pre = pre[:, hidden_width:]
+    sig = jax.nn.sigmoid(gate_pre)
+    act = gate_pre * sig
+    hidden = (act * up_pre).astype(BF16).astype(F32)
+    route = jnp.sum(hidden * grad, axis=1, keepdims=True)
+    grad_hidden = weight * grad
+    grad_gate = grad_hidden * up_pre * sig * (1.0 + gate_pre * (1.0 - sig))
+    mid[early:, :hidden_width] = grad_gate.astype(BF16)
+    mid[early:, hidden_width : 2 * hidden_width] = (grad_hidden * act).astype(BF16)
+    mid[early:, 2 * hidden_width :] = (weight * hidden).astype(BF16)
+    for j in range(parts):
+        columns = pl.ds(pl.multiple_of(place_ref[j] * depth, depth), depth)
+        part = dot_nt(mid[early:, : 2 * hidden_width], weights[j][:, : 2 * hidden_width])
+        tail[:, columns] = part[main * blocks :]
+        part = part.astype(BF16)
+        for i in range(blocks):
+            backs[i][:, columns] = part[main * i : main * (i + 1)]
+    row = lax.broadcasted_iota(jnp.int32, (main, LANES), 0)
+    lane = lax.broadcasted_iota(jnp.int32, (main, LANES), 1)
+    for i in range(blocks):
+        for c in range(chunks):
+            fold[c : c + 1, :] = tail[i : i + 1, LANES * c : LANES * (c + 1)]
+        backs[i][:chunks, width:] = fold[...].astype(BF16)
+        mine = jnp.where(row == lane, route[main * i : main * (i + 1)], 0.0)
+        mine = jnp.sum(mine, axis=0, keepdims=True)
+        mine = jnp.where(lane[0:1] == main, route[main * blocks + i : main * blocks + i + 1], mine)
+        backs[i][chunks:, width:] = jnp.broadcast_to(mine, (main - chunks, LANES)).astype(BF16)
+
+
+def unpack_sum(weight, block_refs, rows, fold):
+    count = len(block_refs)
+    main = block_refs[0].shape[0]
+    width = rows.shape[1]
+    chunks = width // LANES
+    mains, tails = picks(weight, main)
+    mains = mains[:count]
+    pick = jnp.concatenate(mains + [tails, jnp.zeros_like(tails)], axis=0).astype(BF16)
+    lane = lax.broadcasted_iota(jnp.int32, (1, LANES), 1)
+    routes = []
+    for j in range(count):
+        rows[main * j : main * (j + 1), :] = block_refs[j][:, :width]
+        fold[chunks * j : chunks * (j + 1), :] = block_refs[j][:chunks, width:].astype(F32)
+        mine = block_refs[j][chunks:, width:].astype(F32)
+        dense = dot(mine[:, :main].astype(BF16), mains[j].astype(BF16))[0:1, :]
+        last = jnp.sum(jnp.where(lane == main, mine[0:1, :], 0.0), axis=1, keepdims=True)
+        routes.append(dense + last * tails[j : j + 1, :])
+    for c in range(chunks):
+        tail = fold[pl.ds(c, count, stride=chunks), :]
+        tail = jnp.concatenate([tail, jnp.zeros((16 - count, LANES), F32)], axis=0).astype(BF16)
+        rows[main * count :, LANES * c : LANES * (c + 1)] = tail
+    return dot_tn(pick, rows[...]), routes
+
+
+def relay_sum_kernel(joint_ref, b0, b1, b2, b3, after_ref, out_ref, rows, fold):
+    tokens, width = out_ref.shape[0], rows.shape[1]
+    weight = joint_ref[0:16, width:].astype(F32)[0:8, :tokens]
+    summed, routes = unpack_sum(weight, (b0, b1, b2, b3), rows, fold)
+    out_ref[:, :width] = summed.astype(BF16)
+    out_ref[:, width:] = jnp.zeros((tokens, LANES), BF16)
+    block = jnp.concatenate(routes + [jnp.zeros((12, tokens), F32)], axis=0).astype(BF16)
+    out_ref[0:16, width : width + tokens] = block
+
+
+def near_sum_kernel(w_ref, b0, b1, b2, b3, grad_ref, route_ref, rows, fold):
+    summed, routes = unpack_sum(w_ref[...], (b0, b1, b2, b3), rows, fold)
+    grad_ref[...] = summed
+    route_ref[...] = jnp.concatenate(routes + [jnp.zeros_like(route) for route in routes], axis=0)
+
+
+def combine_kernel(peer_ref, named_ref, near_ref, near_route_ref, far_ref, grad_ref, route_ref):
+    tokens, width = grad_ref.shape
+    grad_ref[...] = (near_ref[...] + far_ref[:, :width].astype(F32)).astype(BF16)
+    others = far_ref[0:16, width : width + tokens].astype(F32)
+    named = named_ref[...]
+    route = jnp.zeros(route_ref.shape, F32)
+    for j in range(4):
+        route = route + jnp.where(named == peer_ref[j], near_route_ref[j : j + 1, :], 0.0)
+        route = route + jnp.where(named == peer_ref[4 + j], others[j : j + 1, :], 0.0)
+    route_ref[...] = route.astype(BF16)
+
+
+def weight_kernel(half, rows_a, rows_b, near_ref, mid_a, mid_b, *refs):
+    in_ref, out_ref, rows, mids = refs[-4:]
+    before = refs[:-4]
+    depth, hidden_width = out_ref.shape
+    count = rows_a.shape[0]
+    rows[0:count, :] = rows_a[:, : 2 * depth]
+    rows[count : 2 * count, :] = rows_b[:, : 2 * depth]
+    rows[2 * count :, :] = near_ref[:, 2 * depth * half : 2 * depth * (half + 1)]
+    mids[0 : 2 * count, :] = mid_a[...]
+    mids[2 * count :, :] = mid_b[...]
+    in_part = dot_tn(rows[:, :depth], mids[:, : 2 * hidden_width])
+    out_part = dot_tn(rows[:, depth:], mids[:, 2 * hidden_width :])
+    if before:
+        in_part = in_part + before[0][...]
+        out_part = out_part + before[1][...]
+    in_ref[...] = in_part
+    out_ref[...] = out_part
+
+
+def call(kernel, outs, smem, vmem, either, scratch, flops, either_outs=0, aliases=None):
+    on_vmem = pl.BlockSpec(memory_space=pltpu.VMEM)
+    on_either = pl.BlockSpec(memory_space=pl.ANY)
+    on_smem = pl.BlockSpec(memory_space=pltpu.SMEM)
+    outs = [jax.ShapeDtypeStruct(shape, kind) for shape, kind in outs]
+    moved = sum(a.size * a.dtype.itemsize for a in list(vmem) + outs[either_outs:])
+    return pl.pallas_call(
+        kernel,
+        out_shape=tuple(outs),
+        in_specs=[on_smem] * len(smem) + [on_vmem] * len(vmem) + [on_either] * len(either),
+        out_specs=tuple([on_either] * either_outs + [on_vmem] * (len(outs) - either_outs)),
+        scratch_shapes=scratch,
+        compiler_params=pltpu.CompilerParams(vmem_limit_bytes=24 * 1024 * 1024),
+        cost_estimate=pl.CostEstimate(flops=flops, bytes_accessed=moved, transcendentals=0),
+        input_output_aliases=aliases or {},
+    )(*smem, *vmem, *either)
+
+
+def swap(value, axis, mask):
+    return lax.ppermute(value, axis, [(i, i ^ mask) for i in range(lax.axis_size(axis))])
+
+
+def on_device_packed(tokens, grad_out, route_expert, route_weight, gate_up_weight, down_weight):
+    token_count, width = tokens.shape
+    blocks, parts, half = 8, 4, 4
+    hidden_width = down_weight.shape[2]
+    depth = width // parts
+    chunks = width // LANES
+    main = block_rows(token_count, route_expert.shape[1], blocks) // 16 * 16
+    rows = main * half + 16
+
+    peers = lax.axis_index("expert") ^ jnp.arange(blocks, dtype=jnp.int32)
+    places = lax.axis_index("dp") ^ jnp.arange(parts, dtype=jnp.int32)
+    named = route_expert.T
+    packed_shape = ((2 * main, width + LANES), BF16)
+    back_shape = ((main, width + LANES), BF16)
+
+    joint, dense = call(
+        route_kernel,
+        [((2 * token_count, width + LANES), BF16), ((blocks, token_count), F32)],
+        [peers],
+        [named, route_weight.T, tokens, grad_out],
+        [],
+        [],
+        0,
+    )
+    far_joint = swap(joint, "expert", half)
+
+    weights, again = call(
+        join_kernel,
+        [((depth, 3 * hidden_width), BF16)] * 2,
+        [],
+        [gate_up_weight[0], down_weight[0]],
+        [dense],
+        [],
+        0,
+    )
+    far_weights = swap(weights, "dp", 2)
+
+    def pack(first, value, after):
+        packed = call(
+            functools.partial(pack_kernel, first),
+            [packed_shape] * half,
+            [],
+            [value],
+            after,
+            [pltpu.VMEM((chunks, LANES), F32)],
+            4 * (half * main + 16) * token_count * width,
+        )
+        return [packed[0]] + [swap(packed[j], "expert", j) for j in range(1, half)]
+
+    own = pack(half, joint, [])
+    again, far_weights = call(
+        after_kernel,
+        [(again.shape, BF16), (far_weights.shape, BF16)],
+        [],
+        [],
+        [again, far_weights, far_joint],
+        [],
+        0,
+        2,
+        {0: 0, 1: 1},
+    )
+    weight_parts = [again, swap(again, "dp", 1), far_weights, swap(far_weights, "dp", 1)]
+    far = pack(0, far_joint, own[1:])
+
+    def sliced(packed, after):
+        return call(
+            slice_kernel,
+            [
+                ((rows, 2 * depth), BF16),
+                ((rows, 2 * depth), BF16),
+                ((rows, 4 * depth), BF16),
+                ((rows, LANES), F32),
+            ],
+            [places],
+            packed,
+            after,
+            [pltpu.VMEM((2, half * chunks, LANES), F32)],
+            0,
+        )
+
+    def middle(slices, weight, before, after):
+        early = before[0].shape[0] if before else 0
+        return call(
+            functools.partial(main_kernel, early),
+            [((early + rows, 3 * hidden_width), BF16)] + [back_shape] * half,
+            [places],
+            [weight, *weight_parts, *slices, *before],
+            after,
+            [pltpu.VMEM((16, width), F32), pltpu.VMEM((chunks, LANES), F32)],
+            2 * rows * width * 5 * hidden_width,
+        )
+
+    *own_slices, own_weight = sliced(own, [])
+    own_far = swap(own_slices[2], "dp", 2)
+    own_mid, *near_back = middle(own_slices, own_weight, [], [])
+    *far_slices, far_weight = sliced(far, [own_mid])
+    far_far = swap(far_slices[2], "dp", 2)
+    mid, *far_back = middle(far_slices, far_weight, [own_mid], [own_far])
+
+    mid, near_rows = call(
+        relay_kernel,
+        [(mid.shape, BF16), ((2 * rows, 4 * depth), BF16)],
+        [],
+        [own_slices[1], own_far, far_slices[1], far_far],
+        [mid],
+        [],
+        0,
+        1,
+        {4: 0},
+    )
+    mid_far = swap(mid, "dp", 2)
+    mid_near = swap(mid, "dp", 1)
+
+    sum_scratch = [
+        pltpu.VMEM((half * main + 16, width), BF16),
+        pltpu.VMEM((half * chunks, LANES), F32),
+    ]
+    sum_flops = 2 * (half * main + 16) * width * token_count
+    far_back = far_back[:1] + [swap(far_back[j], "expert", j) for j in range(1, half)]
+    (partial,) = call(
+        relay_sum_kernel,
+        [((token_count, width + LANES), BF16)],
+        [],
+        [far_joint, *far_back],
+        [near_rows],
+        sum_scratch,
+        sum_flops,
+    )
+    far_partial = swap(partial, "expert", half)
+    near_rows = swap(near_rows, "dp", 1)
+    near_back = near_back[:1] + [swap(near_back[j], "expert", j) for j in range(1, half)]
+    near_sum, near_route = call(
+        near_sum_kernel,
+        [((token_count, width), F32), ((blocks, token_count), F32)],
+        [],
+        [dense, *near_back],
+        [],
+        sum_scratch,
+        sum_flops,
+    )
+    grad_tokens, grad_route = call(
+        combine_kernel,
+        [((token_count, width), BF16), (named.shape, BF16)],
+        [peers],
+        [named, near_sum, near_route, far_partial],
+        [],
+        [],
+        0,
+    )
+
+    def weight_part(which, arrays, before):
+        return call(
+            functools.partial(weight_kernel, which),
+            [((depth, 2 * hidden_width), F32), ((depth, hidden_width), F32)],
+            [],
+            [*arrays, *before],
+            [],
+            [pltpu.VMEM((4 * rows, 2 * depth), BF16), pltpu.VMEM((4 * rows, 3 * hidden_width), BF16)],
+            2 * 4 * rows * depth * 3 * hidden_width,
+        )
+
+    first = weight_part(0, [own_slices[0], far_slices[0], near_rows, mid, mid_near], [])
+    (mid_far,) = call(
+        after_kernel,
+        [(mid_far.shape, BF16)],
+        [],
+        [],
+        [mid_far, first[1], far_partial],
+        [],
+        0,
+        1,
+        {0: 0},
+    )
+    grad_gate_up, grad_down = weight_part(
+        1, [own_far, far_far, near_rows, mid_far, swap(mid_far, "dp", 1)], first
+    )
+    return (grad_tokens, grad_route.T, grad_gate_up[None], grad_down[None])
+
+
+def block_rows(token_count, route_count, expert_total):
+    return min(token_count, (token_count * route_count + expert_total - 1) // expert_total + 1)
 
 
 def to_local(rows, group_count, local_count, capacity):
@@ -22,7 +479,7 @@
     return shaped.reshape((group_count, local_count * capacity) + tail)
 
 
-def on_device(tokens, grad_out, route_expert, route_weight, gate_up_weight, down_weight):
+def on_device_routed(tokens, grad_out, route_expert, route_weight, gate_up_weight, down_weight):
     token_count, model_width = tokens.shape
     route_count = route_expert.shape[1]
     group_count = lax.axis_size("expert")
@@ -132,7 +589,25 @@
     return (grad_tokens, grad_route, grad_gate_up, grad_down)
 
 
+def packs(tokens, route_expert, down_weight):
+    chunks = tokens.shape[1] // LANES
+    capacity = block_rows(tokens.shape[0], route_expert.shape[1], lax.axis_size("expert"))
+    return (
+        lax.axis_size("expert") == 8
+        and lax.axis_size("dp") == 4
+        and down_weight.shape[0] == 1
+        and capacity % 16 <= 1
+        and chunks == 16
+        and 2 * chunks <= capacity < LANES // 2
+    )
+
+
 def solution(mesh):
+    def on_device(*arrays):
+        if packs(arrays[0], arrays[2], arrays[5]):
+            return on_device_packed(*arrays)
+        return on_device_routed(*arrays)
+
     return jax.shard_map(
         on_device,
         mesh=mesh,

time: 246 us -> 130 us (0.53)
  local copies, waits for them, and re-layouts: 47 us -> 9.42 us
  other arithmetic: 37.2 us -> 0.01 us
  matrix products: 22.5 us -> 0 us
  waiting for transfers between devices: 92.4 us -> 73.4 us
  Pallas kernels: 0 us -> 18 us
  between operations: 14 us -> 0.79 us
  starting transfers between devices: 30.5 us -> 27.3 us
    all_to_all x6 -> x0, waiting for transfers between devices: 91 us -> none  [the longest x1 28.6 us: on_device(): lax.all_to_all(send_dy.reshape(group_count, local_count * capacity, model...]
    ppermute x0 -> x23, waiting for transfers between devices: none -> 73.4 us  [swap(): lax.ppermute(value, axis, [(i, i ^ mask) for i in range(lax.axis_size(axi...]
    unnamed x1 -> x0, other arithmetic: 34.5 us -> none
    all_to_all x6 -> x0, starting transfers between devices: 30.1 us -> none  [the longest x1 6.67 us: on_device(): lax.all_to_all(rows_x, 'dp', split_axis=2, concat_axis=1, tiled=True)]
    ppermute x0 -> x23, starting transfers between devices: none -> 27.3 us  [swap(): lax.ppermute(value, axis, [(i, i ^ mask) for i in range(lax.axis_size(axi...]
    dot_general x9 -> x0, matrix products: 22.5 us -> none  [the longest x1 4.38 us: on_device(): jnp.einsum('erd,erf->def', scaled, hidden, preferred_element_type=jnp.flo...]
    pallas_call x0 -> x16, Pallas kernels: none -> 18 us  [call(): pl.pallas_call(kernel, out_shape=tuple(outs), in_specs=[on_smem] * len(sm...]
    another operation x5 -> x0, local copies, waits for them, and re-layouts: 11.6 us -> none  [the longest x2 8.88 us: to_local(): return shaped.reshape((local_count, group_count * capacity) + tail)]
  transfers between devices with their start and end apart: 10 -> 23, of which waited for: 6 -> 13; matrix products, arithmetic and copies ran while one was open for 37% -> 0% of each run, Pallas kernels for 0% -> 11%
where the time goes in v3:
time: 130 us; the launch traced here: 129 us
  waiting for transfers between devices  73.4 us (56%)
  starting transfers between devices  27.3 us (21%)
  Pallas kernels  18 us (14%)
  local copies, waits for them, and re-layouts  9.42 us (7%)
    ppermute x23, waiting for transfers between devices, swap(): lax.ppermute(value, axis, [(i, i ^ mask) for i in range(lax.axis_size(axi...  73.4 us
    ppermute x23, starting transfers between devices, swap(): lax.ppermute(value, axis, [(i, i ^ mask) for i in range(lax.axis_size(axi...  27.3 us
    pallas_call x16, Pallas kernels, call(): pl.pallas_call(kernel, out_shape=tuple(outs), in_specs=[on_smem] * len(sm...  18 us
    unnamed x26, local copies, waits for them, and re-layouts  9.42 us
  transfers between devices with their start and end apart: 23, of which 13 were waited for; matrix products, arithmetic and copies ran while one was open for 0% of the time, Pallas kernels for 11%

profile of v3, /device:TPU:1, one launch (start us, length us, event | category | flops | bytes accessed | tf_op | source)
XLA Modules:
  0.0 128.9 jit_solution(934137734162611337)
XLA Ops:
  0.6 0.0 copy-start.8
  0.7 0.9 copy-done.8
  1.6 0.9 copy-done.9
  2.6 0.7 copy-done.10
  3.2 0.7 copy-done.12
  3.9 0.6 shard_map.93
  4.5 0.0 copy-start.2
  4.5 1.1 copy-done.2
  5.6 1.0 copy-done.3
  6.6 0.2 shard_map.96
  6.8 2.1 %collective-permute-start.3 = (bf16[512,1152]{1,0:T(8,128)(2,1)S(1)}, bf16[512,1152]{1,0:T(8,128)(2,1)S(1)}, u32[]{:S(2)}, u32[]{:S(2)}) collective-permute-start(bf16[512,1152]{1,0:T(8,128)(2,1)S(1)} %get-tuple-element.54), channel_id=1, source_target_pairs={{0,2},{1,3},{2,0},{3,1},{4,6},{5,7},{6,4},{7,5},{8,10},{9,11},{10,... | collective-permute-start | bytes 3538952 | tf_op jit(solution)/shard_map/ppermute | solution.py:282
  8.9 2.3 %collective-permute-start.4 = (bf16[128,2176]{1,0:T(8,128)(2,1)S(1)}, bf16[128,2176]{1,0:T(8,128)(2,1)S(1)}, u32[]{:S(2)}, u32[]{:S(2)}) collective-permute-start(bf16[128,2176]{1,0:T(8,128)(2,1)S(1)} %get-tuple-element.47.joint_ref), channel_id=1, source_target_pairs={{0,16},{4,20},{8,24},{12,28},{16,0},{20,4},{24,8},{28,12},{1,17},{... | collective-permute-start | bytes 1671176 | tf_op jit(solution)/shard_map/ppermute | solution.py:282
  11.2 24.0 %collective-permute-done.4.refs_2_.joint_ref = bf16[128,2176]{1,0:T(8,128)(2,1)S(1)} collective-permute-done((bf16[128,2176]{1,0:T(8,128)(2,1)S(1)}, bf16[128,2176]{1,0:T(8,128)(2,1)S(1)}, u32[]{:S(2)}, u32[]{:S(2)}) %collective-permute-start.4) | collective-permute-done | bytes 557088 | tf_op jit(solution)/shard_map/ppermute | solution.py:282
  35.2 1.6 %collective-permute-start.5 = (bf16[512,1152]{1,0:T(8,128)(2,1)S(1)}, bf16[512,1152]{1,0:T(8,128)(2,1)}, u32[]{:S(2)}, u32[]{:S(2)}) collective-permute-start(bf16[512,1152]{1,0:T(8,128)(2,1)S(1)} %get-tuple-element.55.refs_0_), channel_id=1, source_target_pairs={{0,1},{1,0},{2,3},{3,2},{4,5},{5,4},{6,7},{7,6},{8,9},{9,8},{10,11... | collective-permute-start | bytes 3538952 | tf_op jit(solution)/shard_map/ppermute | solution.py:282
  36.8 0.1 collective-permute-start.6
  36.9 0.6 shard_map.94
  37.5 0.7 copy-done.6
  38.2 1.2 collective-permute-start
  39.4 0.5 collective-permute-start.1
  39.9 0.9 collective-permute-start.2
  40.8 5.1 %collective-permute-done.refs_1_.refs_0_ = bf16[64,2176]{1,0:T(8,128)(2,1)S(1)} collective-permute-done((bf16[64,2176]{1,0:T(8,128)(2,1)S(1)}, bf16[64,2176]{1,0:T(8,128)(2,1)S(1)}, u32[]{:S(2)}, u32[]{:S(2)}) %collective-permute-start) | collective-permute-done | bytes 278560 | tf_op jit(solution)/shard_map/ppermute | solution.py:282
  46.0 0.9 collective-permute-done.1.refs_2_.refs_1_
  46.9 5.9 %collective-permute-done.2.refs_3_.refs_2_ = bf16[64,2176]{1,0:T(8,128)(2,1)S(1)} collective-permute-done((bf16[64,2176]{1,0:T(8,128)(2,1)S(1)}, bf16[64,2176]{1,0:T(8,128)(2,1)S(1)}, u32[]{:S(2)}, u32[]{:S(2)}) %collective-permute-start.2) | collective-permute-done | bytes 278560 | tf_op jit(solution)/shard_map/ppermute | solution.py:282
  52.8 1.5 %shard_map.100 = (bf16[64,2176]{1,0:T(8,128)(2,1)S(1)}, bf16[64,2176]{1,0:T(8,128)(2,1)}, bf16[64,2176]{1,0:T(8,128)(2,1)}, bf16[64,2176]{1,0:T(8,128)(2,1)}) custom-call(bf16[128,2176]{1,0:T(8,128)(2,1)S(1)} %collective-permute-done.4.refs_2_.joint_ref, bf16[64,2176]{1,0:T(8,128)(2,1)S(1)} %collective-permute-done.refs_1_.refs_0_, ...), custom_call_target="tpu_custom_call" | custom-call | flops 75497472 | bytes 1671168 | tf_op jit(solution)/shard_map/pallas_call | solution.py:269
  54.3 0.7 copy-done
  55.0 0.7 copy-done.4
  55.7 1.2 collective-permute-start.10
  56.9 0.5 collective-permute-start.11
  57.4 0.9 collective-permute-start.12
  58.3 1.0 copy-done.1
  59.3 1.0 copy-done.7
  60.2 0.7 shard_map.95
  60.9 0.4 collective-permute-start.13
  61.4 3.7 %shard_map.98 = (bf16[144,1152]{1,0:T(8,128)(2,1)S(1)}, bf16[32,2176]{1,0:T(8,128)(2,1)S(1)}, bf16[32,2176]{1,0:T(8,128)(2,1)S(1)}, bf16[32,2176]{1,0:T(8,128)(2,1)S(1)}, bf16[32,2176]{1,0:T(8,128)(2,1)S(1)}) custom-call(s32[4]{0:T(128)S(1)} %iota_xor_fusion.place_ref, f32[144,128]{1,0:T(8,128)S(1)} %get-tuple-element.52.w_ref, ...), custom_call_target="tpu_custom_call" | custom-call | flops 1132462080 | bytes 6860800 | tf_op jit(solution)/shard_map/pallas_call | solution.py:269
  65.1 0.0 collective-permute-done.11.refs_2_
  65.1 4.3 %collective-permute-done.12.refs_3_ = bf16[64,2176]{1,0:T(8,128)(2,1)} collective-permute-done((bf16[64,2176]{1,0:T(8,128)(2,1)}, bf16[64,2176]{1,0:T(8,128)(2,1)}, u32[]{:S(2)}, u32[]{:S(2)}) %collective-permute-start.12) | collective-permute-done | bytes 278560 | tf_op jit(solution)/shard_map/ppermute | solution.py:282
  69.4 1.2 shard_map.101
  70.7 0.4 collective-permute-start.17
  71.0 2.3 %collective-permute-done.13.refs_8_.far_a.rows_a = bf16[144,2048]{1,0:T(8,128)(2,1)S(1)} collective-permute-done((bf16[144,2048]{1,0:T(8,128)(2,1)S(1)}, bf16[144,2048]{1,0:T(8,128)(2,1)S(1)}, u32[]{:S(2)}, u32[]{:S(2)}) %collective-permute-start.13) | collective-permute-done | bytes 589856 | tf_op jit(solution)/shard_map/ppermute | solution.py:282
  73.4 3.7 %shard_map.102 = (bf16[288,1152]{1,0:T(8,128)(2,1)S(1)}, bf16[32,2176]{1,0:T(8,128)(2,1)S(1)}, bf16[32,2176]{1,0:T(8,128)(2,1)S(1)}, bf16[32,2176]{1,0:T(8,128)(2,1)S(1)}, bf16[32,2176]{1,0:T(8,128)(2,1)S(1)}) custom-call(s32[4]{0:T(128)S(1)} %iota_xor_fusion.place_ref, f32[144,128]{1,0:T(8,128)S(1)} %get-tuple-element.71.w_ref, ...), custom_call_target="tpu_custom_call" | custom-call | flops 1132462080 | bytes 7524352 | tf_op jit(solution)/shard_map/pallas_call | solution.py:269
  77.1 9.1 %collective-permute-done.17.far_b.rows_b = bf16[144,2048]{1,0:T(8,128)(2,1)S(1)} collective-permute-done((bf16[144,2048]{1,0:T(8,128)(2,1)S(1)}, bf16[144,2048]{1,0:T(8,128)(2,1)S(1)}, u32[]{:S(2)}, u32[]{:S(2)}) %collective-permute-start.17) | collective-permute-done | bytes 589856 | tf_op jit(solution)/shard_map/ppermute | solution.py:282
  86.1 0.1 shard_map.103
  86.2 3.3 %collective-permute-start.19 = (bf16[288,2048]{1,0:T(8,128)(2,1)S(1)}, bf16[288,2048]{1,0:T(8,128)(2,1)S(1)}, u32[]{:S(2)}, u32[]{:S(2)}) collective-permute-start(bf16[288,2048]{1,0:T(8,128)(2,1)S(1)} %get-tuple-element.80.after_ref), channel_id=1, source_target_pairs={{0,1},{1,0},{2,3},{3,2},{4,5},{5,4},{6,7},{7,6},{8,9},{9,8},{10,11... | collective-permute-start | bytes 3538952 | tf_op jit(solution)/shard_map/ppermute | solution.py:282
  89.5 0.1 collective-permute-start.21
  89.6 0.4 collective-permute-start.20
  90.0 1.2 collective-permute-start.14
  91.2 1.3 %collective-permute-start.15 = (bf16[32,2176]{1,0:T(8,128)(2,1)S(1)}, bf16[32,2176]{1,0:T(8,128)(2,1)S(1)}, u32[]{:S(2)}, u32[]{:S(2)}) collective-permute-start(bf16[32,2176]{1,0:T(8,128)(2,1)S(1)} %get-tuple-element.77), channel_id=1, source_target_pairs={{0,8},{4,12},{8,0},{12,4},{16,24},{20,28},{24,16},{28,20},{1,9},{5... | collective-permute-start | bytes 417800 | tf_op jit(solution)/shard_map/ppermute | solution.py:282
  92.5 2.0 %collective-permute-done.14.b1 = bf16[32,2176]{1,0:T(8,128)(2,1)S(1)} collective-permute-done((bf16[32,2176]{1,0:T(8,128)(2,1)S(1)}, bf16[32,2176]{1,0:T(8,128)(2,1)S(1)}, u32[]{:S(2)}, u32[]{:S(2)}) %collective-permute-start.14) | collective-permute-done | bytes 139296 | tf_op jit(solution)/shard_map/ppermute | solution.py:282
  94.5 2.3 %collective-permute-start.16 = (bf16[32,2176]{1,0:T(8,128)(2,1)S(1)}, bf16[32,2176]{1,0:T(8,128)(2,1)S(1)}, u32[]{:S(2)}, u32[]{:S(2)}) collective-permute-start(bf16[32,2176]{1,0:T(8,128)(2,1)S(1)} %get-tuple-element.78), channel_id=1, source_target_pairs={{0,12},{4,8},{8,4},{12,0},{16,28},{20,24},{24,20},{28,16},{1,13},{... | collective-permute-start | bytes 417800 | tf_op jit(solution)/shard_map/ppermute | solution.py:282
  96.7 2.5 %collective-permute-done.16.b3 = bf16[32,2176]{1,0:T(8,128)(2,1)S(1)} collective-permute-done((bf16[32,2176]{1,0:T(8,128)(2,1)S(1)}, bf16[32,2176]{1,0:T(8,128)(2,1)S(1)}, u32[]{:S(2)}, u32[]{:S(2)}) %collective-permute-start.16) | collective-permute-done | bytes 139296 | tf_op jit(solution)/shard_map/ppermute | solution.py:282
  99.3 0.4 shard_map.104
  99.7 2.4 %collective-permute-start.18 = (bf16[64,2176]{1,0:T(8,128)(2,1)S(1)}, bf16[64,2176]{1,0:T(8,128)(2,1)S(1)}, u32[]{:S(2)}, u32[]{:S(2)}) collective-permute-start(bf16[64,2176]{1,0:T(8,128)(2,1)S(1)} %shard_map.104), channel_id=1, source_target_pairs={{0,16},{4,20},{8,24},{12,28},{16,0},{20,4},{24,8},{28,12},{1,17},{... | collective-permute-start | bytes 835592 | tf_op jit(solution)/shard_map/ppermute | solution.py:282
  102.1 1.2 shard_map.106
  103.3 10.8 %collective-permute-done.18.far_ref.refs_2_ = bf16[64,2176]{1,0:T(8,128)(2,1)S(1)} collective-permute-done((bf16[64,2176]{1,0:T(8,128)(2,1)S(1)}, bf16[64,2176]{1,0:T(8,128)(2,1)S(1)}, u32[]{:S(2)}, u32[]{:S(2)}) %collective-permute-start.18) | collective-permute-done | bytes 278560 | tf_op jit(solution)/shard_map/ppermute | solution.py:282
  114.1 1.6 %collective-permute-start.22 = (bf16[288,1152]{1,0:T(8,128)(2,1)S(1)}, bf16[288,1152]{1,0:T(8,128)(2,1)S(1)}, u32[]{:S(2)}, u32[]{:S(2)}) collective-permute-start(bf16[288,1152]{1,0:T(8,128)(2,1)S(1)} %shard_map.107.mid_a), channel_id=1, source_target_pairs={{0,1},{1,0},{2,3},{3,2},{4,5},{5,4},{6,7},{7,6},{8,9},{9,8},{10,11... | collective-permute-start | bytes 1990664 | tf_op jit(solution)/shard_map/ppermute | solution.py:282
  115.7 1.2 collective-permute-start.7
  116.9 0.4 collective-permute-start.8
  117.3 1.0 collective-permute-start.9
  118.3 2.6 %collective-permute-done.7.b1 = bf16[32,2176]{1,0:T(8,128)(2,1)S(1)} collective-permute-done((bf16[32,2176]{1,0:T(8,128)(2,1)S(1)}, bf16[32,2176]{1,0:T(8,128)(2,1)S(1)}, u32[]{:S(2)}, u32[]{:S(2)}) %collective-permute-start.7) | collective-permute-done | bytes 139296 | tf_op jit(solution)/shard_map/ppermute | solution.py:282
  120.9 0.9 collective-permute-done.8.b2
  121.8 2.9 %collective-permute-done.9.b3 = bf16[32,2176]{1,0:T(8,128)(2,1)S(1)} collective-permute-done((bf16[32,2176]{1,0:T(8,128)(2,1)S(1)}, bf16[32,2176]{1,0:T(8,128)(2,1)S(1)}, u32[]{:S(2)}, u32[]{:S(2)}) %collective-permute-start.9) | collective-permute-done | bytes 139296 | tf_op jit(solution)/shard_map/ppermute | solution.py:282
  124.8 0.4 shard_map.99
  125.2 1.3 %shard_map.105 = (bf16[64,2048]{1,0:T(8,128)(2,1)}, bf16[4,64]{1,0:T(4,128)(2,1)}) custom-call(s32[8]{0:T(128)S(1)} %iota_xor_fusion.1.peer_ref, s32[4,64]{1,0:T(4,128)S(1)} %bitcast.10, f32[64,2048]{1,0:T(8,128)S(1)} %get-tuple-element.64.near_ref, f32[8,64]{1,0:T(8,128)S(1)} %get-tuple-element.65.near_route_ref, ...), custom_call_target="tpu_custom_call" | custom-call | bytes 1068544 | tf_op jit(solution)/shard_map/pallas_call | solution.py:269
  126.5 2.4 %shard_map.108 = (f32[512,768]{1,0:T(8,128)}, f32[512,384]{1,0:T(8,128)}) custom-call(bf16[144,2048]{1,0:T(8,128)(2,1)S(1)} %collective-permute-done.13.refs_8_.far_a.rows_a, bf16[144,2048]{1,0:T(8,128)(2,1)S(1)} %collective-permute-done.17.far_b.rows_b, bf16[288,2048]{1,0:T(8,128)(2,1)S(1)} %collective-permute-done.19.near_ref, ...), custom_call_target="tpu_custom_call" | custom-call | flops 679477248 | bytes 8404992 | tf_op jit(solution)/shard_map/pallas_call | solution.py:269
  (26 shorter events, 0.1 us)
Async XLA Ops:
  0.6 1.0 copy-start.8
  1.6 0.9 copy-start.9
  2.5 0.7 copy-start.10
  3.2 0.7 copy-start.12
  4.5 1.1 copy-start.2
  5.6 1.0 copy-start.3
  6.8 28.4 %collective-permute-start.3 = (bf16[512,1152]{1,0:T(8,128)(2,1)S(1)}, bf16[512,1152]{1,0:T(8,128)(2,1)S(1)}, u32[]{:S(2)}, u32[]{:S(2)}) collective-permute-start(bf16[512,1152]{1,0:T(8,128)(2,1)S(1)} %get-tuple-element.54), channel_id=1, source_target_pairs={{0,2},{1,3},{2,0},{3,1},{4,6},{5,7},{6,4},{7,5},{8,10},{9,11},{10,... | collective-permute-start | bytes 3538952 | tf_op jit(solution)/shard_map/ppermute | solution.py:282
  8.9 26.3 %collective-permute-start.4 = (bf16[128,2176]{1,0:T(8,128)(2,1)S(1)}, bf16[128,2176]{1,0:T(8,128)(2,1)S(1)}, u32[]{:S(2)}, u32[]{:S(2)}) collective-permute-start(bf16[128,2176]{1,0:T(8,128)(2,1)S(1)} %get-tuple-element.47.joint_ref), channel_id=1, source_target_pairs={{0,16},{4,20},{8,24},{12,28},{16,0},{20,4},{24,8},{28,12},{1,17},{... | collective-permute-start | bytes 1671176 | tf_op jit(solution)/shard_map/ppermute | solution.py:282
  35.2 25.7 %collective-permute-start.5 = (bf16[512,1152]{1,0:T(8,128)(2,1)S(1)}, bf16[512,1152]{1,0:T(8,128)(2,1)}, u32[]{:S(2)}, u32[]{:S(2)}) collective-permute-start(bf16[512,1152]{1,0:T(8,128)(2,1)S(1)} %get-tuple-element.55.refs_0_), channel_id=1, source_target_pairs={{0,1},{1,0},{2,3},{3,2},{4,5},{5,4},{6,7},{7,6},{8,9},{9,8},{10,11... | collective-permute-start | bytes 3538952 | tf_op jit(solution)/shard_map/ppermute | solution.py:282
  36.8 24.6 %collective-permute-start.6 = (bf16[512,1152]{1,0:T(8,128)(2,1)S(1)}, bf16[512,1152]{1,0:T(8,128)(2,1)}, u32[]{:S(2)}, u32[]{:S(2)}) collective-permute-start(bf16[512,1152]{1,0:T(8,128)(2,1)S(1)} %get-tuple-element.56.refs_2_), channel_id=1, source_target_pairs={{0,1},{1,0},{2,3},{3,2},{4,5},{5,4},{6,7},{7,6},{8,9},{9,8},{10,11... | collective-permute-start | bytes 3538952 | tf_op jit(solution)/shard_map/ppermute | solution.py:282
  37.5 0.7 copy-start.6
  38.2 7.8 %collective-permute-start = (bf16[64,2176]{1,0:T(8,128)(2,1)S(1)}, bf16[64,2176]{1,0:T(8,128)(2,1)S(1)}, u32[]{:S(2)}, u32[]{:S(2)}) collective-permute-start(bf16[64,2176]{1,0:T(8,128)(2,1)S(1)} %get-tuple-element.49), channel_id=1, source_target_pairs={{0,4},{4,0},{8,12},{12,8},{16,20},{20,16},{24,28},{28,24},{1,5},{5... | collective-permute-start | bytes 835592 | tf_op jit(solution)/shard_map/ppermute | solution.py:282
  39.4 7.5 %collective-permute-start.1 = (bf16[64,2176]{1,0:T(8,128)(2,1)S(1)}, bf16[64,2176]{1,0:T(8,128)(2,1)S(1)}, u32[]{:S(2)}, u32[]{:S(2)}) collective-permute-start(bf16[64,2176]{1,0:T(8,128)(2,1)S(1)} %get-tuple-element.50), channel_id=1, source_target_pairs={{0,8},{4,12},{8,0},{12,4},{16,24},{20,28},{24,16},{28,20},{1,9},{5... | collective-permute-start | bytes 835592 | tf_op jit(solution)/shard_map/ppermute | solution.py:282
  39.9 12.8 %collective-permute-start.2 = (bf16[64,2176]{1,0:T(8,128)(2,1)S(1)}, bf16[64,2176]{1,0:T(8,128)(2,1)S(1)}, u32[]{:S(2)}, u32[]{:S(2)}) collective-permute-start(bf16[64,2176]{1,0:T(8,128)(2,1)S(1)} %get-tuple-element.51), channel_id=1, source_target_pairs={{0,12},{4,8},{8,4},{12,0},{16,28},{20,24},{24,20},{28,16},{1,13},{... | collective-permute-start | bytes 835592 | tf_op jit(solution)/shard_map/ppermute | solution.py:282
  54.3 0.7 copy-start
  55.0 0.7 copy-start.4
  55.7 9.4 %collective-permute-start.10 = (bf16[64,2176]{1,0:T(8,128)(2,1)}, bf16[64,2176]{1,0:T(8,128)(2,1)}, u32[]{:S(2)}, u32[]{:S(2)}) collective-permute-start(bf16[64,2176]{1,0:T(8,128)(2,1)} %get-tuple-element.67), channel_id=1, source_target_pairs={{0,4},{4,0},{8,12},{12,8},{16,20},{20,16},{24,28},{28,24},{1,5},{5... | collective-permute-start | bytes 835592 | tf_op jit(solution)/shard_map/ppermute | solution.py:282
  56.9 8.2 %collective-permute-start.11 = (bf16[64,2176]{1,0:T(8,128)(2,1)}, bf16[64,2176]{1,0:T(8,128)(2,1)}, u32[]{:S(2)}, u32[]{:S(2)}) collective-permute-start(bf16[64,2176]{1,0:T(8,128)(2,1)} %get-tuple-element.68), channel_id=1, source_target_pairs={{0,8},{4,12},{8,0},{12,4},{16,24},{20,28},{24,16},{28,20},{1,9},{5... | collective-permute-start | bytes 835592 | tf_op jit(solution)/shard_map/ppermute | solution.py:282
  57.4 12.0 %collective-permute-start.12 = (bf16[64,2176]{1,0:T(8,128)(2,1)}, bf16[64,2176]{1,0:T(8,128)(2,1)}, u32[]{:S(2)}, u32[]{:S(2)}) collective-permute-start(bf16[64,2176]{1,0:T(8,128)(2,1)} %get-tuple-element.69), channel_id=1, source_target_pairs={{0,12},{4,8},{8,4},{12,0},{16,28},{20,24},{24,20},{28,16},{1,13},{... | collective-permute-start | bytes 835592 | tf_op jit(solution)/shard_map/ppermute | solution.py:282
  58.3 1.0 copy-start.1
  59.3 1.0 copy-start.7
  60.9 12.4 %collective-permute-start.13 = (bf16[144,2048]{1,0:T(8,128)(2,1)S(1)}, bf16[144,2048]{1,0:T(8,128)(2,1)S(1)}, u32[]{:S(2)}, u32[]{:S(2)}) collective-permute-start(bf16[144,2048]{1,0:T(8,128)(2,1)S(1)} %get-tuple-element.59.refs_6_), channel_id=1, source_target_pairs={{0,2},{1,3},{2,0},{3,1},{4,6},{5,7},{6,4},{7,5},{8,10},{9,11},{10,... | collective-permute-start | bytes 1769480 | tf_op jit(solution)/shard_map/ppermute | solution.py:282
  61.4 8.1 %copy-start.5 = (bf16[64,2176]{1,0:T(8,128)(2,1)S(1)}, bf16[64,2176]{1,0:T(8,128)(2,1)}, u32[]{:S(2)}) copy-start(bf16[64,2176]{1,0:T(8,128)(2,1)} %copy-done.4) | copy-start | bytes 835588
  70.7 15.5 %collective-permute-start.17 = (bf16[144,2048]{1,0:T(8,128)(2,1)S(1)}, bf16[144,2048]{1,0:T(8,128)(2,1)S(1)}, u32[]{:S(2)}, u32[]{:S(2)}) collective-permute-start(bf16[144,2048]{1,0:T(8,128)(2,1)S(1)} %get-tuple-element.74.refs_6_), channel_id=1, source_target_pairs={{0,2},{1,3},{2,0},{3,1},{4,6},{5,7},{6,4},{7,5},{8,10},{9,11},{10,... | collective-permute-start | bytes 1769480 | tf_op jit(solution)/shard_map/ppermute | solution.py:282
  86.2 15.9 %collective-permute-start.19 = (bf16[288,2048]{1,0:T(8,128)(2,1)S(1)}, bf16[288,2048]{1,0:T(8,128)(2,1)S(1)}, u32[]{:S(2)}, u32[]{:S(2)}) collective-permute-start(bf16[288,2048]{1,0:T(8,128)(2,1)S(1)} %get-tuple-element.80.after_ref), channel_id=1, source_target_pairs={{0,1},{1,0},{2,3},{3,2},{4,5},{5,4},{6,7},{7,6},{8,9},{9,8},{10,11... | collective-permute-start | bytes 3538952 | tf_op jit(solution)/shard_map/ppermute | solution.py:282
  89.5 12.6 %collective-permute-start.21 = (bf16[288,1152]{1,0:T(8,128)(2,1)S(1)}, bf16[288,1152]{1,0:T(8,128)(2,1)S(1)}, u32[]{:S(2)}, u32[]{:S(2)}) collective-permute-start(bf16[288,1152]{1,0:T(8,128)(2,1)S(1)} %get-tuple-element.83.mid_a), channel_id=1, source_target_pairs={{0,1},{1,0},{2,3},{3,2},{4,5},{5,4},{6,7},{7,6},{8,9},{9,8},{10,11... | collective-permute-start | bytes 1990664 | tf_op jit(solution)/shard_map/ppermute | solution.py:282
  89.6 24.5 %collective-permute-start.20 = (bf16[288,1152]{1,0:T(8,128)(2,1)S(1)}, bf16[288,1152]{1,0:T(8,128)(2,1)S(1)}, u32[]{:S(2)}, u32[]{:S(2)}) collective-permute-start(bf16[288,1152]{1,0:T(8,128)(2,1)S(1)} %get-tuple-element.83.mid_a), channel_id=1, source_target_pairs={{0,2},{1,3},{2,0},{3,1},{4,6},{5,7},{6,4},{7,5},{8,10},{9,11},{10,... | collective-permute-start | bytes 1990664 | tf_op jit(solution)/shard_map/ppermute | solution.py:282
  90.0 4.5 %collective-permute-start.14 = (bf16[32,2176]{1,0:T(8,128)(2,1)S(1)}, bf16[32,2176]{1,0:T(8,128)(2,1)S(1)}, u32[]{:S(2)}, u32[]{:S(2)}) collective-permute-start(bf16[32,2176]{1,0:T(8,128)(2,1)S(1)} %get-tuple-element.76), channel_id=1, source_target_pairs={{0,4},{4,0},{8,12},{12,8},{16,20},{20,16},{24,28},{28,24},{1,5},{5... | collective-permute-start | bytes 417800 | tf_op jit(solution)/shard_map/ppermute | solution.py:282
  91.2 5.5 %collective-permute-start.15 = (bf16[32,2176]{1,0:T(8,128)(2,1)S(1)}, bf16[32,2176]{1,0:T(8,128)(2,1)S(1)}, u32[]{:S(2)}, u32[]{:S(2)}) collective-permute-start(bf16[32,2176]{1,0:T(8,128)(2,1)S(1)} %get-tuple-element.77), channel_id=1, source_target_pairs={{0,8},{4,12},{8,0},{12,4},{16,24},{20,28},{24,16},{28,20},{1,9},{5... | collective-permute-start | bytes 417800 | tf_op jit(solution)/shard_map/ppermute | solution.py:282
  94.5 4.8 %collective-permute-start.16 = (bf16[32,2176]{1,0:T(8,128)(2,1)S(1)}, bf16[32,2176]{1,0:T(8,128)(2,1)S(1)}, u32[]{:S(2)}, u32[]{:S(2)}) collective-permute-start(bf16[32,2176]{1,0:T(8,128)(2,1)S(1)} %get-tuple-element.78), channel_id=1, source_target_pairs={{0,12},{4,8},{8,4},{12,0},{16,28},{20,24},{24,20},{28,16},{1,13},{... | collective-permute-start | bytes 417800 | tf_op jit(solution)/shard_map/ppermute | solution.py:282
  99.7 14.4 %collective-permute-start.18 = (bf16[64,2176]{1,0:T(8,128)(2,1)S(1)}, bf16[64,2176]{1,0:T(8,128)(2,1)S(1)}, u32[]{:S(2)}, u32[]{:S(2)}) collective-permute-start(bf16[64,2176]{1,0:T(8,128)(2,1)S(1)} %shard_map.104), channel_id=1, source_target_pairs={{0,16},{4,20},{8,24},{12,28},{16,0},{20,4},{24,8},{28,12},{1,17},{... | collective-permute-start | bytes 835592 | tf_op jit(solution)/shard_map/ppermute | solution.py:282
  114.1 11.1 %copy-start.11 = (s32[64,4]{0,1:T(4,128)S(1)}, s32[64,4]{0,1:T(4,128)}, u32[]{:S(2)}) copy-start(s32[64,4]{0,1:T(4,128)} %param.8) | copy-start | bytes 3076
  114.1 12.4 %collective-permute-start.22 = (bf16[288,1152]{1,0:T(8,128)(2,1)S(1)}, bf16[288,1152]{1,0:T(8,128)(2,1)S(1)}, u32[]{:S(2)}, u32[]{:S(2)}) collective-permute-start(bf16[288,1152]{1,0:T(8,128)(2,1)S(1)} %shard_map.107.mid_a), channel_id=1, source_target_pairs={{0,1},{1,0},{2,3},{3,2},{4,5},{5,4},{6,7},{7,6},{8,9},{9,8},{10,11... | collective-permute-start | bytes 1990664 | tf_op jit(solution)/shard_map/ppermute | solution.py:282
  115.7 5.2 %collective-permute-start.7 = (bf16[32,2176]{1,0:T(8,128)(2,1)S(1)}, bf16[32,2176]{1,0:T(8,128)(2,1)S(1)}, u32[]{:S(2)}, u32[]{:S(2)}) collective-permute-start(bf16[32,2176]{1,0:T(8,128)(2,1)S(1)} %get-tuple-element.61), channel_id=1, source_target_pairs={{0,4},{4,0},{8,12},{12,8},{16,20},{20,16},{24,28},{28,24},{1,5},{5... | collective-permute-start | bytes 417800 | tf_op jit(solution)/shard_map/ppermute | solution.py:282
  116.9 4.9 %collective-permute-start.8 = (bf16[32,2176]{1,0:T(8,128)(2,1)S(1)}, bf16[32,2176]{1,0:T(8,128)(2,1)S(1)}, u32[]{:S(2)}, u32[]{:S(2)}) collective-permute-start(bf16[32,2176]{1,0:T(8,128)(2,1)S(1)} %get-tuple-element.62), channel_id=1, source_target_pairs={{0,8},{4,12},{8,0},{12,4},{16,24},{20,28},{24,16},{28,20},{1,9},{5... | collective-permute-start | bytes 417800 | tf_op jit(solution)/shard_map/ppermute | solution.py:282
  117.3 7.4 %collective-permute-start.9 = (bf16[32,2176]{1,0:T(8,128)(2,1)S(1)}, bf16[32,2176]{1,0:T(8,128)(2,1)S(1)}, u32[]{:S(2)}, u32[]{:S(2)}) collective-permute-start(bf16[32,2176]{1,0:T(8,128)(2,1)S(1)} %get-tuple-element.63), channel_id=1, source_target_pairs={{0,12},{4,8},{8,4},{12,0},{16,28},{20,24},{24,20},{28,16},{1,13},{... | collective-permute-start | bytes 417800 | tf_op jit(solution)/shard_map/ppermute | solution.py:282

commit v4 on v3

--- a/solution.py
+++ b/solution.py
@@ -59,27 +59,34 @@
     joint_ref[0:16, width : width + count] = turned.astype(BF16)
 
 
-def join_kernel(in_ref, out_ref, after_ref, joint_ref, again_ref):
+def join_kernel(in_ref, out_ref, joint_ref):
     width = in_ref.shape[1]
-    for target in (joint_ref, again_ref):
-        target[:, :width] = in_ref[...]
-        target[:, width:] = out_ref[...]
+    joint_ref[:, :width] = in_ref[...]
+    joint_ref[:, width:] = out_ref[...]
+
+
+def stack_kernel(own_ref, far_ref, after_ref, stacked_ref):
+    count = own_ref.shape[0]
+    stacked_ref[0:count, :] = own_ref[...]
+    stacked_ref[count:, :] = far_ref[...]
 
 
 def after_kernel(*refs):
     pass
 
 
-def relay_kernel(near_a, far_a, near_b, far_b, mid_ref, mid_out_ref, joint_ref):
+def relay_kernel(near_a, far_a, near_b, far_b, mid_ref, after_ref, joint_ref):
     count, width = near_a.shape
     for at, near, far in ((0, near_a, far_a), (count, near_b, far_b)):
         joint_ref[at : at + count, :width] = near[...]
-        joint_ref[at : at + count, width:] = far[:, width:]
+        joint_ref[at : at + count, width : 2 * width] = far[:, width:]
+    joint_ref[:, 2 * width :] = mid_ref[...]
 
 
 def pack_kernel(first, joint_ref, *refs):
     count = 4
-    out_refs, fold = refs[-1 - count : -1], refs[-1]
+    fold = refs[-1]
+    out_refs = refs[-1 - count : -1]
     tokens, width = joint_ref.shape[0] // 2, joint_ref.shape[1] - LANES
     chunks = width // LANES
     main = out_refs[0].shape[0] // 2
@@ -142,8 +149,8 @@
 
 def main_kernel(early, place_ref, w_ref, *refs):
     blocks, parts = 4, 4
-    weights = refs[:parts]
-    keep_ref, near_ref, far_ref = refs[parts : parts + 3]
+    own_ref, other_ref = refs[:2]
+    keep_ref, near_ref, far_ref = refs[2:5]
     mid, backs, (tail, fold) = refs[-3 - blocks], refs[-2 - blocks : -2], refs[-2:]
     depth = keep_ref.shape[1] // 2
     width = parts * depth
@@ -151,13 +158,15 @@
     main = backs[0].shape[0]
     chunks = width // LANES
     total = keep_ref.shape[0]
+    first, second = pl.ds(0, depth), pl.ds(depth, depth)
+    weights = [own_ref.at[first], other_ref.at[first], own_ref.at[second], other_ref.at[second]]
     pre = jnp.zeros((total, 2 * hidden_width), F32)
     grad = jnp.zeros((total, hidden_width), F32)
     for j, (ref, shift) in enumerate([(keep_ref, 0), (near_ref, 0), (far_ref, 0), (far_ref, 2 * depth)]):
         pre += dot(ref[:, shift : shift + depth], weights[j][:, : 2 * hidden_width])
         grad += dot(ref[:, shift + depth : shift + 2 * depth], weights[j][:, 2 * hidden_width :])
     if early:
-        mid[0:early, :] = refs[parts + 3][...]
+        mid[0:early, :] = refs[5][...]
     weight = w_ref[:, 0:1]
     gate_pre = pre[:, :hidden_width]
     up_pre = pre[:, hidden_width:]
@@ -213,7 +222,7 @@
     return dot_tn(pick, rows[...]), routes
 
 
-def relay_sum_kernel(joint_ref, b0, b1, b2, b3, after_ref, out_ref, rows, fold):
+def relay_sum_kernel(joint_ref, b0, b1, b2, b3, out_ref, rows, fold):
     tokens, width = out_ref.shape[0], rows.shape[1]
     weight = joint_ref[0:16, width:].astype(F32)[0:8, :tokens]
     summed, routes = unpack_sum(weight, (b0, b1, b2, b3), rows, fold)
@@ -241,16 +250,19 @@
     route_ref[...] = route.astype(BF16)
 
 
-def weight_kernel(half, rows_a, rows_b, near_ref, mid_a, mid_b, *refs):
+def weight_kernel(half, rows_a, rows_b, near_ref, *refs):
     in_ref, out_ref, rows, mids = refs[-4:]
-    before = refs[:-4]
+    if half:
+        mid_a, mid_b, before = refs[0][...], refs[1][...], refs[2:4]
+    else:
+        mid_a, mid_b, before = refs[0][...], near_ref[:, 2 * rows.shape[1] :], ()
     depth, hidden_width = out_ref.shape
     count = rows_a.shape[0]
     rows[0:count, :] = rows_a[:, : 2 * depth]
     rows[count : 2 * count, :] = rows_b[:, : 2 * depth]
     rows[2 * count :, :] = near_ref[:, 2 * depth * half : 2 * depth * (half + 1)]
-    mids[0 : 2 * count, :] = mid_a[...]
-    mids[2 * count :, :] = mid_b[...]
+    mids[0 : 2 * count, :] = mid_a
+    mids[2 * count :, :] = mid_b
     in_part = dot_tn(rows[:, :depth], mids[:, : 2 * hidden_width])
     out_part = dot_tn(rows[:, depth:], mids[:, 2 * hidden_width :])
     if before:
@@ -272,7 +284,7 @@
         in_specs=[on_smem] * len(smem) + [on_vmem] * len(vmem) + [on_either] * len(either),
         out_specs=tuple([on_either] * either_outs + [on_vmem] * (len(outs) - either_outs)),
         scratch_shapes=scratch,
-        compiler_params=pltpu.CompilerParams(vmem_limit_bytes=24 * 1024 * 1024),
+        compiler_params=pltpu.CompilerParams(vmem_limit_bytes=16 * 1024 * 1024),
         cost_estimate=pl.CostEstimate(flops=flops, bytes_accessed=moved, transcendentals=0),
         input_output_aliases=aliases or {},
     )(*smem, *vmem, *either)
@@ -308,12 +320,12 @@
     )
     far_joint = swap(joint, "expert", half)
 
-    weights, again = call(
+    (weights,) = call(
         join_kernel,
-        [((depth, 3 * hidden_width), BF16)] * 2,
+        [((depth, 3 * hidden_width), BF16)],
         [],
         [gate_up_weight[0], down_weight[0]],
-        [dense],
+        [],
         [],
         0,
     )
@@ -330,21 +342,6 @@
             4 * (half * main + 16) * token_count * width,
         )
         return [packed[0]] + [swap(packed[j], "expert", j) for j in range(1, half)]
-
-    own = pack(half, joint, [])
-    again, far_weights = call(
-        after_kernel,
-        [(again.shape, BF16), (far_weights.shape, BF16)],
-        [],
-        [],
-        [again, far_weights, far_joint],
-        [],
-        0,
-        2,
-        {0: 0, 1: 1},
-    )
-    weight_parts = [again, swap(again, "dp", 1), far_weights, swap(far_weights, "dp", 1)]
-    far = pack(0, far_joint, own[1:])
 
     def sliced(packed, after):
         return call(
@@ -362,38 +359,37 @@
             0,
         )
 
-    def middle(slices, weight, before, after):
+    own = pack(half, joint, [])
+    *own_slices, own_weight = sliced(own, [far_joint])
+    own_far = swap(own_slices[2], "dp", 2)
+    far = pack(0, far_joint, [own_slices[0], far_weights])
+    (stacked,) = call(
+        stack_kernel,
+        [((2 * depth, 3 * hidden_width), BF16)],
+        [],
+        [weights, far_weights],
+        [far[0]],
+        [],
+        0,
+    )
+    weight_parts = [stacked, swap(stacked, "dp", 1)]
+
+    def middle(slices, weight, before):
         early = before[0].shape[0] if before else 0
         return call(
             functools.partial(main_kernel, early),
             [((early + rows, 3 * hidden_width), BF16)] + [back_shape] * half,
             [places],
             [weight, *weight_parts, *slices, *before],
-            after,
+            [],
             [pltpu.VMEM((16, width), F32), pltpu.VMEM((chunks, LANES), F32)],
             2 * rows * width * 5 * hidden_width,
         )
 
-    *own_slices, own_weight = sliced(own, [])
-    own_far = swap(own_slices[2], "dp", 2)
-    own_mid, *near_back = middle(own_slices, own_weight, [], [])
+    own_mid, *near_back = middle(own_slices, own_weight, [])
     *far_slices, far_weight = sliced(far, [own_mid])
     far_far = swap(far_slices[2], "dp", 2)
-    mid, *far_back = middle(far_slices, far_weight, [own_mid], [own_far])
-
-    mid, near_rows = call(
-        relay_kernel,
-        [(mid.shape, BF16), ((2 * rows, 4 * depth), BF16)],
-        [],
-        [own_slices[1], own_far, far_slices[1], far_far],
-        [mid],
-        [],
-        0,
-        1,
-        {4: 0},
-    )
-    mid_far = swap(mid, "dp", 2)
-    mid_near = swap(mid, "dp", 1)
+    mid, *far_back = middle(far_slices, far_weight, [own_mid])
 
     sum_scratch = [
         pltpu.VMEM((half * main + 16, width), BF16),
@@ -406,12 +402,23 @@
         [((token_count, width + LANES), BF16)],
         [],
         [far_joint, *far_back],
-        [near_rows],
+        [],
         sum_scratch,
         sum_flops,
     )
     far_partial = swap(partial, "expert", half)
-    near_rows = swap(near_rows, "dp", 1)
+
+    mid_far = swap(mid, "dp", 2)
+    (near,) = call(
+        relay_kernel,
+        [((2 * rows, 4 * depth + 3 * hidden_width), BF16)],
+        [],
+        [own_slices[1], own_far, far_slices[1], far_far, mid],
+        [partial],
+        [],
+        0,
+    )
+    near = swap(near, "dp", 1)
     near_back = near_back[:1] + [swap(near_back[j], "expert", j) for j in range(1, half)]
     near_sum, near_route = call(
         near_sum_kernel,
@@ -443,21 +450,19 @@
             2 * 4 * rows * depth * 3 * hidden_width,
         )
 
-    first = weight_part(0, [own_slices[0], far_slices[0], near_rows, mid, mid_near], [])
+    first = weight_part(0, [own_slices[0], far_slices[0], near, mid], [])
     (mid_far,) = call(
         after_kernel,
         [(mid_far.shape, BF16)],
         [],
         [],
-        [mid_far, first[1], far_partial],
+        [mid_far, first[1], far_partial, near_sum],
         [],
         0,
         1,
         {0: 0},
     )
-    grad_gate_up, grad_down = weight_part(
-        1, [own_far, far_far, near_rows, mid_far, swap(mid_far, "dp", 1)], first
-    )
+    grad_gate_up, grad_down = weight_part(1, [own_far, far_far, near, mid_far, swap(mid_far, "dp", 1)], first)
     return (grad_tokens, grad_route.T, grad_gate_up[None], grad_down[None])
 
 

time: 130 us -> 97.4 us (0.75)
  waiting for transfers between devices: 73.4 us -> 48.8 us
  local copies, waits for them, and re-layouts: 9.42 us -> 3.81 us
  Pallas kernels: 18 us -> 15.9 us
    ppermute x23 -> x21, waiting for transfers between devices: 73.4 us -> 48.8 us  [swap(): lax.ppermute(value, axis, [(i, i ^ mask) for i in range(lax.axis_size(axi...]
    unnamed x26 -> x16, local copies, waits for them, and re-layouts: 9.42 us -> 3.81 us
    pallas_call x16, Pallas kernels: 18 us -> 15.9 us  [call(): pl.pallas_call(kernel, out_shape=tuple(outs), in_specs=[on_smem] * len(sm...]
    ppermute x23 -> x21, starting transfers between devices: 27.3 us -> 27.5 us  [swap(): lax.ppermute(value, axis, [(i, i ^ mask) for i in range(lax.axis_size(axi...]
  transfers between devices with their start and end apart: 23 -> 21, of which waited for: 13 -> 16; matrix products, arithmetic and copies ran while one was open for 0% -> 0% of each run, Pallas kernels for 11% -> 13%
where the time goes in v4:
time: 97.4 us; the launch traced here: 96.8 us
  waiting for transfers between devices  48.8 us (50%)
  starting transfers between devices  27.5 us (28%)
  Pallas kernels  15.9 us (16%)
  local copies, waits for them, and re-layouts  3.81 us (4%)
    ppermute x21, waiting for transfers between devices, swap(): lax.ppermute(value, axis, [(i, i ^ mask) for i in range(lax.axis_size(axi...  48.8 us
    ppermute x21, starting transfers between devices, swap(): lax.ppermute(value, axis, [(i, i ^ mask) for i in range(lax.axis_size(axi...  27.5 us
    pallas_call x16, Pallas kernels, call(): pl.pallas_call(kernel, out_shape=tuple(outs), in_specs=[on_smem] * len(sm...  15.9 us
    unnamed x16, local copies, waits for them, and re-layouts  3.81 us
  transfers between devices with their start and end apart: 21, of which 16 were waited for; matrix products, arithmetic and copies ran while one was open for 0% of the time, Pallas kernels for 13%

profile of v4, /device:TPU:1, one launch (start us, length us, event | category | flops | bytes accessed | tf_op | source)
XLA Modules:
  0.0 96.8 jit_solution(16361804202276198156)
XLA Ops:
  0.6 0.0 copy-start.6
  0.6 0.0 copy-start.7
  0.7 0.0 copy-start
  0.7 1.1 %copy-done = bf16[1,512,768]{2,1,0:T(8,128)(2,1)S(1)} copy-done((bf16[1,512,768]{2,1,0:T(8,128)(2,1)S(1)}, bf16[1,512,768]{2,1,0:T(8,128)(2,1)}, u32[]{:S(2)}) %copy-start) | copy-done | bytes 786456
  1.8 1.0 %copy-done.1 = bf16[1,512,384]{2,1,0:T(8,128)(2,1)S(1)} copy-done((bf16[1,512,384]{2,1,0:T(8,128)(2,1)S(1)}, bf16[1,512,384]{2,1,0:T(8,128)(2,1)}, u32[]{:S(2)}) %copy-start.1) | copy-done | bytes 393240
  2.8 0.1 shard_map.96.own_ref
  2.9 2.1 %collective-permute-start.4 = (bf16[512,1152]{1,0:T(8,128)(2,1)S(1)}, bf16[512,1152]{1,0:T(8,128)(2,1)S(1)}, u32[]{:S(2)}, u32[]{:S(2)}) collective-permute-start(bf16[512,1152]{1,0:T(8,128)(2,1)S(1)} %shard_map.96.own_ref), channel_id=1, source_target_pairs={{0,2},{1,3},{2,0},{3,1},{4,6},{5,7},{6,4},{7,5},{8,10},{9,11},{10,... | collective-permute-start | bytes 3538952 | tf_op jit(solution)/shard_map/ppermute | solution.py:294
  5.0 0.6 shard_map.93
  5.6 2.4 %collective-permute-start.3 = (bf16[128,2176]{1,0:T(8,128)(2,1)S(1)}, bf16[128,2176]{1,0:T(8,128)(2,1)S(1)}, u32[]{:S(2)}, u32[]{:S(2)}) collective-permute-start(bf16[128,2176]{1,0:T(8,128)(2,1)S(1)} %get-tuple-element.41.joint_ref), channel_id=1, source_target_pairs={{0,16},{4,20},{8,24},{12,28},{16,0},{20,4},{24,8},{28,12},{1,17},{... | collective-permute-start | bytes 1671176 | tf_op jit(solution)/shard_map/ppermute | solution.py:294
  8.0 1.5 %shard_map.94 = (bf16[64,2176]{1,0:T(8,128)(2,1)S(1)}, bf16[64,2176]{1,0:T(8,128)(2,1)}, bf16[64,2176]{1,0:T(8,128)(2,1)}, bf16[64,2176]{1,0:T(8,128)(2,1)}) custom-call(bf16[128,2176]{1,0:T(8,128)(2,1)S(1)} %get-tuple-element.41.joint_ref), custom_call_target="tpu_custom_call" | custom-call | flops 75497472 | bytes 1671168 | tf_op jit(solution)/shard_map/pallas_call | solution.py:281
  9.5 0.7 copy-done.2
  10.2 1.2 %collective-permute-start = (bf16[64,2176]{1,0:T(8,128)(2,1)}, bf16[64,2176]{1,0:T(8,128)(2,1)}, u32[]{:S(2)}, u32[]{:S(2)}) collective-permute-start(bf16[64,2176]{1,0:T(8,128)(2,1)} %get-tuple-element.43), channel_id=1, source_target_pairs={{0,4},{4,0},{8,12},{12,8},{16,20},{20,16},{24,28},{28,24},{1,5},{5... | collective-permute-start | bytes 835592 | tf_op jit(solution)/shard_map/ppermute | solution.py:294
  11.4 1.3 %collective-permute-start.1 = (bf16[64,2176]{1,0:T(8,128)(2,1)}, bf16[64,2176]{1,0:T(8,128)(2,1)}, u32[]{:S(2)}, u32[]{:S(2)}) collective-permute-start(bf16[64,2176]{1,0:T(8,128)(2,1)} %get-tuple-element.44), channel_id=1, source_target_pairs={{0,8},{4,12},{8,0},{12,4},{16,24},{20,28},{24,16},{28,20},{1,9},{5... | collective-permute-start | bytes 835592 | tf_op jit(solution)/shard_map/ppermute | solution.py:294
  12.7 0.1 collective-permute-start.2
  12.8 4.6 %collective-permute-done.refs_1_ = bf16[64,2176]{1,0:T(8,128)(2,1)} collective-permute-done((bf16[64,2176]{1,0:T(8,128)(2,1)}, bf16[64,2176]{1,0:T(8,128)(2,1)}, u32[]{:S(2)}, u32[]{:S(2)}) %collective-permute-start) | collective-permute-done | bytes 278560 | tf_op jit(solution)/shard_map/ppermute | solution.py:294
  17.4 7.7 %collective-permute-done.1.refs_2_ = bf16[64,2176]{1,0:T(8,128)(2,1)} collective-permute-done((bf16[64,2176]{1,0:T(8,128)(2,1)}, bf16[64,2176]{1,0:T(8,128)(2,1)}, u32[]{:S(2)}, u32[]{:S(2)}) %collective-permute-start.1) | collective-permute-done | bytes 278560 | tf_op jit(solution)/shard_map/ppermute | solution.py:294
  25.1 10.0 %collective-permute-done.2.refs_3_ = bf16[64,2176]{1,0:T(8,128)(2,1)} collective-permute-done((bf16[64,2176]{1,0:T(8,128)(2,1)}, bf16[64,2176]{1,0:T(8,128)(2,1)}, u32[]{:S(2)}, u32[]{:S(2)}) %collective-permute-start.2) | collective-permute-done | bytes 278560 | tf_op jit(solution)/shard_map/ppermute | solution.py:294
  35.1 0.0 collective-permute-done.3.refs_4_.joint_ref
  35.1 1.0 copy-done.3
  36.1 1.2 %shard_map.95 = (bf16[144,1024]{1,0:T(8,128)(2,1)S(1)}, bf16[144,1024]{1,0:T(8,128)(2,1)S(1)}, bf16[144,2048]{1,0:T(8,128)(2,1)S(1)}, f32[144,128]{1,0:T(8,128)S(1)}) custom-call(s32[4]{0:T(128)S(1)} %iota_xor_fusion.place_ref, bf16[64,2176]{1,0:T(8,128)(2,1)S(1)} %copy-done.3, bf16[64,2176]{1,0:T(8,128)(2,1)} %collective-permute-done.refs_1_, ...), custom_call_target="tpu_custom_call" | custom-call | bytes 2367488 | tf_op jit(solution)/shard_map/pallas_call | solution.py:281
  37.3 0.0 collective-permute-done.4.refs_1_.far_ref
  37.3 0.6 shard_map.97
  37.9 0.2 shard_map.98.refs_0_
  38.1 2.5 %collective-permute-start.5 = (bf16[1024,1152]{1,0:T(8,128)(2,1)S(1)}, bf16[1024,1152]{1,0:T(8,128)(2,1)S(1)}, u32[]{:S(2)}, u32[]{:S(2)}) collective-permute-start(bf16[1024,1152]{1,0:T(8,128)(2,1)S(1)} %shard_map.98.refs_0_), channel_id=1, source_target_pairs={{0,1},{1,0},{2,3},{3,2},{4,5},{5,4},{6,7},{7,6},{8,9},{9,8},{10,11... | collective-permute-start | bytes 7077896 | tf_op jit(solution)/shard_map/ppermute | solution.py:294
  40.6 1.3 %collective-permute-start.9 = (bf16[64,2176]{1,0:T(8,128)(2,1)S(1)}, bf16[64,2176]{1,0:T(8,128)(2,1)S(1)}, u32[]{:S(2)}, u32[]{:S(2)}) collective-permute-start(bf16[64,2176]{1,0:T(8,128)(2,1)S(1)} %get-tuple-element.57), channel_id=1, source_target_pairs={{0,4},{4,0},{8,12},{12,8},{16,20},{20,16},{24,28},{28,24},{1,5},{5... | collective-permute-start | bytes 835592 | tf_op jit(solution)/shard_map/ppermute | solution.py:294
  41.9 0.0 collective-permute-start.10
  41.9 1.4 %collective-permute-start.11 = (bf16[64,2176]{1,0:T(8,128)(2,1)S(1)}, bf16[64,2176]{1,0:T(8,128)(2,1)S(1)}, u32[]{:S(2)}, u32[]{:S(2)}) collective-permute-start(bf16[64,2176]{1,0:T(8,128)(2,1)S(1)} %get-tuple-element.59), channel_id=1, source_target_pairs={{0,12},{4,8},{8,4},{12,0},{16,28},{20,24},{24,20},{28,16},{1,13},{... | collective-permute-start | bytes 835592 | tf_op jit(solution)/shard_map/ppermute | solution.py:294
  43.3 0.8 collective-permute-start.16
  44.1 0.7 collective-permute-done.5.refs_1_
  44.8 2.6 %shard_map.99 = (bf16[144,1152]{1,0:T(8,128)(2,1)S(1)}, bf16[32,2176]{1,0:T(8,128)(2,1)S(1)}, bf16[32,2176]{1,0:T(8,128)(2,1)S(1)}, bf16[32,2176]{1,0:T(8,128)(2,1)S(1)}, bf16[32,2176]{1,0:T(8,128)(2,1)S(1)}) custom-call(s32[4]{0:T(128)S(1)} %iota_xor_fusion.place_ref, f32[144,128]{1,0:T(8,128)S(1)} %get-tuple-element.46.w_ref, ...), custom_call_target="tpu_custom_call" | custom-call | flops 1132462080 | bytes 6860800 | tf_op jit(solution)/shard_map/pallas_call | solution.py:281
  47.4 1.4 %collective-permute-done.9.refs_1_ = bf16[64,2176]{1,0:T(8,128)(2,1)S(1)} collective-permute-done((bf16[64,2176]{1,0:T(8,128)(2,1)S(1)}, bf16[64,2176]{1,0:T(8,128)(2,1)S(1)}, u32[]{:S(2)}, u32[]{:S(2)}) %collective-permute-start.9) | collective-permute-done | bytes 278560 | tf_op jit(solution)/shard_map/ppermute | solution.py:294
  48.8 0.9 collective-permute-done.10.refs_2_
  49.8 5.9 %collective-permute-done.11.refs_3_ = bf16[64,2176]{1,0:T(8,128)(2,1)S(1)} collective-permute-done((bf16[64,2176]{1,0:T(8,128)(2,1)S(1)}, bf16[64,2176]{1,0:T(8,128)(2,1)S(1)}, u32[]{:S(2)}, u32[]{:S(2)}) %collective-permute-start.11) | collective-permute-done | bytes 278560 | tf_op jit(solution)/shard_map/ppermute | solution.py:294
  55.7 0.7 shard_map.101
  56.3 0.9 collective-permute-start.17
  57.2 2.6 %shard_map.102 = (bf16[288,1152]{1,0:T(8,128)(2,1)S(1)}, bf16[32,2176]{1,0:T(8,128)(2,1)S(1)}, bf16[32,2176]{1,0:T(8,128)(2,1)S(1)}, bf16[32,2176]{1,0:T(8,128)(2,1)S(1)}, bf16[32,2176]{1,0:T(8,128)(2,1)S(1)}) custom-call(s32[4]{0:T(128)S(1)} %iota_xor_fusion.place_ref, f32[144,128]{1,0:T(8,128)S(1)} %get-tuple-element.61.w_ref, ...), custom_call_target="tpu_custom_call" | custom-call | flops 1132462080 | bytes 7524352 | tf_op jit(solution)/shard_map/pallas_call | solution.py:281
  59.9 1.3 %collective-permute-start.12 = (bf16[32,2176]{1,0:T(8,128)(2,1)S(1)}, bf16[32,2176]{1,0:T(8,128)(2,1)S(1)}, u32[]{:S(2)}, u32[]{:S(2)}) collective-permute-start(bf16[32,2176]{1,0:T(8,128)(2,1)S(1)} %get-tuple-element.66), channel_id=1, source_target_pairs={{0,4},{4,0},{8,12},{12,8},{16,20},{20,16},{24,28},{28,24},{1,5},{5... | collective-permute-start | bytes 417800 | tf_op jit(solution)/shard_map/ppermute | solution.py:294
  61.2 0.3 collective-permute-start.13
  61.5 1.1 %collective-permute-start.14 = (bf16[32,2176]{1,0:T(8,128)(2,1)S(1)}, bf16[32,2176]{1,0:T(8,128)(2,1)S(1)}, u32[]{:S(2)}, u32[]{:S(2)}) collective-permute-start(bf16[32,2176]{1,0:T(8,128)(2,1)S(1)} %get-tuple-element.68), channel_id=1, source_target_pairs={{0,12},{4,8},{8,4},{12,0},{16,28},{20,24},{24,20},{28,16},{1,13},{... | collective-permute-start | bytes 417800 | tf_op jit(solution)/shard_map/ppermute | solution.py:294
  62.6 1.6 %collective-permute-done.12.b1 = bf16[32,2176]{1,0:T(8,128)(2,1)S(1)} collective-permute-done((bf16[32,2176]{1,0:T(8,128)(2,1)S(1)}, bf16[32,2176]{1,0:T(8,128)(2,1)S(1)}, u32[]{:S(2)}, u32[]{:S(2)}) %collective-permute-start.12) | collective-permute-done | bytes 139296 | tf_op jit(solution)/shard_map/ppermute | solution.py:294
  64.1 1.2 %collective-permute-done.13.b2 = bf16[32,2176]{1,0:T(8,128)(2,1)S(1)} collective-permute-done((bf16[32,2176]{1,0:T(8,128)(2,1)S(1)}, bf16[32,2176]{1,0:T(8,128)(2,1)S(1)}, u32[]{:S(2)}, u32[]{:S(2)}) %collective-permute-start.13) | collective-permute-done | bytes 139296 | tf_op jit(solution)/shard_map/ppermute | solution.py:294
  65.4 1.9 %collective-permute-done.14.b3 = bf16[32,2176]{1,0:T(8,128)(2,1)S(1)} collective-permute-done((bf16[32,2176]{1,0:T(8,128)(2,1)S(1)}, bf16[32,2176]{1,0:T(8,128)(2,1)S(1)}, u32[]{:S(2)}, u32[]{:S(2)}) %collective-permute-start.14) | collective-permute-done | bytes 139296 | tf_op jit(solution)/shard_map/ppermute | solution.py:294
  67.2 0.4 shard_map.103.after_ref
  67.6 0.0 collective-permute-done.16.far_a.rows_a
  67.7 2.4 %collective-permute-done.17.far_b.rows_b = bf16[144,2048]{1,0:T(8,128)(2,1)S(1)} collective-permute-done((bf16[144,2048]{1,0:T(8,128)(2,1)S(1)}, bf16[144,2048]{1,0:T(8,128)(2,1)S(1)}, u32[]{:S(2)}, u32[]{:S(2)}) %collective-permute-start.17) | collective-permute-done | bytes 589856 | tf_op jit(solution)/shard_map/ppermute | solution.py:294
  70.0 0.1 shard_map.105
  70.2 2.2 %collective-permute-start.18 = (bf16[288,3200]{1,0:T(8,128)(2,1)S(1)}, bf16[288,3200]{1,0:T(8,128)(2,1)S(1)}, u32[]{:S(2)}, u32[]{:S(2)}) collective-permute-start(bf16[288,3200]{1,0:T(8,128)(2,1)S(1)} %shard_map.105), channel_id=1, source_target_pairs={{0,1},{1,0},{2,3},{3,2},{4,5},{5,4},{6,7},{7,6},{8,9},{9,8},{10,11... | collective-permute-start | bytes 5529608 | tf_op jit(solution)/shard_map/ppermute | solution.py:294
  72.3 0.9 collective-permute-start.19
  73.2 1.2 %collective-permute-start.6 = (bf16[32,2176]{1,0:T(8,128)(2,1)S(1)}, bf16[32,2176]{1,0:T(8,128)(2,1)S(1)}, u32[]{:S(2)}, u32[]{:S(2)}) collective-permute-start(bf16[32,2176]{1,0:T(8,128)(2,1)S(1)} %get-tuple-element.52), channel_id=1, source_target_pairs={{0,4},{4,0},{8,12},{12,8},{16,20},{20,16},{24,28},{28,24},{1,5},{5... | collective-permute-start | bytes 417800 | tf_op jit(solution)/shard_map/ppermute | solution.py:294
  74.4 1.2 %collective-permute-start.15 = (bf16[64,2176]{1,0:T(8,128)(2,1)S(1)}, bf16[64,2176]{1,0:T(8,128)(2,1)S(1)}, u32[]{:S(2)}, u32[]{:S(2)}) collective-permute-start(bf16[64,2176]{1,0:T(8,128)(2,1)S(1)} %shard_map.103.after_ref), channel_id=1, source_target_pairs={{0,16},{4,20},{8,24},{12,28},{16,0},{20,4},{24,8},{28,12},{1,17},{... | collective-permute-start | bytes 835592 | tf_op jit(solution)/shard_map/ppermute | solution.py:294
  75.7 1.1 %collective-permute-start.7 = (bf16[32,2176]{1,0:T(8,128)(2,1)S(1)}, bf16[32,2176]{1,0:T(8,128)(2,1)S(1)}, u32[]{:S(2)}, u32[]{:S(2)}) collective-permute-start(bf16[32,2176]{1,0:T(8,128)(2,1)S(1)} %get-tuple-element.53), channel_id=1, source_target_pairs={{0,8},{4,12},{8,0},{12,4},{16,24},{20,28},{24,16},{28,20},{1,9},{5... | collective-permute-start | bytes 417800 | tf_op jit(solution)/shard_map/ppermute | solution.py:294
  76.8 1.3 %collective-permute-done.6.b1 = bf16[32,2176]{1,0:T(8,128)(2,1)S(1)} collective-permute-done((bf16[32,2176]{1,0:T(8,128)(2,1)S(1)}, bf16[32,2176]{1,0:T(8,128)(2,1)S(1)}, u32[]{:S(2)}, u32[]{:S(2)}) %collective-permute-start.6) | collective-permute-done | bytes 139296 | tf_op jit(solution)/shard_map/ppermute | solution.py:294
  78.1 1.3 %collective-permute-start.8 = (bf16[32,2176]{1,0:T(8,128)(2,1)S(1)}, bf16[32,2176]{1,0:T(8,128)(2,1)S(1)}, u32[]{:S(2)}, u32[]{:S(2)}) collective-permute-start(bf16[32,2176]{1,0:T(8,128)(2,1)S(1)} %get-tuple-element.54), channel_id=1, source_target_pairs={{0,12},{4,8},{8,4},{12,0},{16,28},{20,24},{24,20},{28,16},{1,13},{... | collective-permute-start | bytes 417800 | tf_op jit(solution)/shard_map/ppermute | solution.py:294
  79.4 4.7 %collective-permute-done.7.b2 = bf16[32,2176]{1,0:T(8,128)(2,1)S(1)} collective-permute-done((bf16[32,2176]{1,0:T(8,128)(2,1)S(1)}, bf16[32,2176]{1,0:T(8,128)(2,1)S(1)}, u32[]{:S(2)}, u32[]{:S(2)}) %collective-permute-start.7) | collective-permute-done | bytes 139296 | tf_op jit(solution)/shard_map/ppermute | solution.py:294
  84.1 3.0 %collective-permute-done.8.b3 = bf16[32,2176]{1,0:T(8,128)(2,1)S(1)} collective-permute-done((bf16[32,2176]{1,0:T(8,128)(2,1)S(1)}, bf16[32,2176]{1,0:T(8,128)(2,1)S(1)}, u32[]{:S(2)}, u32[]{:S(2)}) %collective-permute-start.8) | collective-permute-done | bytes 139296 | tf_op jit(solution)/shard_map/ppermute | solution.py:294
  87.1 0.4 shard_map.100
  87.5 0.0 collective-permute-done.18.near_ref
  87.5 1.2 %shard_map.106 = (f32[512,768]{1,0:T(8,128)S(1)}, f32[512,384]{1,0:T(8,128)S(1)}) custom-call(bf16[144,1024]{1,0:T(8,128)(2,1)S(1)} %get-tuple-element.47.refs_0_.refs_2_.rows_a, bf16[144,1024]{1,0:T(8,128)(2,1)S(1)} %get-tuple-element.62.refs_2_.rows_b, bf16[288,3200]{1,0:T(8,128)(2,1)S(1)} %collective-permute-done.18.near_ref, ...), custom_call_target="tpu_custom_call" | custom-call | flops 679477248 | bytes 5455872 | tf_op jit(solution)/shard_map/pallas_call | solution.py:281
  88.8 1.1 %collective-permute-done.15.far_ref.refs_2_ = bf16[64,2176]{1,0:T(8,128)(2,1)S(1)} collective-permute-done((bf16[64,2176]{1,0:T(8,128)(2,1)S(1)}, bf16[64,2176]{1,0:T(8,128)(2,1)S(1)}, u32[]{:S(2)}, u32[]{:S(2)}) %collective-permute-start.15) | collective-permute-done | bytes 278560 | tf_op jit(solution)/shard_map/ppermute | solution.py:294
  89.9 0.0 collective-permute-done.19.refs_0_
  89.9 2.8 %collective-permute-start.20 = (bf16[288,1152]{1,0:T(8,128)(2,1)S(1)}, bf16[288,1152]{1,0:T(8,128)(2,1)S(1)}, u32[]{:S(2)}, u32[]{:S(2)}) collective-permute-start(bf16[288,1152]{1,0:T(8,128)(2,1)S(1)} %shard_map.107.refs_0_), channel_id=1, source_target_pairs={{0,1},{1,0},{2,3},{3,2},{4,5},{5,4},{6,7},{7,6},{8,9},{9,8},{10,11... | collective-permute-start | bytes 1990664 | tf_op jit(solution)/shard_map/ppermute | solution.py:294
  92.7 1.3 %shard_map.104 = (bf16[64,2048]{1,0:T(8,128)(2,1)}, bf16[4,64]{1,0:T(4,128)(2,1)}) custom-call(s32[8]{0:T(128)S(1)} %iota_xor_fusion.1.peer_ref, s32[4,64]{1,0:T(4,128)S(1)} %bitcast.10, f32[64,2048]{1,0:T(8,128)S(1)} %get-tuple-element.55.near_ref.refs_3_, f32[8,64]{1,0:T(8,128)S(1)} %get-tuple-element.56.near_route_ref, ...), custom_call_target="tpu_custom_call" | custom-call | bytes 1068544 | tf_op jit(solution)/shard_map/pallas_call | solution.py:281
  94.0 0.4 collective-permute-done.20.refs_1_
  94.4 2.4 %shard_map.108 = (f32[512,768]{1,0:T(8,128)}, f32[512,384]{1,0:T(8,128)}) custom-call(bf16[144,2048]{1,0:T(8,128)(2,1)S(1)} %collective-permute-done.16.far_a.rows_a, bf16[144,2048]{1,0:T(8,128)(2,1)S(1)} %collective-permute-done.17.far_b.rows_b, bf16[288,3200]{1,0:T(8,128)(2,1)S(1)} %collective-permute-done.18.near_ref, ...), custom_call_target="tpu_custom_call" | custom-call | flops 679477248 | bytes 9068544 | tf_op jit(solution)/shard_map/pallas_call | solution.py:281
  (12 shorter events, 0.0 us)
Async XLA Ops:
  0.6 4.4 %copy-start.6 = (s32[64,4]{0,1:T(4,128)S(1)}, s32[64,4]{0,1:T(4,128)}, u32[]{:S(2)}) copy-start(s32[64,4]{0,1:T(4,128)} %param.8) | copy-start | bytes 3076
  0.6 4.4 %copy-start.7 = (bf16[64,4]{0,1:T(4,128)(2,1)S(1)}, bf16[64,4]{0,1:T(4,128)(2,1)}, u32[]{:S(2)}) copy-start(bf16[64,4]{0,1:T(4,128)(2,1)} %param.9) | copy-start | bytes 1540
  0.7 1.1 %copy-start = (bf16[1,512,768]{2,1,0:T(8,128)(2,1)S(1)}, bf16[1,512,768]{2,1,0:T(8,128)(2,1)}, u32[]{:S(2)}) copy-start(bf16[1,512,768]{2,1,0:T(8,128)(2,1)} %param.10) | copy-start | bytes 2359300
  1.8 1.0 %copy-start.1 = (bf16[1,512,384]{2,1,0:T(8,128)(2,1)S(1)}, bf16[1,512,384]{2,1,0:T(8,128)(2,1)}, u32[]{:S(2)}) copy-start(bf16[1,512,384]{2,1,0:T(8,128)(2,1)} %param.11) | copy-start | bytes 1179652
  2.8 2.2 %copy-start.4 = (bf16[64,2048]{1,0:T(8,128)(2,1)S(1)}, bf16[64,2048]{1,0:T(8,128)(2,1)}, u32[]{:S(2)}) copy-start(bf16[64,2048]{1,0:T(8,128)(2,1)} %x_ref.1) | copy-start | bytes 786436
  2.8 2.2 %copy-start.5 = (bf16[64,2048]{1,0:T(8,128)(2,1)S(1)}, bf16[64,2048]{1,0:T(8,128)(2,1)}, u32[]{:S(2)}) copy-start(bf16[64,2048]{1,0:T(8,128)(2,1)} %dy_ref.1) | copy-start | bytes 786436
  2.9 34.4 %collective-permute-start.4 = (bf16[512,1152]{1,0:T(8,128)(2,1)S(1)}, bf16[512,1152]{1,0:T(8,128)(2,1)S(1)}, u32[]{:S(2)}, u32[]{:S(2)}) collective-permute-start(bf16[512,1152]{1,0:T(8,128)(2,1)S(1)} %shard_map.96.own_ref), channel_id=1, source_target_pairs={{0,2},{1,3},{2,0},{3,1},{4,6},{5,7},{6,4},{7,5},{8,10},{9,11},{10,... | collective-permute-start | bytes 3538952 | tf_op jit(solution)/shard_map/ppermute | solution.py:294
  5.6 29.5 %collective-permute-start.3 = (bf16[128,2176]{1,0:T(8,128)(2,1)S(1)}, bf16[128,2176]{1,0:T(8,128)(2,1)S(1)}, u32[]{:S(2)}, u32[]{:S(2)}) collective-permute-start(bf16[128,2176]{1,0:T(8,128)(2,1)S(1)} %get-tuple-element.41.joint_ref), channel_id=1, source_target_pairs={{0,16},{4,20},{8,24},{12,28},{16,0},{20,4},{24,8},{28,12},{1,17},{... | collective-permute-start | bytes 1671176 | tf_op jit(solution)/shard_map/ppermute | solution.py:294
  9.5 0.7 copy-start.2
  10.2 7.2 %collective-permute-start = (bf16[64,2176]{1,0:T(8,128)(2,1)}, bf16[64,2176]{1,0:T(8,128)(2,1)}, u32[]{:S(2)}, u32[]{:S(2)}) collective-permute-start(bf16[64,2176]{1,0:T(8,128)(2,1)} %get-tuple-element.43), channel_id=1, source_target_pairs={{0,4},{4,0},{8,12},{12,8},{16,20},{20,16},{24,28},{28,24},{1,5},{5... | collective-permute-start | bytes 835592 | tf_op jit(solution)/shard_map/ppermute | solution.py:294
  11.4 13.7 %collective-permute-start.1 = (bf16[64,2176]{1,0:T(8,128)(2,1)}, bf16[64,2176]{1,0:T(8,128)(2,1)}, u32[]{:S(2)}, u32[]{:S(2)}) collective-permute-start(bf16[64,2176]{1,0:T(8,128)(2,1)} %get-tuple-element.44), channel_id=1, source_target_pairs={{0,8},{4,12},{8,0},{12,4},{16,24},{20,28},{24,16},{28,20},{1,9},{5... | collective-permute-start | bytes 835592 | tf_op jit(solution)/shard_map/ppermute | solution.py:294
  12.7 22.4 %collective-permute-start.2 = (bf16[64,2176]{1,0:T(8,128)(2,1)}, bf16[64,2176]{1,0:T(8,128)(2,1)}, u32[]{:S(2)}, u32[]{:S(2)}) collective-permute-start(bf16[64,2176]{1,0:T(8,128)(2,1)} %get-tuple-element.45), channel_id=1, source_target_pairs={{0,12},{4,8},{8,4},{12,0},{16,28},{20,24},{24,20},{28,16},{1,13},{... | collective-permute-start | bytes 835592 | tf_op jit(solution)/shard_map/ppermute | solution.py:294
  35.1 1.0 copy-start.3
  38.1 6.7 %collective-permute-start.5 = (bf16[1024,1152]{1,0:T(8,128)(2,1)S(1)}, bf16[1024,1152]{1,0:T(8,128)(2,1)S(1)}, u32[]{:S(2)}, u32[]{:S(2)}) collective-permute-start(bf16[1024,1152]{1,0:T(8,128)(2,1)S(1)} %shard_map.98.refs_0_), channel_id=1, source_target_pairs={{0,1},{1,0},{2,3},{3,2},{4,5},{5,4},{6,7},{7,6},{8,9},{9,8},{10,11... | collective-permute-start | bytes 7077896 | tf_op jit(solution)/shard_map/ppermute | solution.py:294
  40.6 8.2 %collective-permute-start.9 = (bf16[64,2176]{1,0:T(8,128)(2,1)S(1)}, bf16[64,2176]{1,0:T(8,128)(2,1)S(1)}, u32[]{:S(2)}, u32[]{:S(2)}) collective-permute-start(bf16[64,2176]{1,0:T(8,128)(2,1)S(1)} %get-tuple-element.57), channel_id=1, source_target_pairs={{0,4},{4,0},{8,12},{12,8},{16,20},{20,16},{24,28},{28,24},{1,5},{5... | collective-permute-start | bytes 835592 | tf_op jit(solution)/shard_map/ppermute | solution.py:294
  41.9 7.9 %collective-permute-start.10 = (bf16[64,2176]{1,0:T(8,128)(2,1)S(1)}, bf16[64,2176]{1,0:T(8,128)(2,1)S(1)}, u32[]{:S(2)}, u32[]{:S(2)}) collective-permute-start(bf16[64,2176]{1,0:T(8,128)(2,1)S(1)} %get-tuple-element.58), channel_id=1, source_target_pairs={{0,8},{4,12},{8,0},{12,4},{16,24},{20,28},{24,16},{28,20},{1,9},{5... | collective-permute-start | bytes 835592 | tf_op jit(solution)/shard_map/ppermute | solution.py:294
  41.9 13.8 %collective-permute-start.11 = (bf16[64,2176]{1,0:T(8,128)(2,1)S(1)}, bf16[64,2176]{1,0:T(8,128)(2,1)S(1)}, u32[]{:S(2)}, u32[]{:S(2)}) collective-permute-start(bf16[64,2176]{1,0:T(8,128)(2,1)S(1)} %get-tuple-element.59), channel_id=1, source_target_pairs={{0,12},{4,8},{8,4},{12,0},{16,28},{20,24},{24,20},{28,16},{1,13},{... | collective-permute-start | bytes 835592 | tf_op jit(solution)/shard_map/ppermute | solution.py:294
  43.3 24.4 %collective-permute-start.16 = (bf16[144,2048]{1,0:T(8,128)(2,1)S(1)}, bf16[144,2048]{1,0:T(8,128)(2,1)S(1)}, u32[]{:S(2)}, u32[]{:S(2)}) collective-permute-start(bf16[144,2048]{1,0:T(8,128)(2,1)S(1)} %get-tuple-element.50.refs_4_), channel_id=1, source_target_pairs={{0,2},{1,3},{2,0},{3,1},{4,6},{5,7},{6,4},{7,5},{8,10},{9,11},{10,... | collective-permute-start | bytes 1769480 | tf_op jit(solution)/shard_map/ppermute | solution.py:294
  56.3 13.7 %collective-permute-start.17 = (bf16[144,2048]{1,0:T(8,128)(2,1)S(1)}, bf16[144,2048]{1,0:T(8,128)(2,1)S(1)}, u32[]{:S(2)}, u32[]{:S(2)}) collective-permute-start(bf16[144,2048]{1,0:T(8,128)(2,1)S(1)} %get-tuple-element.64.refs_4_), channel_id=1, source_target_pairs={{0,2},{1,3},{2,0},{3,1},{4,6},{5,7},{6,4},{7,5},{8,10},{9,11},{10,... | collective-permute-start | bytes 1769480 | tf_op jit(solution)/shard_map/ppermute | solution.py:294
  59.9 4.3 %collective-permute-start.12 = (bf16[32,2176]{1,0:T(8,128)(2,1)S(1)}, bf16[32,2176]{1,0:T(8,128)(2,1)S(1)}, u32[]{:S(2)}, u32[]{:S(2)}) collective-permute-start(bf16[32,2176]{1,0:T(8,128)(2,1)S(1)} %get-tuple-element.66), channel_id=1, source_target_pairs={{0,4},{4,0},{8,12},{12,8},{16,20},{20,16},{24,28},{28,24},{1,5},{5... | collective-permute-start | bytes 417800 | tf_op jit(solution)/shard_map/ppermute | solution.py:294
  61.2 4.2 %collective-permute-start.13 = (bf16[32,2176]{1,0:T(8,128)(2,1)S(1)}, bf16[32,2176]{1,0:T(8,128)(2,1)S(1)}, u32[]{:S(2)}, u32[]{:S(2)}) collective-permute-start(bf16[32,2176]{1,0:T(8,128)(2,1)S(1)} %get-tuple-element.67), channel_id=1, source_target_pairs={{0,8},{4,12},{8,0},{12,4},{16,24},{20,28},{24,16},{28,20},{1,9},{5... | collective-permute-start | bytes 417800 | tf_op jit(solution)/shard_map/ppermute | solution.py:294
  61.5 5.7 %collective-permute-start.14 = (bf16[32,2176]{1,0:T(8,128)(2,1)S(1)}, bf16[32,2176]{1,0:T(8,128)(2,1)S(1)}, u32[]{:S(2)}, u32[]{:S(2)}) collective-permute-start(bf16[32,2176]{1,0:T(8,128)(2,1)S(1)} %get-tuple-element.68), channel_id=1, source_target_pairs={{0,12},{4,8},{8,4},{12,0},{16,28},{20,24},{24,20},{28,16},{1,13},{... | collective-permute-start | bytes 417800 | tf_op jit(solution)/shard_map/ppermute | solution.py:294
  70.2 17.3 %collective-permute-start.18 = (bf16[288,3200]{1,0:T(8,128)(2,1)S(1)}, bf16[288,3200]{1,0:T(8,128)(2,1)S(1)}, u32[]{:S(2)}, u32[]{:S(2)}) collective-permute-start(bf16[288,3200]{1,0:T(8,128)(2,1)S(1)} %shard_map.105), channel_id=1, source_target_pairs={{0,1},{1,0},{2,3},{3,2},{4,5},{5,4},{6,7},{7,6},{8,9},{9,8},{10,11... | collective-permute-start | bytes 5529608 | tf_op jit(solution)/shard_map/ppermute | solution.py:294
  72.3 17.5 %collective-permute-start.19 = (bf16[288,1152]{1,0:T(8,128)(2,1)S(1)}, bf16[288,1152]{1,0:T(8,128)(2,1)S(1)}, u32[]{:S(2)}, u32[]{:S(2)}) collective-permute-start(bf16[288,1152]{1,0:T(8,128)(2,1)S(1)} %get-tuple-element.71.mid_ref.refs_0_), channel_id=1, source_target_pairs={{0,2},{1,3},{2,0},{3,1},{4,6},{5,7},{6,4},{7,5},{8,10},{9,11},{10,... | collective-permute-start | bytes 1990664 | tf_op jit(solution)/shard_map/ppermute | solution.py:294
  73.2 4.9 %collective-permute-start.6 = (bf16[32,2176]{1,0:T(8,128)(2,1)S(1)}, bf16[32,2176]{1,0:T(8,128)(2,1)S(1)}, u32[]{:S(2)}, u32[]{:S(2)}) collective-permute-start(bf16[32,2176]{1,0:T(8,128)(2,1)S(1)} %get-tuple-element.52), channel_id=1, source_target_pairs={{0,4},{4,0},{8,12},{12,8},{16,20},{20,16},{24,28},{28,24},{1,5},{5... | collective-permute-start | bytes 417800 | tf_op jit(solution)/shard_map/ppermute | solution.py:294
  74.4 15.4 %collective-permute-start.15 = (bf16[64,2176]{1,0:T(8,128)(2,1)S(1)}, bf16[64,2176]{1,0:T(8,128)(2,1)S(1)}, u32[]{:S(2)}, u32[]{:S(2)}) collective-permute-start(bf16[64,2176]{1,0:T(8,128)(2,1)S(1)} %shard_map.103.after_ref), channel_id=1, source_target_pairs={{0,16},{4,20},{8,24},{12,28},{16,0},{20,4},{24,8},{28,12},{1,17},{... | collective-permute-start | bytes 835592 | tf_op jit(solution)/shard_map/ppermute | solution.py:294
  75.7 8.5 %collective-permute-start.7 = (bf16[32,2176]{1,0:T(8,128)(2,1)S(1)}, bf16[32,2176]{1,0:T(8,128)(2,1)S(1)}, u32[]{:S(2)}, u32[]{:S(2)}) collective-permute-start(bf16[32,2176]{1,0:T(8,128)(2,1)S(1)} %get-tuple-element.53), channel_id=1, source_target_pairs={{0,8},{4,12},{8,0},{12,4},{16,24},{20,28},{24,16},{28,20},{1,9},{5... | collective-permute-start | bytes 417800 | tf_op jit(solution)/shard_map/ppermute | solution.py:294
  78.1 9.0 %collective-permute-start.8 = (bf16[32,2176]{1,0:T(8,128)(2,1)S(1)}, bf16[32,2176]{1,0:T(8,128)(2,1)S(1)}, u32[]{:S(2)}, u32[]{:S(2)}) collective-permute-start(bf16[32,2176]{1,0:T(8,128)(2,1)S(1)} %get-tuple-element.54), channel_id=1, source_target_pairs={{0,12},{4,8},{8,4},{12,0},{16,28},{20,24},{24,20},{28,16},{1,13},{... | collective-permute-start | bytes 417800 | tf_op jit(solution)/shard_map/ppermute | solution.py:294
  89.9 4.5 %collective-permute-start.20 = (bf16[288,1152]{1,0:T(8,128)(2,1)S(1)}, bf16[288,1152]{1,0:T(8,128)(2,1)S(1)}, u32[]{:S(2)}, u32[]{:S(2)}) collective-permute-start(bf16[288,1152]{1,0:T(8,128)(2,1)S(1)} %shard_map.107.refs_0_), channel_id=1, source_target_pairs={{0,1},{1,0},{2,3},{3,2},{4,5},{5,4},{6,7},{7,6},{8,9},{9,8},{10,11... | collective-permute-start | bytes 1990664 | tf_op jit(solution)/shard_map/ppermute | solution.py:294

commit v5 on v4

--- a/solution.py
+++ b/solution.py
@@ -26,6 +26,12 @@
 
 def dot_tn(a, b):
     return lax.dot_general(a, b, (((0,), (0,)), ((), ())), preferred_element_type=F32)
+
+
+def start(source, target, sem):
+    copy = pltpu.make_async_copy(source, target, sem)
+    copy.start()
+    return copy
 
 
 def picks(weight, main):
@@ -75,7 +81,8 @@
     pass
 
 
-def relay_kernel(near_a, far_a, near_b, far_b, mid_ref, after_ref, joint_ref):
+def relay_kernel(near_a, far_a, near_b, far_b, mid_ref, *refs):
+    joint_ref = refs[-1]
     count, width = near_a.shape
     for at, near, far in ((0, near_a, far_a), (count, near_b, far_b)):
         joint_ref[at : at + count, :width] = near[...]
@@ -85,8 +92,9 @@
 
 def pack_kernel(first, joint_ref, *refs):
     count = 4
-    fold = refs[-1]
-    out_refs = refs[-1 - count : -1]
+    kept, fold, sem = refs[-3:]
+    kept_ref, *out_refs = refs[-3 - count : -3]
+    out_refs = [kept, *out_refs]
     tokens, width = joint_ref.shape[0] // 2, joint_ref.shape[1] - LANES
     chunks = width // LANES
     main = out_refs[0].shape[0] // 2
@@ -108,11 +116,16 @@
         column = jnp.sum(mains[j] * mine, axis=1, keepdims=True)
         last = jnp.sum(tails[first + j : first + j + 1, :] * mine, axis=1, keepdims=True)
         out_refs[j][main:, width:] = jnp.where(lane < LANES // 2, column, last).astype(BF16)
-
-
-def slice_kernel(place_ref, *refs):
+        if j == 0:
+            copy = start(kept, kept_ref, sem)
+    copy.wait()
+
+
+def slice_kernel(there, place_ref, *refs):
     blocks, parts = 4, 4
-    in_refs, (keep_ref, near_ref, far_ref, weight_ref, fold) = refs[:blocks], refs[-5:]
+    keep_ref, near_ref, far_ref, weight_ref, fold, held, sems = refs[-7:]
+    copies = {i: start(refs[i], held.at[i - there], sems.at[i - there]) for i in range(there, blocks)}
+    in_refs = list(refs[:there]) + [held.at[i - there] for i in range(there, blocks)]
     main = in_refs[0].shape[0] // 2
     depth = keep_ref.shape[1] // 2
     width = parts * depth
@@ -121,6 +134,8 @@
     lane = lax.broadcasted_iota(jnp.int32, (1, LANES), 1)
     lasts = []
     for i in range(blocks):
+        if i in copies:
+            copies[i].wait()
         for j, (target, shift) in enumerate(targets):
             columns = pl.ds(pl.multiple_of(place_ref[j] * depth, depth), depth)
             for side in range(2):
@@ -232,7 +247,7 @@
     out_ref[0:16, width : width + tokens] = block
 
 
-def near_sum_kernel(w_ref, b0, b1, b2, b3, grad_ref, route_ref, rows, fold):
+def near_sum_kernel(w_ref, b0, b1, b2, b3, after_ref, grad_ref, route_ref, rows, fold):
     summed, routes = unpack_sum(w_ref[...], (b0, b1, b2, b3), rows, fold)
     grad_ref[...] = summed
     route_ref[...] = jnp.concatenate(routes + [jnp.zeros_like(route) for route in routes], axis=0)
@@ -250,26 +265,40 @@
     route_ref[...] = route.astype(BF16)
 
 
-def weight_kernel(half, rows_a, rows_b, near_ref, *refs):
-    in_ref, out_ref, rows, mids = refs[-4:]
-    if half:
-        mid_a, mid_b, before = refs[0][...], refs[1][...], refs[2:4]
-    else:
-        mid_a, mid_b, before = refs[0][...], near_ref[:, 2 * rows.shape[1] :], ()
-    depth, hidden_width = out_ref.shape
+def fill(rows, mids, rows_a, rows_b, rows_c, mid_a, mid_b):
     count = rows_a.shape[0]
-    rows[0:count, :] = rows_a[:, : 2 * depth]
-    rows[count : 2 * count, :] = rows_b[:, : 2 * depth]
-    rows[2 * count :, :] = near_ref[:, 2 * depth * half : 2 * depth * (half + 1)]
+    rows[0:count, :] = rows_a
+    rows[count : 2 * count, :] = rows_b
+    rows[2 * count :, :] = rows_c
     mids[0 : 2 * count, :] = mid_a
     mids[2 * count :, :] = mid_b
-    in_part = dot_tn(rows[:, :depth], mids[:, : 2 * hidden_width])
-    out_part = dot_tn(rows[:, depth:], mids[:, 2 * hidden_width :])
-    if before:
-        in_part = in_part + before[0][...]
-        out_part = out_part + before[1][...]
-    in_ref[...] = in_part
-    out_ref[...] = out_part
+
+
+def first_weight_kernel(rows_a, rows_b, near_ref, mid_ref, in_ref, out_ref, rows, mids):
+    depth, hidden_width = out_ref.shape
+    near, near_mid = near_ref[:, : 2 * depth], near_ref[:, 4 * depth :]
+    fill(rows, mids, rows_a[...], rows_b[...], near, mid_ref[...], near_mid)
+    in_ref[...] = dot_tn(rows[:, :depth], mids[:, : 2 * hidden_width])
+    out_ref[...] = dot_tn(rows[:, depth:], mids[:, 2 * hidden_width :])
+
+
+def second_weight_kernel(rows_a, rows_b, near_ref, mid_a, mid_b, in_part, out_part, *refs):
+    in_ref, out_ref, rows, mids, in_held, out_held, sems = refs
+    depth, hidden_width = out_part.shape
+    span = slice(0, 2 * depth)
+    fill(rows, mids, rows_a[:, span], rows_b[:, span], near_ref[:, 2 * depth : 4 * depth], mid_a[...], mid_b[...])
+    copies = []
+    step = depth // 4
+    for m in range(4):
+        at = slice(m * step, (m + 1) * step)
+        lines = pl.ds(m * step, step)
+        in_held[at, :] = in_part[at, :] + dot_tn(rows[:, at], mids[:, : 2 * hidden_width])
+        copies.append(start(in_held.at[lines], in_ref.at[lines], sems.at[0, m]))
+        other = slice(depth + m * step, depth + (m + 1) * step)
+        out_held[at, :] = out_part[at, :] + dot_tn(rows[:, other], mids[:, 2 * hidden_width :])
+        copies.append(start(out_held.at[lines], out_ref.at[lines], sems.at[1, m]))
+    for copy in copies:
+        copy.wait()
 
 
 def call(kernel, outs, smem, vmem, either, scratch, flops, either_outs=0, aliases=None):
@@ -338,14 +367,15 @@
             [],
             [value],
             after,
-            [pltpu.VMEM((chunks, LANES), F32)],
+            [pltpu.VMEM(*packed_shape), pltpu.VMEM((chunks, LANES), F32), pltpu.SemaphoreType.DMA],
             4 * (half * main + 16) * token_count * width,
+            1,
         )
         return [packed[0]] + [swap(packed[j], "expert", j) for j in range(1, half)]
 
-    def sliced(packed, after):
+    def sliced(there, others, after):
         return call(
-            slice_kernel,
+            functools.partial(slice_kernel, len(there)),
             [
                 ((rows, 2 * depth), BF16),
                 ((rows, 2 * depth), BF16),
@@ -353,16 +383,20 @@
                 ((rows, LANES), F32),
             ],
             [places],
-            packed,
-            after,
-            [pltpu.VMEM((2, half * chunks, LANES), F32)],
+            there,
+            others + after,
+            [
+                pltpu.VMEM((2, half * chunks, LANES), F32),
+                pltpu.VMEM((len(others), *packed_shape[0]), BF16),
+                pltpu.SemaphoreType.DMA((len(others),)),
+            ],
             0,
         )
 
     own = pack(half, joint, [])
-    *own_slices, own_weight = sliced(own, [far_joint])
+    far = pack(0, far_joint, [*own[1:], far_weights])
+    *own_slices, own_weight = sliced([], own, [far[0]])
     own_far = swap(own_slices[2], "dp", 2)
-    far = pack(0, far_joint, [own_slices[0], far_weights])
     (stacked,) = call(
         stack_kernel,
         [((2 * depth, 3 * hidden_width), BF16)],
@@ -374,29 +408,29 @@
     )
     weight_parts = [stacked, swap(stacked, "dp", 1)]
 
-    def middle(slices, weight, before):
+    def middle(slices, weight, before, after):
         early = before[0].shape[0] if before else 0
         return call(
             functools.partial(main_kernel, early),
             [((early + rows, 3 * hidden_width), BF16)] + [back_shape] * half,
             [places],
             [weight, *weight_parts, *slices, *before],
-            [],
+            after,
             [pltpu.VMEM((16, width), F32), pltpu.VMEM((chunks, LANES), F32)],
             2 * rows * width * 5 * hidden_width,
         )
 
-    own_mid, *near_back = middle(own_slices, own_weight, [])
-    *far_slices, far_weight = sliced(far, [own_mid])
+    own_mid, *near_back = middle(own_slices, own_weight, [], [])
+    *far_slices, far_weight = sliced(far[1:], far[:1], [own_mid])
     far_far = swap(far_slices[2], "dp", 2)
-    mid, *far_back = middle(far_slices, far_weight, [own_mid])
+    mid, *far_back = middle(far_slices, far_weight, [own_mid], [own_far])
 
     sum_scratch = [
         pltpu.VMEM((half * main + 16, width), BF16),
         pltpu.VMEM((half * chunks, LANES), F32),
     ]
     sum_flops = 2 * (half * main + 16) * width * token_count
-    far_back = far_back[:1] + [swap(far_back[j], "expert", j) for j in range(1, half)]
+    far_back = far_back[-1:] + [swap(far_back[j - 1], "expert", j) for j in range(1, half)]
     (partial,) = call(
         relay_sum_kernel,
         [((token_count, width + LANES), BF16)],
@@ -407,6 +441,7 @@
         sum_flops,
     )
     far_partial = swap(partial, "expert", half)
+    near_back = near_back[:1] + [swap(near_back[j], "expert", j) for j in range(1, half)]
 
     mid_far = swap(mid, "dp", 2)
     (near,) = call(
@@ -414,18 +449,29 @@
         [((2 * rows, 4 * depth + 3 * hidden_width), BF16)],
         [],
         [own_slices[1], own_far, far_slices[1], far_far, mid],
-        [partial],
+        [partial, near_back[1]],
         [],
         0,
     )
     near = swap(near, "dp", 1)
-    near_back = near_back[:1] + [swap(near_back[j], "expert", j) for j in range(1, half)]
+    weight_shapes = [((depth, 2 * hidden_width), F32), ((depth, hidden_width), F32)]
+    weight_scratch = [pltpu.VMEM((4 * rows, 2 * depth), BF16), pltpu.VMEM((4 * rows, 3 * hidden_width), BF16)]
+    weight_flops = 2 * 4 * rows * depth * 3 * hidden_width
+    first = call(
+        first_weight_kernel,
+        weight_shapes,
+        [],
+        [own_slices[0], far_slices[0], near, mid],
+        [],
+        weight_scratch,
+        weight_flops,
+    )
     near_sum, near_route = call(
         near_sum_kernel,
         [((token_count, width), F32), ((blocks, token_count), F32)],
         [],
         [dense, *near_back],
-        [],
+        [first[1]],
         sum_scratch,
         sum_flops,
     )
@@ -439,18 +485,6 @@
         0,
     )
 
-    def weight_part(which, arrays, before):
-        return call(
-            functools.partial(weight_kernel, which),
-            [((depth, 2 * hidden_width), F32), ((depth, hidden_width), F32)],
-            [],
-            [*arrays, *before],
-            [],
-            [pltpu.VMEM((4 * rows, 2 * depth), BF16), pltpu.VMEM((4 * rows, 3 * hidden_width), BF16)],
-            2 * 4 * rows * depth * 3 * hidden_width,
-        )
-
-    first = weight_part(0, [own_slices[0], far_slices[0], near, mid], [])
     (mid_far,) = call(
         after_kernel,
         [(mid_far.shape, BF16)],
@@ -462,7 +496,21 @@
         1,
         {0: 0},
     )
-    grad_gate_up, grad_down = weight_part(1, [own_far, far_far, near, mid_far, swap(mid_far, "dp", 1)], first)
+    grad_gate_up, grad_down = call(
+        second_weight_kernel,
+        weight_shapes,
+        [],
+        [own_far, far_far, near, mid_far, swap(mid_far, "dp", 1), *first],
+        [],
+        weight_scratch
+        + [
+            pltpu.VMEM((depth, 2 * hidden_width), F32),
+            pltpu.VMEM((depth, hidden_width), F32),
+            pltpu.SemaphoreType.DMA((2, 4)),
+        ],
+        weight_flops,
+        2,
+    )
     return (grad_tokens, grad_route.T, grad_gate_up[None], grad_down[None])
 
 

time: 97.4 us -> 104 us (1.068)
  local copies, waits for them, and re-layouts: 3.81 us -> 11.4 us
  waiting for transfers between devices: 48.8 us -> 45.2 us
  Pallas kernels: 15.9 us -> 17.4 us
  starting transfers between devices: 27.5 us -> 28.7 us
    unnamed x16 -> x48, local copies, waits for them, and re-layouts: 3.81 us -> 11.4 us
    ppermute x21, waiting for transfers between devices: 48.8 us -> 45.2 us  [swap(): lax.ppermute(value, axis, [(i, i ^ mask) for i in range(lax.axis_size(axi...]
    pallas_call x16, Pallas kernels: 15.9 us -> 17.4 us  [call(): pl.pallas_call(kernel, out_shape=tuple(outs), in_specs=[on_smem] * len(sm...]
    ppermute x21, starting transfers between devices: 27.5 us -> 28.7 us  [swap(): lax.ppermute(value, axis, [(i, i ^ mask) for i in range(lax.axis_size(axi...]
  transfers between devices with their start and end apart: 21 -> 21, of which waited for: 16 -> 15; matrix products, arithmetic and copies ran while one was open for 0% -> 0% of each run, Pallas kernels for 13% -> 14%
where the time goes in v5:
time: 104 us
  waiting for transfers between devices  45.2 us (43%)
  starting transfers between devices  28.7 us (28%)
  Pallas kernels  17.4 us (17%)
  local copies, waits for them, and re-layouts  11.4 us (11%)
    ppermute x21, waiting for transfers between devices, swap(): lax.ppermute(value, axis, [(i, i ^ mask) for i in range(lax.axis_size(axi...  45.2 us
    ppermute x21, starting transfers between devices, swap(): lax.ppermute(value, axis, [(i, i ^ mask) for i in range(lax.axis_size(axi...  28.7 us
    pallas_call x16, Pallas kernels, call(): pl.pallas_call(kernel, out_shape=tuple(outs), in_specs=[on_smem] * len(sm...  17.4 us
    unnamed x48, local copies, waits for them, and re-layouts  11.4 us
  transfers between devices with their start and end apart: 21, of which 15 were waited for; matrix products, arithmetic and copies ran while one was open for 0% of the time, Pallas kernels for 14%

profile of v5, /device:TPU:1, one launch (start us, length us, event | category | flops | bytes accessed | tf_op | source)
XLA Modules:
  0.0 103.6 jit_solution(11058599224441546574)
XLA Ops:
  0.7 1.1 %copy-done.13 = bf16[1,512,768]{2,1,0:T(8,128)(2,1)S(1)} copy-done((bf16[1,512,768]{2,1,0:T(8,128)(2,1)S(1)}, bf16[1,512,768]{2,1,0:T(8,128)(2,1)}, u32[]{:S(2)}) %copy-start.13) | copy-done | bytes 786456
  1.8 1.0 copy-done.14
  2.8 0.1 shard_map.95.own_ref
  2.9 2.1 %collective-permute-start.4 = (bf16[512,1152]{1,0:T(8,128)(2,1)S(1)}, bf16[512,1152]{1,0:T(8,128)(2,1)S(1)}, u32[]{:S(2)}, u32[]{:S(2)}) collective-permute-start(bf16[512,1152]{1,0:T(8,128)(2,1)S(1)} %shard_map.95.own_ref), channel_id=1, source_target_pairs={{0,2},{1,3},{2,0},{3,1},{4,6},{5,7},{6,4},{7,5},{8,10},{9,11},{10,... | collective-permute-start | bytes 3538952 | tf_op jit(solution)/shard_map/ppermute | solution.py:323
  5.0 0.6 shard_map.93
  5.6 2.4 %collective-permute-start.3 = (bf16[128,2176]{1,0:T(8,128)(2,1)S(1)}, bf16[128,2176]{1,0:T(8,128)(2,1)S(1)}, u32[]{:S(2)}, u32[]{:S(2)}) collective-permute-start(bf16[128,2176]{1,0:T(8,128)(2,1)S(1)} %get-tuple-element.41.joint_ref), channel_id=1, source_target_pairs={{0,16},{4,20},{8,24},{12,28},{16,0},{20,4},{24,8},{28,12},{1,17},{... | collective-permute-start | bytes 1671176 | tf_op jit(solution)/shard_map/ppermute | solution.py:323
  8.0 0.7 shard_map.94
  8.8 0.7 copy-done.15
  9.5 1.2 %collective-permute-start = (bf16[64,2176]{1,0:T(8,128)(2,1)S(1)}, bf16[64,2176]{1,0:T(8,128)(2,1)S(1)}, u32[]{:S(2)}, u32[]{:S(2)}) collective-permute-start(bf16[64,2176]{1,0:T(8,128)(2,1)S(1)} %get-tuple-element.43), channel_id=1, source_target_pairs={{0,4},{4,0},{8,12},{12,8},{16,20},{20,16},{24,28},{28,24},{1,5},{5... | collective-permute-start | bytes 835592 | tf_op jit(solution)/shard_map/ppermute | solution.py:323
  10.7 1.3 %collective-permute-start.1 = (bf16[64,2176]{1,0:T(8,128)(2,1)S(1)}, bf16[64,2176]{1,0:T(8,128)(2,1)S(1)}, u32[]{:S(2)}, u32[]{:S(2)}) collective-permute-start(bf16[64,2176]{1,0:T(8,128)(2,1)S(1)} %get-tuple-element.44), channel_id=1, source_target_pairs={{0,8},{4,12},{8,0},{12,4},{16,24},{20,28},{24,16},{28,20},{1,9},{5... | collective-permute-start | bytes 835592 | tf_op jit(solution)/shard_map/ppermute | solution.py:323
  12.0 0.1 collective-permute-start.2
  12.1 4.3 %collective-permute-done.refs_0_.refs_1_ = bf16[64,2176]{1,0:T(8,128)(2,1)S(1)} collective-permute-done((bf16[64,2176]{1,0:T(8,128)(2,1)S(1)}, bf16[64,2176]{1,0:T(8,128)(2,1)S(1)}, u32[]{:S(2)}, u32[]{:S(2)}) %collective-permute-start) | collective-permute-done | bytes 278560 | tf_op jit(solution)/shard_map/ppermute | solution.py:323
  16.4 8.6 %collective-permute-done.1.refs_1_.refs_2_ = bf16[64,2176]{1,0:T(8,128)(2,1)S(1)} collective-permute-done((bf16[64,2176]{1,0:T(8,128)(2,1)S(1)}, bf16[64,2176]{1,0:T(8,128)(2,1)S(1)}, u32[]{:S(2)}, u32[]{:S(2)}) %collective-permute-start.1) | collective-permute-done | bytes 278560 | tf_op jit(solution)/shard_map/ppermute | solution.py:323
  25.0 6.0 %collective-permute-done.2.refs_2_.refs_3_ = bf16[64,2176]{1,0:T(8,128)(2,1)S(1)} collective-permute-done((bf16[64,2176]{1,0:T(8,128)(2,1)S(1)}, bf16[64,2176]{1,0:T(8,128)(2,1)S(1)}, u32[]{:S(2)}, u32[]{:S(2)}) %collective-permute-start.2) | collective-permute-done | bytes 278560 | tf_op jit(solution)/shard_map/ppermute | solution.py:323
  30.9 1.1 %collective-permute-done.3.joint_ref = bf16[128,2176]{1,0:T(8,128)(2,1)S(1)} collective-permute-done((bf16[128,2176]{1,0:T(8,128)(2,1)S(1)}, bf16[128,2176]{1,0:T(8,128)(2,1)S(1)}, u32[]{:S(2)}, u32[]{:S(2)}) %collective-permute-start.3) | collective-permute-done | bytes 557088 | tf_op jit(solution)/shard_map/ppermute | solution.py:323
  32.0 0.0 collective-permute-done.4.refs_3_.far_ref
  32.0 0.7 shard_map.96
  32.8 0.3 copy-done
  33.1 0.7 copy-done.21
  33.8 0.7 copy-done.22
  34.5 0.7 copy-done.23
  35.2 1.4 %copy-done.1 = bf16[512,1152]{1,0:T(8,128)(2,1)S(1)} copy-done((bf16[512,1152]{1,0:T(8,128)(2,1)S(1)}, bf16[512,1152]{1,0:T(8,128)(2,1)}, u32[]{:S(2)}) %copy-start.1) | copy-done | bytes 1179672
  36.6 0.2 shard_map.98.refs_0_
  36.8 4.6 %collective-permute-start.5 = (bf16[1024,1152]{1,0:T(8,128)(2,1)S(1)}, bf16[1024,1152]{1,0:T(8,128)(2,1)}, u32[]{:S(2)}, u32[]{:S(2)}) collective-permute-start(bf16[1024,1152]{1,0:T(8,128)(2,1)S(1)} %shard_map.98.refs_0_), channel_id=1, source_target_pairs={{0,1},{1,0},{2,3},{3,2},{4,5},{5,4},{6,7},{7,6},{8,9},{9,8},{10,11... | collective-permute-start | bytes 7077896 | tf_op jit(solution)/shard_map/ppermute | solution.py:323
  41.4 1.3 %collective-permute-start.9 = (bf16[64,2176]{1,0:T(8,128)(2,1)}, bf16[64,2176]{1,0:T(8,128)(2,1)S(1)}, u32[]{:S(2)}, u32[]{:S(2)}) collective-permute-start(bf16[64,2176]{1,0:T(8,128)(2,1)} %copy-done.23), channel_id=1, source_target_pairs={{0,4},{4,0},{8,12},{12,8},{16,20},{20,16},{24,28},{28,24},{1,5},{5... | collective-permute-start | bytes 835592 | tf_op jit(solution)/shard_map/ppermute | solution.py:323
  42.6 1.4 %collective-permute-start.11 = (bf16[64,2176]{1,0:T(8,128)(2,1)}, bf16[64,2176]{1,0:T(8,128)(2,1)S(1)}, u32[]{:S(2)}, u32[]{:S(2)}) collective-permute-start(bf16[64,2176]{1,0:T(8,128)(2,1)} %copy-done.21), channel_id=1, source_target_pairs={{0,12},{4,8},{8,4},{12,0},{16,28},{20,24},{24,20},{28,16},{1,13},{... | collective-permute-start | bytes 835592 | tf_op jit(solution)/shard_map/ppermute | solution.py:323
  44.1 1.0 copy-done.3
  45.0 1.0 copy-done.8
  46.0 1.0 copy-done.10
  46.9 1.0 copy-done.12
  47.9 1.0 copy-done.16
  48.8 1.1 %shard_map.97 = (bf16[144,1024]{1,0:T(8,128)(2,1)S(1)}, bf16[144,1024]{1,0:T(8,128)(2,1)S(1)}, bf16[144,2048]{1,0:T(8,128)(2,1)S(1)}, f32[144,128]{1,0:T(8,128)S(1)}) custom-call(s32[4]{0:T(128)S(1)} %iota_xor_fusion.place_ref, bf16[64,2176]{1,0:T(8,128)(2,1)S(1)} %copy-done.16, bf16[64,2176]{1,0:T(8,128)(2,1)S(1)} %copy-done.8, ...), custom_call_target="tpu_custom_call" | custom-call | bytes 1253376 | tf_op jit(solution)/shard_map/pallas_call | solution.py:310
  49.9 0.9 collective-permute-start.12
  50.8 3.8 %shard_map.99 = (bf16[144,1152]{1,0:T(8,128)(2,1)S(1)}, bf16[32,2176]{1,0:T(8,128)(2,1)S(1)}, bf16[32,2176]{1,0:T(8,128)(2,1)S(1)}, bf16[32,2176]{1,0:T(8,128)(2,1)S(1)}, bf16[32,2176]{1,0:T(8,128)(2,1)S(1)}) custom-call(s32[4]{0:T(128)S(1)} %iota_xor_fusion.place_ref, f32[144,128]{1,0:T(8,128)S(1)} %get-tuple-element.47.w_ref, ...), custom_call_target="tpu_custom_call" | custom-call | flops 1132462080 | bytes 6860800 | tf_op jit(solution)/shard_map/pallas_call | solution.py:310
  54.6 2.0 %collective-permute-done.11.refs_2_ = bf16[64,2176]{1,0:T(8,128)(2,1)S(1)} collective-permute-done((bf16[64,2176]{1,0:T(8,128)(2,1)}, bf16[64,2176]{1,0:T(8,128)(2,1)S(1)}, u32[]{:S(2)}, u32[]{:S(2)}) %collective-permute-start.11) | collective-permute-done | bytes 278560 | tf_op jit(solution)/shard_map/ppermute | solution.py:323
  56.7 0.7 shard_map.100
  57.4 0.9 collective-permute-start.13
  58.3 5.6 %collective-permute-done.12.refs_6_.far_a.rows_a = bf16[144,2048]{1,0:T(8,128)(2,1)S(1)} collective-permute-done((bf16[144,2048]{1,0:T(8,128)(2,1)S(1)}, bf16[144,2048]{1,0:T(8,128)(2,1)S(1)}, u32[]{:S(2)}, u32[]{:S(2)}) %collective-permute-start.12) | collective-permute-done | bytes 589856 | tf_op jit(solution)/shard_map/ppermute | solution.py:323
  63.9 3.8 %shard_map.101 = (bf16[288,1152]{1,0:T(8,128)(2,1)S(1)}, bf16[32,2176]{1,0:T(8,128)(2,1)S(1)}, bf16[32,2176]{1,0:T(8,128)(2,1)S(1)}, bf16[32,2176]{1,0:T(8,128)(2,1)S(1)}, bf16[32,2176]{1,0:T(8,128)(2,1)S(1)}) custom-call(s32[4]{0:T(128)S(1)} %iota_xor_fusion.place_ref, f32[144,128]{1,0:T(8,128)S(1)} %get-tuple-element.62.w_ref, ...), custom_call_target="tpu_custom_call" | custom-call | flops 1132462080 | bytes 7524352 | tf_op jit(solution)/shard_map/pallas_call | solution.py:310
  67.7 1.3 %collective-permute-start.14 = (bf16[32,2176]{1,0:T(8,128)(2,1)S(1)}, bf16[32,2176]{1,0:T(8,128)(2,1)S(1)}, u32[]{:S(2)}, u32[]{:S(2)}) collective-permute-start(bf16[32,2176]{1,0:T(8,128)(2,1)S(1)} %get-tuple-element.65), channel_id=1, source_target_pairs={{0,4},{4,0},{8,12},{12,8},{16,20},{20,16},{24,28},{28,24},{1,5},{5... | collective-permute-start | bytes 417800 | tf_op jit(solution)/shard_map/ppermute | solution.py:323
  69.0 0.3 collective-permute-start.15
  69.3 1.1 %collective-permute-start.16 = (bf16[32,2176]{1,0:T(8,128)(2,1)S(1)}, bf16[32,2176]{1,0:T(8,128)(2,1)S(1)}, u32[]{:S(2)}, u32[]{:S(2)}) collective-permute-start(bf16[32,2176]{1,0:T(8,128)(2,1)S(1)} %get-tuple-element.67), channel_id=1, source_target_pairs={{0,12},{4,8},{8,4},{12,0},{16,28},{20,24},{24,20},{28,16},{1,13},{... | collective-permute-start | bytes 417800 | tf_op jit(solution)/shard_map/ppermute | solution.py:323
  70.4 1.2 %collective-permute-start.6 = (bf16[32,2176]{1,0:T(8,128)(2,1)S(1)}, bf16[32,2176]{1,0:T(8,128)(2,1)S(1)}, u32[]{:S(2)}, u32[]{:S(2)}) collective-permute-start(bf16[32,2176]{1,0:T(8,128)(2,1)S(1)} %get-tuple-element.52), channel_id=1, source_target_pairs={{0,4},{4,0},{8,12},{12,8},{16,20},{20,16},{24,28},{28,24},{1,5},{5... | collective-permute-start | bytes 417800 | tf_op jit(solution)/shard_map/ppermute | solution.py:323
  71.7 0.3 collective-permute-done.14.b1
  72.0 1.2 %collective-permute-done.15.b2 = bf16[32,2176]{1,0:T(8,128)(2,1)S(1)} collective-permute-done((bf16[32,2176]{1,0:T(8,128)(2,1)S(1)}, bf16[32,2176]{1,0:T(8,128)(2,1)S(1)}, u32[]{:S(2)}, u32[]{:S(2)}) %collective-permute-start.15) | collective-permute-done | bytes 139296 | tf_op jit(solution)/shard_map/ppermute | solution.py:323
  73.2 1.2 %collective-permute-done.16.b3 = bf16[32,2176]{1,0:T(8,128)(2,1)S(1)} collective-permute-done((bf16[32,2176]{1,0:T(8,128)(2,1)S(1)}, bf16[32,2176]{1,0:T(8,128)(2,1)S(1)}, u32[]{:S(2)}, u32[]{:S(2)}) %collective-permute-start.16) | collective-permute-done | bytes 139296 | tf_op jit(solution)/shard_map/ppermute | solution.py:323
  74.5 0.4 shard_map.102.refs_0_
  74.9 4.1 %collective-permute-done.6.refs_1_.b1 = bf16[32,2176]{1,0:T(8,128)(2,1)S(1)} collective-permute-done((bf16[32,2176]{1,0:T(8,128)(2,1)S(1)}, bf16[32,2176]{1,0:T(8,128)(2,1)S(1)}, u32[]{:S(2)}, u32[]{:S(2)}) %collective-permute-start.6) | collective-permute-done | bytes 139296 | tf_op jit(solution)/shard_map/ppermute | solution.py:323
  79.0 0.1 shard_map.103
  79.1 2.1 %collective-permute-start.17 = (bf16[288,3200]{1,0:T(8,128)(2,1)S(1)}, bf16[288,3200]{1,0:T(8,128)(2,1)S(1)}, u32[]{:S(2)}, u32[]{:S(2)}) collective-permute-start(bf16[288,3200]{1,0:T(8,128)(2,1)S(1)} %shard_map.103), channel_id=1, source_target_pairs={{0,1},{1,0},{2,3},{3,2},{4,5},{5,4},{6,7},{7,6},{8,9},{9,8},{10,11... | collective-permute-start | bytes 5529608 | tf_op jit(solution)/shard_map/ppermute | solution.py:323
  81.2 0.9 collective-permute-start.19
  82.0 1.3 %collective-permute-start.18 = (bf16[64,2176]{1,0:T(8,128)(2,1)S(1)}, bf16[64,2176]{1,0:T(8,128)(2,1)S(1)}, u32[]{:S(2)}, u32[]{:S(2)}) collective-permute-start(bf16[64,2176]{1,0:T(8,128)(2,1)S(1)} %shard_map.102.refs_0_), channel_id=1, source_target_pairs={{0,16},{4,20},{8,24},{12,28},{16,0},{20,4},{24,8},{28,12},{1,17},{... | collective-permute-start | bytes 835592 | tf_op jit(solution)/shard_map/ppermute | solution.py:323
  83.3 1.1 %collective-permute-start.7 = (bf16[32,2176]{1,0:T(8,128)(2,1)S(1)}, bf16[32,2176]{1,0:T(8,128)(2,1)S(1)}, u32[]{:S(2)}, u32[]{:S(2)}) collective-permute-start(bf16[32,2176]{1,0:T(8,128)(2,1)S(1)} %get-tuple-element.53), channel_id=1, source_target_pairs={{0,8},{4,12},{8,0},{12,4},{16,24},{20,28},{24,16},{28,20},{1,9},{5... | collective-permute-start | bytes 417800 | tf_op jit(solution)/shard_map/ppermute | solution.py:323
  84.4 1.3 %collective-permute-start.8 = (bf16[32,2176]{1,0:T(8,128)(2,1)S(1)}, bf16[32,2176]{1,0:T(8,128)(2,1)S(1)}, u32[]{:S(2)}, u32[]{:S(2)}) collective-permute-start(bf16[32,2176]{1,0:T(8,128)(2,1)S(1)} %get-tuple-element.54), channel_id=1, source_target_pairs={{0,12},{4,8},{8,4},{12,0},{16,28},{20,24},{24,20},{28,16},{1,13},{... | collective-permute-start | bytes 417800 | tf_op jit(solution)/shard_map/ppermute | solution.py:323
  85.7 1.2 %shard_map.104 = (f32[512,768]{1,0:T(8,128)S(1)}, f32[512,384]{1,0:T(8,128)S(1)}) custom-call(bf16[144,1024]{1,0:T(8,128)(2,1)S(1)} %get-tuple-element.48.refs_2_.rows_a, bf16[144,1024]{1,0:T(8,128)(2,1)S(1)} %get-tuple-element.59.refs_2_.rows_b, bf16[288,3200]{1,0:T(8,128)(2,1)S(1)} %collective-permute-done.17.near_ref, ...), custom_call_target="tpu_custom_call" | custom-call | flops 679477248 | bytes 5455872 | tf_op jit(solution)/shard_map/pallas_call | solution.py:310
  86.9 5.1 %collective-permute-done.7.b2 = bf16[32,2176]{1,0:T(8,128)(2,1)S(1)} collective-permute-done((bf16[32,2176]{1,0:T(8,128)(2,1)S(1)}, bf16[32,2176]{1,0:T(8,128)(2,1)S(1)}, u32[]{:S(2)}, u32[]{:S(2)}) %collective-permute-start.7) | collective-permute-done | bytes 139296 | tf_op jit(solution)/shard_map/ppermute | solution.py:323
  92.0 3.0 %collective-permute-done.8.b3 = bf16[32,2176]{1,0:T(8,128)(2,1)S(1)} collective-permute-done((bf16[32,2176]{1,0:T(8,128)(2,1)S(1)}, bf16[32,2176]{1,0:T(8,128)(2,1)S(1)}, u32[]{:S(2)}, u32[]{:S(2)}) %collective-permute-start.8) | collective-permute-done | bytes 139296 | tf_op jit(solution)/shard_map/ppermute | solution.py:323
  95.0 0.4 shard_map.105
  95.4 2.0 %collective-permute-done.18.far_ref.refs_2_ = bf16[64,2176]{1,0:T(8,128)(2,1)S(1)} collective-permute-done((bf16[64,2176]{1,0:T(8,128)(2,1)S(1)}, bf16[64,2176]{1,0:T(8,128)(2,1)S(1)}, u32[]{:S(2)}, u32[]{:S(2)}) %collective-permute-start.18) | collective-permute-done | bytes 278560 | tf_op jit(solution)/shard_map/ppermute | solution.py:323
  97.4 0.2 collective-permute-done.19.refs_0_
  97.7 2.0 %collective-permute-start.20 = (bf16[288,1152]{1,0:T(8,128)(2,1)S(1)}, bf16[288,1152]{1,0:T(8,128)(2,1)S(1)}, u32[]{:S(2)}, u32[]{:S(2)}) collective-permute-start(bf16[288,1152]{1,0:T(8,128)(2,1)S(1)} %shard_map.107.mid_a), channel_id=1, source_target_pairs={{0,1},{1,0},{2,3},{3,2},{4,5},{5,4},{6,7},{7,6},{8,9},{9,8},{10,11... | collective-permute-start | bytes 1990664 | tf_op jit(solution)/shard_map/ppermute | solution.py:323
  99.6 1.3 %shard_map.106 = (bf16[64,2048]{1,0:T(8,128)(2,1)}, bf16[4,64]{1,0:T(4,128)(2,1)}) custom-call(s32[8]{0:T(128)S(1)} %iota_xor_fusion.1.peer_ref, s32[4,64]{1,0:T(4,128)S(1)} %bitcast.10, f32[64,2048]{1,0:T(8,128)S(1)} %get-tuple-element.69.near_ref.refs_3_, f32[8,64]{1,0:T(8,128)S(1)} %get-tuple-element.70.near_route_ref, ...), custom_call_target="tpu_custom_call" | custom-call | bytes 1068544 | tf_op jit(solution)/shard_map/pallas_call | solution.py:310
  100.9 0.4 collective-permute-done.20.mid_b
  101.4 2.2 %shard_map.108 = (f32[512,768]{1,0:T(8,128)}, f32[512,384]{1,0:T(8,128)}) custom-call(bf16[144,2048]{1,0:T(8,128)(2,1)S(1)} %collective-permute-done.12.refs_6_.far_a.rows_a, bf16[144,2048]{1,0:T(8,128)(2,1)S(1)} %collective-permute-done.13.far_b.rows_b, bf16[288,3200]{1,0:T(8,128)(2,1)S(1)} %collective-permute-done.17.near_ref, ...), custom_call_target="tpu_custom_call" | custom-call | flops 679477248 | bytes 6709248 | tf_op jit(solution)/shard_map/pallas_call | solution.py:310
  (44 shorter events, 0.1 us)
Async XLA Ops:
  0.6 4.4 %copy-start.20 = (bf16[64,4]{0,1:T(4,128)(2,1)S(1)}, bf16[64,4]{0,1:T(4,128)(2,1)}, u32[]{:S(2)}) copy-start(bf16[64,4]{0,1:T(4,128)(2,1)} %param.9) | copy-start | bytes 1540
  0.6 4.4 %copy-start.19 = (s32[64,4]{0,1:T(4,128)S(1)}, s32[64,4]{0,1:T(4,128)}, u32[]{:S(2)}) copy-start(s32[64,4]{0,1:T(4,128)} %param.8) | copy-start | bytes 3076
  0.7 1.1 %copy-start.13 = (bf16[1,512,768]{2,1,0:T(8,128)(2,1)S(1)}, bf16[1,512,768]{2,1,0:T(8,128)(2,1)}, u32[]{:S(2)}) copy-start(bf16[1,512,768]{2,1,0:T(8,128)(2,1)} %param.10) | copy-start | bytes 2359300
  1.8 1.0 copy-start.14
  2.8 2.2 %copy-start.17 = (bf16[64,2048]{1,0:T(8,128)(2,1)S(1)}, bf16[64,2048]{1,0:T(8,128)(2,1)}, u32[]{:S(2)}) copy-start(bf16[64,2048]{1,0:T(8,128)(2,1)} %x_ref.1) | copy-start | bytes 786436
  2.8 2.2 %copy-start.18 = (bf16[64,2048]{1,0:T(8,128)(2,1)S(1)}, bf16[64,2048]{1,0:T(8,128)(2,1)}, u32[]{:S(2)}) copy-start(bf16[64,2048]{1,0:T(8,128)(2,1)} %dy_ref.1) | copy-start | bytes 786436
  2.9 29.2 %collective-permute-start.4 = (bf16[512,1152]{1,0:T(8,128)(2,1)S(1)}, bf16[512,1152]{1,0:T(8,128)(2,1)S(1)}, u32[]{:S(2)}, u32[]{:S(2)}) collective-permute-start(bf16[512,1152]{1,0:T(8,128)(2,1)S(1)} %shard_map.95.own_ref), channel_id=1, source_target_pairs={{0,2},{1,3},{2,0},{3,1},{4,6},{5,7},{6,4},{7,5},{8,10},{9,11},{10,... | collective-permute-start | bytes 3538952 | tf_op jit(solution)/shard_map/ppermute | solution.py:323
  5.6 26.4 %collective-permute-start.3 = (bf16[128,2176]{1,0:T(8,128)(2,1)S(1)}, bf16[128,2176]{1,0:T(8,128)(2,1)S(1)}, u32[]{:S(2)}, u32[]{:S(2)}) collective-permute-start(bf16[128,2176]{1,0:T(8,128)(2,1)S(1)} %get-tuple-element.41.joint_ref), channel_id=1, source_target_pairs={{0,16},{4,20},{8,24},{12,28},{16,0},{20,4},{24,8},{28,12},{1,17},{... | collective-permute-start | bytes 1671176 | tf_op jit(solution)/shard_map/ppermute | solution.py:323
  8.7 0.7 copy-start.15
  9.5 6.9 %collective-permute-start = (bf16[64,2176]{1,0:T(8,128)(2,1)S(1)}, bf16[64,2176]{1,0:T(8,128)(2,1)S(1)}, u32[]{:S(2)}, u32[]{:S(2)}) collective-permute-start(bf16[64,2176]{1,0:T(8,128)(2,1)S(1)} %get-tuple-element.43), channel_id=1, source_target_pairs={{0,4},{4,0},{8,12},{12,8},{16,20},{20,16},{24,28},{28,24},{1,5},{5... | collective-permute-start | bytes 835592 | tf_op jit(solution)/shard_map/ppermute | solution.py:323
  10.7 14.3 %collective-permute-start.1 = (bf16[64,2176]{1,0:T(8,128)(2,1)S(1)}, bf16[64,2176]{1,0:T(8,128)(2,1)S(1)}, u32[]{:S(2)}, u32[]{:S(2)}) collective-permute-start(bf16[64,2176]{1,0:T(8,128)(2,1)S(1)} %get-tuple-element.44), channel_id=1, source_target_pairs={{0,8},{4,12},{8,0},{12,4},{16,24},{20,28},{24,16},{28,20},{1,9},{5... | collective-permute-start | bytes 835592 | tf_op jit(solution)/shard_map/ppermute | solution.py:323
  12.0 19.0 %collective-permute-start.2 = (bf16[64,2176]{1,0:T(8,128)(2,1)S(1)}, bf16[64,2176]{1,0:T(8,128)(2,1)S(1)}, u32[]{:S(2)}, u32[]{:S(2)}) collective-permute-start(bf16[64,2176]{1,0:T(8,128)(2,1)S(1)} %get-tuple-element.45), channel_id=1, source_target_pairs={{0,12},{4,8},{8,4},{12,0},{16,28},{20,24},{24,20},{28,16},{1,13},{... | collective-permute-start | bytes 835592 | tf_op jit(solution)/shard_map/ppermute | solution.py:323
  16.4 16.4 %copy-start.7 = (bf16[64,2176]{1,0:T(8,128)(2,1)}, bf16[64,2176]{1,0:T(8,128)(2,1)S(1)}, u32[]{:S(2)}) copy-start(bf16[64,2176]{1,0:T(8,128)(2,1)S(1)} %collective-permute-done.refs_0_.refs_1_) | copy-start | bytes 835588
  25.0 7.8 %copy-start.9 = (bf16[64,2176]{1,0:T(8,128)(2,1)}, bf16[64,2176]{1,0:T(8,128)(2,1)S(1)}, u32[]{:S(2)}) copy-start(bf16[64,2176]{1,0:T(8,128)(2,1)S(1)} %collective-permute-done.1.refs_1_.refs_2_) | copy-start | bytes 835588
  30.9 1.9 %copy-start.11 = (bf16[64,2176]{1,0:T(8,128)(2,1)}, bf16[64,2176]{1,0:T(8,128)(2,1)S(1)}, u32[]{:S(2)}) copy-start(bf16[64,2176]{1,0:T(8,128)(2,1)S(1)} %collective-permute-done.2.refs_2_.refs_3_) | copy-start | bytes 835588
  32.0 4.7 %copy-start.5 = (bf16[128,2176]{1,0:T(8,128)(2,1)}, bf16[128,2176]{1,0:T(8,128)(2,1)S(1)}, u32[]{:S(2)}) copy-start(bf16[128,2176]{1,0:T(8,128)(2,1)S(1)} %collective-permute-done.3.joint_ref) | copy-start | bytes 1671172
  32.0 1.1 %copy-start = (bf16[512,1152]{1,0:T(8,128)(2,1)}, bf16[512,1152]{1,0:T(8,128)(2,1)S(1)}, u32[]{:S(2)}) copy-start(bf16[512,1152]{1,0:T(8,128)(2,1)S(1)} %collective-permute-done.4.refs_3_.far_ref) | copy-start | bytes 3538948
  33.1 0.7 copy-start.21
  33.8 0.7 copy-start.22
  34.5 0.7 copy-start.23
  35.2 1.6 %copy-start.2 = (bf16[64,2176]{1,0:T(8,128)(2,1)}, bf16[64,2176]{1,0:T(8,128)(2,1)S(1)}, u32[]{:S(2)}) copy-start(bf16[64,2176]{1,0:T(8,128)(2,1)S(1)} %get-tuple-element.46.refs_4_.after_ref.refs_3_) | copy-start | bytes 835588
  35.2 1.4 %copy-start.1 = (bf16[512,1152]{1,0:T(8,128)(2,1)S(1)}, bf16[512,1152]{1,0:T(8,128)(2,1)}, u32[]{:S(2)}) copy-start(bf16[512,1152]{1,0:T(8,128)(2,1)} %copy-done) | copy-start | bytes 3538948
  36.8 14.0 %collective-permute-start.5 = (bf16[1024,1152]{1,0:T(8,128)(2,1)S(1)}, bf16[1024,1152]{1,0:T(8,128)(2,1)}, u32[]{:S(2)}, u32[]{:S(2)}) collective-permute-start(bf16[1024,1152]{1,0:T(8,128)(2,1)S(1)} %shard_map.98.refs_0_), channel_id=1, source_target_pairs={{0,1},{1,0},{2,3},{3,2},{4,5},{5,4},{6,7},{7,6},{8,9},{9,8},{10,11... | collective-permute-start | bytes 7077896 | tf_op jit(solution)/shard_map/ppermute | solution.py:323
  41.4 13.2 %collective-permute-start.9 = (bf16[64,2176]{1,0:T(8,128)(2,1)}, bf16[64,2176]{1,0:T(8,128)(2,1)S(1)}, u32[]{:S(2)}, u32[]{:S(2)}) collective-permute-start(bf16[64,2176]{1,0:T(8,128)(2,1)} %copy-done.23), channel_id=1, source_target_pairs={{0,4},{4,0},{8,12},{12,8},{16,20},{20,16},{24,28},{28,24},{1,5},{5... | collective-permute-start | bytes 835592 | tf_op jit(solution)/shard_map/ppermute | solution.py:323
  42.6 12.0 %collective-permute-start.10 = (bf16[64,2176]{1,0:T(8,128)(2,1)}, bf16[64,2176]{1,0:T(8,128)(2,1)S(1)}, u32[]{:S(2)}, u32[]{:S(2)}) collective-permute-start(bf16[64,2176]{1,0:T(8,128)(2,1)} %copy-done.22), channel_id=1, source_target_pairs={{0,8},{4,12},{8,0},{12,4},{16,24},{20,28},{24,16},{28,20},{1,9},{5... | collective-permute-start | bytes 835592 | tf_op jit(solution)/shard_map/ppermute | solution.py:323
  42.6 14.0 %collective-permute-start.11 = (bf16[64,2176]{1,0:T(8,128)(2,1)}, bf16[64,2176]{1,0:T(8,128)(2,1)S(1)}, u32[]{:S(2)}, u32[]{:S(2)}) collective-permute-start(bf16[64,2176]{1,0:T(8,128)(2,1)} %copy-done.21), channel_id=1, source_target_pairs={{0,12},{4,8},{8,4},{12,0},{16,28},{20,24},{24,20},{28,16},{1,13},{... | collective-permute-start | bytes 835592 | tf_op jit(solution)/shard_map/ppermute | solution.py:323
  44.0 1.0 copy-start.3
  45.0 1.0 copy-start.8
  46.0 1.0 copy-start.10
  46.9 1.0 copy-start.12
  47.9 1.0 copy-start.16
  49.9 14.0 %collective-permute-start.12 = (bf16[144,2048]{1,0:T(8,128)(2,1)S(1)}, bf16[144,2048]{1,0:T(8,128)(2,1)S(1)}, u32[]{:S(2)}, u32[]{:S(2)}) collective-permute-start(bf16[144,2048]{1,0:T(8,128)(2,1)S(1)} %get-tuple-element.50.refs_4_), channel_id=1, source_target_pairs={{0,2},{1,3},{2,0},{3,1},{4,6},{5,7},{6,4},{7,5},{8,10},{9,11},{10,... | collective-permute-start | bytes 1769480 | tf_op jit(solution)/shard_map/ppermute | solution.py:323
  50.8 5.9 %copy-start.4 = (bf16[64,2176]{1,0:T(8,128)(2,1)S(1)}, bf16[64,2176]{1,0:T(8,128)(2,1)}, u32[]{:S(2)}) copy-start(bf16[64,2176]{1,0:T(8,128)(2,1)} %copy-done.2) | copy-start | bytes 835588
  57.4 21.6 %collective-permute-start.13 = (bf16[144,2048]{1,0:T(8,128)(2,1)S(1)}, bf16[144,2048]{1,0:T(8,128)(2,1)S(1)}, u32[]{:S(2)}, u32[]{:S(2)}) collective-permute-start(bf16[144,2048]{1,0:T(8,128)(2,1)S(1)} %get-tuple-element.61.refs_4_), channel_id=1, source_target_pairs={{0,2},{1,3},{2,0},{3,1},{4,6},{5,7},{6,4},{7,5},{8,10},{9,11},{10,... | collective-permute-start | bytes 1769480 | tf_op jit(solution)/shard_map/ppermute | solution.py:323
  63.9 10.6 %copy-start.6 = (bf16[128,2176]{1,0:T(8,128)(2,1)S(1)}, bf16[128,2176]{1,0:T(8,128)(2,1)}, u32[]{:S(2)}) copy-start(bf16[128,2176]{1,0:T(8,128)(2,1)} %copy-done.5) | copy-start | bytes 1671172
  67.7 4.3 %collective-permute-start.14 = (bf16[32,2176]{1,0:T(8,128)(2,1)S(1)}, bf16[32,2176]{1,0:T(8,128)(2,1)S(1)}, u32[]{:S(2)}, u32[]{:S(2)}) collective-permute-start(bf16[32,2176]{1,0:T(8,128)(2,1)S(1)} %get-tuple-element.65), channel_id=1, source_target_pairs={{0,4},{4,0},{8,12},{12,8},{16,20},{20,16},{24,28},{28,24},{1,5},{5... | collective-permute-start | bytes 417800 | tf_op jit(solution)/shard_map/ppermute | solution.py:323
  69.0 4.2 %collective-permute-start.15 = (bf16[32,2176]{1,0:T(8,128)(2,1)S(1)}, bf16[32,2176]{1,0:T(8,128)(2,1)S(1)}, u32[]{:S(2)}, u32[]{:S(2)}) collective-permute-start(bf16[32,2176]{1,0:T(8,128)(2,1)S(1)} %get-tuple-element.66), channel_id=1, source_target_pairs={{0,8},{4,12},{8,0},{12,4},{16,24},{20,28},{24,16},{28,20},{1,9},{5... | collective-permute-start | bytes 417800 | tf_op jit(solution)/shard_map/ppermute | solution.py:323
  69.3 5.1 %collective-permute-start.16 = (bf16[32,2176]{1,0:T(8,128)(2,1)S(1)}, bf16[32,2176]{1,0:T(8,128)(2,1)S(1)}, u32[]{:S(2)}, u32[]{:S(2)}) collective-permute-start(bf16[32,2176]{1,0:T(8,128)(2,1)S(1)} %get-tuple-element.67), channel_id=1, source_target_pairs={{0,12},{4,8},{8,4},{12,0},{16,28},{20,24},{24,20},{28,16},{1,13},{... | collective-permute-start | bytes 417800 | tf_op jit(solution)/shard_map/ppermute | solution.py:323
  70.4 8.6 %collective-permute-start.6 = (bf16[32,2176]{1,0:T(8,128)(2,1)S(1)}, bf16[32,2176]{1,0:T(8,128)(2,1)S(1)}, u32[]{:S(2)}, u32[]{:S(2)}) collective-permute-start(bf16[32,2176]{1,0:T(8,128)(2,1)S(1)} %get-tuple-element.52), channel_id=1, source_target_pairs={{0,4},{4,0},{8,12},{12,8},{16,20},{20,16},{24,28},{28,24},{1,5},{5... | collective-permute-start | bytes 417800 | tf_op jit(solution)/shard_map/ppermute | solution.py:323
  79.1 6.6 %collective-permute-start.17 = (bf16[288,3200]{1,0:T(8,128)(2,1)S(1)}, bf16[288,3200]{1,0:T(8,128)(2,1)S(1)}, u32[]{:S(2)}, u32[]{:S(2)}) collective-permute-start(bf16[288,3200]{1,0:T(8,128)(2,1)S(1)} %shard_map.103), channel_id=1, source_target_pairs={{0,1},{1,0},{2,3},{3,2},{4,5},{5,4},{6,7},{7,6},{8,9},{9,8},{10,11... | collective-permute-start | bytes 5529608 | tf_op jit(solution)/shard_map/ppermute | solution.py:323
  81.2 16.5 %collective-permute-start.19 = (bf16[288,1152]{1,0:T(8,128)(2,1)S(1)}, bf16[288,1152]{1,0:T(8,128)(2,1)S(1)}, u32[]{:S(2)}, u32[]{:S(2)}) collective-permute-start(bf16[288,1152]{1,0:T(8,128)(2,1)S(1)} %get-tuple-element.63.mid_ref), channel_id=1, source_target_pairs={{0,2},{1,3},{2,0},{3,1},{4,6},{5,7},{6,4},{7,5},{8,10},{9,11},{10,... | collective-permute-start | bytes 1990664 | tf_op jit(solution)/shard_map/ppermute | solution.py:323
  82.0 15.4 %collective-permute-start.18 = (bf16[64,2176]{1,0:T(8,128)(2,1)S(1)}, bf16[64,2176]{1,0:T(8,128)(2,1)S(1)}, u32[]{:S(2)}, u32[]{:S(2)}) collective-permute-start(bf16[64,2176]{1,0:T(8,128)(2,1)S(1)} %shard_map.102.refs_0_), channel_id=1, source_target_pairs={{0,16},{4,20},{8,24},{12,28},{16,0},{20,4},{24,8},{28,12},{1,17},{... | collective-permute-start | bytes 835592 | tf_op jit(solution)/shard_map/ppermute | solution.py:323
  83.3 8.7 %collective-permute-start.7 = (bf16[32,2176]{1,0:T(8,128)(2,1)S(1)}, bf16[32,2176]{1,0:T(8,128)(2,1)S(1)}, u32[]{:S(2)}, u32[]{:S(2)}) collective-permute-start(bf16[32,2176]{1,0:T(8,128)(2,1)S(1)} %get-tuple-element.53), channel_id=1, source_target_pairs={{0,8},{4,12},{8,0},{12,4},{16,24},{20,28},{24,16},{28,20},{1,9},{5... | collective-permute-start | bytes 417800 | tf_op jit(solution)/shard_map/ppermute | solution.py:323
  84.4 10.6 %collective-permute-start.8 = (bf16[32,2176]{1,0:T(8,128)(2,1)S(1)}, bf16[32,2176]{1,0:T(8,128)(2,1)S(1)}, u32[]{:S(2)}, u32[]{:S(2)}) collective-permute-start(bf16[32,2176]{1,0:T(8,128)(2,1)S(1)} %get-tuple-element.54), channel_id=1, source_target_pairs={{0,12},{4,8},{8,4},{12,0},{16,28},{20,24},{24,20},{28,16},{1,13},{... | collective-permute-start | bytes 417800 | tf_op jit(solution)/shard_map/ppermute | solution.py:323
  97.7 3.7 %collective-permute-start.20 = (bf16[288,1152]{1,0:T(8,128)(2,1)S(1)}, bf16[288,1152]{1,0:T(8,128)(2,1)S(1)}, u32[]{:S(2)}, u32[]{:S(2)}) collective-permute-start(bf16[288,1152]{1,0:T(8,128)(2,1)S(1)} %shard_map.107.mid_a), channel_id=1, source_target_pairs={{0,1},{1,0},{2,3},{3,2},{4,5},{5,4},{6,7},{7,6},{8,9},{9,8},{10,11... | collective-permute-start | bytes 1990664 | tf_op jit(solution)/shard_map/ppermute | solution.py:323

commit v6 on v5

--- a/solution.py
+++ b/solution.py
@@ -81,8 +81,7 @@
     pass
 
 
-def relay_kernel(near_a, far_a, near_b, far_b, mid_ref, *refs):
-    joint_ref = refs[-1]
+def relay_kernel(near_a, far_a, near_b, far_b, mid_ref, after_ref, joint_ref):
     count, width = near_a.shape
     for at, near, far in ((0, near_a, far_a), (count, near_b, far_b)):
         joint_ref[at : at + count, :width] = near[...]
@@ -92,9 +91,8 @@
 
 def pack_kernel(first, joint_ref, *refs):
     count = 4
-    kept, fold, sem = refs[-3:]
-    kept_ref, *out_refs = refs[-3 - count : -3]
-    out_refs = [kept, *out_refs]
+    fold = refs[-1]
+    out_refs = refs[-1 - count : -1]
     tokens, width = joint_ref.shape[0] // 2, joint_ref.shape[1] - LANES
     chunks = width // LANES
     main = out_refs[0].shape[0] // 2
@@ -116,16 +114,11 @@
         column = jnp.sum(mains[j] * mine, axis=1, keepdims=True)
         last = jnp.sum(tails[first + j : first + j + 1, :] * mine, axis=1, keepdims=True)
         out_refs[j][main:, width:] = jnp.where(lane < LANES // 2, column, last).astype(BF16)
-        if j == 0:
-            copy = start(kept, kept_ref, sem)
-    copy.wait()
-
-
-def slice_kernel(there, place_ref, *refs):
+
+
+def slice_kernel(place_ref, *refs):
     blocks, parts = 4, 4
-    keep_ref, near_ref, far_ref, weight_ref, fold, held, sems = refs[-7:]
-    copies = {i: start(refs[i], held.at[i - there], sems.at[i - there]) for i in range(there, blocks)}
-    in_refs = list(refs[:there]) + [held.at[i - there] for i in range(there, blocks)]
+    in_refs, (keep_ref, near_ref, far_ref, weight_ref, fold) = refs[:blocks], refs[-5:]
     main = in_refs[0].shape[0] // 2
     depth = keep_ref.shape[1] // 2
     width = parts * depth
@@ -134,8 +127,6 @@
     lane = lax.broadcasted_iota(jnp.int32, (1, LANES), 1)
     lasts = []
     for i in range(blocks):
-        if i in copies:
-            copies[i].wait()
         for j, (target, shift) in enumerate(targets):
             columns = pl.ds(pl.multiple_of(place_ref[j] * depth, depth), depth)
             for side in range(2):
@@ -367,15 +358,14 @@
             [],
             [value],
             after,
-            [pltpu.VMEM(*packed_shape), pltpu.VMEM((chunks, LANES), F32), pltpu.SemaphoreType.DMA],
+            [pltpu.VMEM((chunks, LANES), F32)],
             4 * (half * main + 16) * token_count * width,
-            1,
         )
         return [packed[0]] + [swap(packed[j], "expert", j) for j in range(1, half)]
 
-    def sliced(there, others, after):
+    def sliced(packed, after):
         return call(
-            functools.partial(slice_kernel, len(there)),
+            slice_kernel,
             [
                 ((rows, 2 * depth), BF16),
                 ((rows, 2 * depth), BF16),
@@ -383,20 +373,16 @@
                 ((rows, LANES), F32),
             ],
             [places],
-            there,
-            others + after,
-            [
-                pltpu.VMEM((2, half * chunks, LANES), F32),
-                pltpu.VMEM((len(others), *packed_shape[0]), BF16),
-                pltpu.SemaphoreType.DMA((len(others),)),
-            ],
+            packed,
+            after,
+            [pltpu.VMEM((2, half * chunks, LANES), F32)],
             0,
         )
 
     own = pack(half, joint, [])
-    far = pack(0, far_joint, [*own[1:], far_weights])
-    *own_slices, own_weight = sliced([], own, [far[0]])
+    *own_slices, own_weight = sliced(own, [far_joint])
     own_far = swap(own_slices[2], "dp", 2)
+    far = pack(0, far_joint, [own_slices[0], far_weights])
     (stacked,) = call(
         stack_kernel,
         [((2 * depth, 3 * hidden_width), BF16)],
@@ -408,29 +394,30 @@
     )
     weight_parts = [stacked, swap(stacked, "dp", 1)]
 
-    def middle(slices, weight, before, after):
+    def middle(slices, weight, before):
         early = before[0].shape[0] if before else 0
         return call(
             functools.partial(main_kernel, early),
             [((early + rows, 3 * hidden_width), BF16)] + [back_shape] * half,
             [places],
             [weight, *weight_parts, *slices, *before],
-            after,
+            [],
             [pltpu.VMEM((16, width), F32), pltpu.VMEM((chunks, LANES), F32)],
             2 * rows * width * 5 * hidden_width,
         )
 
-    own_mid, *near_back = middle(own_slices, own_weight, [], [])
-    *far_slices, far_weight = sliced(far[1:], far[:1], [own_mid])
+    own_mid, *near_back = middle(own_slices, own_weight, [])
+    near_back[1] = swap(near_back[1], "expert", 1)
+    *far_slices, far_weight = sliced(far, [own_mid, near_back[1]])
     far_far = swap(far_slices[2], "dp", 2)
-    mid, *far_back = middle(far_slices, far_weight, [own_mid], [own_far])
+    mid, *far_back = middle(far_slices, far_weight, [own_mid])
 
     sum_scratch = [
         pltpu.VMEM((half * main + 16, width), BF16),
         pltpu.VMEM((half * chunks, LANES), F32),
     ]
     sum_flops = 2 * (half * main + 16) * width * token_count
-    far_back = far_back[-1:] + [swap(far_back[j - 1], "expert", j) for j in range(1, half)]
+    far_back = far_back[:1] + [swap(far_back[j], "expert", j) for j in range(1, half)]
     (partial,) = call(
         relay_sum_kernel,
         [((token_count, width + LANES), BF16)],
@@ -441,7 +428,6 @@
         sum_flops,
     )
     far_partial = swap(partial, "expert", half)
-    near_back = near_back[:1] + [swap(near_back[j], "expert", j) for j in range(1, half)]
 
     mid_far = swap(mid, "dp", 2)
     (near,) = call(
@@ -449,11 +435,12 @@
         [((2 * rows, 4 * depth + 3 * hidden_width), BF16)],
         [],
         [own_slices[1], own_far, far_slices[1], far_far, mid],
-        [partial, near_back[1]],
+        [partial],
         [],
         0,
     )
     near = swap(near, "dp", 1)
+    near_back = near_back[:2] + [swap(near_back[j], "expert", j) for j in range(2, half)]
     weight_shapes = [((depth, 2 * hidden_width), F32), ((depth, hidden_width), F32)]
     weight_scratch = [pltpu.VMEM((4 * rows, 2 * depth), BF16), pltpu.VMEM((4 * rows, 3 * hidden_width), BF16)]
     weight_flops = 2 * 4 * rows * depth * 3 * hidden_width

time: 104 us -> 99.2 us (0.954)
  waiting for transfers between devices: 45.2 us -> 54.5 us
  local copies, waits for them, and re-layouts: 11.4 us -> 3.81 us
  starting transfers between devices: 28.7 us -> 23.7 us
  Pallas kernels: 17.4 us -> 15.8 us
    ppermute x21, waiting for transfers between devices: 45.2 us -> 54.5 us  [swap(): lax.ppermute(value, axis, [(i, i ^ mask) for i in range(lax.axis_size(axi...]
    unnamed x48 -> x16, local copies, waits for them, and re-layouts: 11.4 us -> 3.81 us
    ppermute x21, starting transfers between devices: 28.7 us -> 23.7 us  [swap(): lax.ppermute(value, axis, [(i, i ^ mask) for i in range(lax.axis_size(axi...]
    pallas_call x16, Pallas kernels: 17.4 us -> 15.8 us  [call(): pl.pallas_call(kernel, out_shape=tuple(outs), in_specs=[on_smem] * len(sm...]
  transfers between devices with their start and end apart: 21 -> 21, of which waited for: 15 -> 17; matrix products, arithmetic and copies ran while one was open for 0% -> 0% of each run, Pallas kernels for 14% -> 13%
where the time goes in v6:
time: 99.2 us; the launch traced here: 98.6 us
  waiting for transfers between devices  54.5 us (55%)
  starting transfers between devices  23.7 us (24%)
  Pallas kernels  15.8 us (16%)
  local copies, waits for them, and re-layouts  3.81 us (4%)
    ppermute x21, waiting for transfers between devices, swap(): lax.ppermute(value, axis, [(i, i ^ mask) for i in range(lax.axis_size(axi...  54.5 us
    ppermute x21, starting transfers between devices, swap(): lax.ppermute(value, axis, [(i, i ^ mask) for i in range(lax.axis_size(axi...  23.7 us
    pallas_call x16, Pallas kernels, call(): pl.pallas_call(kernel, out_shape=tuple(outs), in_specs=[on_smem] * len(sm...  15.8 us
    unnamed x16, local copies, waits for them, and re-layouts  3.81 us
  transfers between devices with their start and end apart: 21, of which 17 were waited for; matrix products, arithmetic and copies ran while one was open for 0% of the time, Pallas kernels for 13%

profile of v6, /device:TPU:1, one launch (start us, length us, event | category | flops | bytes accessed | tf_op | source)
XLA Modules:
  0.0 98.6 jit_solution(15134521571744142370)
XLA Ops:
  0.6 0.0 copy-start.7
  0.6 0.0 copy-start.6
  0.7 1.1 %copy-done = bf16[1,512,768]{2,1,0:T(8,128)(2,1)S(1)} copy-done((bf16[1,512,768]{2,1,0:T(8,128)(2,1)S(1)}, bf16[1,512,768]{2,1,0:T(8,128)(2,1)}, u32[]{:S(2)}) %copy-start) | copy-done | bytes 786456
  1.8 1.0 %copy-done.1 = bf16[1,512,384]{2,1,0:T(8,128)(2,1)S(1)} copy-done((bf16[1,512,384]{2,1,0:T(8,128)(2,1)S(1)}, bf16[1,512,384]{2,1,0:T(8,128)(2,1)}, u32[]{:S(2)}) %copy-start.1) | copy-done | bytes 393240
  2.8 0.1 shard_map.96.own_ref
  2.9 2.1 %collective-permute-start.4 = (bf16[512,1152]{1,0:T(8,128)(2,1)S(1)}, bf16[512,1152]{1,0:T(8,128)(2,1)S(1)}, u32[]{:S(2)}, u32[]{:S(2)}) collective-permute-start(bf16[512,1152]{1,0:T(8,128)(2,1)S(1)} %shard_map.96.own_ref), channel_id=1, source_target_pairs={{0,2},{1,3},{2,0},{3,1},{4,6},{5,7},{6,4},{7,5},{8,10},{9,11},{10,... | collective-permute-start | bytes 3538952 | tf_op jit(solution)/shard_map/ppermute | solution.py:314
  5.0 0.0 copy-done.7
  5.0 0.6 shard_map.93
  5.6 2.4 %collective-permute-start.3 = (bf16[128,2176]{1,0:T(8,128)(2,1)S(1)}, bf16[128,2176]{1,0:T(8,128)(2,1)S(1)}, u32[]{:S(2)}, u32[]{:S(2)}) collective-permute-start(bf16[128,2176]{1,0:T(8,128)(2,1)S(1)} %get-tuple-element.41.joint_ref), channel_id=1, source_target_pairs={{0,16},{4,20},{8,24},{12,28},{16,0},{20,4},{24,8},{28,12},{1,17},{... | collective-permute-start | bytes 1671176 | tf_op jit(solution)/shard_map/ppermute | solution.py:314
  8.0 1.5 %shard_map.94 = (bf16[64,2176]{1,0:T(8,128)(2,1)S(1)}, bf16[64,2176]{1,0:T(8,128)(2,1)}, bf16[64,2176]{1,0:T(8,128)(2,1)}, bf16[64,2176]{1,0:T(8,128)(2,1)}) custom-call(bf16[128,2176]{1,0:T(8,128)(2,1)S(1)} %get-tuple-element.41.joint_ref), custom_call_target="tpu_custom_call" | custom-call | flops 75497472 | bytes 1671168 | tf_op jit(solution)/shard_map/pallas_call | solution.py:301
  9.5 0.7 copy-done.2
  10.2 1.2 %collective-permute-start = (bf16[64,2176]{1,0:T(8,128)(2,1)}, bf16[64,2176]{1,0:T(8,128)(2,1)}, u32[]{:S(2)}, u32[]{:S(2)}) collective-permute-start(bf16[64,2176]{1,0:T(8,128)(2,1)} %get-tuple-element.43), channel_id=1, source_target_pairs={{0,4},{4,0},{8,12},{12,8},{16,20},{20,16},{24,28},{28,24},{1,5},{5... | collective-permute-start | bytes 835592 | tf_op jit(solution)/shard_map/ppermute | solution.py:314
  11.4 1.3 %collective-permute-start.1 = (bf16[64,2176]{1,0:T(8,128)(2,1)}, bf16[64,2176]{1,0:T(8,128)(2,1)}, u32[]{:S(2)}, u32[]{:S(2)}) collective-permute-start(bf16[64,2176]{1,0:T(8,128)(2,1)} %get-tuple-element.44), channel_id=1, source_target_pairs={{0,8},{4,12},{8,0},{12,4},{16,24},{20,28},{24,16},{28,20},{1,9},{5... | collective-permute-start | bytes 835592 | tf_op jit(solution)/shard_map/ppermute | solution.py:314
  12.7 0.1 collective-permute-start.2
  12.8 4.6 %collective-permute-done.refs_1_ = bf16[64,2176]{1,0:T(8,128)(2,1)} collective-permute-done((bf16[64,2176]{1,0:T(8,128)(2,1)}, bf16[64,2176]{1,0:T(8,128)(2,1)}, u32[]{:S(2)}, u32[]{:S(2)}) %collective-permute-start) | collective-permute-done | bytes 278560 | tf_op jit(solution)/shard_map/ppermute | solution.py:314
  17.4 7.7 %collective-permute-done.1.refs_2_ = bf16[64,2176]{1,0:T(8,128)(2,1)} collective-permute-done((bf16[64,2176]{1,0:T(8,128)(2,1)}, bf16[64,2176]{1,0:T(8,128)(2,1)}, u32[]{:S(2)}, u32[]{:S(2)}) %collective-permute-start.1) | collective-permute-done | bytes 278560 | tf_op jit(solution)/shard_map/ppermute | solution.py:314
  25.1 10.0 %collective-permute-done.2.refs_3_ = bf16[64,2176]{1,0:T(8,128)(2,1)} collective-permute-done((bf16[64,2176]{1,0:T(8,128)(2,1)}, bf16[64,2176]{1,0:T(8,128)(2,1)}, u32[]{:S(2)}, u32[]{:S(2)}) %collective-permute-start.2) | collective-permute-done | bytes 278560 | tf_op jit(solution)/shard_map/ppermute | solution.py:314
  35.1 0.0 collective-permute-done.3.refs_4_.joint_ref
  35.1 1.0 copy-done.3
  36.1 1.2 %shard_map.95 = (bf16[144,1024]{1,0:T(8,128)(2,1)S(1)}, bf16[144,1024]{1,0:T(8,128)(2,1)S(1)}, bf16[144,2048]{1,0:T(8,128)(2,1)S(1)}, f32[144,128]{1,0:T(8,128)S(1)}) custom-call(s32[4]{0:T(128)S(1)} %iota_xor_fusion.place_ref, bf16[64,2176]{1,0:T(8,128)(2,1)S(1)} %copy-done.3, bf16[64,2176]{1,0:T(8,128)(2,1)} %collective-permute-done.refs_1_, ...), custom_call_target="tpu_custom_call" | custom-call | bytes 2367488 | tf_op jit(solution)/shard_map/pallas_call | solution.py:301
  37.3 0.0 collective-permute-done.4.refs_1_.far_ref
  37.3 0.6 shard_map.97
  37.9 0.2 shard_map.98.refs_0_
  38.1 2.5 %collective-permute-start.5 = (bf16[1024,1152]{1,0:T(8,128)(2,1)S(1)}, bf16[1024,1152]{1,0:T(8,128)(2,1)S(1)}, u32[]{:S(2)}, u32[]{:S(2)}) collective-permute-start(bf16[1024,1152]{1,0:T(8,128)(2,1)S(1)} %shard_map.98.refs_0_), channel_id=1, source_target_pairs={{0,1},{1,0},{2,3},{3,2},{4,5},{5,4},{6,7},{7,6},{8,9},{9,8},{10,11... | collective-permute-start | bytes 7077896 | tf_op jit(solution)/shard_map/ppermute | solution.py:314
  40.6 1.3 %collective-permute-start.9 = (bf16[64,2176]{1,0:T(8,128)(2,1)S(1)}, bf16[64,2176]{1,0:T(8,128)(2,1)S(1)}, u32[]{:S(2)}, u32[]{:S(2)}) collective-permute-start(bf16[64,2176]{1,0:T(8,128)(2,1)S(1)} %get-tuple-element.55), channel_id=1, source_target_pairs={{0,4},{4,0},{8,12},{12,8},{16,20},{20,16},{24,28},{28,24},{1,5},{5... | collective-permute-start | bytes 835592 | tf_op jit(solution)/shard_map/ppermute | solution.py:314
  41.9 0.0 collective-permute-start.10
  41.9 1.4 %collective-permute-start.11 = (bf16[64,2176]{1,0:T(8,128)(2,1)S(1)}, bf16[64,2176]{1,0:T(8,128)(2,1)S(1)}, u32[]{:S(2)}, u32[]{:S(2)}) collective-permute-start(bf16[64,2176]{1,0:T(8,128)(2,1)S(1)} %get-tuple-element.57), channel_id=1, source_target_pairs={{0,12},{4,8},{8,4},{12,0},{16,28},{20,24},{24,20},{28,16},{1,13},{... | collective-permute-start | bytes 835592 | tf_op jit(solution)/shard_map/ppermute | solution.py:314
  43.3 1.5 %collective-permute-done.5.refs_1_ = bf16[1024,1152]{1,0:T(8,128)(2,1)S(1)} collective-permute-done((bf16[1024,1152]{1,0:T(8,128)(2,1)S(1)}, bf16[1024,1152]{1,0:T(8,128)(2,1)S(1)}, u32[]{:S(2)}, u32[]{:S(2)}) %collective-permute-start.5) | collective-permute-done | bytes 2359328 | tf_op jit(solution)/shard_map/ppermute | solution.py:314
  44.8 2.6 %shard_map.99 = (bf16[144,1152]{1,0:T(8,128)(2,1)S(1)}, bf16[32,2176]{1,0:T(8,128)(2,1)S(1)}, bf16[32,2176]{1,0:T(8,128)(2,1)S(1)}, bf16[32,2176]{1,0:T(8,128)(2,1)S(1)}, bf16[32,2176]{1,0:T(8,128)(2,1)S(1)}) custom-call(s32[4]{0:T(128)S(1)} %iota_xor_fusion.place_ref, f32[144,128]{1,0:T(8,128)S(1)} %get-tuple-element.46.w_ref, ...), custom_call_target="tpu_custom_call" | custom-call | flops 1132462080 | bytes 6860800 | tf_op jit(solution)/shard_map/pallas_call | solution.py:301
  47.4 1.3 %collective-permute-start.6 = (bf16[32,2176]{1,0:T(8,128)(2,1)S(1)}, bf16[32,2176]{1,0:T(8,128)(2,1)S(1)}, u32[]{:S(2)}, u32[]{:S(2)}) collective-permute-start(bf16[32,2176]{1,0:T(8,128)(2,1)S(1)} %get-tuple-element.52), channel_id=1, source_target_pairs={{0,4},{4,0},{8,12},{12,8},{16,20},{20,16},{24,28},{28,24},{1,5},{5... | collective-permute-start | bytes 417800 | tf_op jit(solution)/shard_map/ppermute | solution.py:314
  48.7 0.8 collective-permute-start.12
  49.5 0.0 collective-permute-done.9.refs_1_
  49.6 0.2 collective-permute-done.10.refs_2_
  49.8 6.0 %collective-permute-done.11.refs_3_ = bf16[64,2176]{1,0:T(8,128)(2,1)S(1)} collective-permute-done((bf16[64,2176]{1,0:T(8,128)(2,1)S(1)}, bf16[64,2176]{1,0:T(8,128)(2,1)S(1)}, u32[]{:S(2)}, u32[]{:S(2)}) %collective-permute-start.11) | collective-permute-done | bytes 278560 | tf_op jit(solution)/shard_map/ppermute | solution.py:314
  55.7 2.8 %collective-permute-done.6.refs_5_.b1 = bf16[32,2176]{1,0:T(8,128)(2,1)S(1)} collective-permute-done((bf16[32,2176]{1,0:T(8,128)(2,1)S(1)}, bf16[32,2176]{1,0:T(8,128)(2,1)S(1)}, u32[]{:S(2)}, u32[]{:S(2)}) %collective-permute-start.6) | collective-permute-done | bytes 139296 | tf_op jit(solution)/shard_map/ppermute | solution.py:314
  58.5 0.7 shard_map.100
  59.2 0.9 collective-permute-start.13
  60.1 2.6 %shard_map.101 = (bf16[288,1152]{1,0:T(8,128)(2,1)S(1)}, bf16[32,2176]{1,0:T(8,128)(2,1)S(1)}, bf16[32,2176]{1,0:T(8,128)(2,1)S(1)}, bf16[32,2176]{1,0:T(8,128)(2,1)S(1)}, bf16[32,2176]{1,0:T(8,128)(2,1)S(1)}) custom-call(s32[4]{0:T(128)S(1)} %iota_xor_fusion.place_ref, f32[144,128]{1,0:T(8,128)S(1)} %get-tuple-element.62.w_ref, ...), custom_call_target="tpu_custom_call" | custom-call | flops 1132462080 | bytes 7524352 | tf_op jit(solution)/shard_map/pallas_call | solution.py:301
  62.7 1.3 %collective-permute-start.14 = (bf16[32,2176]{1,0:T(8,128)(2,1)S(1)}, bf16[32,2176]{1,0:T(8,128)(2,1)S(1)}, u32[]{:S(2)}, u32[]{:S(2)}) collective-permute-start(bf16[32,2176]{1,0:T(8,128)(2,1)S(1)} %get-tuple-element.65), channel_id=1, source_target_pairs={{0,4},{4,0},{8,12},{12,8},{16,20},{20,16},{24,28},{28,24},{1,5},{5... | collective-permute-start | bytes 417800 | tf_op jit(solution)/shard_map/ppermute | solution.py:314
  64.0 0.0 collective-permute-start.15
  64.0 1.4 %collective-permute-start.16 = (bf16[32,2176]{1,0:T(8,128)(2,1)S(1)}, bf16[32,2176]{1,0:T(8,128)(2,1)S(1)}, u32[]{:S(2)}, u32[]{:S(2)}) collective-permute-start(bf16[32,2176]{1,0:T(8,128)(2,1)S(1)} %get-tuple-element.67), channel_id=1, source_target_pairs={{0,12},{4,8},{8,4},{12,0},{16,28},{20,24},{24,20},{28,16},{1,13},{... | collective-permute-start | bytes 417800 | tf_op jit(solution)/shard_map/ppermute | solution.py:314
  65.4 1.6 %collective-permute-done.14.b1 = bf16[32,2176]{1,0:T(8,128)(2,1)S(1)} collective-permute-done((bf16[32,2176]{1,0:T(8,128)(2,1)S(1)}, bf16[32,2176]{1,0:T(8,128)(2,1)S(1)}, u32[]{:S(2)}, u32[]{:S(2)}) %collective-permute-start.14) | collective-permute-done | bytes 139296 | tf_op jit(solution)/shard_map/ppermute | solution.py:314
  67.0 1.2 %collective-permute-done.15.b2 = bf16[32,2176]{1,0:T(8,128)(2,1)S(1)} collective-permute-done((bf16[32,2176]{1,0:T(8,128)(2,1)S(1)}, bf16[32,2176]{1,0:T(8,128)(2,1)S(1)}, u32[]{:S(2)}, u32[]{:S(2)}) %collective-permute-start.15) | collective-permute-done | bytes 139296 | tf_op jit(solution)/shard_map/ppermute | solution.py:314
  68.2 2.2 %collective-permute-done.16.b3 = bf16[32,2176]{1,0:T(8,128)(2,1)S(1)} collective-permute-done((bf16[32,2176]{1,0:T(8,128)(2,1)S(1)}, bf16[32,2176]{1,0:T(8,128)(2,1)S(1)}, u32[]{:S(2)}, u32[]{:S(2)}) %collective-permute-start.16) | collective-permute-done | bytes 139296 | tf_op jit(solution)/shard_map/ppermute | solution.py:314
  70.5 0.4 shard_map.102.after_ref
  70.9 0.0 collective-permute-done.12.far_a.rows_a
  70.9 4.7 %collective-permute-done.13.far_b.rows_b = bf16[144,2048]{1,0:T(8,128)(2,1)S(1)} collective-permute-done((bf16[144,2048]{1,0:T(8,128)(2,1)S(1)}, bf16[144,2048]{1,0:T(8,128)(2,1)S(1)}, u32[]{:S(2)}, u32[]{:S(2)}) %collective-permute-start.13) | collective-permute-done | bytes 589856 | tf_op jit(solution)/shard_map/ppermute | solution.py:314
  75.6 0.1 shard_map.103
  75.7 1.6 %collective-permute-start.17 = (bf16[288,3200]{1,0:T(8,128)(2,1)S(1)}, bf16[288,3200]{1,0:T(8,128)(2,1)S(1)}, u32[]{:S(2)}, u32[]{:S(2)}) collective-permute-start(bf16[288,3200]{1,0:T(8,128)(2,1)S(1)} %shard_map.103), channel_id=1, source_target_pairs={{0,1},{1,0},{2,3},{3,2},{4,5},{5,4},{6,7},{7,6},{8,9},{9,8},{10,11... | collective-permute-start | bytes 5529608 | tf_op jit(solution)/shard_map/ppermute | solution.py:314
  77.3 0.9 collective-permute-start.19
  78.1 0.0 collective-permute-start.18
  78.1 2.4 %collective-permute-start.7 = (bf16[32,2176]{1,0:T(8,128)(2,1)S(1)}, bf16[32,2176]{1,0:T(8,128)(2,1)S(1)}, u32[]{:S(2)}, u32[]{:S(2)}) collective-permute-start(bf16[32,2176]{1,0:T(8,128)(2,1)S(1)} %get-tuple-element.53), channel_id=1, source_target_pairs={{0,8},{4,12},{8,0},{12,4},{16,24},{20,28},{24,16},{28,20},{1,9},{5... | collective-permute-start | bytes 417800 | tf_op jit(solution)/shard_map/ppermute | solution.py:314
  80.5 0.0 collective-permute-start.8
  80.5 0.2 collective-permute-done.17.near_ref
  80.7 1.2 %shard_map.104 = (f32[512,768]{1,0:T(8,128)S(1)}, f32[512,384]{1,0:T(8,128)S(1)}) custom-call(bf16[144,1024]{1,0:T(8,128)(2,1)S(1)} %get-tuple-element.47.refs_0_.refs_2_.rows_a, bf16[144,1024]{1,0:T(8,128)(2,1)S(1)} %get-tuple-element.59.refs_2_.rows_b, bf16[288,3200]{1,0:T(8,128)(2,1)S(1)} %collective-permute-done.17.near_ref, ...), custom_call_target="tpu_custom_call" | custom-call | flops 679477248 | bytes 5455872 | tf_op jit(solution)/shard_map/pallas_call | solution.py:301
  81.9 5.2 %collective-permute-done.7.b2 = bf16[32,2176]{1,0:T(8,128)(2,1)S(1)} collective-permute-done((bf16[32,2176]{1,0:T(8,128)(2,1)S(1)}, bf16[32,2176]{1,0:T(8,128)(2,1)S(1)}, u32[]{:S(2)}, u32[]{:S(2)}) %collective-permute-start.7) | collective-permute-done | bytes 139296 | tf_op jit(solution)/shard_map/ppermute | solution.py:314
  87.2 3.0 %collective-permute-done.8.b3 = bf16[32,2176]{1,0:T(8,128)(2,1)S(1)} collective-permute-done((bf16[32,2176]{1,0:T(8,128)(2,1)S(1)}, bf16[32,2176]{1,0:T(8,128)(2,1)S(1)}, u32[]{:S(2)}, u32[]{:S(2)}) %collective-permute-start.8) | collective-permute-done | bytes 139296 | tf_op jit(solution)/shard_map/ppermute | solution.py:314
  90.2 0.4 shard_map.105
  90.6 2.8 %collective-permute-done.18.far_ref.refs_2_ = bf16[64,2176]{1,0:T(8,128)(2,1)S(1)} collective-permute-done((bf16[64,2176]{1,0:T(8,128)(2,1)S(1)}, bf16[64,2176]{1,0:T(8,128)(2,1)S(1)}, u32[]{:S(2)}, u32[]{:S(2)}) %collective-permute-start.18) | collective-permute-done | bytes 278560 | tf_op jit(solution)/shard_map/ppermute | solution.py:314
  93.4 0.4 collective-permute-done.19.refs_0_
  93.8 0.8 collective-permute-start.20
  94.6 1.3 %shard_map.106 = (bf16[64,2048]{1,0:T(8,128)(2,1)}, bf16[4,64]{1,0:T(4,128)(2,1)}) custom-call(s32[8]{0:T(128)S(1)} %iota_xor_fusion.1.peer_ref, s32[4,64]{1,0:T(4,128)S(1)} %bitcast.10, f32[64,2048]{1,0:T(8,128)S(1)} %get-tuple-element.69.near_ref.refs_3_, f32[8,64]{1,0:T(8,128)S(1)} %get-tuple-element.70.near_route_ref, ...), custom_call_target="tpu_custom_call" | custom-call | bytes 1068544 | tf_op jit(solution)/shard_map/pallas_call | solution.py:301
  95.9 0.4 collective-permute-done.20.mid_b
  96.4 2.3 %shard_map.108 = (f32[512,768]{1,0:T(8,128)}, f32[512,384]{1,0:T(8,128)}) custom-call(bf16[144,2048]{1,0:T(8,128)(2,1)S(1)} %collective-permute-done.12.far_a.rows_a, bf16[144,2048]{1,0:T(8,128)(2,1)S(1)} %collective-permute-done.13.far_b.rows_b, bf16[288,3200]{1,0:T(8,128)(2,1)S(1)} %collective-permute-done.17.near_ref, ...), custom_call_target="tpu_custom_call" | custom-call | flops 679477248 | bytes 6709248 | tf_op jit(solution)/shard_map/pallas_call | solution.py:301
  (12 shorter events, 0.0 us)
Async XLA Ops:
  0.6 4.4 %copy-start.7 = (bf16[64,4]{0,1:T(4,128)(2,1)S(1)}, bf16[64,4]{0,1:T(4,128)(2,1)}, u32[]{:S(2)}) copy-start(bf16[64,4]{0,1:T(4,128)(2,1)} %param.9) | copy-start | bytes 1540
  0.6 4.4 %copy-start.6 = (s32[64,4]{0,1:T(4,128)S(1)}, s32[64,4]{0,1:T(4,128)}, u32[]{:S(2)}) copy-start(s32[64,4]{0,1:T(4,128)} %param.8) | copy-start | bytes 3076
  0.7 1.1 %copy-start = (bf16[1,512,768]{2,1,0:T(8,128)(2,1)S(1)}, bf16[1,512,768]{2,1,0:T(8,128)(2,1)}, u32[]{:S(2)}) copy-start(bf16[1,512,768]{2,1,0:T(8,128)(2,1)} %param.10) | copy-start | bytes 2359300
  1.8 1.0 %copy-start.1 = (bf16[1,512,384]{2,1,0:T(8,128)(2,1)S(1)}, bf16[1,512,384]{2,1,0:T(8,128)(2,1)}, u32[]{:S(2)}) copy-start(bf16[1,512,384]{2,1,0:T(8,128)(2,1)} %param.11) | copy-start | bytes 1179652
  2.8 2.2 %copy-start.4 = (bf16[64,2048]{1,0:T(8,128)(2,1)S(1)}, bf16[64,2048]{1,0:T(8,128)(2,1)}, u32[]{:S(2)}) copy-start(bf16[64,2048]{1,0:T(8,128)(2,1)} %x_ref.1) | copy-start | bytes 786436
  2.8 2.2 %copy-start.5 = (bf16[64,2048]{1,0:T(8,128)(2,1)S(1)}, bf16[64,2048]{1,0:T(8,128)(2,1)}, u32[]{:S(2)}) copy-start(bf16[64,2048]{1,0:T(8,128)(2,1)} %dy_ref.1) | copy-start | bytes 786436
  2.9 34.4 %collective-permute-start.4 = (bf16[512,1152]{1,0:T(8,128)(2,1)S(1)}, bf16[512,1152]{1,0:T(8,128)(2,1)S(1)}, u32[]{:S(2)}, u32[]{:S(2)}) collective-permute-start(bf16[512,1152]{1,0:T(8,128)(2,1)S(1)} %shard_map.96.own_ref), channel_id=1, source_target_pairs={{0,2},{1,3},{2,0},{3,1},{4,6},{5,7},{6,4},{7,5},{8,10},{9,11},{10,... | collective-permute-start | bytes 3538952 | tf_op jit(solution)/shard_map/ppermute | solution.py:314
  5.6 29.5 %collective-permute-start.3 = (bf16[128,2176]{1,0:T(8,128)(2,1)S(1)}, bf16[128,2176]{1,0:T(8,128)(2,1)S(1)}, u32[]{:S(2)}, u32[]{:S(2)}) collective-permute-start(bf16[128,2176]{1,0:T(8,128)(2,1)S(1)} %get-tuple-element.41.joint_ref), channel_id=1, source_target_pairs={{0,16},{4,20},{8,24},{12,28},{16,0},{20,4},{24,8},{28,12},{1,17},{... | collective-permute-start | bytes 1671176 | tf_op jit(solution)/shard_map/ppermute | solution.py:314
  9.5 0.7 copy-start.2
  10.2 7.2 %collective-permute-start = (bf16[64,2176]{1,0:T(8,128)(2,1)}, bf16[64,2176]{1,0:T(8,128)(2,1)}, u32[]{:S(2)}, u32[]{:S(2)}) collective-permute-start(bf16[64,2176]{1,0:T(8,128)(2,1)} %get-tuple-element.43), channel_id=1, source_target_pairs={{0,4},{4,0},{8,12},{12,8},{16,20},{20,16},{24,28},{28,24},{1,5},{5... | collective-permute-start | bytes 835592 | tf_op jit(solution)/shard_map/ppermute | solution.py:314
  11.4 13.7 %collective-permute-start.1 = (bf16[64,2176]{1,0:T(8,128)(2,1)}, bf16[64,2176]{1,0:T(8,128)(2,1)}, u32[]{:S(2)}, u32[]{:S(2)}) collective-permute-start(bf16[64,2176]{1,0:T(8,128)(2,1)} %get-tuple-element.44), channel_id=1, source_target_pairs={{0,8},{4,12},{8,0},{12,4},{16,24},{20,28},{24,16},{28,20},{1,9},{5... | collective-permute-start | bytes 835592 | tf_op jit(solution)/shard_map/ppermute | solution.py:314
  12.7 22.4 %collective-permute-start.2 = (bf16[64,2176]{1,0:T(8,128)(2,1)}, bf16[64,2176]{1,0:T(8,128)(2,1)}, u32[]{:S(2)}, u32[]{:S(2)}) collective-permute-start(bf16[64,2176]{1,0:T(8,128)(2,1)} %get-tuple-element.45), channel_id=1, source_target_pairs={{0,12},{4,8},{8,4},{12,0},{16,28},{20,24},{24,20},{28,16},{1,13},{... | collective-permute-start | bytes 835592 | tf_op jit(solution)/shard_map/ppermute | solution.py:314
  35.1 1.0 copy-start.3
  38.1 6.7 %collective-permute-start.5 = (bf16[1024,1152]{1,0:T(8,128)(2,1)S(1)}, bf16[1024,1152]{1,0:T(8,128)(2,1)S(1)}, u32[]{:S(2)}, u32[]{:S(2)}) collective-permute-start(bf16[1024,1152]{1,0:T(8,128)(2,1)S(1)} %shard_map.98.refs_0_), channel_id=1, source_target_pairs={{0,1},{1,0},{2,3},{3,2},{4,5},{5,4},{6,7},{7,6},{8,9},{9,8},{10,11... | collective-permute-start | bytes 7077896 | tf_op jit(solution)/shard_map/ppermute | solution.py:314
  40.6 8.9 %collective-permute-start.9 = (bf16[64,2176]{1,0:T(8,128)(2,1)S(1)}, bf16[64,2176]{1,0:T(8,128)(2,1)S(1)}, u32[]{:S(2)}, u32[]{:S(2)}) collective-permute-start(bf16[64,2176]{1,0:T(8,128)(2,1)S(1)} %get-tuple-element.55), channel_id=1, source_target_pairs={{0,4},{4,0},{8,12},{12,8},{16,20},{20,16},{24,28},{28,24},{1,5},{5... | collective-permute-start | bytes 835592 | tf_op jit(solution)/shard_map/ppermute | solution.py:314
  41.9 7.9 %collective-permute-start.10 = (bf16[64,2176]{1,0:T(8,128)(2,1)S(1)}, bf16[64,2176]{1,0:T(8,128)(2,1)S(1)}, u32[]{:S(2)}, u32[]{:S(2)}) collective-permute-start(bf16[64,2176]{1,0:T(8,128)(2,1)S(1)} %get-tuple-element.56), channel_id=1, source_target_pairs={{0,8},{4,12},{8,0},{12,4},{16,24},{20,28},{24,16},{28,20},{1,9},{5... | collective-permute-start | bytes 835592 | tf_op jit(solution)/shard_map/ppermute | solution.py:314
  41.9 13.9 %collective-permute-start.11 = (bf16[64,2176]{1,0:T(8,128)(2,1)S(1)}, bf16[64,2176]{1,0:T(8,128)(2,1)S(1)}, u32[]{:S(2)}, u32[]{:S(2)}) collective-permute-start(bf16[64,2176]{1,0:T(8,128)(2,1)S(1)} %get-tuple-element.57), channel_id=1, source_target_pairs={{0,12},{4,8},{8,4},{12,0},{16,28},{20,24},{24,20},{28,16},{1,13},{... | collective-permute-start | bytes 835592 | tf_op jit(solution)/shard_map/ppermute | solution.py:314
  47.4 11.1 %collective-permute-start.6 = (bf16[32,2176]{1,0:T(8,128)(2,1)S(1)}, bf16[32,2176]{1,0:T(8,128)(2,1)S(1)}, u32[]{:S(2)}, u32[]{:S(2)}) collective-permute-start(bf16[32,2176]{1,0:T(8,128)(2,1)S(1)} %get-tuple-element.52), channel_id=1, source_target_pairs={{0,4},{4,0},{8,12},{12,8},{16,20},{20,16},{24,28},{28,24},{1,5},{5... | collective-permute-start | bytes 417800 | tf_op jit(solution)/shard_map/ppermute | solution.py:314
  48.7 22.2 %collective-permute-start.12 = (bf16[144,2048]{1,0:T(8,128)(2,1)S(1)}, bf16[144,2048]{1,0:T(8,128)(2,1)S(1)}, u32[]{:S(2)}, u32[]{:S(2)}) collective-permute-start(bf16[144,2048]{1,0:T(8,128)(2,1)S(1)} %get-tuple-element.50.refs_4_), channel_id=1, source_target_pairs={{0,2},{1,3},{2,0},{3,1},{4,6},{5,7},{6,4},{7,5},{8,10},{9,11},{10,... | collective-permute-start | bytes 1769480 | tf_op jit(solution)/shard_map/ppermute | solution.py:314
  59.2 16.4 %collective-permute-start.13 = (bf16[144,2048]{1,0:T(8,128)(2,1)S(1)}, bf16[144,2048]{1,0:T(8,128)(2,1)S(1)}, u32[]{:S(2)}, u32[]{:S(2)}) collective-permute-start(bf16[144,2048]{1,0:T(8,128)(2,1)S(1)} %get-tuple-element.61.refs_4_), channel_id=1, source_target_pairs={{0,2},{1,3},{2,0},{3,1},{4,6},{5,7},{6,4},{7,5},{8,10},{9,11},{10,... | collective-permute-start | bytes 1769480 | tf_op jit(solution)/shard_map/ppermute | solution.py:314
  62.7 4.3 %collective-permute-start.14 = (bf16[32,2176]{1,0:T(8,128)(2,1)S(1)}, bf16[32,2176]{1,0:T(8,128)(2,1)S(1)}, u32[]{:S(2)}, u32[]{:S(2)}) collective-permute-start(bf16[32,2176]{1,0:T(8,128)(2,1)S(1)} %get-tuple-element.65), channel_id=1, source_target_pairs={{0,4},{4,0},{8,12},{12,8},{16,20},{20,16},{24,28},{28,24},{1,5},{5... | collective-permute-start | bytes 417800 | tf_op jit(solution)/shard_map/ppermute | solution.py:314
  64.0 4.2 %collective-permute-start.15 = (bf16[32,2176]{1,0:T(8,128)(2,1)S(1)}, bf16[32,2176]{1,0:T(8,128)(2,1)S(1)}, u32[]{:S(2)}, u32[]{:S(2)}) collective-permute-start(bf16[32,2176]{1,0:T(8,128)(2,1)S(1)} %get-tuple-element.66), channel_id=1, source_target_pairs={{0,8},{4,12},{8,0},{12,4},{16,24},{20,28},{24,16},{28,20},{1,9},{5... | collective-permute-start | bytes 417800 | tf_op jit(solution)/shard_map/ppermute | solution.py:314
  64.0 6.4 %collective-permute-start.16 = (bf16[32,2176]{1,0:T(8,128)(2,1)S(1)}, bf16[32,2176]{1,0:T(8,128)(2,1)S(1)}, u32[]{:S(2)}, u32[]{:S(2)}) collective-permute-start(bf16[32,2176]{1,0:T(8,128)(2,1)S(1)} %get-tuple-element.67), channel_id=1, source_target_pairs={{0,12},{4,8},{8,4},{12,0},{16,28},{20,24},{24,20},{28,16},{1,13},{... | collective-permute-start | bytes 417800 | tf_op jit(solution)/shard_map/ppermute | solution.py:314
  75.7 5.0 %collective-permute-start.17 = (bf16[288,3200]{1,0:T(8,128)(2,1)S(1)}, bf16[288,3200]{1,0:T(8,128)(2,1)S(1)}, u32[]{:S(2)}, u32[]{:S(2)}) collective-permute-start(bf16[288,3200]{1,0:T(8,128)(2,1)S(1)} %shard_map.103), channel_id=1, source_target_pairs={{0,1},{1,0},{2,3},{3,2},{4,5},{5,4},{6,7},{7,6},{8,9},{9,8},{10,11... | collective-permute-start | bytes 5529608 | tf_op jit(solution)/shard_map/ppermute | solution.py:314
  77.3 16.5 %collective-permute-start.19 = (bf16[288,1152]{1,0:T(8,128)(2,1)S(1)}, bf16[288,1152]{1,0:T(8,128)(2,1)S(1)}, u32[]{:S(2)}, u32[]{:S(2)}) collective-permute-start(bf16[288,1152]{1,0:T(8,128)(2,1)S(1)} %get-tuple-element.63.mid_ref), channel_id=1, source_target_pairs={{0,2},{1,3},{2,0},{3,1},{4,6},{5,7},{6,4},{7,5},{8,10},{9,11},{10,... | collective-permute-start | bytes 1990664 | tf_op jit(solution)/shard_map/ppermute | solution.py:314
  78.1 15.2 %collective-permute-start.18 = (bf16[64,2176]{1,0:T(8,128)(2,1)S(1)}, bf16[64,2176]{1,0:T(8,128)(2,1)S(1)}, u32[]{:S(2)}, u32[]{:S(2)}) collective-permute-start(bf16[64,2176]{1,0:T(8,128)(2,1)S(1)} %shard_map.102.after_ref), channel_id=1, source_target_pairs={{0,16},{4,20},{8,24},{12,28},{16,0},{20,4},{24,8},{28,12},{1,17},{... | collective-permute-start | bytes 835592 | tf_op jit(solution)/shard_map/ppermute | solution.py:314
  78.1 9.0 %collective-permute-start.7 = (bf16[32,2176]{1,0:T(8,128)(2,1)S(1)}, bf16[32,2176]{1,0:T(8,128)(2,1)S(1)}, u32[]{:S(2)}, u32[]{:S(2)}) collective-permute-start(bf16[32,2176]{1,0:T(8,128)(2,1)S(1)} %get-tuple-element.53), channel_id=1, source_target_pairs={{0,8},{4,12},{8,0},{12,4},{16,24},{20,28},{24,16},{28,20},{1,9},{5... | collective-permute-start | bytes 417800 | tf_op jit(solution)/shard_map/ppermute | solution.py:314
  80.5 9.7 %collective-permute-start.8 = (bf16[32,2176]{1,0:T(8,128)(2,1)S(1)}, bf16[32,2176]{1,0:T(8,128)(2,1)S(1)}, u32[]{:S(2)}, u32[]{:S(2)}) collective-permute-start(bf16[32,2176]{1,0:T(8,128)(2,1)S(1)} %get-tuple-element.54), channel_id=1, source_target_pairs={{0,12},{4,8},{8,4},{12,0},{16,28},{20,24},{24,20},{28,16},{1,13},{... | collective-permute-start | bytes 417800 | tf_op jit(solution)/shard_map/ppermute | solution.py:314
  93.8 2.6 %collective-permute-start.20 = (bf16[288,1152]{1,0:T(8,128)(2,1)S(1)}, bf16[288,1152]{1,0:T(8,128)(2,1)S(1)}, u32[]{:S(2)}, u32[]{:S(2)}) collective-permute-start(bf16[288,1152]{1,0:T(8,128)(2,1)S(1)} %shard_map.107.mid_a), channel_id=1, source_target_pairs={{0,1},{1,0},{2,3},{3,2},{4,5},{5,4},{6,7},{7,6},{8,9},{9,8},{10,11... | collective-permute-start | bytes 1990664 | tf_op jit(solution)/shard_map/ppermute | solution.py:314

commit v7 on v6

--- a/solution.py
+++ b/solution.py
@@ -59,16 +59,10 @@
     dense = jnp.concatenate(lines, axis=0)
     dense_ref[...] = dense
     turned = jnp.concatenate(lines[experts // 2 :] + lines[: experts // 2] + [jnp.zeros_like(dense)], axis=0)
-    joint_ref[0:count, :width] = x_ref[...]
-    joint_ref[count:, :width] = dy_ref[...]
-    joint_ref[:, width:] = jnp.zeros((2 * count, LANES), BF16)
-    joint_ref[0:16, width : width + count] = turned.astype(BF16)
-
-
-def join_kernel(in_ref, out_ref, joint_ref):
-    width = in_ref.shape[1]
-    joint_ref[:, :width] = in_ref[...]
-    joint_ref[:, width:] = out_ref[...]
+    joint_ref[:, :width] = x_ref[...]
+    joint_ref[:, width : 2 * width] = dy_ref[...]
+    joint_ref[:, 2 * width :] = jnp.zeros((count, LANES), BF16)
+    joint_ref[0:16, 2 * width : 2 * width + count] = turned.astype(BF16)
 
 
 def stack_kernel(own_ref, far_ref, after_ref, stacked_ref):
@@ -81,7 +75,8 @@
     pass
 
 
-def relay_kernel(near_a, far_a, near_b, far_b, mid_ref, after_ref, joint_ref):
+def relay_kernel(near_a, far_a, near_b, far_b, mid_ref, *refs):
+    joint_ref = refs[-1]
     count, width = near_a.shape
     for at, near, far in ((0, near_a, far_a), (count, near_b, far_b)):
         joint_ref[at : at + count, :width] = near[...]
@@ -89,36 +84,41 @@
     joint_ref[:, 2 * width :] = mid_ref[...]
 
 
-def pack_kernel(first, joint_ref, *refs):
-    count = 4
-    fold = refs[-1]
-    out_refs = refs[-1 - count : -1]
-    tokens, width = joint_ref.shape[0] // 2, joint_ref.shape[1] - LANES
+def pack_blocks(experts, joint_ref, out_refs, fold):
+    count = len(experts)
+    tokens, width = joint_ref.shape[0], out_refs[0].shape[1] - LANES
     chunks = width // LANES
     main = out_refs[0].shape[0] // 2
-    weight = joint_ref[0:16, width:].astype(F32)[0:8, :tokens]
+    weight = joint_ref[0:16, 2 * width :].astype(F32)[0:8, :tokens]
     mains, tails = picks(weight, main)
-    mains = mains[first : first + count]
-    pick = jnp.concatenate(mains + [tails, jnp.zeros_like(tails)], axis=0).astype(BF16)
+    pick = jnp.concatenate([mains[e] for e in experts] + [tails, jnp.zeros_like(tails)], axis=0).astype(BF16)
     lane = lax.broadcasted_iota(jnp.int32, (main, LANES), 1)
-    for at, base, low in ((0, 0, 0), (tokens, main, chunks)):
-        rows = dot(pick, joint_ref[at : at + tokens, :width])
-        for j in range(count):
+    for at, base, low in ((0, 0, 0), (width, main, chunks)):
+        rows = dot(pick, joint_ref[:, at : at + width])
+        for j, e in enumerate(experts):
             out_refs[j][base : base + main, :width] = rows[main * j : main * (j + 1)].astype(BF16)
-            line = main * count + first + j
+            line = main * count + e
             for c in range(chunks):
                 fold[c : c + 1, :] = rows[line : line + 1, LANES * c : LANES * (c + 1)]
             out_refs[j][low : low + chunks, width:] = fold[...].astype(BF16)
-    for j in range(count):
-        mine = weight[first + j : first + j + 1, :]
-        column = jnp.sum(mains[j] * mine, axis=1, keepdims=True)
-        last = jnp.sum(tails[first + j : first + j + 1, :] * mine, axis=1, keepdims=True)
+    for j, e in enumerate(experts):
+        mine = weight[e : e + 1, :]
+        column = jnp.sum(mains[e] * mine, axis=1, keepdims=True)
+        last = jnp.sum(tails[e : e + 1, :] * mine, axis=1, keepdims=True)
         out_refs[j][main:, width:] = jnp.where(lane < LANES // 2, column, last).astype(BF16)
 
 
-def slice_kernel(place_ref, *refs):
+def pack_kernel(experts, joint_ref, *refs):
+    pack_blocks(experts, joint_ref, refs[-1 - len(experts) : -1], refs[-1])
+
+
+def slice_kernel(own, place_ref, *refs):
     blocks, parts = 4, 4
-    in_refs, (keep_ref, near_ref, far_ref, weight_ref, fold) = refs[:blocks], refs[-5:]
+    keep_ref, near_ref, far_ref, weight_ref, fold, kept = refs[-6:]
+    in_refs = list(refs[:blocks])
+    if own:
+        in_refs[0] = kept
+        pack_blocks([own], refs[0], [kept], fold.at[0, pl.ds(0, 16)])
     main = in_refs[0].shape[0] // 2
     depth = keep_ref.shape[1] // 2
     width = parts * depth
@@ -229,13 +229,15 @@
 
 
 def relay_sum_kernel(joint_ref, b0, b1, b2, b3, out_ref, rows, fold):
-    tokens, width = out_ref.shape[0], rows.shape[1]
-    weight = joint_ref[0:16, width:].astype(F32)[0:8, :tokens]
+    tokens, width = joint_ref.shape[0], rows.shape[1]
+    weight = joint_ref[0:16, 2 * width :].astype(F32)[0:8, :tokens]
     summed, routes = unpack_sum(weight, (b0, b1, b2, b3), rows, fold)
-    out_ref[:, :width] = summed.astype(BF16)
-    out_ref[:, width:] = jnp.zeros((tokens, LANES), BF16)
+    lines = tokens // 2
+    out_ref[:, :width] = summed[0:lines].astype(BF16)
+    out_ref[:, width : 2 * width] = summed[lines:].astype(BF16)
+    out_ref[:, 2 * width :] = jnp.zeros((lines, LANES), BF16)
     block = jnp.concatenate(routes + [jnp.zeros((12, tokens), F32)], axis=0).astype(BF16)
-    out_ref[0:16, width : width + tokens] = block
+    out_ref[0:16, 2 * width : 2 * width + tokens] = block
 
 
 def near_sum_kernel(w_ref, b0, b1, b2, b3, after_ref, grad_ref, route_ref, rows, fold):
@@ -246,8 +248,11 @@
 
 def combine_kernel(peer_ref, named_ref, near_ref, near_route_ref, far_ref, grad_ref, route_ref):
     tokens, width = grad_ref.shape
-    grad_ref[...] = (near_ref[...] + far_ref[:, :width].astype(F32)).astype(BF16)
-    others = far_ref[0:16, width : width + tokens].astype(F32)
+    lines = tokens // 2
+    for half in range(2):
+        at, columns = slice(half * lines, (half + 1) * lines), slice(half * width, (half + 1) * width)
+        grad_ref[at, :] = (near_ref[at, :] + far_ref[:, columns].astype(F32)).astype(BF16)
+    others = far_ref[0:16, 2 * width : 2 * width + tokens].astype(F32)
     named = named_ref[...]
     route = jnp.zeros(route_ref.shape, F32)
     for j in range(4):
@@ -273,20 +278,27 @@
     out_ref[...] = dot_tn(rows[:, depth:], mids[:, 2 * hidden_width :])
 
 
-def second_weight_kernel(rows_a, rows_b, near_ref, mid_a, mid_b, in_part, out_part, *refs):
-    in_ref, out_ref, rows, mids, in_held, out_held, sems = refs
+def second_weight_kernel(rows_a, rows_b, mid_ref, in_part, out_part, in_ref, out_ref, rows):
+    depth, hidden_width = out_ref.shape
+    count = rows_a.shape[0]
+    rows[0:count, :] = rows_a[:, : 2 * depth]
+    rows[count:, :] = rows_b[:, : 2 * depth]
+    in_ref[...] = in_part[...] + dot_tn(rows[:, :depth], mid_ref[:, : 2 * hidden_width])
+    out_ref[...] = out_part[...] + dot_tn(rows[:, depth:], mid_ref[:, 2 * hidden_width :])
+
+
+def last_weight_kernel(near_ref, mid_ref, in_part, out_part, in_ref, out_ref, in_held, out_held, sems):
     depth, hidden_width = out_part.shape
-    span = slice(0, 2 * depth)
-    fill(rows, mids, rows_a[:, span], rows_b[:, span], near_ref[:, 2 * depth : 4 * depth], mid_a[...], mid_b[...])
     copies = []
     step = depth // 4
     for m in range(4):
         at = slice(m * step, (m + 1) * step)
         lines = pl.ds(m * step, step)
-        in_held[at, :] = in_part[at, :] + dot_tn(rows[:, at], mids[:, : 2 * hidden_width])
+        base = 2 * depth + m * step
+        in_held[at, :] = in_part[at, :] + dot_tn(near_ref[:, base : base + step], mid_ref[:, : 2 * hidden_width])
         copies.append(start(in_held.at[lines], in_ref.at[lines], sems.at[0, m]))
-        other = slice(depth + m * step, depth + (m + 1) * step)
-        out_held[at, :] = out_part[at, :] + dot_tn(rows[:, other], mids[:, 2 * hidden_width :])
+        base += depth
+        out_held[at, :] = out_part[at, :] + dot_tn(near_ref[:, base : base + step], mid_ref[:, 2 * hidden_width :])
         copies.append(start(out_held.at[lines], out_ref.at[lines], sems.at[1, m]))
     for copy in copies:
         copy.wait()
@@ -331,7 +343,7 @@
 
     joint, dense = call(
         route_kernel,
-        [((2 * token_count, width + LANES), BF16), ((blocks, token_count), F32)],
+        [((token_count, 2 * width + LANES), BF16), ((blocks, token_count), F32)],
         [peers],
         [named, route_weight.T, tokens, grad_out],
         [],
@@ -340,32 +352,23 @@
     )
     far_joint = swap(joint, "expert", half)
 
-    (weights,) = call(
-        join_kernel,
-        [((depth, 3 * hidden_width), BF16)],
-        [],
-        [gate_up_weight[0], down_weight[0]],
-        [],
-        [],
-        0,
-    )
+    weights = jnp.concatenate([gate_up_weight[0], down_weight[0]], axis=1)
     far_weights = swap(weights, "dp", 2)
 
-    def pack(first, value, after):
-        packed = call(
-            functools.partial(pack_kernel, first),
-            [packed_shape] * half,
+    def pack(experts, value, after):
+        return call(
+            functools.partial(pack_kernel, experts),
+            [packed_shape] * len(experts),
             [],
             [value],
             after,
             [pltpu.VMEM((chunks, LANES), F32)],
-            4 * (half * main + 16) * token_count * width,
+            4 * (len(experts) * main + 16) * token_count * width,
         )
-        return [packed[0]] + [swap(packed[j], "expert", j) for j in range(1, half)]
-
-    def sliced(packed, after):
+
+    def sliced(own, packed, after):
         return call(
-            slice_kernel,
+            functools.partial(slice_kernel, own),
             [
                 ((rows, 2 * depth), BF16),
                 ((rows, 2 * depth), BF16),
@@ -375,14 +378,15 @@
             [places],
             packed,
             after,
-            [pltpu.VMEM((2, half * chunks, LANES), F32)],
+            [pltpu.VMEM((2, half * chunks, LANES), F32), pltpu.VMEM(*packed_shape)],
             0,
         )
 
-    own = pack(half, joint, [])
-    *own_slices, own_weight = sliced(own, [far_joint])
+    own = [swap(value, "expert", j + 1) for j, value in enumerate(pack(range(half + 1, blocks), joint, []))]
+    *own_slices, own_weight = sliced(half, [joint, *own], [far_joint])
     own_far = swap(own_slices[2], "dp", 2)
-    far = pack(0, far_joint, [own_slices[0], far_weights])
+    far = pack(range(half), far_joint, [own_slices[0], far_weights])
+    far = [far[0]] + [swap(far[j], "expert", j) for j in range(1, half)]
     (stacked,) = call(
         stack_kernel,
         [((2 * depth, 3 * hidden_width), BF16)],
@@ -394,23 +398,23 @@
     )
     weight_parts = [stacked, swap(stacked, "dp", 1)]
 
-    def middle(slices, weight, before):
+    def middle(slices, weight, before, after):
         early = before[0].shape[0] if before else 0
         return call(
             functools.partial(main_kernel, early),
             [((early + rows, 3 * hidden_width), BF16)] + [back_shape] * half,
             [places],
             [weight, *weight_parts, *slices, *before],
-            [],
+            after,
             [pltpu.VMEM((16, width), F32), pltpu.VMEM((chunks, LANES), F32)],
             2 * rows * width * 5 * hidden_width,
         )
 
-    own_mid, *near_back = middle(own_slices, own_weight, [])
-    near_back[1] = swap(near_back[1], "expert", 1)
-    *far_slices, far_weight = sliced(far, [own_mid, near_back[1]])
+    own_mid, *near_back = middle(own_slices, own_weight, [], [])
+    near_back = near_back[:1] + [swap(near_back[j], "expert", j) for j in range(1, half)]
+    *far_slices, far_weight = sliced(None, far, [own_mid, own_far])
     far_far = swap(far_slices[2], "dp", 2)
-    mid, *far_back = middle(far_slices, far_weight, [own_mid])
+    mid, *far_back = middle(far_slices, far_weight, [own_mid], [])
 
     sum_scratch = [
         pltpu.VMEM((half * main + 16, width), BF16),
@@ -420,7 +424,7 @@
     far_back = far_back[:1] + [swap(far_back[j], "expert", j) for j in range(1, half)]
     (partial,) = call(
         relay_sum_kernel,
-        [((token_count, width + LANES), BF16)],
+        [((token_count // 2, 2 * width + LANES), BF16)],
         [],
         [far_joint, *far_back],
         [],
@@ -435,12 +439,11 @@
         [((2 * rows, 4 * depth + 3 * hidden_width), BF16)],
         [],
         [own_slices[1], own_far, far_slices[1], far_far, mid],
-        [partial],
+        [partial, near_back[1]],
         [],
         0,
     )
     near = swap(near, "dp", 1)
-    near_back = near_back[:2] + [swap(near_back[j], "expert", j) for j in range(2, half)]
     weight_shapes = [((depth, 2 * hidden_width), F32), ((depth, hidden_width), F32)]
     weight_scratch = [pltpu.VMEM((4 * rows, 2 * depth), BF16), pltpu.VMEM((4 * rows, 3 * hidden_width), BF16)]
     weight_flops = 2 * 4 * rows * depth * 3 * hidden_width
@@ -483,19 +486,27 @@
         1,
         {0: 0},
     )
-    grad_gate_up, grad_down = call(
+    second = call(
         second_weight_kernel,
         weight_shapes,
         [],
-        [own_far, far_far, near, mid_far, swap(mid_far, "dp", 1), *first],
-        [],
-        weight_scratch
-        + [
+        [own_far, far_far, mid_far, *first],
+        [],
+        [pltpu.VMEM((2 * rows, 2 * depth), BF16)],
+        weight_flops // 2,
+    )
+    grad_gate_up, grad_down = call(
+        last_weight_kernel,
+        weight_shapes,
+        [],
+        [near, swap(mid_far, "dp", 1), *second],
+        [],
+        [
             pltpu.VMEM((depth, 2 * hidden_width), F32),
             pltpu.VMEM((depth, hidden_width), F32),
             pltpu.SemaphoreType.DMA((2, 4)),
         ],
-        weight_flops,
+        weight_flops // 2,
         2,
     )
     return (grad_tokens, grad_route.T, grad_gate_up[None], grad_down[None])

time: 99.2 us -> 92.5 us (0.932)
  waiting for transfers between devices: 54.5 us -> 49.2 us
  local copies, waits for them, and re-layouts: 3.81 us -> 0.02 us
  other arithmetic: 0.01 us -> 1.41 us
    ppermute x21, waiting for transfers between devices: 54.5 us -> 49.2 us  [swap(): lax.ppermute(value, axis, [(i, i ^ mask) for i in range(lax.axis_size(axi...]
    unnamed x16 -> x8, local copies, waits for them, and re-layouts: 3.81 us -> 0.02 us
    concatenate x0 -> x1, other arithmetic: none -> 1.4 us  [on_device_packed(): weights = jnp.concatenate([gate_up_weight[0], down_weight[0]], axis=1)]
  transfers between devices with their start and end apart: 21 -> 21, of which waited for: 17 -> 14; matrix products, arithmetic and copies ran while one was open for 0% -> 0% of each run, Pallas kernels for 13% -> 14%
where the time goes in v7:
time: 92.5 us; the launch traced here: 92.3 us
  waiting for transfers between devices  49.2 us (53%)
  starting transfers between devices  24.5 us (26%)
  Pallas kernels  16.4 us (18%)
  other arithmetic  1.41 us (2%)
    ppermute x21, waiting for transfers between devices, swap(): lax.ppermute(value, axis, [(i, i ^ mask) for i in range(lax.axis_size(axi...  49.2 us
    ppermute x21, starting transfers between devices, swap(): lax.ppermute(value, axis, [(i, i ^ mask) for i in range(lax.axis_size(axi...  24.5 us
    pallas_call x16, Pallas kernels, call(): pl.pallas_call(kernel, out_shape=tuple(outs), in_specs=[on_smem] * len(sm...  16.4 us
  transfers between devices with their start and end apart: 21, of which 14 were waited for; matrix products, arithmetic and copies ran while one was open for 0% of the time, Pallas kernels for 14%

profile of v7, /device:TPU:1, one launch (start us, length us, event | category | flops | bytes accessed | tf_op | source)
XLA Modules:
  0.0 92.3 jit_solution(7734482675728786038)
XLA Ops:
  0.6 0.0 copy-start.3
  0.6 0.0 copy-start.2
  0.7 0.0 copy-start.1
  0.7 0.0 copy-start
  0.7 1.4 %pad_maximum_fusion.own_ref = bf16[512,1152]{1,0:T(8,128)(2,1)S(1)} fusion(bf16[512,384]{1,0:T(8,128)(2,1)} %bitcast.11, bf16[512,768]{1,0:T(8,128)(2,1)} %bitcast.10), kind=kLoop, calls=%fused_computation | loop fusion | flops 2359296 | bytes 2359296 | tf_op jit(solution)/shard_map/concatenate | solution.py:355
  2.1 2.1 %collective-permute-start.4 = (bf16[512,1152]{1,0:T(8,128)(2,1)S(1)}, bf16[512,1152]{1,0:T(8,128)(2,1)S(1)}, u32[]{:S(2)}, u32[]{:S(2)}) collective-permute-start(bf16[512,1152]{1,0:T(8,128)(2,1)S(1)} %pad_maximum_fusion.own_ref), channel_id=1, source_target_pairs={{0,2},{1,3},{2,0},{3,1},{4,6},{5,7},{6,4},{7,5},{8,10},{9,11},{10,... | collective-permute-start | bytes 3538952 | tf_op jit(solution)/shard_map/ppermute | solution.py:326
  4.2 0.0 copy-done.3
  4.2 0.0 copy-done.2
  4.2 0.6 shard_map.93
  4.8 2.4 %collective-permute-start.3 = (bf16[64,4224]{1,0:T(8,128)(2,1)S(1)}, bf16[64,4224]{1,0:T(8,128)(2,1)S(1)}, u32[]{:S(2)}, u32[]{:S(2)}) collective-permute-start(bf16[64,4224]{1,0:T(8,128)(2,1)S(1)} %get-tuple-element.42.joint_ref.refs_0_), channel_id=1, source_target_pairs={{0,16},{4,20},{8,24},{12,28},{16,0},{20,4},{24,8},{28,12},{1,17},{... | collective-permute-start | bytes 1622024 | tf_op jit(solution)/shard_map/ppermute | solution.py:326
  7.2 1.4 %shard_map.94 = (bf16[64,2176]{1,0:T(8,128)(2,1)}, bf16[64,2176]{1,0:T(8,128)(2,1)}, bf16[64,2176]{1,0:T(8,128)(2,1)}) custom-call(bf16[64,4224]{1,0:T(8,128)(2,1)S(1)} %get-tuple-element.42.joint_ref.refs_0_), custom_call_target="tpu_custom_call" | custom-call | flops 58720256 | bytes 1376256 | tf_op jit(solution)/shard_map/pallas_call | solution.py:313
  8.6 1.2 %collective-permute-start = (bf16[64,2176]{1,0:T(8,128)(2,1)}, bf16[64,2176]{1,0:T(8,128)(2,1)}, u32[]{:S(2)}, u32[]{:S(2)}) collective-permute-start(bf16[64,2176]{1,0:T(8,128)(2,1)} %get-tuple-element.43), channel_id=1, source_target_pairs={{0,4},{4,0},{8,12},{12,8},{16,20},{20,16},{24,28},{28,24},{1,5},{5... | collective-permute-start | bytes 835592 | tf_op jit(solution)/shard_map/ppermute | solution.py:326
  9.8 1.3 %collective-permute-start.1 = (bf16[64,2176]{1,0:T(8,128)(2,1)}, bf16[64,2176]{1,0:T(8,128)(2,1)}, u32[]{:S(2)}, u32[]{:S(2)}) collective-permute-start(bf16[64,2176]{1,0:T(8,128)(2,1)} %get-tuple-element.44), channel_id=1, source_target_pairs={{0,8},{4,12},{8,0},{12,4},{16,24},{20,28},{24,16},{28,20},{1,9},{5... | collective-permute-start | bytes 835592 | tf_op jit(solution)/shard_map/ppermute | solution.py:326
  11.1 0.1 collective-permute-start.2
  11.2 4.6 %collective-permute-done.refs_1_ = bf16[64,2176]{1,0:T(8,128)(2,1)} collective-permute-done((bf16[64,2176]{1,0:T(8,128)(2,1)}, bf16[64,2176]{1,0:T(8,128)(2,1)}, u32[]{:S(2)}, u32[]{:S(2)}) %collective-permute-start) | collective-permute-done | bytes 278560 | tf_op jit(solution)/shard_map/ppermute | solution.py:326
  15.8 8.1 %collective-permute-done.1.refs_2_ = bf16[64,2176]{1,0:T(8,128)(2,1)} collective-permute-done((bf16[64,2176]{1,0:T(8,128)(2,1)}, bf16[64,2176]{1,0:T(8,128)(2,1)}, u32[]{:S(2)}, u32[]{:S(2)}) %collective-permute-start.1) | collective-permute-done | bytes 278560 | tf_op jit(solution)/shard_map/ppermute | solution.py:326
  23.9 9.2 %collective-permute-done.2.refs_3_ = bf16[64,2176]{1,0:T(8,128)(2,1)} collective-permute-done((bf16[64,2176]{1,0:T(8,128)(2,1)}, bf16[64,2176]{1,0:T(8,128)(2,1)}, u32[]{:S(2)}, u32[]{:S(2)}) %collective-permute-start.2) | collective-permute-done | bytes 278560 | tf_op jit(solution)/shard_map/ppermute | solution.py:326
  33.2 0.0 collective-permute-done.3.refs_4_.joint_ref
  33.2 1.6 %shard_map.95 = (bf16[144,1024]{1,0:T(8,128)(2,1)S(1)}, bf16[144,1024]{1,0:T(8,128)(2,1)S(1)}, bf16[144,2048]{1,0:T(8,128)(2,1)S(1)}, f32[144,128]{1,0:T(8,128)S(1)}) custom-call(s32[4]{0:T(128)S(1)} %iota_xor_fusion.place_ref, bf16[64,4224]{1,0:T(8,128)(2,1)S(1)} %get-tuple-element.42.joint_ref.refs_0_, bf16[64,2176]{1,0:T(8,128)(2,1)} %collective-permute-done.refs_1_, ...), custom_call_target="tpu_custom_call" | custom-call | bytes 2629632 | tf_op jit(solution)/shard_map/pallas_call | solution.py:313
  34.8 0.0 collective-permute-done.4.refs_1_.far_ref
  34.8 0.6 shard_map.96
  35.4 0.2 shard_map.97.refs_0_
  35.6 2.5 %collective-permute-start.5 = (bf16[1024,1152]{1,0:T(8,128)(2,1)S(1)}, bf16[1024,1152]{1,0:T(8,128)(2,1)S(1)}, u32[]{:S(2)}, u32[]{:S(2)}) collective-permute-start(bf16[1024,1152]{1,0:T(8,128)(2,1)S(1)} %shard_map.97.refs_0_), channel_id=1, source_target_pairs={{0,1},{1,0},{2,3},{3,2},{4,5},{5,4},{6,7},{7,6},{8,9},{9,8},{10,11... | collective-permute-start | bytes 7077896 | tf_op jit(solution)/shard_map/ppermute | solution.py:326
  38.1 0.3 collective-permute-start.12
  38.3 1.2 %collective-permute-start.9 = (bf16[64,2176]{1,0:T(8,128)(2,1)S(1)}, bf16[64,2176]{1,0:T(8,128)(2,1)S(1)}, u32[]{:S(2)}, u32[]{:S(2)}) collective-permute-start(bf16[64,2176]{1,0:T(8,128)(2,1)S(1)} %get-tuple-element.55), channel_id=1, source_target_pairs={{0,4},{4,0},{8,12},{12,8},{16,20},{20,16},{24,28},{28,24},{1,5},{5... | collective-permute-start | bytes 835592 | tf_op jit(solution)/shard_map/ppermute | solution.py:326
  39.5 0.0 collective-permute-start.10
  39.5 1.5 %collective-permute-start.11 = (bf16[64,2176]{1,0:T(8,128)(2,1)S(1)}, bf16[64,2176]{1,0:T(8,128)(2,1)S(1)}, u32[]{:S(2)}, u32[]{:S(2)}) collective-permute-start(bf16[64,2176]{1,0:T(8,128)(2,1)S(1)} %get-tuple-element.57), channel_id=1, source_target_pairs={{0,12},{4,8},{8,4},{12,0},{16,28},{20,24},{24,20},{28,16},{1,13},{... | collective-permute-start | bytes 835592 | tf_op jit(solution)/shard_map/ppermute | solution.py:326
  41.0 1.2 %collective-permute-done.5.refs_1_ = bf16[1024,1152]{1,0:T(8,128)(2,1)S(1)} collective-permute-done((bf16[1024,1152]{1,0:T(8,128)(2,1)S(1)}, bf16[1024,1152]{1,0:T(8,128)(2,1)S(1)}, u32[]{:S(2)}, u32[]{:S(2)}) %collective-permute-start.5) | collective-permute-done | bytes 2359328 | tf_op jit(solution)/shard_map/ppermute | solution.py:326
  42.2 2.6 %shard_map.98 = (bf16[144,1152]{1,0:T(8,128)(2,1)S(1)}, bf16[32,2176]{1,0:T(8,128)(2,1)S(1)}, bf16[32,2176]{1,0:T(8,128)(2,1)S(1)}, bf16[32,2176]{1,0:T(8,128)(2,1)S(1)}, bf16[32,2176]{1,0:T(8,128)(2,1)S(1)}) custom-call(s32[4]{0:T(128)S(1)} %iota_xor_fusion.place_ref, f32[144,128]{1,0:T(8,128)S(1)} %get-tuple-element.46.w_ref, ...), custom_call_target="tpu_custom_call" | custom-call | flops 1132462080 | bytes 6860800 | tf_op jit(solution)/shard_map/pallas_call | solution.py:313
  44.9 8.1 %collective-permute-done.12.refs_5_.far_a.rows_a = bf16[144,2048]{1,0:T(8,128)(2,1)S(1)} collective-permute-done((bf16[144,2048]{1,0:T(8,128)(2,1)S(1)}, bf16[144,2048]{1,0:T(8,128)(2,1)S(1)}, u32[]{:S(2)}, u32[]{:S(2)}) %collective-permute-start.12) | collective-permute-done | bytes 589856 | tf_op jit(solution)/shard_map/ppermute | solution.py:326
  53.0 0.0 collective-permute-done.9.refs_1_
  53.0 0.0 collective-permute-done.10.refs_2_
  53.0 0.1 collective-permute-done.11.refs_3_
  53.1 0.7 shard_map.99
  53.7 1.3 %collective-permute-start.13 = (bf16[144,2048]{1,0:T(8,128)(2,1)S(1)}, bf16[144,2048]{1,0:T(8,128)(2,1)S(1)}, u32[]{:S(2)}, u32[]{:S(2)}) collective-permute-start(bf16[144,2048]{1,0:T(8,128)(2,1)S(1)} %get-tuple-element.61.refs_4_), channel_id=1, source_target_pairs={{0,2},{1,3},{2,0},{3,1},{4,6},{5,7},{6,4},{7,5},{8,10},{9,11},{10,... | collective-permute-start | bytes 1769480 | tf_op jit(solution)/shard_map/ppermute | solution.py:326
  55.0 2.6 %shard_map.100 = (bf16[288,1152]{1,0:T(8,128)(2,1)S(1)}, bf16[32,2176]{1,0:T(8,128)(2,1)S(1)}, bf16[32,2176]{1,0:T(8,128)(2,1)S(1)}, bf16[32,2176]{1,0:T(8,128)(2,1)S(1)}, bf16[32,2176]{1,0:T(8,128)(2,1)S(1)}) custom-call(s32[4]{0:T(128)S(1)} %iota_xor_fusion.place_ref, f32[144,128]{1,0:T(8,128)S(1)} %get-tuple-element.62.w_ref, ...), custom_call_target="tpu_custom_call" | custom-call | flops 1132462080 | bytes 7524352 | tf_op jit(solution)/shard_map/pallas_call | solution.py:313
  57.6 1.3 %collective-permute-start.14 = (bf16[32,2176]{1,0:T(8,128)(2,1)S(1)}, bf16[32,2176]{1,0:T(8,128)(2,1)S(1)}, u32[]{:S(2)}, u32[]{:S(2)}) collective-permute-start(bf16[32,2176]{1,0:T(8,128)(2,1)S(1)} %get-tuple-element.65), channel_id=1, source_target_pairs={{0,4},{4,0},{8,12},{12,8},{16,20},{20,16},{24,28},{28,24},{1,5},{5... | collective-permute-start | bytes 417800 | tf_op jit(solution)/shard_map/ppermute | solution.py:326
  58.9 0.3 collective-permute-start.15
  59.3 1.1 %collective-permute-start.16 = (bf16[32,2176]{1,0:T(8,128)(2,1)S(1)}, bf16[32,2176]{1,0:T(8,128)(2,1)S(1)}, u32[]{:S(2)}, u32[]{:S(2)}) collective-permute-start(bf16[32,2176]{1,0:T(8,128)(2,1)S(1)} %get-tuple-element.67), channel_id=1, source_target_pairs={{0,12},{4,8},{8,4},{12,0},{16,28},{20,24},{24,20},{28,16},{1,13},{... | collective-permute-start | bytes 417800 | tf_op jit(solution)/shard_map/ppermute | solution.py:326
  60.4 1.2 %collective-permute-start.6 = (bf16[32,2176]{1,0:T(8,128)(2,1)S(1)}, bf16[32,2176]{1,0:T(8,128)(2,1)S(1)}, u32[]{:S(2)}, u32[]{:S(2)}) collective-permute-start(bf16[32,2176]{1,0:T(8,128)(2,1)S(1)} %get-tuple-element.52), channel_id=1, source_target_pairs={{0,4},{4,0},{8,12},{12,8},{16,20},{20,16},{24,28},{28,24},{1,5},{5... | collective-permute-start | bytes 417800 | tf_op jit(solution)/shard_map/ppermute | solution.py:326
  61.6 0.3 collective-permute-done.14.b1
  61.9 1.2 %collective-permute-done.15.b2 = bf16[32,2176]{1,0:T(8,128)(2,1)S(1)} collective-permute-done((bf16[32,2176]{1,0:T(8,128)(2,1)S(1)}, bf16[32,2176]{1,0:T(8,128)(2,1)S(1)}, u32[]{:S(2)}, u32[]{:S(2)}) %collective-permute-start.15) | collective-permute-done | bytes 139296 | tf_op jit(solution)/shard_map/ppermute | solution.py:326
  63.1 1.6 %collective-permute-done.16.b3 = bf16[32,2176]{1,0:T(8,128)(2,1)S(1)} collective-permute-done((bf16[32,2176]{1,0:T(8,128)(2,1)S(1)}, bf16[32,2176]{1,0:T(8,128)(2,1)S(1)}, u32[]{:S(2)}, u32[]{:S(2)}) %collective-permute-start.16) | collective-permute-done | bytes 139296 | tf_op jit(solution)/shard_map/ppermute | solution.py:326
  64.8 0.4 shard_map.101.refs_0_
  65.2 3.7 %collective-permute-done.6.refs_1_.b1 = bf16[32,2176]{1,0:T(8,128)(2,1)S(1)} collective-permute-done((bf16[32,2176]{1,0:T(8,128)(2,1)S(1)}, bf16[32,2176]{1,0:T(8,128)(2,1)S(1)}, u32[]{:S(2)}, u32[]{:S(2)}) %collective-permute-start.6) | collective-permute-done | bytes 139296 | tf_op jit(solution)/shard_map/ppermute | solution.py:326
  68.9 0.0 collective-permute-done.13.far_b.rows_b
  68.9 0.1 shard_map.102
  69.1 1.6 %collective-permute-start.17 = (bf16[288,3200]{1,0:T(8,128)(2,1)S(1)}, bf16[288,3200]{1,0:T(8,128)(2,1)S(1)}, u32[]{:S(2)}, u32[]{:S(2)}) collective-permute-start(bf16[288,3200]{1,0:T(8,128)(2,1)S(1)} %shard_map.102), channel_id=1, source_target_pairs={{0,1},{1,0},{2,3},{3,2},{4,5},{5,4},{6,7},{7,6},{8,9},{9,8},{10,11... | collective-permute-start | bytes 5529608 | tf_op jit(solution)/shard_map/ppermute | solution.py:326
  70.7 0.3 collective-permute-start.19
  71.0 1.2 %collective-permute-start.18 = (bf16[32,4224]{1,0:T(8,128)(2,1)S(1)}, bf16[32,4224]{1,0:T(8,128)(2,1)S(1)}, u32[]{:S(2)}, u32[]{:S(2)}) collective-permute-start(bf16[32,4224]{1,0:T(8,128)(2,1)S(1)} %shard_map.101.refs_0_), channel_id=1, source_target_pairs={{0,16},{4,20},{8,24},{12,28},{16,0},{20,4},{24,8},{28,12},{1,17},{... | collective-permute-start | bytes 811016 | tf_op jit(solution)/shard_map/ppermute | solution.py:326
  72.2 1.2 %collective-permute-start.7 = (bf16[32,2176]{1,0:T(8,128)(2,1)S(1)}, bf16[32,2176]{1,0:T(8,128)(2,1)S(1)}, u32[]{:S(2)}, u32[]{:S(2)}) collective-permute-start(bf16[32,2176]{1,0:T(8,128)(2,1)S(1)} %get-tuple-element.53), channel_id=1, source_target_pairs={{0,8},{4,12},{8,0},{12,4},{16,24},{20,28},{24,16},{28,20},{1,9},{5... | collective-permute-start | bytes 417800 | tf_op jit(solution)/shard_map/ppermute | solution.py:326
  73.3 1.3 %collective-permute-start.8 = (bf16[32,2176]{1,0:T(8,128)(2,1)S(1)}, bf16[32,2176]{1,0:T(8,128)(2,1)S(1)}, u32[]{:S(2)}, u32[]{:S(2)}) collective-permute-start(bf16[32,2176]{1,0:T(8,128)(2,1)S(1)} %get-tuple-element.54), channel_id=1, source_target_pairs={{0,12},{4,8},{8,4},{12,0},{16,28},{20,24},{24,20},{28,16},{1,13},{... | collective-permute-start | bytes 417800 | tf_op jit(solution)/shard_map/ppermute | solution.py:326
  74.6 0.0 collective-permute-done.17.near_ref
  74.6 1.2 %shard_map.103 = (f32[512,768]{1,0:T(8,128)S(1)}, f32[512,384]{1,0:T(8,128)S(1)}) custom-call(bf16[144,1024]{1,0:T(8,128)(2,1)S(1)} %get-tuple-element.47.refs_0_.refs_2_.rows_a, bf16[144,1024]{1,0:T(8,128)(2,1)S(1)} %get-tuple-element.59.refs_2_.rows_b, bf16[288,3200]{1,0:T(8,128)(2,1)S(1)} %collective-permute-done.17.near_ref, ...), custom_call_target="tpu_custom_call" | custom-call | flops 679477248 | bytes 5455872 | tf_op jit(solution)/shard_map/pallas_call | solution.py:313
  75.8 4.9 %collective-permute-done.7.b2 = bf16[32,2176]{1,0:T(8,128)(2,1)S(1)} collective-permute-done((bf16[32,2176]{1,0:T(8,128)(2,1)S(1)}, bf16[32,2176]{1,0:T(8,128)(2,1)S(1)}, u32[]{:S(2)}, u32[]{:S(2)}) %collective-permute-start.7) | collective-permute-done | bytes 139296 | tf_op jit(solution)/shard_map/ppermute | solution.py:326
  80.7 3.0 %collective-permute-done.8.b3 = bf16[32,2176]{1,0:T(8,128)(2,1)S(1)} collective-permute-done((bf16[32,2176]{1,0:T(8,128)(2,1)S(1)}, bf16[32,2176]{1,0:T(8,128)(2,1)S(1)}, u32[]{:S(2)}, u32[]{:S(2)}) %collective-permute-start.8) | collective-permute-done | bytes 139296 | tf_op jit(solution)/shard_map/ppermute | solution.py:326
  83.7 0.4 shard_map.104
  84.1 2.0 %collective-permute-done.18.far_ref.refs_2_ = bf16[32,4224]{1,0:T(8,128)(2,1)S(1)} collective-permute-done((bf16[32,4224]{1,0:T(8,128)(2,1)S(1)}, bf16[32,4224]{1,0:T(8,128)(2,1)S(1)}, u32[]{:S(2)}, u32[]{:S(2)}) %collective-permute-start.18) | collective-permute-done | bytes 270368 | tf_op jit(solution)/shard_map/ppermute | solution.py:326
  86.1 1.1 %collective-permute-done.19.refs_0_ = bf16[288,1152]{1,0:T(8,128)(2,1)S(1)} collective-permute-done((bf16[288,1152]{1,0:T(8,128)(2,1)S(1)}, bf16[288,1152]{1,0:T(8,128)(2,1)S(1)}, u32[]{:S(2)}, u32[]{:S(2)}) %collective-permute-start.19) | collective-permute-done | bytes 663584 | tf_op jit(solution)/shard_map/ppermute | solution.py:326
  87.2 1.2 %collective-permute-start.20 = (bf16[288,1152]{1,0:T(8,128)(2,1)S(1)}, bf16[288,1152]{1,0:T(8,128)(2,1)S(1)}, u32[]{:S(2)}, u32[]{:S(2)}) collective-permute-start(bf16[288,1152]{1,0:T(8,128)(2,1)S(1)} %shard_map.106.mid_ref), channel_id=1, source_target_pairs={{0,1},{1,0},{2,3},{3,2},{4,5},{5,4},{6,7},{7,6},{8,9},{9,8},{10,11... | collective-permute-start | bytes 1990664 | tf_op jit(solution)/shard_map/ppermute | solution.py:326
  88.4 1.3 %shard_map.105 = (bf16[64,2048]{1,0:T(8,128)(2,1)}, bf16[4,64]{1,0:T(4,128)(2,1)}) custom-call(s32[8]{0:T(128)S(1)} %iota_xor_fusion.1.peer_ref, s32[4,64]{1,0:T(4,128)S(1)} %bitcast.8, f32[64,2048]{1,0:T(8,128)S(1)} %get-tuple-element.69.near_ref.refs_3_, f32[8,64]{1,0:T(8,128)S(1)} %get-tuple-element.70.near_route_ref, ...), custom_call_target="tpu_custom_call" | custom-call | bytes 1060352 | tf_op jit(solution)/shard_map/pallas_call | solution.py:313
  89.7 0.9 shard_map.107
  90.5 0.0 collective-permute-done.20.mid_ref
  90.6 1.8 %shard_map.108 = (f32[512,768]{1,0:T(8,128)}, f32[512,384]{1,0:T(8,128)}) custom-call(bf16[288,3200]{1,0:T(8,128)(2,1)S(1)} %collective-permute-done.17.near_ref, bf16[288,1152]{1,0:T(8,128)(2,1)S(1)} %collective-permute-done.20.mid_ref, f32[512,768]{1,0:T(8,128)S(1)} %get-tuple-element.74.in_part, f32[512,384]{1,0:T(8,128)S(1)} %get-tuple-element.75.out_part), custom_call_target="tpu_custom_call" | custom-call | flops 339738624 | bytes 4866048 | tf_op jit(solution)/shard_map/pallas_call | solution.py:313
  (5 shorter events, 0.0 us)
Async XLA Ops:
  0.6 3.6 %copy-start.3 = (bf16[64,4]{0,1:T(4,128)(2,1)S(1)}, bf16[64,4]{0,1:T(4,128)(2,1)}, u32[]{:S(2)}) copy-start(bf16[64,4]{0,1:T(4,128)(2,1)} %param.9) | copy-start | bytes 1540
  0.6 3.5 %copy-start.2 = (s32[64,4]{0,1:T(4,128)S(1)}, s32[64,4]{0,1:T(4,128)}, u32[]{:S(2)}) copy-start(s32[64,4]{0,1:T(4,128)} %param.8) | copy-start | bytes 3076
  0.7 3.5 %copy-start.1 = (bf16[64,2048]{1,0:T(8,128)(2,1)S(1)}, bf16[64,2048]{1,0:T(8,128)(2,1)}, u32[]{:S(2)}) copy-start(bf16[64,2048]{1,0:T(8,128)(2,1)} %dy_ref.1) | copy-start | bytes 786436
  0.7 3.5 %copy-start = (bf16[64,2048]{1,0:T(8,128)(2,1)S(1)}, bf16[64,2048]{1,0:T(8,128)(2,1)}, u32[]{:S(2)}) copy-start(bf16[64,2048]{1,0:T(8,128)(2,1)} %x_ref.1) | copy-start | bytes 786436
  2.1 32.7 %collective-permute-start.4 = (bf16[512,1152]{1,0:T(8,128)(2,1)S(1)}, bf16[512,1152]{1,0:T(8,128)(2,1)S(1)}, u32[]{:S(2)}, u32[]{:S(2)}) collective-permute-start(bf16[512,1152]{1,0:T(8,128)(2,1)S(1)} %pad_maximum_fusion.own_ref), channel_id=1, source_target_pairs={{0,2},{1,3},{2,0},{3,1},{4,6},{5,7},{6,4},{7,5},{8,10},{9,11},{10,... | collective-permute-start | bytes 3538952 | tf_op jit(solution)/shard_map/ppermute | solution.py:326
  4.8 28.4 %collective-permute-start.3 = (bf16[64,4224]{1,0:T(8,128)(2,1)S(1)}, bf16[64,4224]{1,0:T(8,128)(2,1)S(1)}, u32[]{:S(2)}, u32[]{:S(2)}) collective-permute-start(bf16[64,4224]{1,0:T(8,128)(2,1)S(1)} %get-tuple-element.42.joint_ref.refs_0_), channel_id=1, source_target_pairs={{0,16},{4,20},{8,24},{12,28},{16,0},{20,4},{24,8},{28,12},{1,17},{... | collective-permute-start | bytes 1622024 | tf_op jit(solution)/shard_map/ppermute | solution.py:326
  8.6 7.2 %collective-permute-start = (bf16[64,2176]{1,0:T(8,128)(2,1)}, bf16[64,2176]{1,0:T(8,128)(2,1)}, u32[]{:S(2)}, u32[]{:S(2)}) collective-permute-start(bf16[64,2176]{1,0:T(8,128)(2,1)} %get-tuple-element.43), channel_id=1, source_target_pairs={{0,4},{4,0},{8,12},{12,8},{16,20},{20,16},{24,28},{28,24},{1,5},{5... | collective-permute-start | bytes 835592 | tf_op jit(solution)/shard_map/ppermute | solution.py:326
  9.8 14.1 %collective-permute-start.1 = (bf16[64,2176]{1,0:T(8,128)(2,1)}, bf16[64,2176]{1,0:T(8,128)(2,1)}, u32[]{:S(2)}, u32[]{:S(2)}) collective-permute-start(bf16[64,2176]{1,0:T(8,128)(2,1)} %get-tuple-element.44), channel_id=1, source_target_pairs={{0,8},{4,12},{8,0},{12,4},{16,24},{20,28},{24,16},{28,20},{1,9},{5... | collective-permute-start | bytes 835592 | tf_op jit(solution)/shard_map/ppermute | solution.py:326
  11.1 22.0 %collective-permute-start.2 = (bf16[64,2176]{1,0:T(8,128)(2,1)}, bf16[64,2176]{1,0:T(8,128)(2,1)}, u32[]{:S(2)}, u32[]{:S(2)}) collective-permute-start(bf16[64,2176]{1,0:T(8,128)(2,1)} %get-tuple-element.45), channel_id=1, source_target_pairs={{0,12},{4,8},{8,4},{12,0},{16,28},{20,24},{24,20},{28,16},{1,13},{... | collective-permute-start | bytes 835592 | tf_op jit(solution)/shard_map/ppermute | solution.py:326
  35.6 6.7 %collective-permute-start.5 = (bf16[1024,1152]{1,0:T(8,128)(2,1)S(1)}, bf16[1024,1152]{1,0:T(8,128)(2,1)S(1)}, u32[]{:S(2)}, u32[]{:S(2)}) collective-permute-start(bf16[1024,1152]{1,0:T(8,128)(2,1)S(1)} %shard_map.97.refs_0_), channel_id=1, source_target_pairs={{0,1},{1,0},{2,3},{3,2},{4,5},{5,4},{6,7},{7,6},{8,9},{9,8},{10,11... | collective-permute-start | bytes 7077896 | tf_op jit(solution)/shard_map/ppermute | solution.py:326
  38.1 14.9 %collective-permute-start.12 = (bf16[144,2048]{1,0:T(8,128)(2,1)S(1)}, bf16[144,2048]{1,0:T(8,128)(2,1)S(1)}, u32[]{:S(2)}, u32[]{:S(2)}) collective-permute-start(bf16[144,2048]{1,0:T(8,128)(2,1)S(1)} %get-tuple-element.50.refs_4_), channel_id=1, source_target_pairs={{0,2},{1,3},{2,0},{3,1},{4,6},{5,7},{6,4},{7,5},{8,10},{9,11},{10,... | collective-permute-start | bytes 1769480 | tf_op jit(solution)/shard_map/ppermute | solution.py:326
  38.3 14.6 %collective-permute-start.9 = (bf16[64,2176]{1,0:T(8,128)(2,1)S(1)}, bf16[64,2176]{1,0:T(8,128)(2,1)S(1)}, u32[]{:S(2)}, u32[]{:S(2)}) collective-permute-start(bf16[64,2176]{1,0:T(8,128)(2,1)S(1)} %get-tuple-element.55), channel_id=1, source_target_pairs={{0,4},{4,0},{8,12},{12,8},{16,20},{20,16},{24,28},{28,24},{1,5},{5... | collective-permute-start | bytes 835592 | tf_op jit(solution)/shard_map/ppermute | solution.py:326
  39.5 13.4 %collective-permute-start.10 = (bf16[64,2176]{1,0:T(8,128)(2,1)S(1)}, bf16[64,2176]{1,0:T(8,128)(2,1)S(1)}, u32[]{:S(2)}, u32[]{:S(2)}) collective-permute-start(bf16[64,2176]{1,0:T(8,128)(2,1)S(1)} %get-tuple-element.56), channel_id=1, source_target_pairs={{0,8},{4,12},{8,0},{12,4},{16,24},{20,28},{24,16},{28,20},{1,9},{5... | collective-permute-start | bytes 835592 | tf_op jit(solution)/shard_map/ppermute | solution.py:326
  39.5 13.5 %collective-permute-start.11 = (bf16[64,2176]{1,0:T(8,128)(2,1)S(1)}, bf16[64,2176]{1,0:T(8,128)(2,1)S(1)}, u32[]{:S(2)}, u32[]{:S(2)}) collective-permute-start(bf16[64,2176]{1,0:T(8,128)(2,1)S(1)} %get-tuple-element.57), channel_id=1, source_target_pairs={{0,12},{4,8},{8,4},{12,0},{16,28},{20,24},{24,20},{28,16},{1,13},{... | collective-permute-start | bytes 835592 | tf_op jit(solution)/shard_map/ppermute | solution.py:326
  53.7 15.2 %collective-permute-start.13 = (bf16[144,2048]{1,0:T(8,128)(2,1)S(1)}, bf16[144,2048]{1,0:T(8,128)(2,1)S(1)}, u32[]{:S(2)}, u32[]{:S(2)}) collective-permute-start(bf16[144,2048]{1,0:T(8,128)(2,1)S(1)} %get-tuple-element.61.refs_4_), channel_id=1, source_target_pairs={{0,2},{1,3},{2,0},{3,1},{4,6},{5,7},{6,4},{7,5},{8,10},{9,11},{10,... | collective-permute-start | bytes 1769480 | tf_op jit(solution)/shard_map/ppermute | solution.py:326
  57.6 4.3 %collective-permute-start.14 = (bf16[32,2176]{1,0:T(8,128)(2,1)S(1)}, bf16[32,2176]{1,0:T(8,128)(2,1)S(1)}, u32[]{:S(2)}, u32[]{:S(2)}) collective-permute-start(bf16[32,2176]{1,0:T(8,128)(2,1)S(1)} %get-tuple-element.65), channel_id=1, source_target_pairs={{0,4},{4,0},{8,12},{12,8},{16,20},{20,16},{24,28},{28,24},{1,5},{5... | collective-permute-start | bytes 417800 | tf_op jit(solution)/shard_map/ppermute | solution.py:326
  58.9 4.2 %collective-permute-start.15 = (bf16[32,2176]{1,0:T(8,128)(2,1)S(1)}, bf16[32,2176]{1,0:T(8,128)(2,1)S(1)}, u32[]{:S(2)}, u32[]{:S(2)}) collective-permute-start(bf16[32,2176]{1,0:T(8,128)(2,1)S(1)} %get-tuple-element.66), channel_id=1, source_target_pairs={{0,8},{4,12},{8,0},{12,4},{16,24},{20,28},{24,16},{28,20},{1,9},{5... | collective-permute-start | bytes 417800 | tf_op jit(solution)/shard_map/ppermute | solution.py:326
  59.3 5.5 %collective-permute-start.16 = (bf16[32,2176]{1,0:T(8,128)(2,1)S(1)}, bf16[32,2176]{1,0:T(8,128)(2,1)S(1)}, u32[]{:S(2)}, u32[]{:S(2)}) collective-permute-start(bf16[32,2176]{1,0:T(8,128)(2,1)S(1)} %get-tuple-element.67), channel_id=1, source_target_pairs={{0,12},{4,8},{8,4},{12,0},{16,28},{20,24},{24,20},{28,16},{1,13},{... | collective-permute-start | bytes 417800 | tf_op jit(solution)/shard_map/ppermute | solution.py:326
  60.4 8.6 %collective-permute-start.6 = (bf16[32,2176]{1,0:T(8,128)(2,1)S(1)}, bf16[32,2176]{1,0:T(8,128)(2,1)S(1)}, u32[]{:S(2)}, u32[]{:S(2)}) collective-permute-start(bf16[32,2176]{1,0:T(8,128)(2,1)S(1)} %get-tuple-element.52), channel_id=1, source_target_pairs={{0,4},{4,0},{8,12},{12,8},{16,20},{20,16},{24,28},{28,24},{1,5},{5... | collective-permute-start | bytes 417800 | tf_op jit(solution)/shard_map/ppermute | solution.py:326
  69.1 5.5 %collective-permute-start.17 = (bf16[288,3200]{1,0:T(8,128)(2,1)S(1)}, bf16[288,3200]{1,0:T(8,128)(2,1)S(1)}, u32[]{:S(2)}, u32[]{:S(2)}) collective-permute-start(bf16[288,3200]{1,0:T(8,128)(2,1)S(1)} %shard_map.102), channel_id=1, source_target_pairs={{0,1},{1,0},{2,3},{3,2},{4,5},{5,4},{6,7},{7,6},{8,9},{9,8},{10,11... | collective-permute-start | bytes 5529608 | tf_op jit(solution)/shard_map/ppermute | solution.py:326
  70.7 16.5 %collective-permute-start.19 = (bf16[288,1152]{1,0:T(8,128)(2,1)S(1)}, bf16[288,1152]{1,0:T(8,128)(2,1)S(1)}, u32[]{:S(2)}, u32[]{:S(2)}) collective-permute-start(bf16[288,1152]{1,0:T(8,128)(2,1)S(1)} %get-tuple-element.63.mid_ref), channel_id=1, source_target_pairs={{0,2},{1,3},{2,0},{3,1},{4,6},{5,7},{6,4},{7,5},{8,10},{9,11},{10,... | collective-permute-start | bytes 1990664 | tf_op jit(solution)/shard_map/ppermute | solution.py:326
  71.0 15.1 %collective-permute-start.18 = (bf16[32,4224]{1,0:T(8,128)(2,1)S(1)}, bf16[32,4224]{1,0:T(8,128)(2,1)S(1)}, u32[]{:S(2)}, u32[]{:S(2)}) collective-permute-start(bf16[32,4224]{1,0:T(8,128)(2,1)S(1)} %shard_map.101.refs_0_), channel_id=1, source_target_pairs={{0,16},{4,20},{8,24},{12,28},{16,0},{20,4},{24,8},{28,12},{1,17},{... | collective-permute-start | bytes 811016 | tf_op jit(solution)/shard_map/ppermute | solution.py:326
  72.2 8.6 %collective-permute-start.7 = (bf16[32,2176]{1,0:T(8,128)(2,1)S(1)}, bf16[32,2176]{1,0:T(8,128)(2,1)S(1)}, u32[]{:S(2)}, u32[]{:S(2)}) collective-permute-start(bf16[32,2176]{1,0:T(8,128)(2,1)S(1)} %get-tuple-element.53), channel_id=1, source_target_pairs={{0,8},{4,12},{8,0},{12,4},{16,24},{20,28},{24,16},{28,20},{1,9},{5... | collective-permute-start | bytes 417800 | tf_op jit(solution)/shard_map/ppermute | solution.py:326
  73.3 10.4 %collective-permute-start.8 = (bf16[32,2176]{1,0:T(8,128)(2,1)S(1)}, bf16[32,2176]{1,0:T(8,128)(2,1)S(1)}, u32[]{:S(2)}, u32[]{:S(2)}) collective-permute-start(bf16[32,2176]{1,0:T(8,128)(2,1)S(1)} %get-tuple-element.54), channel_id=1, source_target_pairs={{0,12},{4,8},{8,4},{12,0},{16,28},{20,24},{24,20},{28,16},{1,13},{... | collective-permute-start | bytes 417800 | tf_op jit(solution)/shard_map/ppermute | solution.py:326
  87.2 3.4 %collective-permute-start.20 = (bf16[288,1152]{1,0:T(8,128)(2,1)S(1)}, bf16[288,1152]{1,0:T(8,128)(2,1)S(1)}, u32[]{:S(2)}, u32[]{:S(2)}) collective-permute-start(bf16[288,1152]{1,0:T(8,128)(2,1)S(1)} %shard_map.106.mid_ref), channel_id=1, source_target_pairs={{0,1},{1,0},{2,3},{3,2},{4,5},{5,4},{6,7},{7,6},{8,9},{9,8},{10,11... | collective-permute-start | bytes 1990664 | tf_op jit(solution)/shard_map/ppermute | solution.py:326

commit v8 on v7

--- a/solution.py
+++ b/solution.py
@@ -65,10 +65,22 @@
     joint_ref[0:16, 2 * width : 2 * width + count] = turned.astype(BF16)
 
 
-def stack_kernel(own_ref, far_ref, after_ref, stacked_ref):
-    count = own_ref.shape[0]
-    stacked_ref[0:count, :] = own_ref[...]
-    stacked_ref[count:, :] = far_ref[...]
+def join_kernel(in_ref, out_ref, after_ref, *pieces):
+    width = in_ref.shape[1]
+    at = 0
+    for piece in pieces:
+        to = at + piece.shape[0]
+        piece[:, :width] = in_ref[at:to, :]
+        piece[:, width:] = out_ref[at:to, :]
+        at = to
+
+
+def stack_kernel(*refs):
+    *pieces, after_ref, stacked_ref = refs
+    at = 0
+    for piece in pieces:
+        stacked_ref[at : at + piece.shape[0], :] = piece[...]
+        at += piece.shape[0]
 
 
 def after_kernel(*refs):
@@ -108,17 +120,20 @@
         out_refs[j][main:, width:] = jnp.where(lane < LANES // 2, column, last).astype(BF16)
 
 
+def pack_all_kernel(experts, spot_ref, joint_ref, out_ref, fold):
+    pack_blocks(experts, joint_ref, [out_ref.at[spot_ref[j]] for j in range(len(experts))], fold)
+
+
 def pack_kernel(experts, joint_ref, *refs):
     pack_blocks(experts, joint_ref, refs[-1 - len(experts) : -1], refs[-1])
 
 
 def slice_kernel(own, place_ref, *refs):
     blocks, parts = 4, 4
-    keep_ref, near_ref, far_ref, weight_ref, fold, kept = refs[-6:]
+    keep_ref, near_ref, far_ref, weight_ref, fold = refs[-5:]
     in_refs = list(refs[:blocks])
     if own:
-        in_refs[0] = kept
-        pack_blocks([own], refs[0], [kept], fold.at[0, pl.ds(0, 16)])
+        in_refs = [refs[1].at[refs[0][i]] for i in range(blocks)]
     main = in_refs[0].shape[0] // 2
     depth = keep_ref.shape[1] // 2
     width = parts * depth
@@ -352,8 +367,17 @@
     )
     far_joint = swap(joint, "expert", half)
 
-    weights = jnp.concatenate([gate_up_weight[0], down_weight[0]], axis=1)
-    far_weights = swap(weights, "dp", 2)
+    cuts = (0, 176, 352, depth)
+    weights = call(
+        join_kernel,
+        [((high - low, 3 * hidden_width), BF16) for low, high in zip(cuts, cuts[1:])],
+        [],
+        [gate_up_weight[0], down_weight[0]],
+        [dense],
+        [],
+        0,
+    )
+    far_weights = [swap(piece, "dp", 2) for piece in weights]
 
     def pack(experts, value, after):
         return call(
@@ -366,32 +390,49 @@
             4 * (len(experts) * main + 16) * token_count * width,
         )
 
-    def sliced(own, packed, after):
+    def sliced(spots, packed, after):
         return call(
-            functools.partial(slice_kernel, own),
+            functools.partial(slice_kernel, len(spots)),
             [
                 ((rows, 2 * depth), BF16),
                 ((rows, 2 * depth), BF16),
                 ((rows, 4 * depth), BF16),
                 ((rows, LANES), F32),
             ],
-            [places],
+            [places, *spots],
             packed,
             after,
-            [pltpu.VMEM((2, half * chunks, LANES), F32), pltpu.VMEM(*packed_shape)],
+            [pltpu.VMEM((2, half * chunks, LANES), F32)],
             0,
         )
 
-    own = [swap(value, "expert", j + 1) for j, value in enumerate(pack(range(half + 1, blocks), joint, []))]
-    *own_slices, own_weight = sliced(half, [joint, *own], [far_joint])
+    spots = peers[:half] % half
+    (packed,) = call(
+        functools.partial(pack_all_kernel, range(half, blocks)),
+        [((half, *packed_shape[0]), BF16)],
+        [spots],
+        [joint],
+        [],
+        [pltpu.VMEM((chunks, LANES), F32)],
+        4 * (half * main + 16) * token_count * width,
+    )
+    own = lax.all_to_all(
+        packed,
+        "expert",
+        split_axis=0,
+        concat_axis=0,
+        tiled=True,
+        axis_index_groups=[list(range(half)), list(range(half, blocks))],
+    )
+    *own_slices, own_weight = sliced([spots], [own], [far_joint])
     own_far = swap(own_slices[2], "dp", 2)
-    far = pack(range(half), far_joint, [own_slices[0], far_weights])
+    far = pack(range(half), far_joint, [own_slices[0], *far_weights])
     far = [far[0]] + [swap(far[j], "expert", j) for j in range(1, half)]
     (stacked,) = call(
         stack_kernel,
         [((2 * depth, 3 * hidden_width), BF16)],
         [],
-        [weights, far_weights],
+        [*weights, *far_weights],
         [far[0]],
         [],
         0,
@@ -412,7 +453,7 @@
 
     own_mid, *near_back = middle(own_slices, own_weight, [], [])
     near_back = near_back[:1] + [swap(near_back[j], "expert", j) for j in range(1, half)]
-    *far_slices, far_weight = sliced(None, far, [own_mid, own_far])
+    *far_slices, far_weight = sliced([], far, [own_mid, own_far])
     far_far = swap(far_slices[2], "dp", 2)
     mid, *far_back = middle(far_slices, far_weight, [own_mid], [])
 

time: 92.5 us -> 99.5 us (1.076)
  local copies, waits for them, and re-layouts: 0.02 us -> 3.27 us
  Pallas kernels: 16.4 us -> 18.5 us
  starting transfers between devices: 24.5 us -> 26.2 us
  other arithmetic: 1.41 us -> 0.02 us
  waiting for transfers between devices: 49.2 us -> 50.4 us
    all_to_all x0 -> x1, starting transfers between devices: none -> 4.35 us  [on_device_packed(): lax.all_to_all(packed, 'expert', split_axis=0, concat_axis=0, tiled=True,...]
    unnamed x8 -> x14, local copies, waits for them, and re-layouts: 0.02 us -> 3.27 us
    ppermute x21 -> x20, starting transfers between devices: 24.5 us -> 21.8 us  [swap(): lax.ppermute(value, axis, [(i, i ^ mask) for i in range(lax.axis_size(axi...]
    all_to_all x0 -> x1, waiting for transfers between devices: none -> 2.38 us  [on_device_packed(): lax.all_to_all(packed, 'expert', split_axis=0, concat_axis=0, tiled=True,...]
    pallas_call x16 -> x17, Pallas kernels: 16.4 us -> 18.5 us  [call(): pl.pallas_call(kernel, out_shape=tuple(outs), in_specs=[on_smem] * len(sm...]
    concatenate x1 -> x0, other arithmetic: 1.4 us -> none  [on_device_packed(): weights = jnp.concatenate([gate_up_weight[0], down_weight[0]], axis=1)]
    ppermute x21 -> x20, waiting for transfers between devices: 49.2 us -> 48 us  [swap(): lax.ppermute(value, axis, [(i, i ^ mask) for i in range(lax.axis_size(axi...]
  transfers between devices with their start and end apart: 21 -> 21, of which waited for: 14 -> 15; matrix products, arithmetic and copies ran while one was open for 0% -> 0% of each run, Pallas kernels for 14% -> 11%
where the time goes in v8:
time: 99.5 us; the launch traced here: 99.2 us
  waiting for transfers between devices  50.4 us (51%)
  starting transfers between devices  26.2 us (26%)
  Pallas kernels  18.5 us (19%)
  local copies, waits for them, and re-layouts  3.27 us (3%)
    ppermute x20, waiting for transfers between devices, swap(): lax.ppermute(value, axis, [(i, i ^ mask) for i in range(lax.axis_size(axi...  48 us
    ppermute x20, starting transfers between devices, swap(): lax.ppermute(value, axis, [(i, i ^ mask) for i in range(lax.axis_size(axi...  21.8 us
    pallas_call x17, Pallas kernels, call(): pl.pallas_call(kernel, out_shape=tuple(outs), in_specs=[on_smem] * len(sm...  18.5 us
    all_to_all x1, starting transfers between devices, on_device_packed(): lax.all_to_all(packed, 'expert', split_axis=0, concat_axis=0, tiled=True,...  4.35 us
    unnamed x14, local copies, waits for them, and re-layouts  3.27 us
    all_to_all x1, waiting for transfers between devices, on_device_packed(): lax.all_to_all(packed, 'expert', split_axis=0, concat_axis=0, tiled=True,...  2.38 us
  transfers between devices with their start and end apart: 21, of which 15 were waited for; matrix products, arithmetic and copies ran while one was open for 0% of the time, Pallas kernels for 11%

profile of v8, /device:TPU:1, one launch (start us, length us, event | category | flops | bytes accessed | tf_op | source)
XLA Modules:
  0.0 99.2 jit_solution(6442485147555713607)
XLA Ops:
  0.7 0.0 copy-start.2
  0.7 0.9 copy-done.2
  1.6 0.9 copy-done.3
  2.6 0.7 copy-done.4
  3.2 0.7 copy-done.6
  3.9 0.6 shard_map.93
  4.5 0.0 copy-start
  4.5 0.0 copy-start.1
  4.5 2.2 %shard_map.94 = bf16[4,64,2176]{2,1,0:T(8,128)(2,1)} custom-call(s32[4]{0:T(128)S(1)} %and_select_fusion.spot_ref.refs_0_, bf16[64,4224]{1,0:T(8,128)(2,1)S(1)} %get-tuple-element.42.joint_ref), custom_call_target="tpu_custom_call" | custom-call | flops 75497472 | bytes 1654784 | tf_op jit(solution)/shard_map/pallas_call | solution.py:328
  6.7 4.3 %all-to-all-start = ((bf16[4,64,2176]{2,1,0:T(8,128)(2,1)}), bf16[4,64,2176]{2,1,0:T(8,128)(2,1)S(1)}, u32[]{:S(2)}, u32[]{:S(2)}) async-start(bf16[4,64,2176]{2,1,0:T(8,128)(2,1)} %shard_map.94), calls=%async_computation | async-start | bytes 2228224 | tf_op jit(solution)/shard_map/all_to_all | solution.py:419
  11.1 2.4 %collective-permute-start = (bf16[64,4224]{1,0:T(8,128)(2,1)S(1)}, bf16[64,4224]{1,0:T(8,128)(2,1)S(1)}, u32[]{:S(2)}, u32[]{:S(2)}) collective-permute-start(bf16[64,4224]{1,0:T(8,128)(2,1)S(1)} %get-tuple-element.42.joint_ref), channel_id=1, source_target_pairs={{0,16},{4,20},{8,24},{12,28},{16,0},{20,4},{24,8},{28,12},{1,17},{... | collective-permute-start | bytes 1622024 | tf_op jit(solution)/shard_map/ppermute | solution.py:341
  13.5 1.1 %shard_map.96 = (bf16[176,1152]{1,0:T(8,128)(2,1)}, bf16[176,1152]{1,0:T(8,128)(2,1)}, bf16[160,1152]{1,0:T(8,128)(2,1)}) custom-call(bf16[512,768]{1,0:T(8,128)(2,1)S(1)} %bitcast.7, bf16[512,384]{1,0:T(8,128)(2,1)S(1)} %bitcast.8, f32[8,64]{1,0:T(8,128)S(1)} %get-tuple-element.41.after_ref.w_ref), custom_call_target="tpu_custom_call" | custom-call | bytes 2359296 | tf_op jit(solution)/shard_map/pallas_call | solution.py:328
  14.6 1.2 %collective-permute-start.1 = (bf16[176,1152]{1,0:T(8,128)(2,1)}, bf16[176,1152]{1,0:T(8,128)(2,1)S(1)}, u32[]{:S(2)}, u32[]{:S(2)}) collective-permute-start(bf16[176,1152]{1,0:T(8,128)(2,1)} %get-tuple-element.44.refs_0_), channel_id=1, source_target_pairs={{0,2},{1,3},{2,0},{3,1},{4,6},{5,7},{6,4},{7,5},{8,10},{9,11},{10,... | collective-permute-start | bytes 1216520 | tf_op jit(solution)/shard_map/ppermute | solution.py:341
  15.8 0.3 collective-permute-start.2
  16.0 1.2 %collective-permute-start.3 = (bf16[160,1152]{1,0:T(8,128)(2,1)}, bf16[160,1152]{1,0:T(8,128)(2,1)S(1)}, u32[]{:S(2)}, u32[]{:S(2)}) collective-permute-start(bf16[160,1152]{1,0:T(8,128)(2,1)} %get-tuple-element.46.refs_2_), channel_id=1, source_target_pairs={{0,2},{1,3},{2,0},{3,1},{4,6},{5,7},{6,4},{7,5},{8,10},{9,11},{10,... | collective-permute-start | bytes 1105928 | tf_op jit(solution)/shard_map/ppermute | solution.py:341
  17.2 17.0 %collective-permute-done.refs_2_.joint_ref = bf16[64,4224]{1,0:T(8,128)(2,1)S(1)} collective-permute-done((bf16[64,4224]{1,0:T(8,128)(2,1)S(1)}, bf16[64,4224]{1,0:T(8,128)(2,1)S(1)}, u32[]{:S(2)}, u32[]{:S(2)}) %collective-permute-start) | collective-permute-done | bytes 540704 | tf_op jit(solution)/shard_map/ppermute | solution.py:341
  34.3 2.4 %all-to-all-done.refs_1_ = bf16[4,64,2176]{2,1,0:T(8,128)(2,1)S(1)} async-done(((bf16[4,64,2176]{2,1,0:T(8,128)(2,1)}), bf16[4,64,2176]{2,1,0:T(8,128)(2,1)S(1)}, u32[]{:S(2)}, u32[]{:S(2)}) %all-to-all-start) | async-done | bytes 1114144 | tf_op jit(solution)/shard_map/all_to_all | solution.py:419
  36.6 0.7 shard_map.95
  37.3 3.8 %collective-permute-done.3.refs_3_.refs_5_ = bf16[160,1152]{1,0:T(8,128)(2,1)S(1)} collective-permute-done((bf16[160,1152]{1,0:T(8,128)(2,1)}, bf16[160,1152]{1,0:T(8,128)(2,1)S(1)}, u32[]{:S(2)}, u32[]{:S(2)}) %collective-permute-start.3) | collective-permute-done | bytes 368672 | tf_op jit(solution)/shard_map/ppermute | solution.py:341
  41.1 0.0 collective-permute-done.1.refs_1_.refs_3_
  41.1 0.0 collective-permute-done.2.refs_2_.refs_4_
  41.1 0.6 shard_map.97
  41.7 1.4 %shard_map.98.refs_0_ = bf16[1024,1152]{1,0:T(8,128)(2,1)S(1)} custom-call(bf16[176,1152]{1,0:T(8,128)(2,1)} %get-tuple-element.44.refs_0_, bf16[176,1152]{1,0:T(8,128)(2,1)} %get-tuple-element.45.refs_1_, bf16[160,1152]{1,0:T(8,128)(2,1)} %get-tuple-element.46.refs_2_, bf16[176,1152]{1,0:T(8,128)(2,1)S(1)} %collective-permute-done.1.refs_1_.refs_3_, ...), custom_call_target="tpu_custom_call" | custom-call | bytes 4718592 | tf_op jit(solution)/shard_map/pallas_call | solution.py:328
  43.1 2.1 %collective-permute-start.4 = (bf16[1024,1152]{1,0:T(8,128)(2,1)S(1)}, bf16[1024,1152]{1,0:T(8,128)(2,1)S(1)}, u32[]{:S(2)}, u32[]{:S(2)}) collective-permute-start(bf16[1024,1152]{1,0:T(8,128)(2,1)S(1)} %shard_map.98.refs_0_), channel_id=1, source_target_pairs={{0,1},{1,0},{2,3},{3,2},{4,5},{5,4},{6,7},{7,6},{8,9},{9,8},{10,11... | collective-permute-start | bytes 7077896 | tf_op jit(solution)/shard_map/ppermute | solution.py:341
  45.2 1.2 %collective-permute-start.11 = (bf16[144,2048]{1,0:T(8,128)(2,1)S(1)}, bf16[144,2048]{1,0:T(8,128)(2,1)S(1)}, u32[]{:S(2)}, u32[]{:S(2)}) collective-permute-start(bf16[144,2048]{1,0:T(8,128)(2,1)S(1)} %get-tuple-element.50.refs_4_), channel_id=1, source_target_pairs={{0,2},{1,3},{2,0},{3,1},{4,6},{5,7},{6,4},{7,5},{8,10},{9,11},{10,... | collective-permute-start | bytes 1769480 | tf_op jit(solution)/shard_map/ppermute | solution.py:341
  46.5 1.4 %collective-permute-start.8 = (bf16[64,2176]{1,0:T(8,128)(2,1)S(1)}, bf16[64,2176]{1,0:T(8,128)(2,1)S(1)}, u32[]{:S(2)}, u32[]{:S(2)}) collective-permute-start(bf16[64,2176]{1,0:T(8,128)(2,1)S(1)} %get-tuple-element.55), channel_id=1, source_target_pairs={{0,4},{4,0},{8,12},{12,8},{16,20},{20,16},{24,28},{28,24},{1,5},{5... | collective-permute-start | bytes 835592 | tf_op jit(solution)/shard_map/ppermute | solution.py:341
  47.9 1.2 %collective-permute-start.9 = (bf16[64,2176]{1,0:T(8,128)(2,1)S(1)}, bf16[64,2176]{1,0:T(8,128)(2,1)S(1)}, u32[]{:S(2)}, u32[]{:S(2)}) collective-permute-start(bf16[64,2176]{1,0:T(8,128)(2,1)S(1)} %get-tuple-element.56), channel_id=1, source_target_pairs={{0,8},{4,12},{8,0},{12,4},{16,24},{20,28},{24,16},{28,20},{1,9},{5... | collective-permute-start | bytes 835592 | tf_op jit(solution)/shard_map/ppermute | solution.py:341
  49.0 0.1 collective-permute-start.10
  49.1 0.3 collective-permute-done.4.refs_1_
  49.4 2.6 %shard_map.99 = (bf16[144,1152]{1,0:T(8,128)(2,1)S(1)}, bf16[32,2176]{1,0:T(8,128)(2,1)S(1)}, bf16[32,2176]{1,0:T(8,128)(2,1)S(1)}, bf16[32,2176]{1,0:T(8,128)(2,1)S(1)}, bf16[32,2176]{1,0:T(8,128)(2,1)S(1)}) custom-call(s32[4]{0:T(128)S(1)} %iota_xor_fusion.place_ref, f32[144,128]{1,0:T(8,128)S(1)} %get-tuple-element.43.w_ref, ...), custom_call_target="tpu_custom_call" | custom-call | flops 1132462080 | bytes 6860800 | tf_op jit(solution)/shard_map/pallas_call | solution.py:328
  52.0 2.3 %collective-permute-done.8.refs_1_ = bf16[64,2176]{1,0:T(8,128)(2,1)S(1)} collective-permute-done((bf16[64,2176]{1,0:T(8,128)(2,1)S(1)}, bf16[64,2176]{1,0:T(8,128)(2,1)S(1)}, u32[]{:S(2)}, u32[]{:S(2)}) %collective-permute-start.8) | collective-permute-done | bytes 278560 | tf_op jit(solution)/shard_map/ppermute | solution.py:341
  54.4 1.1 %collective-permute-done.9.refs_2_ = bf16[64,2176]{1,0:T(8,128)(2,1)S(1)} collective-permute-done((bf16[64,2176]{1,0:T(8,128)(2,1)S(1)}, bf16[64,2176]{1,0:T(8,128)(2,1)S(1)}, u32[]{:S(2)}, u32[]{:S(2)}) %collective-permute-start.9) | collective-permute-done | bytes 278560 | tf_op jit(solution)/shard_map/ppermute | solution.py:341
  55.4 5.8 %collective-permute-done.10.refs_3_ = bf16[64,2176]{1,0:T(8,128)(2,1)S(1)} collective-permute-done((bf16[64,2176]{1,0:T(8,128)(2,1)S(1)}, bf16[64,2176]{1,0:T(8,128)(2,1)S(1)}, u32[]{:S(2)}, u32[]{:S(2)}) %collective-permute-start.10) | collective-permute-done | bytes 278560 | tf_op jit(solution)/shard_map/ppermute | solution.py:341
  61.2 0.0 collective-permute-done.11.refs_5_.far_a.rows_a
  61.2 0.7 shard_map.100
  61.9 0.3 collective-permute-start.12
  62.2 2.6 %shard_map.101 = (bf16[288,1152]{1,0:T(8,128)(2,1)S(1)}, bf16[32,2176]{1,0:T(8,128)(2,1)S(1)}, bf16[32,2176]{1,0:T(8,128)(2,1)S(1)}, bf16[32,2176]{1,0:T(8,128)(2,1)S(1)}, bf16[32,2176]{1,0:T(8,128)(2,1)S(1)}) custom-call(s32[4]{0:T(128)S(1)} %iota_xor_fusion.place_ref, f32[144,128]{1,0:T(8,128)S(1)} %get-tuple-element.62.w_ref, ...), custom_call_target="tpu_custom_call" | custom-call | flops 1132462080 | bytes 7524352 | tf_op jit(solution)/shard_map/pallas_call | solution.py:328
  64.8 1.5 %collective-permute-start.13 = (bf16[32,2176]{1,0:T(8,128)(2,1)S(1)}, bf16[32,2176]{1,0:T(8,128)(2,1)S(1)}, u32[]{:S(2)}, u32[]{:S(2)}) collective-permute-start(bf16[32,2176]{1,0:T(8,128)(2,1)S(1)} %get-tuple-element.65), channel_id=1, source_target_pairs={{0,4},{4,0},{8,12},{12,8},{16,20},{20,16},{24,28},{28,24},{1,5},{5... | collective-permute-start | bytes 417800 | tf_op jit(solution)/shard_map/ppermute | solution.py:341
  66.3 1.2 %collective-permute-start.14 = (bf16[32,2176]{1,0:T(8,128)(2,1)S(1)}, bf16[32,2176]{1,0:T(8,128)(2,1)S(1)}, u32[]{:S(2)}, u32[]{:S(2)}) collective-permute-start(bf16[32,2176]{1,0:T(8,128)(2,1)S(1)} %get-tuple-element.66), channel_id=1, source_target_pairs={{0,8},{4,12},{8,0},{12,4},{16,24},{20,28},{24,16},{28,20},{1,9},{5... | collective-permute-start | bytes 417800 | tf_op jit(solution)/shard_map/ppermute | solution.py:341
  67.5 0.1 collective-permute-start.15
  67.5 1.4 %collective-permute-start.5 = (bf16[32,2176]{1,0:T(8,128)(2,1)S(1)}, bf16[32,2176]{1,0:T(8,128)(2,1)S(1)}, u32[]{:S(2)}, u32[]{:S(2)}) collective-permute-start(bf16[32,2176]{1,0:T(8,128)(2,1)S(1)} %get-tuple-element.52), channel_id=1, source_target_pairs={{0,4},{4,0},{8,12},{12,8},{16,20},{20,16},{24,28},{28,24},{1,5},{5... | collective-permute-start | bytes 417800 | tf_op jit(solution)/shard_map/ppermute | solution.py:341
  68.9 0.2 collective-permute-done.13.b1
  69.1 1.4 %collective-permute-done.14.b2 = bf16[32,2176]{1,0:T(8,128)(2,1)S(1)} collective-permute-done((bf16[32,2176]{1,0:T(8,128)(2,1)S(1)}, bf16[32,2176]{1,0:T(8,128)(2,1)S(1)}, u32[]{:S(2)}, u32[]{:S(2)}) %collective-permute-start.14) | collective-permute-done | bytes 139296 | tf_op jit(solution)/shard_map/ppermute | solution.py:341
  70.5 3.1 %collective-permute-done.15.b3 = bf16[32,2176]{1,0:T(8,128)(2,1)S(1)} collective-permute-done((bf16[32,2176]{1,0:T(8,128)(2,1)S(1)}, bf16[32,2176]{1,0:T(8,128)(2,1)S(1)}, u32[]{:S(2)}, u32[]{:S(2)}) %collective-permute-start.15) | collective-permute-done | bytes 139296 | tf_op jit(solution)/shard_map/ppermute | solution.py:341
  73.5 0.4 shard_map.102.refs_0_
  74.0 2.2 %collective-permute-done.5.refs_1_.b1 = bf16[32,2176]{1,0:T(8,128)(2,1)S(1)} collective-permute-done((bf16[32,2176]{1,0:T(8,128)(2,1)S(1)}, bf16[32,2176]{1,0:T(8,128)(2,1)S(1)}, u32[]{:S(2)}, u32[]{:S(2)}) %collective-permute-start.5) | collective-permute-done | bytes 139296 | tf_op jit(solution)/shard_map/ppermute | solution.py:341
  76.1 0.0 collective-permute-done.12.far_b.rows_b
  76.1 0.1 shard_map.103
  76.3 1.6 %collective-permute-start.16 = (bf16[288,3200]{1,0:T(8,128)(2,1)S(1)}, bf16[288,3200]{1,0:T(8,128)(2,1)S(1)}, u32[]{:S(2)}, u32[]{:S(2)}) collective-permute-start(bf16[288,3200]{1,0:T(8,128)(2,1)S(1)} %shard_map.103), channel_id=1, source_target_pairs={{0,1},{1,0},{2,3},{3,2},{4,5},{5,4},{6,7},{7,6},{8,9},{9,8},{10,11... | collective-permute-start | bytes 5529608 | tf_op jit(solution)/shard_map/ppermute | solution.py:341
  77.9 1.2 %collective-permute-start.18 = (bf16[288,1152]{1,0:T(8,128)(2,1)S(1)}, bf16[288,1152]{1,0:T(8,128)(2,1)S(1)}, u32[]{:S(2)}, u32[]{:S(2)}) collective-permute-start(bf16[288,1152]{1,0:T(8,128)(2,1)S(1)} %get-tuple-element.63.mid_ref), channel_id=1, source_target_pairs={{0,2},{1,3},{2,0},{3,1},{4,6},{5,7},{6,4},{7,5},{8,10},{9,11},{10,... | collective-permute-start | bytes 1990664 | tf_op jit(solution)/shard_map/ppermute | solution.py:341
  79.1 0.1 collective-permute-start.17
  79.2 1.4 %collective-permute-start.6 = (bf16[32,2176]{1,0:T(8,128)(2,1)S(1)}, bf16[32,2176]{1,0:T(8,128)(2,1)S(1)}, u32[]{:S(2)}, u32[]{:S(2)}) collective-permute-start(bf16[32,2176]{1,0:T(8,128)(2,1)S(1)} %get-tuple-element.53), channel_id=1, source_target_pairs={{0,8},{4,12},{8,0},{12,4},{16,24},{20,28},{24,16},{28,20},{1,9},{5... | collective-permute-start | bytes 417800 | tf_op jit(solution)/shard_map/ppermute | solution.py:341
  80.5 1.2 %collective-permute-start.7 = (bf16[32,2176]{1,0:T(8,128)(2,1)S(1)}, bf16[32,2176]{1,0:T(8,128)(2,1)S(1)}, u32[]{:S(2)}, u32[]{:S(2)}) collective-permute-start(bf16[32,2176]{1,0:T(8,128)(2,1)S(1)} %get-tuple-element.54), channel_id=1, source_target_pairs={{0,12},{4,8},{8,4},{12,0},{16,28},{20,24},{24,20},{28,16},{1,13},{... | collective-permute-start | bytes 417800 | tf_op jit(solution)/shard_map/ppermute | solution.py:341
  81.7 1.2 %shard_map.104 = (f32[512,768]{1,0:T(8,128)S(1)}, f32[512,384]{1,0:T(8,128)S(1)}) custom-call(bf16[144,1024]{1,0:T(8,128)(2,1)S(1)} %get-tuple-element.47.refs_0_.refs_2_.rows_a, bf16[144,1024]{1,0:T(8,128)(2,1)S(1)} %get-tuple-element.59.refs_2_.rows_b, bf16[288,3200]{1,0:T(8,128)(2,1)S(1)} %collective-permute-done.16.near_ref, ...), custom_call_target="tpu_custom_call" | custom-call | flops 679477248 | bytes 5455872 | tf_op jit(solution)/shard_map/pallas_call | solution.py:328
  83.0 4.7 %collective-permute-done.6.b2 = bf16[32,2176]{1,0:T(8,128)(2,1)S(1)} collective-permute-done((bf16[32,2176]{1,0:T(8,128)(2,1)S(1)}, bf16[32,2176]{1,0:T(8,128)(2,1)S(1)}, u32[]{:S(2)}, u32[]{:S(2)}) %collective-permute-start.6) | collective-permute-done | bytes 139296 | tf_op jit(solution)/shard_map/ppermute | solution.py:341
  87.7 3.0 %collective-permute-done.7.b3 = bf16[32,2176]{1,0:T(8,128)(2,1)S(1)} collective-permute-done((bf16[32,2176]{1,0:T(8,128)(2,1)S(1)}, bf16[32,2176]{1,0:T(8,128)(2,1)S(1)}, u32[]{:S(2)}, u32[]{:S(2)}) %collective-permute-start.7) | collective-permute-done | bytes 139296 | tf_op jit(solution)/shard_map/ppermute | solution.py:341
  90.7 0.4 shard_map.105
  91.1 0.0 copy-start.5
  91.1 2.4 %collective-permute-done.17.far_ref.refs_2_ = bf16[32,4224]{1,0:T(8,128)(2,1)S(1)} collective-permute-done((bf16[32,4224]{1,0:T(8,128)(2,1)S(1)}, bf16[32,4224]{1,0:T(8,128)(2,1)S(1)}, u32[]{:S(2)}, u32[]{:S(2)}) %collective-permute-start.17) | collective-permute-done | bytes 270368 | tf_op jit(solution)/shard_map/ppermute | solution.py:341
  93.6 0.8 collective-permute-done.18.refs_0_
  94.4 0.8 collective-permute-start.19
  95.2 1.3 %shard_map.106 = (bf16[64,2048]{1,0:T(8,128)(2,1)}, bf16[4,64]{1,0:T(4,128)(2,1)}) custom-call(s32[8]{0:T(128)S(1)} %iota_xor_fusion.1.peer_ref, s32[4,64]{1,0:T(4,128)S(1)} %bitcast.10, f32[64,2048]{1,0:T(8,128)S(1)} %get-tuple-element.69.near_ref.refs_3_, f32[8,64]{1,0:T(8,128)S(1)} %get-tuple-element.70.near_route_ref, ...), custom_call_target="tpu_custom_call" | custom-call | bytes 1060352 | tf_op jit(solution)/shard_map/pallas_call | solution.py:328
  96.5 0.9 shard_map.108
  97.4 1.8 %shard_map.109 = (f32[512,768]{1,0:T(8,128)}, f32[512,384]{1,0:T(8,128)}) custom-call(bf16[288,3200]{1,0:T(8,128)(2,1)S(1)} %collective-permute-done.16.near_ref, bf16[288,1152]{1,0:T(8,128)(2,1)S(1)} %collective-permute-done.19.mid_ref, f32[512,768]{1,0:T(8,128)S(1)} %get-tuple-element.74.in_part, f32[512,384]{1,0:T(8,128)S(1)} %get-tuple-element.75.out_part), custom_call_target="tpu_custom_call" | custom-call | flops 339738624 | bytes 4866048 | tf_op jit(solution)/shard_map/pallas_call | solution.py:328
  (12 shorter events, 0.0 us)
Async XLA Ops:
  0.7 1.0 copy-start.2
  1.6 0.9 copy-start.3
  2.6 0.7 copy-start.4
  3.2 0.7 copy-start.6
  4.5 9.0 %copy-start = (bf16[1,512,768]{2,1,0:T(8,128)(2,1)S(1)}, bf16[1,512,768]{2,1,0:T(8,128)(2,1)}, u32[]{:S(2)}) copy-start(bf16[1,512,768]{2,1,0:T(8,128)(2,1)} %param.10) | copy-start | bytes 2359300
  4.5 8.9 %copy-start.1 = (bf16[1,512,384]{2,1,0:T(8,128)(2,1)S(1)}, bf16[1,512,384]{2,1,0:T(8,128)(2,1)}, u32[]{:S(2)}) copy-start(bf16[1,512,384]{2,1,0:T(8,128)(2,1)} %param.11) | copy-start | bytes 1179652
  6.7 29.9 %all-to-all-start = ((bf16[4,64,2176]{2,1,0:T(8,128)(2,1)}), bf16[4,64,2176]{2,1,0:T(8,128)(2,1)S(1)}, u32[]{:S(2)}, u32[]{:S(2)}) async-start(bf16[4,64,2176]{2,1,0:T(8,128)(2,1)} %shard_map.94), calls=%async_computation | async-start | bytes 2228224 | tf_op jit(solution)/shard_map/all_to_all | solution.py:419
  11.1 23.2 %collective-permute-start = (bf16[64,4224]{1,0:T(8,128)(2,1)S(1)}, bf16[64,4224]{1,0:T(8,128)(2,1)S(1)}, u32[]{:S(2)}, u32[]{:S(2)}) collective-permute-start(bf16[64,4224]{1,0:T(8,128)(2,1)S(1)} %get-tuple-element.42.joint_ref), channel_id=1, source_target_pairs={{0,16},{4,20},{8,24},{12,28},{16,0},{20,4},{24,8},{28,12},{1,17},{... | collective-permute-start | bytes 1622024 | tf_op jit(solution)/shard_map/ppermute | solution.py:341
  14.6 26.5 %collective-permute-start.1 = (bf16[176,1152]{1,0:T(8,128)(2,1)}, bf16[176,1152]{1,0:T(8,128)(2,1)S(1)}, u32[]{:S(2)}, u32[]{:S(2)}) collective-permute-start(bf16[176,1152]{1,0:T(8,128)(2,1)} %get-tuple-element.44.refs_0_), channel_id=1, source_target_pairs={{0,2},{1,3},{2,0},{3,1},{4,6},{5,7},{6,4},{7,5},{8,10},{9,11},{10,... | collective-permute-start | bytes 1216520 | tf_op jit(solution)/shard_map/ppermute | solution.py:341
  15.8 25.3 %collective-permute-start.2 = (bf16[176,1152]{1,0:T(8,128)(2,1)}, bf16[176,1152]{1,0:T(8,128)(2,1)S(1)}, u32[]{:S(2)}, u32[]{:S(2)}) collective-permute-start(bf16[176,1152]{1,0:T(8,128)(2,1)} %get-tuple-element.45.refs_1_), channel_id=1, source_target_pairs={{0,2},{1,3},{2,0},{3,1},{4,6},{5,7},{6,4},{7,5},{8,10},{9,11},{10,... | collective-permute-start | bytes 1216520 | tf_op jit(solution)/shard_map/ppermute | solution.py:341
  16.0 25.0 %collective-permute-start.3 = (bf16[160,1152]{1,0:T(8,128)(2,1)}, bf16[160,1152]{1,0:T(8,128)(2,1)S(1)}, u32[]{:S(2)}, u32[]{:S(2)}) collective-permute-start(bf16[160,1152]{1,0:T(8,128)(2,1)} %get-tuple-element.46.refs_2_), channel_id=1, source_target_pairs={{0,2},{1,3},{2,0},{3,1},{4,6},{5,7},{6,4},{7,5},{8,10},{9,11},{10,... | collective-permute-start | bytes 1105928 | tf_op jit(solution)/shard_map/ppermute | solution.py:341
  43.1 6.3 %collective-permute-start.4 = (bf16[1024,1152]{1,0:T(8,128)(2,1)S(1)}, bf16[1024,1152]{1,0:T(8,128)(2,1)S(1)}, u32[]{:S(2)}, u32[]{:S(2)}) collective-permute-start(bf16[1024,1152]{1,0:T(8,128)(2,1)S(1)} %shard_map.98.refs_0_), channel_id=1, source_target_pairs={{0,1},{1,0},{2,3},{3,2},{4,5},{5,4},{6,7},{7,6},{8,9},{9,8},{10,11... | collective-permute-start | bytes 7077896 | tf_op jit(solution)/shard_map/ppermute | solution.py:341
  45.2 16.0 %collective-permute-start.11 = (bf16[144,2048]{1,0:T(8,128)(2,1)S(1)}, bf16[144,2048]{1,0:T(8,128)(2,1)S(1)}, u32[]{:S(2)}, u32[]{:S(2)}) collective-permute-start(bf16[144,2048]{1,0:T(8,128)(2,1)S(1)} %get-tuple-element.50.refs_4_), channel_id=1, source_target_pairs={{0,2},{1,3},{2,0},{3,1},{4,6},{5,7},{6,4},{7,5},{8,10},{9,11},{10,... | collective-permute-start | bytes 1769480 | tf_op jit(solution)/shard_map/ppermute | solution.py:341
  46.5 7.9 %collective-permute-start.8 = (bf16[64,2176]{1,0:T(8,128)(2,1)S(1)}, bf16[64,2176]{1,0:T(8,128)(2,1)S(1)}, u32[]{:S(2)}, u32[]{:S(2)}) collective-permute-start(bf16[64,2176]{1,0:T(8,128)(2,1)S(1)} %get-tuple-element.55), channel_id=1, source_target_pairs={{0,4},{4,0},{8,12},{12,8},{16,20},{20,16},{24,28},{28,24},{1,5},{5... | collective-permute-start | bytes 835592 | tf_op jit(solution)/shard_map/ppermute | solution.py:341
  47.9 7.6 %collective-permute-start.9 = (bf16[64,2176]{1,0:T(8,128)(2,1)S(1)}, bf16[64,2176]{1,0:T(8,128)(2,1)S(1)}, u32[]{:S(2)}, u32[]{:S(2)}) collective-permute-start(bf16[64,2176]{1,0:T(8,128)(2,1)S(1)} %get-tuple-element.56), channel_id=1, source_target_pairs={{0,8},{4,12},{8,0},{12,4},{16,24},{20,28},{24,16},{28,20},{1,9},{5... | collective-permute-start | bytes 835592 | tf_op jit(solution)/shard_map/ppermute | solution.py:341
  49.0 12.2 %collective-permute-start.10 = (bf16[64,2176]{1,0:T(8,128)(2,1)S(1)}, bf16[64,2176]{1,0:T(8,128)(2,1)S(1)}, u32[]{:S(2)}, u32[]{:S(2)}) collective-permute-start(bf16[64,2176]{1,0:T(8,128)(2,1)S(1)} %get-tuple-element.57), channel_id=1, source_target_pairs={{0,12},{4,8},{8,4},{12,0},{16,28},{20,24},{24,20},{28,16},{1,13},{... | collective-permute-start | bytes 835592 | tf_op jit(solution)/shard_map/ppermute | solution.py:341
  61.9 14.3 %collective-permute-start.12 = (bf16[144,2048]{1,0:T(8,128)(2,1)S(1)}, bf16[144,2048]{1,0:T(8,128)(2,1)S(1)}, u32[]{:S(2)}, u32[]{:S(2)}) collective-permute-start(bf16[144,2048]{1,0:T(8,128)(2,1)S(1)} %get-tuple-element.61.refs_4_), channel_id=1, source_target_pairs={{0,2},{1,3},{2,0},{3,1},{4,6},{5,7},{6,4},{7,5},{8,10},{9,11},{10,... | collective-permute-start | bytes 1769480 | tf_op jit(solution)/shard_map/ppermute | solution.py:341
  64.8 4.3 %collective-permute-start.13 = (bf16[32,2176]{1,0:T(8,128)(2,1)S(1)}, bf16[32,2176]{1,0:T(8,128)(2,1)S(1)}, u32[]{:S(2)}, u32[]{:S(2)}) collective-permute-start(bf16[32,2176]{1,0:T(8,128)(2,1)S(1)} %get-tuple-element.65), channel_id=1, source_target_pairs={{0,4},{4,0},{8,12},{12,8},{16,20},{20,16},{24,28},{28,24},{1,5},{5... | collective-permute-start | bytes 417800 | tf_op jit(solution)/shard_map/ppermute | solution.py:341
  66.3 4.2 %collective-permute-start.14 = (bf16[32,2176]{1,0:T(8,128)(2,1)S(1)}, bf16[32,2176]{1,0:T(8,128)(2,1)S(1)}, u32[]{:S(2)}, u32[]{:S(2)}) collective-permute-start(bf16[32,2176]{1,0:T(8,128)(2,1)S(1)} %get-tuple-element.66), channel_id=1, source_target_pairs={{0,8},{4,12},{8,0},{12,4},{16,24},{20,28},{24,16},{28,20},{1,9},{5... | collective-permute-start | bytes 417800 | tf_op jit(solution)/shard_map/ppermute | solution.py:341
  67.5 6.1 %collective-permute-start.15 = (bf16[32,2176]{1,0:T(8,128)(2,1)S(1)}, bf16[32,2176]{1,0:T(8,128)(2,1)S(1)}, u32[]{:S(2)}, u32[]{:S(2)}) collective-permute-start(bf16[32,2176]{1,0:T(8,128)(2,1)S(1)} %get-tuple-element.67), channel_id=1, source_target_pairs={{0,12},{4,8},{8,4},{12,0},{16,28},{20,24},{24,20},{28,16},{1,13},{... | collective-permute-start | bytes 417800 | tf_op jit(solution)/shard_map/ppermute | solution.py:341
  67.5 8.6 %collective-permute-start.5 = (bf16[32,2176]{1,0:T(8,128)(2,1)S(1)}, bf16[32,2176]{1,0:T(8,128)(2,1)S(1)}, u32[]{:S(2)}, u32[]{:S(2)}) collective-permute-start(bf16[32,2176]{1,0:T(8,128)(2,1)S(1)} %get-tuple-element.52), channel_id=1, source_target_pairs={{0,4},{4,0},{8,12},{12,8},{16,20},{20,16},{24,28},{28,24},{1,5},{5... | collective-permute-start | bytes 417800 | tf_op jit(solution)/shard_map/ppermute | solution.py:341
  76.3 5.5 %collective-permute-start.16 = (bf16[288,3200]{1,0:T(8,128)(2,1)S(1)}, bf16[288,3200]{1,0:T(8,128)(2,1)S(1)}, u32[]{:S(2)}, u32[]{:S(2)}) collective-permute-start(bf16[288,3200]{1,0:T(8,128)(2,1)S(1)} %shard_map.103), channel_id=1, source_target_pairs={{0,1},{1,0},{2,3},{3,2},{4,5},{5,4},{6,7},{7,6},{8,9},{9,8},{10,11... | collective-permute-start | bytes 5529608 | tf_op jit(solution)/shard_map/ppermute | solution.py:341
  77.9 16.5 %collective-permute-start.18 = (bf16[288,1152]{1,0:T(8,128)(2,1)S(1)}, bf16[288,1152]{1,0:T(8,128)(2,1)S(1)}, u32[]{:S(2)}, u32[]{:S(2)}) collective-permute-start(bf16[288,1152]{1,0:T(8,128)(2,1)S(1)} %get-tuple-element.63.mid_ref), channel_id=1, source_target_pairs={{0,2},{1,3},{2,0},{3,1},{4,6},{5,7},{6,4},{7,5},{8,10},{9,11},{10,... | collective-permute-start | bytes 1990664 | tf_op jit(solution)/shard_map/ppermute | solution.py:341
  79.1 14.5 %collective-permute-start.17 = (bf16[32,4224]{1,0:T(8,128)(2,1)S(1)}, bf16[32,4224]{1,0:T(8,128)(2,1)S(1)}, u32[]{:S(2)}, u32[]{:S(2)}) collective-permute-start(bf16[32,4224]{1,0:T(8,128)(2,1)S(1)} %shard_map.102.refs_0_), channel_id=1, source_target_pairs={{0,16},{4,20},{8,24},{12,28},{16,0},{20,4},{24,8},{28,12},{1,17},{... | collective-permute-start | bytes 811016 | tf_op jit(solution)/shard_map/ppermute | solution.py:341
  79.2 8.6 %collective-permute-start.6 = (bf16[32,2176]{1,0:T(8,128)(2,1)S(1)}, bf16[32,2176]{1,0:T(8,128)(2,1)S(1)}, u32[]{:S(2)}, u32[]{:S(2)}) collective-permute-start(bf16[32,2176]{1,0:T(8,128)(2,1)S(1)} %get-tuple-element.53), channel_id=1, source_target_pairs={{0,8},{4,12},{8,0},{12,4},{16,24},{20,28},{24,16},{28,20},{1,9},{5... | collective-permute-start | bytes 417800 | tf_op jit(solution)/shard_map/ppermute | solution.py:341
  80.5 10.1 %collective-permute-start.7 = (bf16[32,2176]{1,0:T(8,128)(2,1)S(1)}, bf16[32,2176]{1,0:T(8,128)(2,1)S(1)}, u32[]{:S(2)}, u32[]{:S(2)}) collective-permute-start(bf16[32,2176]{1,0:T(8,128)(2,1)S(1)} %get-tuple-element.54), channel_id=1, source_target_pairs={{0,12},{4,8},{8,4},{12,0},{16,28},{20,24},{24,20},{28,16},{1,13},{... | collective-permute-start | bytes 417800 | tf_op jit(solution)/shard_map/ppermute | solution.py:341
  91.1 4.1 %copy-start.5 = (s32[64,4]{0,1:T(4,128)S(1)}, s32[64,4]{0,1:T(4,128)}, u32[]{:S(2)}) copy-start(s32[64,4]{0,1:T(4,128)} %param.8) | copy-start | bytes 3076
  94.4 3.0 %collective-permute-start.19 = (bf16[288,1152]{1,0:T(8,128)(2,1)S(1)}, bf16[288,1152]{1,0:T(8,128)(2,1)S(1)}, u32[]{:S(2)}, u32[]{:S(2)}) collective-permute-start(bf16[288,1152]{1,0:T(8,128)(2,1)S(1)} %shard_map.107.mid_ref), channel_id=1, source_target_pairs={{0,1},{1,0},{2,3},{3,2},{4,5},{5,4},{6,7},{7,6},{8,9},{9,8},{10,11... | collective-permute-start | bytes 1990664 | tf_op jit(solution)/shard_map/ppermute | solution.py:341

commit v9 on v7

--- a/solution.py
+++ b/solution.py
@@ -240,25 +240,24 @@
     out_ref[0:16, 2 * width : 2 * width + tokens] = block
 
 
-def near_sum_kernel(w_ref, b0, b1, b2, b3, after_ref, grad_ref, route_ref, rows, fold):
+def combine_kernel(peer_ref, named_ref, w_ref, b0, b1, b2, b3, far_ref, *refs):
+    grad_ref, route_ref, in_ref, out_ref, held, rows, fold, lines_ref, sem = refs[5:]
+    tokens, width = held.shape
     summed, routes = unpack_sum(w_ref[...], (b0, b1, b2, b3), rows, fold)
-    grad_ref[...] = summed
-    route_ref[...] = jnp.concatenate(routes + [jnp.zeros_like(route) for route in routes], axis=0)
-
-
-def combine_kernel(peer_ref, named_ref, near_ref, near_route_ref, far_ref, grad_ref, route_ref):
-    tokens, width = grad_ref.shape
     lines = tokens // 2
     for half in range(2):
         at, columns = slice(half * lines, (half + 1) * lines), slice(half * width, (half + 1) * width)
-        grad_ref[at, :] = (near_ref[at, :] + far_ref[:, columns].astype(F32)).astype(BF16)
+        held[at, :] = (summed[at, :] + far_ref[:, columns].astype(F32)).astype(BF16)
+    copy = start(held, grad_ref, sem)
     others = far_ref[0:16, 2 * width : 2 * width + tokens].astype(F32)
     named = named_ref[...]
     route = jnp.zeros(route_ref.shape, F32)
     for j in range(4):
-        route = route + jnp.where(named == peer_ref[j], near_route_ref[j : j + 1, :], 0.0)
+        route = route + jnp.where(named == peer_ref[j], routes[j], 0.0)
         route = route + jnp.where(named == peer_ref[4 + j], others[j : j + 1, :], 0.0)
     route_ref[...] = route.astype(BF16)
+    second_weight_part(*refs[:5], in_ref, out_ref, lines_ref)
+    copy.wait()
 
 
 def fill(rows, mids, rows_a, rows_b, rows_c, mid_a, mid_b):
@@ -278,7 +277,7 @@
     out_ref[...] = dot_tn(rows[:, depth:], mids[:, 2 * hidden_width :])
 
 
-def second_weight_kernel(rows_a, rows_b, mid_ref, in_part, out_part, in_ref, out_ref, rows):
+def second_weight_part(rows_a, rows_b, mid_ref, in_part, out_part, in_ref, out_ref, rows):
     depth, hidden_width = out_ref.shape
     count = rows_a.shape[0]
     rows[0:count, :] = rows_a[:, : 2 * depth]
@@ -456,44 +455,31 @@
         weight_scratch,
         weight_flops,
     )
-    near_sum, near_route = call(
-        near_sum_kernel,
-        [((token_count, width), F32), ((blocks, token_count), F32)],
-        [],
-        [dense, *near_back],
-        [first[1]],
-        sum_scratch,
-        sum_flops,
-    )
-    grad_tokens, grad_route = call(
-        combine_kernel,
-        [((token_count, width), BF16), (named.shape, BF16)],
-        [peers],
-        [named, near_sum, near_route, far_partial],
-        [],
-        [],
-        0,
-    )
-
     (mid_far,) = call(
         after_kernel,
         [(mid_far.shape, BF16)],
         [],
         [],
-        [mid_far, first[1], far_partial, near_sum],
+        [mid_far, first[1], far_partial, *near_back[2:]],
         [],
         0,
         1,
         {0: 0},
     )
-    second = call(
-        second_weight_kernel,
-        weight_shapes,
-        [],
-        [own_far, far_far, mid_far, *first],
-        [],
-        [pltpu.VMEM((2 * rows, 2 * depth), BF16)],
-        weight_flops // 2,
+    grad_tokens, grad_route, *second = call(
+        combine_kernel,
+        [((token_count, width), BF16), (named.shape, BF16), *weight_shapes],
+        [peers],
+        [named, dense, *near_back, far_partial, own_far, far_far, mid_far, *first],
+        [],
+        [
+            pltpu.VMEM((token_count, width), BF16),
+            *sum_scratch,
+            pltpu.VMEM((2 * rows, 2 * depth), BF16),
+            pltpu.SemaphoreType.DMA,
+        ],
+        sum_flops + weight_flops // 2,
+        1,
     )
     grad_gate_up, grad_down = call(
         last_weight_kernel,

time: 92.5 us -> 92.2 us (level)
    pallas_call x16 -> x14, Pallas kernels: 16.4 us -> 16.1 us  [call(): pl.pallas_call(kernel, out_shape=tuple(outs), in_specs=[on_smem] * len(sm...]
where the time goes in v9:
time: 92.2 us; the launch traced here: 92.1 us
  waiting for transfers between devices  49.7 us (54%)
  starting transfers between devices  24.2 us (26%)
  Pallas kernels  16.1 us (17%)
  other arithmetic  1.41 us (2%)
    ppermute x21, waiting for transfers between devices, swap(): lax.ppermute(value, axis, [(i, i ^ mask) for i in range(lax.axis_size(axi...  49.7 us
    ppermute x21, starting transfers between devices, swap(): lax.ppermute(value, axis, [(i, i ^ mask) for i in range(lax.axis_size(axi...  24.2 us
    pallas_call x14, Pallas kernels, call(): pl.pallas_call(kernel, out_shape=tuple(outs), in_specs=[on_smem] * len(sm...  16.1 us
  transfers between devices with their start and end apart: 21, of which 14 were waited for; matrix products, arithmetic and copies ran while one was open for 0% of the time, Pallas kernels for 14%

profile of v9, /device:TPU:1, one launch (start us, length us, event | category | flops | bytes accessed | tf_op | source)
XLA Modules:
  0.0 92.1 jit_solution(7503384588604908247)
XLA Ops:
  0.6 0.0 copy-start.3
  0.6 0.0 copy-start.2
  0.7 0.0 copy-start.1
  0.7 0.0 copy-start
  0.7 1.4 %pad_maximum_fusion.own_ref = bf16[512,1152]{1,0:T(8,128)(2,1)S(1)} fusion(bf16[512,384]{1,0:T(8,128)(2,1)} %bitcast.11, bf16[512,768]{1,0:T(8,128)(2,1)} %bitcast.10), kind=kLoop, calls=%fused_computation | loop fusion | flops 2359296 | bytes 2359296 | tf_op jit(solution)/shard_map/concatenate | solution.py:354
  2.1 2.1 %collective-permute-start.4 = (bf16[512,1152]{1,0:T(8,128)(2,1)S(1)}, bf16[512,1152]{1,0:T(8,128)(2,1)S(1)}, u32[]{:S(2)}, u32[]{:S(2)}) collective-permute-start(bf16[512,1152]{1,0:T(8,128)(2,1)S(1)} %pad_maximum_fusion.own_ref), channel_id=1, source_target_pairs={{0,2},{1,3},{2,0},{3,1},{4,6},{5,7},{6,4},{7,5},{8,10},{9,11},{10,... | collective-permute-start | bytes 3538952 | tf_op jit(solution)/shard_map/ppermute | solution.py:325
  4.2 0.0 copy-done.3
  4.2 0.0 copy-done.2
  4.2 0.0 copy-done.1
  4.2 0.0 copy-done
  4.2 0.6 shard_map.93
  4.8 2.4 %collective-permute-start.3 = (bf16[64,4224]{1,0:T(8,128)(2,1)S(1)}, bf16[64,4224]{1,0:T(8,128)(2,1)S(1)}, u32[]{:S(2)}, u32[]{:S(2)}) collective-permute-start(bf16[64,4224]{1,0:T(8,128)(2,1)S(1)} %get-tuple-element.40.joint_ref.refs_0_), channel_id=1, source_target_pairs={{0,16},{4,20},{8,24},{12,28},{16,0},{20,4},{24,8},{28,12},{1,17},{... | collective-permute-start | bytes 1622024 | tf_op jit(solution)/shard_map/ppermute | solution.py:325
  7.2 1.4 %shard_map.94 = (bf16[64,2176]{1,0:T(8,128)(2,1)}, bf16[64,2176]{1,0:T(8,128)(2,1)}, bf16[64,2176]{1,0:T(8,128)(2,1)}) custom-call(bf16[64,4224]{1,0:T(8,128)(2,1)S(1)} %get-tuple-element.40.joint_ref.refs_0_), custom_call_target="tpu_custom_call" | custom-call | flops 58720256 | bytes 1376256 | tf_op jit(solution)/shard_map/pallas_call | solution.py:312
  8.6 1.2 %collective-permute-start = (bf16[64,2176]{1,0:T(8,128)(2,1)}, bf16[64,2176]{1,0:T(8,128)(2,1)}, u32[]{:S(2)}, u32[]{:S(2)}) collective-permute-start(bf16[64,2176]{1,0:T(8,128)(2,1)} %get-tuple-element.41), channel_id=1, source_target_pairs={{0,4},{4,0},{8,12},{12,8},{16,20},{20,16},{24,28},{28,24},{1,5},{5... | collective-permute-start | bytes 835592 | tf_op jit(solution)/shard_map/ppermute | solution.py:325
  9.8 1.3 %collective-permute-start.1 = (bf16[64,2176]{1,0:T(8,128)(2,1)}, bf16[64,2176]{1,0:T(8,128)(2,1)}, u32[]{:S(2)}, u32[]{:S(2)}) collective-permute-start(bf16[64,2176]{1,0:T(8,128)(2,1)} %get-tuple-element.42), channel_id=1, source_target_pairs={{0,8},{4,12},{8,0},{12,4},{16,24},{20,28},{24,16},{28,20},{1,9},{5... | collective-permute-start | bytes 835592 | tf_op jit(solution)/shard_map/ppermute | solution.py:325
  11.1 0.1 collective-permute-start.2
  11.2 4.6 %collective-permute-done.refs_1_ = bf16[64,2176]{1,0:T(8,128)(2,1)} collective-permute-done((bf16[64,2176]{1,0:T(8,128)(2,1)}, bf16[64,2176]{1,0:T(8,128)(2,1)}, u32[]{:S(2)}, u32[]{:S(2)}) %collective-permute-start) | collective-permute-done | bytes 278560 | tf_op jit(solution)/shard_map/ppermute | solution.py:325
  15.8 8.1 %collective-permute-done.1.refs_2_ = bf16[64,2176]{1,0:T(8,128)(2,1)} collective-permute-done((bf16[64,2176]{1,0:T(8,128)(2,1)}, bf16[64,2176]{1,0:T(8,128)(2,1)}, u32[]{:S(2)}, u32[]{:S(2)}) %collective-permute-start.1) | collective-permute-done | bytes 278560 | tf_op jit(solution)/shard_map/ppermute | solution.py:325
  23.9 9.2 %collective-permute-done.2.refs_3_ = bf16[64,2176]{1,0:T(8,128)(2,1)} collective-permute-done((bf16[64,2176]{1,0:T(8,128)(2,1)}, bf16[64,2176]{1,0:T(8,128)(2,1)}, u32[]{:S(2)}, u32[]{:S(2)}) %collective-permute-start.2) | collective-permute-done | bytes 278560 | tf_op jit(solution)/shard_map/ppermute | solution.py:325
  33.2 0.0 collective-permute-done.3.refs_4_.joint_ref
  33.2 1.6 %shard_map.95 = (bf16[144,1024]{1,0:T(8,128)(2,1)S(1)}, bf16[144,1024]{1,0:T(8,128)(2,1)S(1)}, bf16[144,2048]{1,0:T(8,128)(2,1)S(1)}, f32[144,128]{1,0:T(8,128)S(1)}) custom-call(s32[4]{0:T(128)S(1)} %iota_xor_fusion.place_ref, bf16[64,4224]{1,0:T(8,128)(2,1)S(1)} %get-tuple-element.40.joint_ref.refs_0_, bf16[64,2176]{1,0:T(8,128)(2,1)} %collective-permute-done.refs_1_, ...), custom_call_target="tpu_custom_call" | custom-call | bytes 2629632 | tf_op jit(solution)/shard_map/pallas_call | solution.py:312
  34.8 0.0 collective-permute-done.4.refs_1_.far_ref
  34.8 0.6 shard_map.96
  35.4 0.2 shard_map.97.refs_0_
  35.5 2.5 %collective-permute-start.5 = (bf16[1024,1152]{1,0:T(8,128)(2,1)S(1)}, bf16[1024,1152]{1,0:T(8,128)(2,1)S(1)}, u32[]{:S(2)}, u32[]{:S(2)}) collective-permute-start(bf16[1024,1152]{1,0:T(8,128)(2,1)S(1)} %shard_map.97.refs_0_), channel_id=1, source_target_pairs={{0,1},{1,0},{2,3},{3,2},{4,5},{5,4},{6,7},{7,6},{8,9},{9,8},{10,11... | collective-permute-start | bytes 7077896 | tf_op jit(solution)/shard_map/ppermute | solution.py:325
  38.0 0.3 collective-permute-start.12
  38.3 1.2 %collective-permute-start.9 = (bf16[64,2176]{1,0:T(8,128)(2,1)S(1)}, bf16[64,2176]{1,0:T(8,128)(2,1)S(1)}, u32[]{:S(2)}, u32[]{:S(2)}) collective-permute-start(bf16[64,2176]{1,0:T(8,128)(2,1)S(1)} %get-tuple-element.53), channel_id=1, source_target_pairs={{0,4},{4,0},{8,12},{12,8},{16,20},{20,16},{24,28},{28,24},{1,5},{5... | collective-permute-start | bytes 835592 | tf_op jit(solution)/shard_map/ppermute | solution.py:325
  39.5 0.0 collective-permute-start.10
  39.5 1.5 %collective-permute-start.11 = (bf16[64,2176]{1,0:T(8,128)(2,1)S(1)}, bf16[64,2176]{1,0:T(8,128)(2,1)S(1)}, u32[]{:S(2)}, u32[]{:S(2)}) collective-permute-start(bf16[64,2176]{1,0:T(8,128)(2,1)S(1)} %get-tuple-element.55), channel_id=1, source_target_pairs={{0,12},{4,8},{8,4},{12,0},{16,28},{20,24},{24,20},{28,16},{1,13},{... | collective-permute-start | bytes 835592 | tf_op jit(solution)/shard_map/ppermute | solution.py:325
  41.0 1.2 %collective-permute-done.5.refs_1_ = bf16[1024,1152]{1,0:T(8,128)(2,1)S(1)} collective-permute-done((bf16[1024,1152]{1,0:T(8,128)(2,1)S(1)}, bf16[1024,1152]{1,0:T(8,128)(2,1)S(1)}, u32[]{:S(2)}, u32[]{:S(2)}) %collective-permute-start.5) | collective-permute-done | bytes 2359328 | tf_op jit(solution)/shard_map/ppermute | solution.py:325
  42.2 2.6 %shard_map.98 = (bf16[144,1152]{1,0:T(8,128)(2,1)S(1)}, bf16[32,2176]{1,0:T(8,128)(2,1)S(1)}, bf16[32,2176]{1,0:T(8,128)(2,1)S(1)}, bf16[32,2176]{1,0:T(8,128)(2,1)S(1)}, bf16[32,2176]{1,0:T(8,128)(2,1)S(1)}) custom-call(s32[4]{0:T(128)S(1)} %iota_xor_fusion.place_ref, f32[144,128]{1,0:T(8,128)S(1)} %get-tuple-element.44.w_ref, ...), custom_call_target="tpu_custom_call" | custom-call | flops 1132462080 | bytes 6860800 | tf_op jit(solution)/shard_map/pallas_call | solution.py:312
  44.8 8.1 %collective-permute-done.12.refs_5_.far_a.refs_0_ = bf16[144,2048]{1,0:T(8,128)(2,1)S(1)} collective-permute-done((bf16[144,2048]{1,0:T(8,128)(2,1)S(1)}, bf16[144,2048]{1,0:T(8,128)(2,1)S(1)}, u32[]{:S(2)}, u32[]{:S(2)}) %collective-permute-start.12) | collective-permute-done | bytes 589856 | tf_op jit(solution)/shard_map/ppermute | solution.py:325
  53.0 0.0 collective-permute-done.9.refs_1_
  53.0 0.0 collective-permute-done.10.refs_2_
  53.0 0.1 collective-permute-done.11.refs_3_
  53.1 0.7 shard_map.99
  53.7 1.3 %collective-permute-start.17 = (bf16[144,2048]{1,0:T(8,128)(2,1)S(1)}, bf16[144,2048]{1,0:T(8,128)(2,1)S(1)}, u32[]{:S(2)}, u32[]{:S(2)}) collective-permute-start(bf16[144,2048]{1,0:T(8,128)(2,1)S(1)} %get-tuple-element.60.refs_4_), channel_id=1, source_target_pairs={{0,2},{1,3},{2,0},{3,1},{4,6},{5,7},{6,4},{7,5},{8,10},{9,11},{10,... | collective-permute-start | bytes 1769480 | tf_op jit(solution)/shard_map/ppermute | solution.py:325
  55.0 2.6 %shard_map.100 = (bf16[288,1152]{1,0:T(8,128)(2,1)S(1)}, bf16[32,2176]{1,0:T(8,128)(2,1)S(1)}, bf16[32,2176]{1,0:T(8,128)(2,1)S(1)}, bf16[32,2176]{1,0:T(8,128)(2,1)S(1)}, bf16[32,2176]{1,0:T(8,128)(2,1)S(1)}) custom-call(s32[4]{0:T(128)S(1)} %iota_xor_fusion.place_ref, f32[144,128]{1,0:T(8,128)S(1)} %get-tuple-element.57.w_ref, ...), custom_call_target="tpu_custom_call" | custom-call | flops 1132462080 | bytes 7524352 | tf_op jit(solution)/shard_map/pallas_call | solution.py:312
  57.6 1.3 %collective-permute-start.13 = (bf16[32,2176]{1,0:T(8,128)(2,1)S(1)}, bf16[32,2176]{1,0:T(8,128)(2,1)S(1)}, u32[]{:S(2)}, u32[]{:S(2)}) collective-permute-start(bf16[32,2176]{1,0:T(8,128)(2,1)S(1)} %get-tuple-element.62), channel_id=1, source_target_pairs={{0,4},{4,0},{8,12},{12,8},{16,20},{20,16},{24,28},{28,24},{1,5},{5... | collective-permute-start | bytes 417800 | tf_op jit(solution)/shard_map/ppermute | solution.py:325
  58.9 0.3 collective-permute-start.14
  59.3 1.1 %collective-permute-start.15 = (bf16[32,2176]{1,0:T(8,128)(2,1)S(1)}, bf16[32,2176]{1,0:T(8,128)(2,1)S(1)}, u32[]{:S(2)}, u32[]{:S(2)}) collective-permute-start(bf16[32,2176]{1,0:T(8,128)(2,1)S(1)} %get-tuple-element.64), channel_id=1, source_target_pairs={{0,12},{4,8},{8,4},{12,0},{16,28},{20,24},{24,20},{28,16},{1,13},{... | collective-permute-start | bytes 417800 | tf_op jit(solution)/shard_map/ppermute | solution.py:325
  60.3 1.3 %collective-permute-start.6 = (bf16[32,2176]{1,0:T(8,128)(2,1)S(1)}, bf16[32,2176]{1,0:T(8,128)(2,1)S(1)}, u32[]{:S(2)}, u32[]{:S(2)}) collective-permute-start(bf16[32,2176]{1,0:T(8,128)(2,1)S(1)} %get-tuple-element.50), channel_id=1, source_target_pairs={{0,4},{4,0},{8,12},{12,8},{16,20},{20,16},{24,28},{28,24},{1,5},{5... | collective-permute-start | bytes 417800 | tf_op jit(solution)/shard_map/ppermute | solution.py:325
  61.6 0.3 collective-permute-done.13.b1
  61.9 1.3 %collective-permute-done.14.b2 = bf16[32,2176]{1,0:T(8,128)(2,1)S(1)} collective-permute-done((bf16[32,2176]{1,0:T(8,128)(2,1)S(1)}, bf16[32,2176]{1,0:T(8,128)(2,1)S(1)}, u32[]{:S(2)}, u32[]{:S(2)}) %collective-permute-start.14) | collective-permute-done | bytes 139296 | tf_op jit(solution)/shard_map/ppermute | solution.py:325
  63.1 1.6 %collective-permute-done.15.b3 = bf16[32,2176]{1,0:T(8,128)(2,1)S(1)} collective-permute-done((bf16[32,2176]{1,0:T(8,128)(2,1)S(1)}, bf16[32,2176]{1,0:T(8,128)(2,1)S(1)}, u32[]{:S(2)}, u32[]{:S(2)}) %collective-permute-start.15) | collective-permute-done | bytes 139296 | tf_op jit(solution)/shard_map/ppermute | solution.py:325
  64.8 0.4 shard_map.101.refs_0_
  65.2 3.8 %collective-permute-done.6.refs_1_.b1 = bf16[32,2176]{1,0:T(8,128)(2,1)S(1)} collective-permute-done((bf16[32,2176]{1,0:T(8,128)(2,1)S(1)}, bf16[32,2176]{1,0:T(8,128)(2,1)S(1)}, u32[]{:S(2)}, u32[]{:S(2)}) %collective-permute-start.6) | collective-permute-done | bytes 139296 | tf_op jit(solution)/shard_map/ppermute | solution.py:325
  68.9 0.0 collective-permute-done.17.far_b.refs_1_
  68.9 0.1 shard_map.102
  69.1 1.6 %collective-permute-start.19 = (bf16[288,3200]{1,0:T(8,128)(2,1)S(1)}, bf16[288,3200]{1,0:T(8,128)(2,1)S(1)}, u32[]{:S(2)}, u32[]{:S(2)}) collective-permute-start(bf16[288,3200]{1,0:T(8,128)(2,1)S(1)} %shard_map.102), channel_id=1, source_target_pairs={{0,1},{1,0},{2,3},{3,2},{4,5},{5,4},{6,7},{7,6},{8,9},{9,8},{10,11... | collective-permute-start | bytes 5529608 | tf_op jit(solution)/shard_map/ppermute | solution.py:325
  70.7 0.3 collective-permute-start.18
  71.0 1.2 %collective-permute-start.16 = (bf16[32,4224]{1,0:T(8,128)(2,1)S(1)}, bf16[32,4224]{1,0:T(8,128)(2,1)S(1)}, u32[]{:S(2)}, u32[]{:S(2)}) collective-permute-start(bf16[32,4224]{1,0:T(8,128)(2,1)S(1)} %shard_map.101.refs_0_), channel_id=1, source_target_pairs={{0,16},{4,20},{8,24},{12,28},{16,0},{20,4},{24,8},{28,12},{1,17},{... | collective-permute-start | bytes 811016 | tf_op jit(solution)/shard_map/ppermute | solution.py:325
  72.2 1.2 %collective-permute-start.7 = (bf16[32,2176]{1,0:T(8,128)(2,1)S(1)}, bf16[32,2176]{1,0:T(8,128)(2,1)S(1)}, u32[]{:S(2)}, u32[]{:S(2)}) collective-permute-start(bf16[32,2176]{1,0:T(8,128)(2,1)S(1)} %get-tuple-element.51), channel_id=1, source_target_pairs={{0,8},{4,12},{8,0},{12,4},{16,24},{20,28},{24,16},{28,20},{1,9},{5... | collective-permute-start | bytes 417800 | tf_op jit(solution)/shard_map/ppermute | solution.py:325
  73.3 1.2 %collective-permute-start.8 = (bf16[32,2176]{1,0:T(8,128)(2,1)S(1)}, bf16[32,2176]{1,0:T(8,128)(2,1)S(1)}, u32[]{:S(2)}, u32[]{:S(2)}) collective-permute-start(bf16[32,2176]{1,0:T(8,128)(2,1)S(1)} %get-tuple-element.52), channel_id=1, source_target_pairs={{0,12},{4,8},{8,4},{12,0},{16,28},{20,24},{24,20},{28,16},{1,13},{... | collective-permute-start | bytes 417800 | tf_op jit(solution)/shard_map/ppermute | solution.py:325
  74.6 0.0 collective-permute-done.19.near_ref
  74.6 1.2 %shard_map.103 = (f32[512,768]{1,0:T(8,128)S(1)}, f32[512,384]{1,0:T(8,128)S(1)}) custom-call(bf16[144,1024]{1,0:T(8,128)(2,1)S(1)} %get-tuple-element.45.refs_0_.refs_2_.rows_a, bf16[144,1024]{1,0:T(8,128)(2,1)S(1)} %get-tuple-element.58.refs_2_.rows_b, bf16[288,3200]{1,0:T(8,128)(2,1)S(1)} %collective-permute-done.19.near_ref, ...), custom_call_target="tpu_custom_call" | custom-call | flops 679477248 | bytes 5455872 | tf_op jit(solution)/shard_map/pallas_call | solution.py:312
  75.8 4.9 %collective-permute-done.7.refs_3_.b2 = bf16[32,2176]{1,0:T(8,128)(2,1)S(1)} collective-permute-done((bf16[32,2176]{1,0:T(8,128)(2,1)S(1)}, bf16[32,2176]{1,0:T(8,128)(2,1)S(1)}, u32[]{:S(2)}, u32[]{:S(2)}) %collective-permute-start.7) | collective-permute-done | bytes 139296 | tf_op jit(solution)/shard_map/ppermute | solution.py:325
  80.7 3.0 %collective-permute-done.8.refs_4_.b3 = bf16[32,2176]{1,0:T(8,128)(2,1)S(1)} collective-permute-done((bf16[32,2176]{1,0:T(8,128)(2,1)S(1)}, bf16[32,2176]{1,0:T(8,128)(2,1)S(1)}, u32[]{:S(2)}, u32[]{:S(2)}) %collective-permute-start.8) | collective-permute-done | bytes 139296 | tf_op jit(solution)/shard_map/ppermute | solution.py:325
  83.7 2.4 %collective-permute-done.16.refs_2_.far_ref = bf16[32,4224]{1,0:T(8,128)(2,1)S(1)} collective-permute-done((bf16[32,4224]{1,0:T(8,128)(2,1)S(1)}, bf16[32,4224]{1,0:T(8,128)(2,1)S(1)}, u32[]{:S(2)}, u32[]{:S(2)}) %collective-permute-start.16) | collective-permute-done | bytes 270368 | tf_op jit(solution)/shard_map/ppermute | solution.py:325
  86.1 1.1 %collective-permute-done.18.refs_0_ = bf16[288,1152]{1,0:T(8,128)(2,1)S(1)} collective-permute-done((bf16[288,1152]{1,0:T(8,128)(2,1)S(1)}, bf16[288,1152]{1,0:T(8,128)(2,1)S(1)}, u32[]{:S(2)}, u32[]{:S(2)}) %collective-permute-start.18) | collective-permute-done | bytes 663584 | tf_op jit(solution)/shard_map/ppermute | solution.py:325
  87.2 0.8 collective-permute-start.20
  88.0 2.3 %shard_map.105 = (bf16[64,2048]{1,0:T(8,128)(2,1)}, bf16[4,64]{1,0:T(4,128)(2,1)}, f32[512,768]{1,0:T(8,128)S(1)}, f32[512,384]{1,0:T(8,128)S(1)}) custom-call(s32[8]{0:T(128)S(1)} %iota_xor_fusion.1.peer_ref, s32[4,64]{1,0:T(4,128)S(1)} %bitcast.8, f32[8,64]{1,0:T(8,128)S(1)} %get-tuple-element.39.w_ref, bf16[32,2176]{1,0:T(8,128)(2,1)S(1)} %get-tuple-element.49.b0, ...), custom_call_target="tpu_custom_call" | custom-call | flops 377487360 | bytes 7392768 | tf_op jit(solution)/shard_map/pallas_call | solution.py:312
  90.3 0.0 collective-permute-done.20.mid_ref
  90.3 1.8 %shard_map.106 = (f32[512,768]{1,0:T(8,128)}, f32[512,384]{1,0:T(8,128)}) custom-call(bf16[288,3200]{1,0:T(8,128)(2,1)S(1)} %collective-permute-done.19.near_ref, bf16[288,1152]{1,0:T(8,128)(2,1)S(1)} %collective-permute-done.20.mid_ref, f32[512,768]{1,0:T(8,128)S(1)} %get-tuple-element.70.in_part, f32[512,384]{1,0:T(8,128)S(1)} %get-tuple-element.71.out_part), custom_call_target="tpu_custom_call" | custom-call | flops 339738624 | bytes 4866048 | tf_op jit(solution)/shard_map/pallas_call | solution.py:312
  (3 shorter events, 0.0 us)
Async XLA Ops:
  0.6 3.6 %copy-start.3 = (bf16[64,4]{0,1:T(4,128)(2,1)S(1)}, bf16[64,4]{0,1:T(4,128)(2,1)}, u32[]{:S(2)}) copy-start(bf16[64,4]{0,1:T(4,128)(2,1)} %param.9) | copy-start | bytes 1540
  0.6 3.5 %copy-start.2 = (s32[64,4]{0,1:T(4,128)S(1)}, s32[64,4]{0,1:T(4,128)}, u32[]{:S(2)}) copy-start(s32[64,4]{0,1:T(4,128)} %param.8) | copy-start | bytes 3076
  0.7 3.5 %copy-start.1 = (bf16[64,2048]{1,0:T(8,128)(2,1)S(1)}, bf16[64,2048]{1,0:T(8,128)(2,1)}, u32[]{:S(2)}) copy-start(bf16[64,2048]{1,0:T(8,128)(2,1)} %dy_ref.1) | copy-start | bytes 786436
  0.7 3.5 %copy-start = (bf16[64,2048]{1,0:T(8,128)(2,1)S(1)}, bf16[64,2048]{1,0:T(8,128)(2,1)}, u32[]{:S(2)}) copy-start(bf16[64,2048]{1,0:T(8,128)(2,1)} %x_ref.1) | copy-start | bytes 786436
  2.1 32.7 %collective-permute-start.4 = (bf16[512,1152]{1,0:T(8,128)(2,1)S(1)}, bf16[512,1152]{1,0:T(8,128)(2,1)S(1)}, u32[]{:S(2)}, u32[]{:S(2)}) collective-permute-start(bf16[512,1152]{1,0:T(8,128)(2,1)S(1)} %pad_maximum_fusion.own_ref), channel_id=1, source_target_pairs={{0,2},{1,3},{2,0},{3,1},{4,6},{5,7},{6,4},{7,5},{8,10},{9,11},{10,... | collective-permute-start | bytes 3538952 | tf_op jit(solution)/shard_map/ppermute | solution.py:325
  4.8 28.4 %collective-permute-start.3 = (bf16[64,4224]{1,0:T(8,128)(2,1)S(1)}, bf16[64,4224]{1,0:T(8,128)(2,1)S(1)}, u32[]{:S(2)}, u32[]{:S(2)}) collective-permute-start(bf16[64,4224]{1,0:T(8,128)(2,1)S(1)} %get-tuple-element.40.joint_ref.refs_0_), channel_id=1, source_target_pairs={{0,16},{4,20},{8,24},{12,28},{16,0},{20,4},{24,8},{28,12},{1,17},{... | collective-permute-start | bytes 1622024 | tf_op jit(solution)/shard_map/ppermute | solution.py:325
  8.6 7.2 %collective-permute-start = (bf16[64,2176]{1,0:T(8,128)(2,1)}, bf16[64,2176]{1,0:T(8,128)(2,1)}, u32[]{:S(2)}, u32[]{:S(2)}) collective-permute-start(bf16[64,2176]{1,0:T(8,128)(2,1)} %get-tuple-element.41), channel_id=1, source_target_pairs={{0,4},{4,0},{8,12},{12,8},{16,20},{20,16},{24,28},{28,24},{1,5},{5... | collective-permute-start | bytes 835592 | tf_op jit(solution)/shard_map/ppermute | solution.py:325
  9.8 14.1 %collective-permute-start.1 = (bf16[64,2176]{1,0:T(8,128)(2,1)}, bf16[64,2176]{1,0:T(8,128)(2,1)}, u32[]{:S(2)}, u32[]{:S(2)}) collective-permute-start(bf16[64,2176]{1,0:T(8,128)(2,1)} %get-tuple-element.42), channel_id=1, source_target_pairs={{0,8},{4,12},{8,0},{12,4},{16,24},{20,28},{24,16},{28,20},{1,9},{5... | collective-permute-start | bytes 835592 | tf_op jit(solution)/shard_map/ppermute | solution.py:325
  11.1 22.0 %collective-permute-start.2 = (bf16[64,2176]{1,0:T(8,128)(2,1)}, bf16[64,2176]{1,0:T(8,128)(2,1)}, u32[]{:S(2)}, u32[]{:S(2)}) collective-permute-start(bf16[64,2176]{1,0:T(8,128)(2,1)} %get-tuple-element.43), channel_id=1, source_target_pairs={{0,12},{4,8},{8,4},{12,0},{16,28},{20,24},{24,20},{28,16},{1,13},{... | collective-permute-start | bytes 835592 | tf_op jit(solution)/shard_map/ppermute | solution.py:325
  35.5 6.7 %collective-permute-start.5 = (bf16[1024,1152]{1,0:T(8,128)(2,1)S(1)}, bf16[1024,1152]{1,0:T(8,128)(2,1)S(1)}, u32[]{:S(2)}, u32[]{:S(2)}) collective-permute-start(bf16[1024,1152]{1,0:T(8,128)(2,1)S(1)} %shard_map.97.refs_0_), channel_id=1, source_target_pairs={{0,1},{1,0},{2,3},{3,2},{4,5},{5,4},{6,7},{7,6},{8,9},{9,8},{10,11... | collective-permute-start | bytes 7077896 | tf_op jit(solution)/shard_map/ppermute | solution.py:325
  38.0 14.9 %collective-permute-start.12 = (bf16[144,2048]{1,0:T(8,128)(2,1)S(1)}, bf16[144,2048]{1,0:T(8,128)(2,1)S(1)}, u32[]{:S(2)}, u32[]{:S(2)}) collective-permute-start(bf16[144,2048]{1,0:T(8,128)(2,1)S(1)} %get-tuple-element.48.refs_4_), channel_id=1, source_target_pairs={{0,2},{1,3},{2,0},{3,1},{4,6},{5,7},{6,4},{7,5},{8,10},{9,11},{10,... | collective-permute-start | bytes 1769480 | tf_op jit(solution)/shard_map/ppermute | solution.py:325
  38.3 14.6 %collective-permute-start.9 = (bf16[64,2176]{1,0:T(8,128)(2,1)S(1)}, bf16[64,2176]{1,0:T(8,128)(2,1)S(1)}, u32[]{:S(2)}, u32[]{:S(2)}) collective-permute-start(bf16[64,2176]{1,0:T(8,128)(2,1)S(1)} %get-tuple-element.53), channel_id=1, source_target_pairs={{0,4},{4,0},{8,12},{12,8},{16,20},{20,16},{24,28},{28,24},{1,5},{5... | collective-permute-start | bytes 835592 | tf_op jit(solution)/shard_map/ppermute | solution.py:325
  39.5 13.5 %collective-permute-start.10 = (bf16[64,2176]{1,0:T(8,128)(2,1)S(1)}, bf16[64,2176]{1,0:T(8,128)(2,1)S(1)}, u32[]{:S(2)}, u32[]{:S(2)}) collective-permute-start(bf16[64,2176]{1,0:T(8,128)(2,1)S(1)} %get-tuple-element.54), channel_id=1, source_target_pairs={{0,8},{4,12},{8,0},{12,4},{16,24},{20,28},{24,16},{28,20},{1,9},{5... | collective-permute-start | bytes 835592 | tf_op jit(solution)/shard_map/ppermute | solution.py:325
  39.5 13.5 %collective-permute-start.11 = (bf16[64,2176]{1,0:T(8,128)(2,1)S(1)}, bf16[64,2176]{1,0:T(8,128)(2,1)S(1)}, u32[]{:S(2)}, u32[]{:S(2)}) collective-permute-start(bf16[64,2176]{1,0:T(8,128)(2,1)S(1)} %get-tuple-element.55), channel_id=1, source_target_pairs={{0,12},{4,8},{8,4},{12,0},{16,28},{20,24},{24,20},{28,16},{1,13},{... | collective-permute-start | bytes 835592 | tf_op jit(solution)/shard_map/ppermute | solution.py:325
  53.7 15.2 %collective-permute-start.17 = (bf16[144,2048]{1,0:T(8,128)(2,1)S(1)}, bf16[144,2048]{1,0:T(8,128)(2,1)S(1)}, u32[]{:S(2)}, u32[]{:S(2)}) collective-permute-start(bf16[144,2048]{1,0:T(8,128)(2,1)S(1)} %get-tuple-element.60.refs_4_), channel_id=1, source_target_pairs={{0,2},{1,3},{2,0},{3,1},{4,6},{5,7},{6,4},{7,5},{8,10},{9,11},{10,... | collective-permute-start | bytes 1769480 | tf_op jit(solution)/shard_map/ppermute | solution.py:325
  57.6 4.3 %collective-permute-start.13 = (bf16[32,2176]{1,0:T(8,128)(2,1)S(1)}, bf16[32,2176]{1,0:T(8,128)(2,1)S(1)}, u32[]{:S(2)}, u32[]{:S(2)}) collective-permute-start(bf16[32,2176]{1,0:T(8,128)(2,1)S(1)} %get-tuple-element.62), channel_id=1, source_target_pairs={{0,4},{4,0},{8,12},{12,8},{16,20},{20,16},{24,28},{28,24},{1,5},{5... | collective-permute-start | bytes 417800 | tf_op jit(solution)/shard_map/ppermute | solution.py:325
  58.9 4.2 %collective-permute-start.14 = (bf16[32,2176]{1,0:T(8,128)(2,1)S(1)}, bf16[32,2176]{1,0:T(8,128)(2,1)S(1)}, u32[]{:S(2)}, u32[]{:S(2)}) collective-permute-start(bf16[32,2176]{1,0:T(8,128)(2,1)S(1)} %get-tuple-element.63), channel_id=1, source_target_pairs={{0,8},{4,12},{8,0},{12,4},{16,24},{20,28},{24,16},{28,20},{1,9},{5... | collective-permute-start | bytes 417800 | tf_op jit(solution)/shard_map/ppermute | solution.py:325
  59.3 5.5 %collective-permute-start.15 = (bf16[32,2176]{1,0:T(8,128)(2,1)S(1)}, bf16[32,2176]{1,0:T(8,128)(2,1)S(1)}, u32[]{:S(2)}, u32[]{:S(2)}) collective-permute-start(bf16[32,2176]{1,0:T(8,128)(2,1)S(1)} %get-tuple-element.64), channel_id=1, source_target_pairs={{0,12},{4,8},{8,4},{12,0},{16,28},{20,24},{24,20},{28,16},{1,13},{... | collective-permute-start | bytes 417800 | tf_op jit(solution)/shard_map/ppermute | solution.py:325
  60.3 8.6 %collective-permute-start.6 = (bf16[32,2176]{1,0:T(8,128)(2,1)S(1)}, bf16[32,2176]{1,0:T(8,128)(2,1)S(1)}, u32[]{:S(2)}, u32[]{:S(2)}) collective-permute-start(bf16[32,2176]{1,0:T(8,128)(2,1)S(1)} %get-tuple-element.50), channel_id=1, source_target_pairs={{0,4},{4,0},{8,12},{12,8},{16,20},{20,16},{24,28},{28,24},{1,5},{5... | collective-permute-start | bytes 417800 | tf_op jit(solution)/shard_map/ppermute | solution.py:325
  69.1 5.5 %collective-permute-start.19 = (bf16[288,3200]{1,0:T(8,128)(2,1)S(1)}, bf16[288,3200]{1,0:T(8,128)(2,1)S(1)}, u32[]{:S(2)}, u32[]{:S(2)}) collective-permute-start(bf16[288,3200]{1,0:T(8,128)(2,1)S(1)} %shard_map.102), channel_id=1, source_target_pairs={{0,1},{1,0},{2,3},{3,2},{4,5},{5,4},{6,7},{7,6},{8,9},{9,8},{10,11... | collective-permute-start | bytes 5529608 | tf_op jit(solution)/shard_map/ppermute | solution.py:325
  70.7 16.5 %collective-permute-start.18 = (bf16[288,1152]{1,0:T(8,128)(2,1)S(1)}, bf16[288,1152]{1,0:T(8,128)(2,1)S(1)}, u32[]{:S(2)}, u32[]{:S(2)}) collective-permute-start(bf16[288,1152]{1,0:T(8,128)(2,1)S(1)} %get-tuple-element.65.mid_ref), channel_id=1, source_target_pairs={{0,2},{1,3},{2,0},{3,1},{4,6},{5,7},{6,4},{7,5},{8,10},{9,11},{10,... | collective-permute-start | bytes 1990664 | tf_op jit(solution)/shard_map/ppermute | solution.py:325
  71.0 15.1 %collective-permute-start.16 = (bf16[32,4224]{1,0:T(8,128)(2,1)S(1)}, bf16[32,4224]{1,0:T(8,128)(2,1)S(1)}, u32[]{:S(2)}, u32[]{:S(2)}) collective-permute-start(bf16[32,4224]{1,0:T(8,128)(2,1)S(1)} %shard_map.101.refs_0_), channel_id=1, source_target_pairs={{0,16},{4,20},{8,24},{12,28},{16,0},{20,4},{24,8},{28,12},{1,17},{... | collective-permute-start | bytes 811016 | tf_op jit(solution)/shard_map/ppermute | solution.py:325
  72.2 8.6 %collective-permute-start.7 = (bf16[32,2176]{1,0:T(8,128)(2,1)S(1)}, bf16[32,2176]{1,0:T(8,128)(2,1)S(1)}, u32[]{:S(2)}, u32[]{:S(2)}) collective-permute-start(bf16[32,2176]{1,0:T(8,128)(2,1)S(1)} %get-tuple-element.51), channel_id=1, source_target_pairs={{0,8},{4,12},{8,0},{12,4},{16,24},{20,28},{24,16},{28,20},{1,9},{5... | collective-permute-start | bytes 417800 | tf_op jit(solution)/shard_map/ppermute | solution.py:325
  73.3 10.3 %collective-permute-start.8 = (bf16[32,2176]{1,0:T(8,128)(2,1)S(1)}, bf16[32,2176]{1,0:T(8,128)(2,1)S(1)}, u32[]{:S(2)}, u32[]{:S(2)}) collective-permute-start(bf16[32,2176]{1,0:T(8,128)(2,1)S(1)} %get-tuple-element.52), channel_id=1, source_target_pairs={{0,12},{4,8},{8,4},{12,0},{16,28},{20,24},{24,20},{28,16},{1,13},{... | collective-permute-start | bytes 417800 | tf_op jit(solution)/shard_map/ppermute | solution.py:325
  87.2 3.1 %collective-permute-start.20 = (bf16[288,1152]{1,0:T(8,128)(2,1)S(1)}, bf16[288,1152]{1,0:T(8,128)(2,1)S(1)}, u32[]{:S(2)}, u32[]{:S(2)}) collective-permute-start(bf16[288,1152]{1,0:T(8,128)(2,1)S(1)} %shard_map.104.refs_2_), channel_id=1, source_target_pairs={{0,1},{1,0},{2,3},{3,2},{4,5},{5,4},{6,7},{7,6},{8,9},{9,8},{10,11... | collective-permute-start | bytes 1990664 | tf_op jit(solution)/shard_map/ppermute | solution.py:325

commit v10 on v9

--- a/solution.py
+++ b/solution.py
@@ -438,7 +438,7 @@
         [((2 * rows, 4 * depth + 3 * hidden_width), BF16)],
         [],
         [own_slices[1], own_far, far_slices[1], far_far, mid],
-        [partial, near_back[1]],
+        [partial],
         [],
         0,
     )
@@ -460,7 +460,7 @@
         [(mid_far.shape, BF16)],
         [],
         [],
-        [mid_far, first[1], far_partial, *near_back[2:]],
+        [mid_far, first[1], far_partial, *near_back[1:]],
         [],
         0,
         1,

time: 92.2 us -> 92.4 us (level)
  starting transfers between devices: 24.2 us -> 26.1 us
  waiting for transfers between devices: 49.7 us -> 47.9 us
    ppermute x21, starting transfers between devices: 24.2 us -> 26.1 us  [swap(): lax.ppermute(value, axis, [(i, i ^ mask) for i in range(lax.axis_size(axi...]
    ppermute x21, waiting for transfers between devices: 49.7 us -> 47.9 us  [swap(): lax.ppermute(value, axis, [(i, i ^ mask) for i in range(lax.axis_size(axi...]
  transfers between devices with their start and end apart: 21 -> 21, of which waited for: 14 -> 15; matrix products, arithmetic and copies ran while one was open for 0% -> 0% of each run, Pallas kernels for 14% -> 14%
where the time goes in v10:
time: 92.4 us; the launch traced here: 92.2 us
  waiting for transfers between devices  47.9 us (52%)
  starting transfers between devices  26.1 us (28%)
  Pallas kernels  16 us (17%)
  other arithmetic  1.41 us (2%)
    ppermute x21, waiting for transfers between devices, swap(): lax.ppermute(value, axis, [(i, i ^ mask) for i in range(lax.axis_size(axi...  47.9 us
    ppermute x21, starting transfers between devices, swap(): lax.ppermute(value, axis, [(i, i ^ mask) for i in range(lax.axis_size(axi...  26.1 us
    pallas_call x14, Pallas kernels, call(): pl.pallas_call(kernel, out_shape=tuple(outs), in_specs=[on_smem] * len(sm...  16 us
  transfers between devices with their start and end apart: 21, of which 15 were waited for; matrix products, arithmetic and copies ran while one was open for 0% of the time, Pallas kernels for 14%

profile of v10, /device:TPU:1, one launch (start us, length us, event | category | flops | bytes accessed | tf_op | source)
XLA Modules:
  0.0 92.2 jit_solution(8736177911074181180)
XLA Ops:
  0.6 0.0 copy-start.3
  0.6 0.0 copy-start.2
  0.7 0.0 copy-start.1
  0.7 0.0 copy-start
  0.7 1.4 %pad_maximum_fusion.own_ref = bf16[512,1152]{1,0:T(8,128)(2,1)S(1)} fusion(bf16[512,384]{1,0:T(8,128)(2,1)} %bitcast.11, bf16[512,768]{1,0:T(8,128)(2,1)} %bitcast.10), kind=kLoop, calls=%fused_computation | loop fusion | flops 2359296 | bytes 2359296 | tf_op jit(solution)/shard_map/concatenate | solution.py:354
  2.1 2.1 %collective-permute-start.4 = (bf16[512,1152]{1,0:T(8,128)(2,1)S(1)}, bf16[512,1152]{1,0:T(8,128)(2,1)S(1)}, u32[]{:S(2)}, u32[]{:S(2)}) collective-permute-start(bf16[512,1152]{1,0:T(8,128)(2,1)S(1)} %pad_maximum_fusion.own_ref), channel_id=1, source_target_pairs={{0,2},{1,3},{2,0},{3,1},{4,6},{5,7},{6,4},{7,5},{8,10},{9,11},{10,... | collective-permute-start | bytes 3538952 | tf_op jit(solution)/shard_map/ppermute | solution.py:325
  4.2 0.0 copy-done.3
  4.2 0.0 copy-done.2
  4.2 0.0 copy-done.1
  4.2 0.0 copy-done
  4.2 0.6 shard_map.93
  4.8 2.4 %collective-permute-start.3 = (bf16[64,4224]{1,0:T(8,128)(2,1)S(1)}, bf16[64,4224]{1,0:T(8,128)(2,1)S(1)}, u32[]{:S(2)}, u32[]{:S(2)}) collective-permute-start(bf16[64,4224]{1,0:T(8,128)(2,1)S(1)} %get-tuple-element.40.joint_ref.refs_0_), channel_id=1, source_target_pairs={{0,16},{4,20},{8,24},{12,28},{16,0},{20,4},{24,8},{28,12},{1,17},{... | collective-permute-start | bytes 1622024 | tf_op jit(solution)/shard_map/ppermute | solution.py:325
  7.2 1.4 %shard_map.94 = (bf16[64,2176]{1,0:T(8,128)(2,1)}, bf16[64,2176]{1,0:T(8,128)(2,1)}, bf16[64,2176]{1,0:T(8,128)(2,1)}) custom-call(bf16[64,4224]{1,0:T(8,128)(2,1)S(1)} %get-tuple-element.40.joint_ref.refs_0_), custom_call_target="tpu_custom_call" | custom-call | flops 58720256 | bytes 1376256 | tf_op jit(solution)/shard_map/pallas_call | solution.py:312
  8.6 1.2 %collective-permute-start = (bf16[64,2176]{1,0:T(8,128)(2,1)}, bf16[64,2176]{1,0:T(8,128)(2,1)}, u32[]{:S(2)}, u32[]{:S(2)}) collective-permute-start(bf16[64,2176]{1,0:T(8,128)(2,1)} %get-tuple-element.41), channel_id=1, source_target_pairs={{0,4},{4,0},{8,12},{12,8},{16,20},{20,16},{24,28},{28,24},{1,5},{5... | collective-permute-start | bytes 835592 | tf_op jit(solution)/shard_map/ppermute | solution.py:325
  9.8 1.3 %collective-permute-start.1 = (bf16[64,2176]{1,0:T(8,128)(2,1)}, bf16[64,2176]{1,0:T(8,128)(2,1)}, u32[]{:S(2)}, u32[]{:S(2)}) collective-permute-start(bf16[64,2176]{1,0:T(8,128)(2,1)} %get-tuple-element.42), channel_id=1, source_target_pairs={{0,8},{4,12},{8,0},{12,4},{16,24},{20,28},{24,16},{28,20},{1,9},{5... | collective-permute-start | bytes 835592 | tf_op jit(solution)/shard_map/ppermute | solution.py:325
  11.1 0.1 collective-permute-start.2
  11.2 4.6 %collective-permute-done.refs_1_ = bf16[64,2176]{1,0:T(8,128)(2,1)} collective-permute-done((bf16[64,2176]{1,0:T(8,128)(2,1)}, bf16[64,2176]{1,0:T(8,128)(2,1)}, u32[]{:S(2)}, u32[]{:S(2)}) %collective-permute-start) | collective-permute-done | bytes 278560 | tf_op jit(solution)/shard_map/ppermute | solution.py:325
  15.8 8.1 %collective-permute-done.1.refs_2_ = bf16[64,2176]{1,0:T(8,128)(2,1)} collective-permute-done((bf16[64,2176]{1,0:T(8,128)(2,1)}, bf16[64,2176]{1,0:T(8,128)(2,1)}, u32[]{:S(2)}, u32[]{:S(2)}) %collective-permute-start.1) | collective-permute-done | bytes 278560 | tf_op jit(solution)/shard_map/ppermute | solution.py:325
  23.9 9.2 %collective-permute-done.2.refs_3_ = bf16[64,2176]{1,0:T(8,128)(2,1)} collective-permute-done((bf16[64,2176]{1,0:T(8,128)(2,1)}, bf16[64,2176]{1,0:T(8,128)(2,1)}, u32[]{:S(2)}, u32[]{:S(2)}) %collective-permute-start.2) | collective-permute-done | bytes 278560 | tf_op jit(solution)/shard_map/ppermute | solution.py:325
  33.2 0.0 collective-permute-done.3.refs_4_.joint_ref
  33.2 1.6 %shard_map.95 = (bf16[144,1024]{1,0:T(8,128)(2,1)S(1)}, bf16[144,1024]{1,0:T(8,128)(2,1)S(1)}, bf16[144,2048]{1,0:T(8,128)(2,1)S(1)}, f32[144,128]{1,0:T(8,128)S(1)}) custom-call(s32[4]{0:T(128)S(1)} %iota_xor_fusion.place_ref, bf16[64,4224]{1,0:T(8,128)(2,1)S(1)} %get-tuple-element.40.joint_ref.refs_0_, bf16[64,2176]{1,0:T(8,128)(2,1)} %collective-permute-done.refs_1_, ...), custom_call_target="tpu_custom_call" | custom-call | bytes 2629632 | tf_op jit(solution)/shard_map/pallas_call | solution.py:312
  34.8 0.0 collective-permute-done.4.refs_1_.far_ref
  34.8 0.6 shard_map.96
  35.4 0.2 shard_map.97.refs_0_
  35.5 2.5 %collective-permute-start.5 = (bf16[1024,1152]{1,0:T(8,128)(2,1)S(1)}, bf16[1024,1152]{1,0:T(8,128)(2,1)S(1)}, u32[]{:S(2)}, u32[]{:S(2)}) collective-permute-start(bf16[1024,1152]{1,0:T(8,128)(2,1)S(1)} %shard_map.97.refs_0_), channel_id=1, source_target_pairs={{0,1},{1,0},{2,3},{3,2},{4,5},{5,4},{6,7},{7,6},{8,9},{9,8},{10,11... | collective-permute-start | bytes 7077896 | tf_op jit(solution)/shard_map/ppermute | solution.py:325
  38.0 0.3 collective-permute-start.12
  38.3 1.2 %collective-permute-start.9 = (bf16[64,2176]{1,0:T(8,128)(2,1)S(1)}, bf16[64,2176]{1,0:T(8,128)(2,1)S(1)}, u32[]{:S(2)}, u32[]{:S(2)}) collective-permute-start(bf16[64,2176]{1,0:T(8,128)(2,1)S(1)} %get-tuple-element.53), channel_id=1, source_target_pairs={{0,4},{4,0},{8,12},{12,8},{16,20},{20,16},{24,28},{28,24},{1,5},{5... | collective-permute-start | bytes 835592 | tf_op jit(solution)/shard_map/ppermute | solution.py:325
  39.5 0.0 collective-permute-start.10
  39.5 1.5 %collective-permute-start.11 = (bf16[64,2176]{1,0:T(8,128)(2,1)S(1)}, bf16[64,2176]{1,0:T(8,128)(2,1)S(1)}, u32[]{:S(2)}, u32[]{:S(2)}) collective-permute-start(bf16[64,2176]{1,0:T(8,128)(2,1)S(1)} %get-tuple-element.55), channel_id=1, source_target_pairs={{0,12},{4,8},{8,4},{12,0},{16,28},{20,24},{24,20},{28,16},{1,13},{... | collective-permute-start | bytes 835592 | tf_op jit(solution)/shard_map/ppermute | solution.py:325
  41.0 1.2 %collective-permute-done.5.refs_1_ = bf16[1024,1152]{1,0:T(8,128)(2,1)S(1)} collective-permute-done((bf16[1024,1152]{1,0:T(8,128)(2,1)S(1)}, bf16[1024,1152]{1,0:T(8,128)(2,1)S(1)}, u32[]{:S(2)}, u32[]{:S(2)}) %collective-permute-start.5) | collective-permute-done | bytes 2359328 | tf_op jit(solution)/shard_map/ppermute | solution.py:325
  42.2 2.6 %shard_map.98 = (bf16[144,1152]{1,0:T(8,128)(2,1)S(1)}, bf16[32,2176]{1,0:T(8,128)(2,1)S(1)}, bf16[32,2176]{1,0:T(8,128)(2,1)S(1)}, bf16[32,2176]{1,0:T(8,128)(2,1)S(1)}, bf16[32,2176]{1,0:T(8,128)(2,1)S(1)}) custom-call(s32[4]{0:T(128)S(1)} %iota_xor_fusion.place_ref, f32[144,128]{1,0:T(8,128)S(1)} %get-tuple-element.44.w_ref, ...), custom_call_target="tpu_custom_call" | custom-call | flops 1132462080 | bytes 6860800 | tf_op jit(solution)/shard_map/pallas_call | solution.py:312
  44.8 8.1 %collective-permute-done.12.refs_5_.far_a.refs_0_ = bf16[144,2048]{1,0:T(8,128)(2,1)S(1)} collective-permute-done((bf16[144,2048]{1,0:T(8,128)(2,1)S(1)}, bf16[144,2048]{1,0:T(8,128)(2,1)S(1)}, u32[]{:S(2)}, u32[]{:S(2)}) %collective-permute-start.12) | collective-permute-done | bytes 589856 | tf_op jit(solution)/shard_map/ppermute | solution.py:325
  53.0 0.0 collective-permute-done.9.refs_1_
  53.0 0.0 collective-permute-done.10.refs_2_
  53.0 0.1 collective-permute-done.11.refs_3_
  53.1 0.7 shard_map.99
  53.7 1.3 %collective-permute-start.17 = (bf16[144,2048]{1,0:T(8,128)(2,1)S(1)}, bf16[144,2048]{1,0:T(8,128)(2,1)S(1)}, u32[]{:S(2)}, u32[]{:S(2)}) collective-permute-start(bf16[144,2048]{1,0:T(8,128)(2,1)S(1)} %get-tuple-element.60.refs_4_), channel_id=1, source_target_pairs={{0,2},{1,3},{2,0},{3,1},{4,6},{5,7},{6,4},{7,5},{8,10},{9,11},{10,... | collective-permute-start | bytes 1769480 | tf_op jit(solution)/shard_map/ppermute | solution.py:325
  55.0 2.6 %shard_map.100 = (bf16[288,1152]{1,0:T(8,128)(2,1)S(1)}, bf16[32,2176]{1,0:T(8,128)(2,1)S(1)}, bf16[32,2176]{1,0:T(8,128)(2,1)S(1)}, bf16[32,2176]{1,0:T(8,128)(2,1)S(1)}, bf16[32,2176]{1,0:T(8,128)(2,1)S(1)}) custom-call(s32[4]{0:T(128)S(1)} %iota_xor_fusion.place_ref, f32[144,128]{1,0:T(8,128)S(1)} %get-tuple-element.57.w_ref, ...), custom_call_target="tpu_custom_call" | custom-call | flops 1132462080 | bytes 7524352 | tf_op jit(solution)/shard_map/pallas_call | solution.py:312
  57.6 1.3 %collective-permute-start.13 = (bf16[32,2176]{1,0:T(8,128)(2,1)S(1)}, bf16[32,2176]{1,0:T(8,128)(2,1)S(1)}, u32[]{:S(2)}, u32[]{:S(2)}) collective-permute-start(bf16[32,2176]{1,0:T(8,128)(2,1)S(1)} %get-tuple-element.62), channel_id=1, source_target_pairs={{0,4},{4,0},{8,12},{12,8},{16,20},{20,16},{24,28},{28,24},{1,5},{5... | collective-permute-start | bytes 417800 | tf_op jit(solution)/shard_map/ppermute | solution.py:325
  58.9 0.3 collective-permute-start.14
  59.3 1.1 %collective-permute-start.15 = (bf16[32,2176]{1,0:T(8,128)(2,1)S(1)}, bf16[32,2176]{1,0:T(8,128)(2,1)S(1)}, u32[]{:S(2)}, u32[]{:S(2)}) collective-permute-start(bf16[32,2176]{1,0:T(8,128)(2,1)S(1)} %get-tuple-element.64), channel_id=1, source_target_pairs={{0,12},{4,8},{8,4},{12,0},{16,28},{20,24},{24,20},{28,16},{1,13},{... | collective-permute-start | bytes 417800 | tf_op jit(solution)/shard_map/ppermute | solution.py:325
  60.3 1.6 %collective-permute-done.13.b1 = bf16[32,2176]{1,0:T(8,128)(2,1)S(1)} collective-permute-done((bf16[32,2176]{1,0:T(8,128)(2,1)S(1)}, bf16[32,2176]{1,0:T(8,128)(2,1)S(1)}, u32[]{:S(2)}, u32[]{:S(2)}) %collective-permute-start.13) | collective-permute-done | bytes 139296 | tf_op jit(solution)/shard_map/ppermute | solution.py:325
  61.9 1.2 %collective-permute-done.14.b2 = bf16[32,2176]{1,0:T(8,128)(2,1)S(1)} collective-permute-done((bf16[32,2176]{1,0:T(8,128)(2,1)S(1)}, bf16[32,2176]{1,0:T(8,128)(2,1)S(1)}, u32[]{:S(2)}, u32[]{:S(2)}) %collective-permute-start.14) | collective-permute-done | bytes 139296 | tf_op jit(solution)/shard_map/ppermute | solution.py:325
  63.1 1.6 %collective-permute-done.15.b3 = bf16[32,2176]{1,0:T(8,128)(2,1)S(1)} collective-permute-done((bf16[32,2176]{1,0:T(8,128)(2,1)S(1)}, bf16[32,2176]{1,0:T(8,128)(2,1)S(1)}, u32[]{:S(2)}, u32[]{:S(2)}) %collective-permute-start.15) | collective-permute-done | bytes 139296 | tf_op jit(solution)/shard_map/ppermute | solution.py:325
  64.8 0.4 shard_map.101.refs_0_
  65.2 1.9 %collective-permute-done.17.far_b.refs_1_ = bf16[144,2048]{1,0:T(8,128)(2,1)S(1)} collective-permute-done((bf16[144,2048]{1,0:T(8,128)(2,1)S(1)}, bf16[144,2048]{1,0:T(8,128)(2,1)S(1)}, u32[]{:S(2)}, u32[]{:S(2)}) %collective-permute-start.17) | collective-permute-done | bytes 589856 | tf_op jit(solution)/shard_map/ppermute | solution.py:325
  67.1 0.1 shard_map.102
  67.2 2.5 %collective-permute-start.19 = (bf16[288,3200]{1,0:T(8,128)(2,1)S(1)}, bf16[288,3200]{1,0:T(8,128)(2,1)S(1)}, u32[]{:S(2)}, u32[]{:S(2)}) collective-permute-start(bf16[288,3200]{1,0:T(8,128)(2,1)S(1)} %shard_map.102), channel_id=1, source_target_pairs={{0,1},{1,0},{2,3},{3,2},{4,5},{5,4},{6,7},{7,6},{8,9},{9,8},{10,11... | collective-permute-start | bytes 5529608 | tf_op jit(solution)/shard_map/ppermute | solution.py:325
  69.7 1.2 %collective-permute-start.18 = (bf16[288,1152]{1,0:T(8,128)(2,1)S(1)}, bf16[288,1152]{1,0:T(8,128)(2,1)S(1)}, u32[]{:S(2)}, u32[]{:S(2)}) collective-permute-start(bf16[288,1152]{1,0:T(8,128)(2,1)S(1)} %get-tuple-element.65.mid_ref), channel_id=1, source_target_pairs={{0,2},{1,3},{2,0},{3,1},{4,6},{5,7},{6,4},{7,5},{8,10},{9,11},{10,... | collective-permute-start | bytes 1990664 | tf_op jit(solution)/shard_map/ppermute | solution.py:325
  70.9 1.2 %collective-permute-start.16 = (bf16[32,4224]{1,0:T(8,128)(2,1)S(1)}, bf16[32,4224]{1,0:T(8,128)(2,1)S(1)}, u32[]{:S(2)}, u32[]{:S(2)}) collective-permute-start(bf16[32,4224]{1,0:T(8,128)(2,1)S(1)} %shard_map.101.refs_0_), channel_id=1, source_target_pairs={{0,16},{4,20},{8,24},{12,28},{16,0},{20,4},{24,8},{28,12},{1,17},{... | collective-permute-start | bytes 811016 | tf_op jit(solution)/shard_map/ppermute | solution.py:325
  72.2 1.2 %collective-permute-start.6 = (bf16[32,2176]{1,0:T(8,128)(2,1)S(1)}, bf16[32,2176]{1,0:T(8,128)(2,1)S(1)}, u32[]{:S(2)}, u32[]{:S(2)}) collective-permute-start(bf16[32,2176]{1,0:T(8,128)(2,1)S(1)} %get-tuple-element.50), channel_id=1, source_target_pairs={{0,4},{4,0},{8,12},{12,8},{16,20},{20,16},{24,28},{28,24},{1,5},{5... | collective-permute-start | bytes 417800 | tf_op jit(solution)/shard_map/ppermute | solution.py:325
  73.4 1.1 %collective-permute-start.7 = (bf16[32,2176]{1,0:T(8,128)(2,1)S(1)}, bf16[32,2176]{1,0:T(8,128)(2,1)S(1)}, u32[]{:S(2)}, u32[]{:S(2)}) collective-permute-start(bf16[32,2176]{1,0:T(8,128)(2,1)S(1)} %get-tuple-element.51), channel_id=1, source_target_pairs={{0,8},{4,12},{8,0},{12,4},{16,24},{20,28},{24,16},{28,20},{1,9},{5... | collective-permute-start | bytes 417800 | tf_op jit(solution)/shard_map/ppermute | solution.py:325
  74.5 0.0 collective-permute-done.19.near_ref
  74.6 0.3 collective-permute-start.8
  74.8 1.2 %shard_map.103 = (f32[512,768]{1,0:T(8,128)S(1)}, f32[512,384]{1,0:T(8,128)S(1)}) custom-call(bf16[144,1024]{1,0:T(8,128)(2,1)S(1)} %get-tuple-element.45.refs_0_.refs_2_.rows_a, bf16[144,1024]{1,0:T(8,128)(2,1)S(1)} %get-tuple-element.58.refs_2_.rows_b, bf16[288,3200]{1,0:T(8,128)(2,1)S(1)} %collective-permute-done.19.near_ref, ...), custom_call_target="tpu_custom_call" | custom-call | flops 679477248 | bytes 5455872 | tf_op jit(solution)/shard_map/pallas_call | solution.py:312
  76.0 0.7 collective-permute-done.6.refs_3_.b1
  76.8 4.0 %collective-permute-done.7.refs_4_.b2 = bf16[32,2176]{1,0:T(8,128)(2,1)S(1)} collective-permute-done((bf16[32,2176]{1,0:T(8,128)(2,1)S(1)}, bf16[32,2176]{1,0:T(8,128)(2,1)S(1)}, u32[]{:S(2)}, u32[]{:S(2)}) %collective-permute-start.7) | collective-permute-done | bytes 139296 | tf_op jit(solution)/shard_map/ppermute | solution.py:325
  80.7 3.0 %collective-permute-done.8.refs_5_.b3 = bf16[32,2176]{1,0:T(8,128)(2,1)S(1)} collective-permute-done((bf16[32,2176]{1,0:T(8,128)(2,1)S(1)}, bf16[32,2176]{1,0:T(8,128)(2,1)S(1)}, u32[]{:S(2)}, u32[]{:S(2)}) %collective-permute-start.8) | collective-permute-done | bytes 139296 | tf_op jit(solution)/shard_map/ppermute | solution.py:325
  83.7 2.3 %collective-permute-done.16.refs_2_.far_ref = bf16[32,4224]{1,0:T(8,128)(2,1)S(1)} collective-permute-done((bf16[32,4224]{1,0:T(8,128)(2,1)S(1)}, bf16[32,4224]{1,0:T(8,128)(2,1)S(1)}, u32[]{:S(2)}, u32[]{:S(2)}) %collective-permute-start.16) | collective-permute-done | bytes 270368 | tf_op jit(solution)/shard_map/ppermute | solution.py:325
  86.0 0.2 collective-permute-done.18.refs_0_
  86.2 1.9 %collective-permute-start.20 = (bf16[288,1152]{1,0:T(8,128)(2,1)S(1)}, bf16[288,1152]{1,0:T(8,128)(2,1)S(1)}, u32[]{:S(2)}, u32[]{:S(2)}) collective-permute-start(bf16[288,1152]{1,0:T(8,128)(2,1)S(1)} %shard_map.104.refs_2_), channel_id=1, source_target_pairs={{0,1},{1,0},{2,3},{3,2},{4,5},{5,4},{6,7},{7,6},{8,9},{9,8},{10,11... | collective-permute-start | bytes 1990664 | tf_op jit(solution)/shard_map/ppermute | solution.py:325
  88.1 2.3 %shard_map.105 = (bf16[64,2048]{1,0:T(8,128)(2,1)}, bf16[4,64]{1,0:T(4,128)(2,1)}, f32[512,768]{1,0:T(8,128)S(1)}, f32[512,384]{1,0:T(8,128)S(1)}) custom-call(s32[8]{0:T(128)S(1)} %iota_xor_fusion.1.peer_ref, s32[4,64]{1,0:T(4,128)S(1)} %bitcast.8, f32[8,64]{1,0:T(8,128)S(1)} %get-tuple-element.39.w_ref, bf16[32,2176]{1,0:T(8,128)(2,1)S(1)} %get-tuple-element.49.b0, ...), custom_call_target="tpu_custom_call" | custom-call | flops 377487360 | bytes 7392768 | tf_op jit(solution)/shard_map/pallas_call | solution.py:312
  90.4 0.0 collective-permute-done.20.mid_ref
  90.4 1.8 %shard_map.106 = (f32[512,768]{1,0:T(8,128)}, f32[512,384]{1,0:T(8,128)}) custom-call(bf16[288,3200]{1,0:T(8,128)(2,1)S(1)} %collective-permute-done.19.near_ref, bf16[288,1152]{1,0:T(8,128)(2,1)S(1)} %collective-permute-done.20.mid_ref, f32[512,768]{1,0:T(8,128)S(1)} %get-tuple-element.70.in_part, f32[512,384]{1,0:T(8,128)S(1)} %get-tuple-element.71.out_part), custom_call_target="tpu_custom_call" | custom-call | flops 339738624 | bytes 4866048 | tf_op jit(solution)/shard_map/pallas_call | solution.py:312
  (3 shorter events, 0.0 us)
Async XLA Ops:
  0.6 3.6 %copy-start.3 = (bf16[64,4]{0,1:T(4,128)(2,1)S(1)}, bf16[64,4]{0,1:T(4,128)(2,1)}, u32[]{:S(2)}) copy-start(bf16[64,4]{0,1:T(4,128)(2,1)} %param.9) | copy-start | bytes 1540
  0.6 3.5 %copy-start.2 = (s32[64,4]{0,1:T(4,128)S(1)}, s32[64,4]{0,1:T(4,128)}, u32[]{:S(2)}) copy-start(s32[64,4]{0,1:T(4,128)} %param.8) | copy-start | bytes 3076
  0.7 3.5 %copy-start.1 = (bf16[64,2048]{1,0:T(8,128)(2,1)S(1)}, bf16[64,2048]{1,0:T(8,128)(2,1)}, u32[]{:S(2)}) copy-start(bf16[64,2048]{1,0:T(8,128)(2,1)} %dy_ref.1) | copy-start | bytes 786436
  0.7 3.5 %copy-start = (bf16[64,2048]{1,0:T(8,128)(2,1)S(1)}, bf16[64,2048]{1,0:T(8,128)(2,1)}, u32[]{:S(2)}) copy-start(bf16[64,2048]{1,0:T(8,128)(2,1)} %x_ref.1) | copy-start | bytes 786436
  2.1 32.7 %collective-permute-start.4 = (bf16[512,1152]{1,0:T(8,128)(2,1)S(1)}, bf16[512,1152]{1,0:T(8,128)(2,1)S(1)}, u32[]{:S(2)}, u32[]{:S(2)}) collective-permute-start(bf16[512,1152]{1,0:T(8,128)(2,1)S(1)} %pad_maximum_fusion.own_ref), channel_id=1, source_target_pairs={{0,2},{1,3},{2,0},{3,1},{4,6},{5,7},{6,4},{7,5},{8,10},{9,11},{10,... | collective-permute-start | bytes 3538952 | tf_op jit(solution)/shard_map/ppermute | solution.py:325
  4.8 28.4 %collective-permute-start.3 = (bf16[64,4224]{1,0:T(8,128)(2,1)S(1)}, bf16[64,4224]{1,0:T(8,128)(2,1)S(1)}, u32[]{:S(2)}, u32[]{:S(2)}) collective-permute-start(bf16[64,4224]{1,0:T(8,128)(2,1)S(1)} %get-tuple-element.40.joint_ref.refs_0_), channel_id=1, source_target_pairs={{0,16},{4,20},{8,24},{12,28},{16,0},{20,4},{24,8},{28,12},{1,17},{... | collective-permute-start | bytes 1622024 | tf_op jit(solution)/shard_map/ppermute | solution.py:325
  8.6 7.2 %collective-permute-start = (bf16[64,2176]{1,0:T(8,128)(2,1)}, bf16[64,2176]{1,0:T(8,128)(2,1)}, u32[]{:S(2)}, u32[]{:S(2)}) collective-permute-start(bf16[64,2176]{1,0:T(8,128)(2,1)} %get-tuple-element.41), channel_id=1, source_target_pairs={{0,4},{4,0},{8,12},{12,8},{16,20},{20,16},{24,28},{28,24},{1,5},{5... | collective-permute-start | bytes 835592 | tf_op jit(solution)/shard_map/ppermute | solution.py:325
  9.8 14.1 %collective-permute-start.1 = (bf16[64,2176]{1,0:T(8,128)(2,1)}, bf16[64,2176]{1,0:T(8,128)(2,1)}, u32[]{:S(2)}, u32[]{:S(2)}) collective-permute-start(bf16[64,2176]{1,0:T(8,128)(2,1)} %get-tuple-element.42), channel_id=1, source_target_pairs={{0,8},{4,12},{8,0},{12,4},{16,24},{20,28},{24,16},{28,20},{1,9},{5... | collective-permute-start | bytes 835592 | tf_op jit(solution)/shard_map/ppermute | solution.py:325
  11.1 22.0 %collective-permute-start.2 = (bf16[64,2176]{1,0:T(8,128)(2,1)}, bf16[64,2176]{1,0:T(8,128)(2,1)}, u32[]{:S(2)}, u32[]{:S(2)}) collective-permute-start(bf16[64,2176]{1,0:T(8,128)(2,1)} %get-tuple-element.43), channel_id=1, source_target_pairs={{0,12},{4,8},{8,4},{12,0},{16,28},{20,24},{24,20},{28,16},{1,13},{... | collective-permute-start | bytes 835592 | tf_op jit(solution)/shard_map/ppermute | solution.py:325
  35.5 6.7 %collective-permute-start.5 = (bf16[1024,1152]{1,0:T(8,128)(2,1)S(1)}, bf16[1024,1152]{1,0:T(8,128)(2,1)S(1)}, u32[]{:S(2)}, u32[]{:S(2)}) collective-permute-start(bf16[1024,1152]{1,0:T(8,128)(2,1)S(1)} %shard_map.97.refs_0_), channel_id=1, source_target_pairs={{0,1},{1,0},{2,3},{3,2},{4,5},{5,4},{6,7},{7,6},{8,9},{9,8},{10,11... | collective-permute-start | bytes 7077896 | tf_op jit(solution)/shard_map/ppermute | solution.py:325
  38.0 14.9 %collective-permute-start.12 = (bf16[144,2048]{1,0:T(8,128)(2,1)S(1)}, bf16[144,2048]{1,0:T(8,128)(2,1)S(1)}, u32[]{:S(2)}, u32[]{:S(2)}) collective-permute-start(bf16[144,2048]{1,0:T(8,128)(2,1)S(1)} %get-tuple-element.48.refs_4_), channel_id=1, source_target_pairs={{0,2},{1,3},{2,0},{3,1},{4,6},{5,7},{6,4},{7,5},{8,10},{9,11},{10,... | collective-permute-start | bytes 1769480 | tf_op jit(solution)/shard_map/ppermute | solution.py:325
  38.3 14.6 %collective-permute-start.9 = (bf16[64,2176]{1,0:T(8,128)(2,1)S(1)}, bf16[64,2176]{1,0:T(8,128)(2,1)S(1)}, u32[]{:S(2)}, u32[]{:S(2)}) collective-permute-start(bf16[64,2176]{1,0:T(8,128)(2,1)S(1)} %get-tuple-element.53), channel_id=1, source_target_pairs={{0,4},{4,0},{8,12},{12,8},{16,20},{20,16},{24,28},{28,24},{1,5},{5... | collective-permute-start | bytes 835592 | tf_op jit(solution)/shard_map/ppermute | solution.py:325
  39.5 13.5 %collective-permute-start.10 = (bf16[64,2176]{1,0:T(8,128)(2,1)S(1)}, bf16[64,2176]{1,0:T(8,128)(2,1)S(1)}, u32[]{:S(2)}, u32[]{:S(2)}) collective-permute-start(bf16[64,2176]{1,0:T(8,128)(2,1)S(1)} %get-tuple-element.54), channel_id=1, source_target_pairs={{0,8},{4,12},{8,0},{12,4},{16,24},{20,28},{24,16},{28,20},{1,9},{5... | collective-permute-start | bytes 835592 | tf_op jit(solution)/shard_map/ppermute | solution.py:325
  39.5 13.5 %collective-permute-start.11 = (bf16[64,2176]{1,0:T(8,128)(2,1)S(1)}, bf16[64,2176]{1,0:T(8,128)(2,1)S(1)}, u32[]{:S(2)}, u32[]{:S(2)}) collective-permute-start(bf16[64,2176]{1,0:T(8,128)(2,1)S(1)} %get-tuple-element.55), channel_id=1, source_target_pairs={{0,12},{4,8},{8,4},{12,0},{16,28},{20,24},{24,20},{28,16},{1,13},{... | collective-permute-start | bytes 835592 | tf_op jit(solution)/shard_map/ppermute | solution.py:325
  53.7 13.4 %collective-permute-start.17 = (bf16[144,2048]{1,0:T(8,128)(2,1)S(1)}, bf16[144,2048]{1,0:T(8,128)(2,1)S(1)}, u32[]{:S(2)}, u32[]{:S(2)}) collective-permute-start(bf16[144,2048]{1,0:T(8,128)(2,1)S(1)} %get-tuple-element.60.refs_4_), channel_id=1, source_target_pairs={{0,2},{1,3},{2,0},{3,1},{4,6},{5,7},{6,4},{7,5},{8,10},{9,11},{10,... | collective-permute-start | bytes 1769480 | tf_op jit(solution)/shard_map/ppermute | solution.py:325
  57.6 4.3 %collective-permute-start.13 = (bf16[32,2176]{1,0:T(8,128)(2,1)S(1)}, bf16[32,2176]{1,0:T(8,128)(2,1)S(1)}, u32[]{:S(2)}, u32[]{:S(2)}) collective-permute-start(bf16[32,2176]{1,0:T(8,128)(2,1)S(1)} %get-tuple-element.62), channel_id=1, source_target_pairs={{0,4},{4,0},{8,12},{12,8},{16,20},{20,16},{24,28},{28,24},{1,5},{5... | collective-permute-start | bytes 417800 | tf_op jit(solution)/shard_map/ppermute | solution.py:325
  58.9 4.2 %collective-permute-start.14 = (bf16[32,2176]{1,0:T(8,128)(2,1)S(1)}, bf16[32,2176]{1,0:T(8,128)(2,1)S(1)}, u32[]{:S(2)}, u32[]{:S(2)}) collective-permute-start(bf16[32,2176]{1,0:T(8,128)(2,1)S(1)} %get-tuple-element.63), channel_id=1, source_target_pairs={{0,8},{4,12},{8,0},{12,4},{16,24},{20,28},{24,16},{28,20},{1,9},{5... | collective-permute-start | bytes 417800 | tf_op jit(solution)/shard_map/ppermute | solution.py:325
  59.3 5.5 %collective-permute-start.15 = (bf16[32,2176]{1,0:T(8,128)(2,1)S(1)}, bf16[32,2176]{1,0:T(8,128)(2,1)S(1)}, u32[]{:S(2)}, u32[]{:S(2)}) collective-permute-start(bf16[32,2176]{1,0:T(8,128)(2,1)S(1)} %get-tuple-element.64), channel_id=1, source_target_pairs={{0,12},{4,8},{8,4},{12,0},{16,28},{20,24},{24,20},{28,16},{1,13},{... | collective-permute-start | bytes 417800 | tf_op jit(solution)/shard_map/ppermute | solution.py:325
  67.2 7.3 %collective-permute-start.19 = (bf16[288,3200]{1,0:T(8,128)(2,1)S(1)}, bf16[288,3200]{1,0:T(8,128)(2,1)S(1)}, u32[]{:S(2)}, u32[]{:S(2)}) collective-permute-start(bf16[288,3200]{1,0:T(8,128)(2,1)S(1)} %shard_map.102), channel_id=1, source_target_pairs={{0,1},{1,0},{2,3},{3,2},{4,5},{5,4},{6,7},{7,6},{8,9},{9,8},{10,11... | collective-permute-start | bytes 5529608 | tf_op jit(solution)/shard_map/ppermute | solution.py:325
  69.7 16.5 %collective-permute-start.18 = (bf16[288,1152]{1,0:T(8,128)(2,1)S(1)}, bf16[288,1152]{1,0:T(8,128)(2,1)S(1)}, u32[]{:S(2)}, u32[]{:S(2)}) collective-permute-start(bf16[288,1152]{1,0:T(8,128)(2,1)S(1)} %get-tuple-element.65.mid_ref), channel_id=1, source_target_pairs={{0,2},{1,3},{2,0},{3,1},{4,6},{5,7},{6,4},{7,5},{8,10},{9,11},{10,... | collective-permute-start | bytes 1990664 | tf_op jit(solution)/shard_map/ppermute | solution.py:325
  70.9 15.1 %collective-permute-start.16 = (bf16[32,4224]{1,0:T(8,128)(2,1)S(1)}, bf16[32,4224]{1,0:T(8,128)(2,1)S(1)}, u32[]{:S(2)}, u32[]{:S(2)}) collective-permute-start(bf16[32,4224]{1,0:T(8,128)(2,1)S(1)} %shard_map.101.refs_0_), channel_id=1, source_target_pairs={{0,16},{4,20},{8,24},{12,28},{16,0},{20,4},{24,8},{28,12},{1,17},{... | collective-permute-start | bytes 811016 | tf_op jit(solution)/shard_map/ppermute | solution.py:325
  72.2 4.6 %collective-permute-start.6 = (bf16[32,2176]{1,0:T(8,128)(2,1)S(1)}, bf16[32,2176]{1,0:T(8,128)(2,1)S(1)}, u32[]{:S(2)}, u32[]{:S(2)}) collective-permute-start(bf16[32,2176]{1,0:T(8,128)(2,1)S(1)} %get-tuple-element.50), channel_id=1, source_target_pairs={{0,4},{4,0},{8,12},{12,8},{16,20},{20,16},{24,28},{28,24},{1,5},{5... | collective-permute-start | bytes 417800 | tf_op jit(solution)/shard_map/ppermute | solution.py:325
  73.4 7.3 %collective-permute-start.7 = (bf16[32,2176]{1,0:T(8,128)(2,1)S(1)}, bf16[32,2176]{1,0:T(8,128)(2,1)S(1)}, u32[]{:S(2)}, u32[]{:S(2)}) collective-permute-start(bf16[32,2176]{1,0:T(8,128)(2,1)S(1)} %get-tuple-element.51), channel_id=1, source_target_pairs={{0,8},{4,12},{8,0},{12,4},{16,24},{20,28},{24,16},{28,20},{1,9},{5... | collective-permute-start | bytes 417800 | tf_op jit(solution)/shard_map/ppermute | solution.py:325
  74.6 9.1 %collective-permute-start.8 = (bf16[32,2176]{1,0:T(8,128)(2,1)S(1)}, bf16[32,2176]{1,0:T(8,128)(2,1)S(1)}, u32[]{:S(2)}, u32[]{:S(2)}) collective-permute-start(bf16[32,2176]{1,0:T(8,128)(2,1)S(1)} %get-tuple-element.52), channel_id=1, source_target_pairs={{0,12},{4,8},{8,4},{12,0},{16,28},{20,24},{24,20},{28,16},{1,13},{... | collective-permute-start | bytes 417800 | tf_op jit(solution)/shard_map/ppermute | solution.py:325
  86.2 4.2 %collective-permute-start.20 = (bf16[288,1152]{1,0:T(8,128)(2,1)S(1)}, bf16[288,1152]{1,0:T(8,128)(2,1)S(1)}, u32[]{:S(2)}, u32[]{:S(2)}) collective-permute-start(bf16[288,1152]{1,0:T(8,128)(2,1)S(1)} %shard_map.104.refs_2_), channel_id=1, source_target_pairs={{0,1},{1,0},{2,3},{3,2},{4,5},{5,4},{6,7},{7,6},{8,9},{9,8},{10,11... | collective-permute-start | bytes 1990664 | tf_op jit(solution)/shard_map/ppermute | solution.py:325

commit v11 on v10

--- a/solution.py
+++ b/solution.py
@@ -204,34 +204,35 @@
         backs[i][chunks:, width:] = jnp.broadcast_to(mine, (main - chunks, LANES)).astype(BF16)
 
 
-def unpack_sum(weight, block_refs, rows, fold):
+def unpack_sum(weight, block_refs, rows, fold, order=(0, 1, 2, 3)):
     count = len(block_refs)
     main = block_refs[0].shape[0]
     width = rows.shape[1]
     chunks = width // LANES
     mains, tails = picks(weight, main)
-    mains = mains[:count]
-    pick = jnp.concatenate(mains + [tails, jnp.zeros_like(tails)], axis=0).astype(BF16)
+    mains = [mains[e] for e in order]
+    tails = jnp.concatenate([tails[e : e + 1, :] for e in order] + [jnp.zeros((16 - count, tails.shape[1]), F32)], axis=0)
+    pick = jnp.concatenate(mains + [tails], axis=0).astype(BF16)
     lane = lax.broadcasted_iota(jnp.int32, (1, LANES), 1)
-    routes = []
+    routes = {}
     for j in range(count):
         rows[main * j : main * (j + 1), :] = block_refs[j][:, :width]
         fold[chunks * j : chunks * (j + 1), :] = block_refs[j][:chunks, width:].astype(F32)
         mine = block_refs[j][chunks:, width:].astype(F32)
         dense = dot(mine[:, :main].astype(BF16), mains[j].astype(BF16))[0:1, :]
         last = jnp.sum(jnp.where(lane == main, mine[0:1, :], 0.0), axis=1, keepdims=True)
-        routes.append(dense + last * tails[j : j + 1, :])
+        routes[order[j]] = dense + last * tails[j : j + 1, :]
     for c in range(chunks):
         tail = fold[pl.ds(c, count, stride=chunks), :]
         tail = jnp.concatenate([tail, jnp.zeros((16 - count, LANES), F32)], axis=0).astype(BF16)
         rows[main * count :, LANES * c : LANES * (c + 1)] = tail
-    return dot_tn(pick, rows[...]), routes
-
-
-def relay_sum_kernel(joint_ref, b0, b1, b2, b3, out_ref, rows, fold):
+    return dot_tn(pick, rows[...]), [routes[e] for e in range(count)]
+
+
+def relay_sum_kernel(joint_ref, b0, b3, b2, b1, out_ref, rows, fold):
     tokens, width = joint_ref.shape[0], rows.shape[1]
     weight = joint_ref[0:16, 2 * width :].astype(F32)[0:8, :tokens]
-    summed, routes = unpack_sum(weight, (b0, b1, b2, b3), rows, fold)
+    summed, routes = unpack_sum(weight, (b0, b3, b2, b1), rows, fold, (0, 3, 2, 1))
     lines = tokens // 2
     out_ref[:, :width] = summed[0:lines].astype(BF16)
     out_ref[:, width : 2 * width] = summed[lines:].astype(BF16)
@@ -240,10 +241,10 @@
     out_ref[0:16, 2 * width : 2 * width + tokens] = block
 
 
-def combine_kernel(peer_ref, named_ref, w_ref, b0, b1, b2, b3, far_ref, *refs):
+def combine_kernel(peer_ref, named_ref, w_ref, b0, b3, b2, b1, far_ref, *refs):
     grad_ref, route_ref, in_ref, out_ref, held, rows, fold, lines_ref, sem = refs[5:]
     tokens, width = held.shape
-    summed, routes = unpack_sum(w_ref[...], (b0, b1, b2, b3), rows, fold)
+    summed, routes = unpack_sum(w_ref[...], (b0, b3, b2, b1), rows, fold, (0, 3, 2, 1))
     lines = tokens // 2
     for half in range(2):
         at, columns = slice(half * lines, (half + 1) * lines), slice(half * width, (half + 1) * width)
@@ -425,7 +426,7 @@
         relay_sum_kernel,
         [((token_count // 2, 2 * width + LANES), BF16)],
         [],
-        [far_joint, *far_back],
+        [far_joint, far_back[0], *far_back[:0:-1]],
         [],
         sum_scratch,
         sum_flops,
@@ -460,7 +461,7 @@
         [(mid_far.shape, BF16)],
         [],
         [],
-        [mid_far, first[1], far_partial, *near_back[1:]],
+        [mid_far, first[1], far_partial, *near_back[:0:-1]],
         [],
         0,
         1,
@@ -470,7 +471,7 @@
         combine_kernel,
         [((token_count, width), BF16), (named.shape, BF16), *weight_shapes],
         [peers],
-        [named, dense, *near_back, far_partial, own_far, far_far, mid_far, *first],
+        [named, dense, near_back[0], *near_back[:0:-1], far_partial, own_far, far_far, mid_far, *first],
         [],
         [
             pltpu.VMEM((token_count, width), BF16),

time: 92.4 us -> 92.2 us (level)
  transfers between devices with their start and end apart: 21 -> 21, of which waited for: 15 -> 11; matrix products, arithmetic and copies ran while one was open for 0% -> 0% of each run, Pallas kernels for 14% -> 14%
where the time goes in v11:
time: 92.2 us; the launch traced here: 92 us
  waiting for transfers between devices  48 us (52%)
  starting transfers between devices  25.7 us (28%)
  Pallas kernels  16.1 us (17%)
  other arithmetic  1.41 us (2%)
    ppermute x21, waiting for transfers between devices, swap(): lax.ppermute(value, axis, [(i, i ^ mask) for i in range(lax.axis_size(axi...  48 us
    ppermute x21, starting transfers between devices, swap(): lax.ppermute(value, axis, [(i, i ^ mask) for i in range(lax.axis_size(axi...  25.7 us
    pallas_call x14, Pallas kernels, call(): pl.pallas_call(kernel, out_shape=tuple(outs), in_specs=[on_smem] * len(sm...  16.1 us
  transfers between devices with their start and end apart: 21, of which 11 were waited for; matrix products, arithmetic and copies ran while one was open for 0% of the time, Pallas kernels for 14%

profile of v11, /device:TPU:1, one launch (start us, length us, event | category | flops | bytes accessed | tf_op | source)
XLA Modules:
  0.0 92.0 jit_solution(13308703214663506465)
XLA Ops:
  0.6 0.0 copy-start.3
  0.6 0.0 copy-start.2
  0.7 0.0 copy-start.1
  0.7 0.0 copy-start
  0.7 1.4 %pad_maximum_fusion.own_ref = bf16[512,1152]{1,0:T(8,128)(2,1)S(1)} fusion(bf16[512,384]{1,0:T(8,128)(2,1)} %bitcast.11, bf16[512,768]{1,0:T(8,128)(2,1)} %bitcast.10), kind=kLoop, calls=%fused_computation | loop fusion | flops 2359296 | bytes 2359296 | tf_op jit(solution)/shard_map/concatenate | solution.py:355
  2.1 2.1 %collective-permute-start.4 = (bf16[512,1152]{1,0:T(8,128)(2,1)S(1)}, bf16[512,1152]{1,0:T(8,128)(2,1)S(1)}, u32[]{:S(2)}, u32[]{:S(2)}) collective-permute-start(bf16[512,1152]{1,0:T(8,128)(2,1)S(1)} %pad_maximum_fusion.own_ref), channel_id=1, source_target_pairs={{0,2},{1,3},{2,0},{3,1},{4,6},{5,7},{6,4},{7,5},{8,10},{9,11},{10,... | collective-permute-start | bytes 3538952 | tf_op jit(solution)/shard_map/ppermute | solution.py:326
  4.2 0.0 copy-done.3
  4.2 0.0 copy-done.2
  4.2 0.0 copy-done.1
  4.2 0.0 copy-done
  4.2 0.6 shard_map.93
  4.8 2.4 %collective-permute-start.3 = (bf16[64,4224]{1,0:T(8,128)(2,1)S(1)}, bf16[64,4224]{1,0:T(8,128)(2,1)S(1)}, u32[]{:S(2)}, u32[]{:S(2)}) collective-permute-start(bf16[64,4224]{1,0:T(8,128)(2,1)S(1)} %get-tuple-element.40.joint_ref.refs_0_), channel_id=1, source_target_pairs={{0,16},{4,20},{8,24},{12,28},{16,0},{20,4},{24,8},{28,12},{1,17},{... | collective-permute-start | bytes 1622024 | tf_op jit(solution)/shard_map/ppermute | solution.py:326
  7.2 1.4 %shard_map.94 = (bf16[64,2176]{1,0:T(8,128)(2,1)}, bf16[64,2176]{1,0:T(8,128)(2,1)}, bf16[64,2176]{1,0:T(8,128)(2,1)}) custom-call(bf16[64,4224]{1,0:T(8,128)(2,1)S(1)} %get-tuple-element.40.joint_ref.refs_0_), custom_call_target="tpu_custom_call" | custom-call | flops 58720256 | bytes 1376256 | tf_op jit(solution)/shard_map/pallas_call | solution.py:313
  8.6 1.2 %collective-permute-start = (bf16[64,2176]{1,0:T(8,128)(2,1)}, bf16[64,2176]{1,0:T(8,128)(2,1)}, u32[]{:S(2)}, u32[]{:S(2)}) collective-permute-start(bf16[64,2176]{1,0:T(8,128)(2,1)} %get-tuple-element.41), channel_id=1, source_target_pairs={{0,4},{4,0},{8,12},{12,8},{16,20},{20,16},{24,28},{28,24},{1,5},{5... | collective-permute-start | bytes 835592 | tf_op jit(solution)/shard_map/ppermute | solution.py:326
  9.8 1.3 %collective-permute-start.1 = (bf16[64,2176]{1,0:T(8,128)(2,1)}, bf16[64,2176]{1,0:T(8,128)(2,1)}, u32[]{:S(2)}, u32[]{:S(2)}) collective-permute-start(bf16[64,2176]{1,0:T(8,128)(2,1)} %get-tuple-element.42), channel_id=1, source_target_pairs={{0,8},{4,12},{8,0},{12,4},{16,24},{20,28},{24,16},{28,20},{1,9},{5... | collective-permute-start | bytes 835592 | tf_op jit(solution)/shard_map/ppermute | solution.py:326
  11.1 0.1 collective-permute-start.2
  11.2 4.6 %collective-permute-done.refs_1_ = bf16[64,2176]{1,0:T(8,128)(2,1)} collective-permute-done((bf16[64,2176]{1,0:T(8,128)(2,1)}, bf16[64,2176]{1,0:T(8,128)(2,1)}, u32[]{:S(2)}, u32[]{:S(2)}) %collective-permute-start) | collective-permute-done | bytes 278560 | tf_op jit(solution)/shard_map/ppermute | solution.py:326
  15.8 8.1 %collective-permute-done.1.refs_2_ = bf16[64,2176]{1,0:T(8,128)(2,1)} collective-permute-done((bf16[64,2176]{1,0:T(8,128)(2,1)}, bf16[64,2176]{1,0:T(8,128)(2,1)}, u32[]{:S(2)}, u32[]{:S(2)}) %collective-permute-start.1) | collective-permute-done | bytes 278560 | tf_op jit(solution)/shard_map/ppermute | solution.py:326
  23.9 9.2 %collective-permute-done.2.refs_3_ = bf16[64,2176]{1,0:T(8,128)(2,1)} collective-permute-done((bf16[64,2176]{1,0:T(8,128)(2,1)}, bf16[64,2176]{1,0:T(8,128)(2,1)}, u32[]{:S(2)}, u32[]{:S(2)}) %collective-permute-start.2) | collective-permute-done | bytes 278560 | tf_op jit(solution)/shard_map/ppermute | solution.py:326
  33.2 0.0 collective-permute-done.3.refs_4_.joint_ref
  33.2 1.6 %shard_map.95 = (bf16[144,1024]{1,0:T(8,128)(2,1)S(1)}, bf16[144,1024]{1,0:T(8,128)(2,1)S(1)}, bf16[144,2048]{1,0:T(8,128)(2,1)S(1)}, f32[144,128]{1,0:T(8,128)S(1)}) custom-call(s32[4]{0:T(128)S(1)} %iota_xor_fusion.place_ref, bf16[64,4224]{1,0:T(8,128)(2,1)S(1)} %get-tuple-element.40.joint_ref.refs_0_, bf16[64,2176]{1,0:T(8,128)(2,1)} %collective-permute-done.refs_1_, ...), custom_call_target="tpu_custom_call" | custom-call | bytes 2629632 | tf_op jit(solution)/shard_map/pallas_call | solution.py:313
  34.8 0.0 collective-permute-done.4.refs_1_.far_ref
  34.8 0.6 shard_map.96
  35.4 0.2 shard_map.97.refs_0_
  35.5 2.5 %collective-permute-start.5 = (bf16[1024,1152]{1,0:T(8,128)(2,1)S(1)}, bf16[1024,1152]{1,0:T(8,128)(2,1)S(1)}, u32[]{:S(2)}, u32[]{:S(2)}) collective-permute-start(bf16[1024,1152]{1,0:T(8,128)(2,1)S(1)} %shard_map.97.refs_0_), channel_id=1, source_target_pairs={{0,1},{1,0},{2,3},{3,2},{4,5},{5,4},{6,7},{7,6},{8,9},{9,8},{10,11... | collective-permute-start | bytes 7077896 | tf_op jit(solution)/shard_map/ppermute | solution.py:326
  38.0 0.3 collective-permute-start.12
  38.3 1.2 %collective-permute-start.9 = (bf16[64,2176]{1,0:T(8,128)(2,1)S(1)}, bf16[64,2176]{1,0:T(8,128)(2,1)S(1)}, u32[]{:S(2)}, u32[]{:S(2)}) collective-permute-start(bf16[64,2176]{1,0:T(8,128)(2,1)S(1)} %get-tuple-element.53), channel_id=1, source_target_pairs={{0,4},{4,0},{8,12},{12,8},{16,20},{20,16},{24,28},{28,24},{1,5},{5... | collective-permute-start | bytes 835592 | tf_op jit(solution)/shard_map/ppermute | solution.py:326
  39.5 0.0 collective-permute-start.10
  39.5 1.5 %collective-permute-start.11 = (bf16[64,2176]{1,0:T(8,128)(2,1)S(1)}, bf16[64,2176]{1,0:T(8,128)(2,1)S(1)}, u32[]{:S(2)}, u32[]{:S(2)}) collective-permute-start(bf16[64,2176]{1,0:T(8,128)(2,1)S(1)} %get-tuple-element.55), channel_id=1, source_target_pairs={{0,12},{4,8},{8,4},{12,0},{16,28},{20,24},{24,20},{28,16},{1,13},{... | collective-permute-start | bytes 835592 | tf_op jit(solution)/shard_map/ppermute | solution.py:326
  41.0 1.2 %collective-permute-done.5.refs_1_ = bf16[1024,1152]{1,0:T(8,128)(2,1)S(1)} collective-permute-done((bf16[1024,1152]{1,0:T(8,128)(2,1)S(1)}, bf16[1024,1152]{1,0:T(8,128)(2,1)S(1)}, u32[]{:S(2)}, u32[]{:S(2)}) %collective-permute-start.5) | collective-permute-done | bytes 2359328 | tf_op jit(solution)/shard_map/ppermute | solution.py:326
  42.2 2.6 %shard_map.98 = (bf16[144,1152]{1,0:T(8,128)(2,1)S(1)}, bf16[32,2176]{1,0:T(8,128)(2,1)S(1)}, bf16[32,2176]{1,0:T(8,128)(2,1)S(1)}, bf16[32,2176]{1,0:T(8,128)(2,1)S(1)}, bf16[32,2176]{1,0:T(8,128)(2,1)S(1)}) custom-call(s32[4]{0:T(128)S(1)} %iota_xor_fusion.place_ref, f32[144,128]{1,0:T(8,128)S(1)} %get-tuple-element.44.w_ref, ...), custom_call_target="tpu_custom_call" | custom-call | flops 1132462080 | bytes 6860800 | tf_op jit(solution)/shard_map/pallas_call | solution.py:313
  44.8 8.1 %collective-permute-done.12.refs_5_.far_a.refs_0_ = bf16[144,2048]{1,0:T(8,128)(2,1)S(1)} collective-permute-done((bf16[144,2048]{1,0:T(8,128)(2,1)S(1)}, bf16[144,2048]{1,0:T(8,128)(2,1)S(1)}, u32[]{:S(2)}, u32[]{:S(2)}) %collective-permute-start.12) | collective-permute-done | bytes 589856 | tf_op jit(solution)/shard_map/ppermute | solution.py:326
  53.0 0.0 collective-permute-done.9.refs_1_
  53.0 0.0 collective-permute-done.10.refs_2_
  53.0 0.1 collective-permute-done.11.refs_3_
  53.1 0.7 shard_map.99
  53.7 1.3 %collective-permute-start.17 = (bf16[144,2048]{1,0:T(8,128)(2,1)S(1)}, bf16[144,2048]{1,0:T(8,128)(2,1)S(1)}, u32[]{:S(2)}, u32[]{:S(2)}) collective-permute-start(bf16[144,2048]{1,0:T(8,128)(2,1)S(1)} %get-tuple-element.60.refs_4_), channel_id=1, source_target_pairs={{0,2},{1,3},{2,0},{3,1},{4,6},{5,7},{6,4},{7,5},{8,10},{9,11},{10,... | collective-permute-start | bytes 1769480 | tf_op jit(solution)/shard_map/ppermute | solution.py:326
  55.0 2.6 %shard_map.100 = (bf16[288,1152]{1,0:T(8,128)(2,1)S(1)}, bf16[32,2176]{1,0:T(8,128)(2,1)S(1)}, bf16[32,2176]{1,0:T(8,128)(2,1)S(1)}, bf16[32,2176]{1,0:T(8,128)(2,1)S(1)}, bf16[32,2176]{1,0:T(8,128)(2,1)S(1)}) custom-call(s32[4]{0:T(128)S(1)} %iota_xor_fusion.place_ref, f32[144,128]{1,0:T(8,128)S(1)} %get-tuple-element.57.w_ref, ...), custom_call_target="tpu_custom_call" | custom-call | flops 1132462080 | bytes 7524352 | tf_op jit(solution)/shard_map/pallas_call | solution.py:313
  57.6 1.3 %collective-permute-start.13 = (bf16[32,2176]{1,0:T(8,128)(2,1)S(1)}, bf16[32,2176]{1,0:T(8,128)(2,1)S(1)}, u32[]{:S(2)}, u32[]{:S(2)}) collective-permute-start(bf16[32,2176]{1,0:T(8,128)(2,1)S(1)} %get-tuple-element.62), channel_id=1, source_target_pairs={{0,12},{4,8},{8,4},{12,0},{16,28},{20,24},{24,20},{28,16},{1,13},{... | collective-permute-start | bytes 417800 | tf_op jit(solution)/shard_map/ppermute | solution.py:326
  59.0 1.1 %collective-permute-start.14 = (bf16[32,2176]{1,0:T(8,128)(2,1)S(1)}, bf16[32,2176]{1,0:T(8,128)(2,1)S(1)}, u32[]{:S(2)}, u32[]{:S(2)}) collective-permute-start(bf16[32,2176]{1,0:T(8,128)(2,1)S(1)} %get-tuple-element.63), channel_id=1, source_target_pairs={{0,8},{4,12},{8,0},{12,4},{16,24},{20,28},{24,16},{28,20},{1,9},{5... | collective-permute-start | bytes 417800 | tf_op jit(solution)/shard_map/ppermute | solution.py:326
  60.1 0.2 collective-permute-start.15
  60.3 2.2 %collective-permute-done.13.b3 = bf16[32,2176]{1,0:T(8,128)(2,1)S(1)} collective-permute-done((bf16[32,2176]{1,0:T(8,128)(2,1)S(1)}, bf16[32,2176]{1,0:T(8,128)(2,1)S(1)}, u32[]{:S(2)}, u32[]{:S(2)}) %collective-permute-start.13) | collective-permute-done | bytes 139296 | tf_op jit(solution)/shard_map/ppermute | solution.py:326
  62.5 2.5 %collective-permute-done.14.b2 = bf16[32,2176]{1,0:T(8,128)(2,1)S(1)} collective-permute-done((bf16[32,2176]{1,0:T(8,128)(2,1)S(1)}, bf16[32,2176]{1,0:T(8,128)(2,1)S(1)}, u32[]{:S(2)}, u32[]{:S(2)}) %collective-permute-start.14) | collective-permute-done | bytes 139296 | tf_op jit(solution)/shard_map/ppermute | solution.py:326
  65.0 0.0 collective-permute-done.15.b1
  65.0 0.4 shard_map.101.refs_0_
  65.4 1.7 %collective-permute-done.17.far_b.refs_1_ = bf16[144,2048]{1,0:T(8,128)(2,1)S(1)} collective-permute-done((bf16[144,2048]{1,0:T(8,128)(2,1)S(1)}, bf16[144,2048]{1,0:T(8,128)(2,1)S(1)}, u32[]{:S(2)}, u32[]{:S(2)}) %collective-permute-start.17) | collective-permute-done | bytes 589856 | tf_op jit(solution)/shard_map/ppermute | solution.py:326
  67.1 0.1 shard_map.102
  67.2 2.5 %collective-permute-start.19 = (bf16[288,3200]{1,0:T(8,128)(2,1)S(1)}, bf16[288,3200]{1,0:T(8,128)(2,1)S(1)}, u32[]{:S(2)}, u32[]{:S(2)}) collective-permute-start(bf16[288,3200]{1,0:T(8,128)(2,1)S(1)} %shard_map.102), channel_id=1, source_target_pairs={{0,1},{1,0},{2,3},{3,2},{4,5},{5,4},{6,7},{7,6},{8,9},{9,8},{10,11... | collective-permute-start | bytes 5529608 | tf_op jit(solution)/shard_map/ppermute | solution.py:326
  69.7 1.2 %collective-permute-start.18 = (bf16[288,1152]{1,0:T(8,128)(2,1)S(1)}, bf16[288,1152]{1,0:T(8,128)(2,1)S(1)}, u32[]{:S(2)}, u32[]{:S(2)}) collective-permute-start(bf16[288,1152]{1,0:T(8,128)(2,1)S(1)} %get-tuple-element.65.mid_ref), channel_id=1, source_target_pairs={{0,2},{1,3},{2,0},{3,1},{4,6},{5,7},{6,4},{7,5},{8,10},{9,11},{10,... | collective-permute-start | bytes 1990664 | tf_op jit(solution)/shard_map/ppermute | solution.py:326
  70.9 1.2 %collective-permute-start.16 = (bf16[32,4224]{1,0:T(8,128)(2,1)S(1)}, bf16[32,4224]{1,0:T(8,128)(2,1)S(1)}, u32[]{:S(2)}, u32[]{:S(2)}) collective-permute-start(bf16[32,4224]{1,0:T(8,128)(2,1)S(1)} %shard_map.101.refs_0_), channel_id=1, source_target_pairs={{0,16},{4,20},{8,24},{12,28},{16,0},{20,4},{24,8},{28,12},{1,17},{... | collective-permute-start | bytes 811016 | tf_op jit(solution)/shard_map/ppermute | solution.py:326
  72.2 2.1 %collective-permute-start.6 = (bf16[32,2176]{1,0:T(8,128)(2,1)S(1)}, bf16[32,2176]{1,0:T(8,128)(2,1)S(1)}, u32[]{:S(2)}, u32[]{:S(2)}) collective-permute-start(bf16[32,2176]{1,0:T(8,128)(2,1)S(1)} %get-tuple-element.50), channel_id=1, source_target_pairs={{0,12},{4,8},{8,4},{12,0},{16,28},{20,24},{24,20},{28,16},{1,13},{... | collective-permute-start | bytes 417800 | tf_op jit(solution)/shard_map/ppermute | solution.py:326
  74.3 0.3 collective-permute-start.7
  74.6 0.0 collective-permute-done.19.near_ref
  74.6 0.2 collective-permute-start.8
  74.8 1.2 %shard_map.103 = (f32[512,768]{1,0:T(8,128)S(1)}, f32[512,384]{1,0:T(8,128)S(1)}) custom-call(bf16[144,1024]{1,0:T(8,128)(2,1)S(1)} %get-tuple-element.45.refs_0_.refs_2_.rows_a, bf16[144,1024]{1,0:T(8,128)(2,1)S(1)} %get-tuple-element.58.refs_2_.rows_b, bf16[288,3200]{1,0:T(8,128)(2,1)S(1)} %collective-permute-done.19.near_ref, ...), custom_call_target="tpu_custom_call" | custom-call | flops 679477248 | bytes 5455872 | tf_op jit(solution)/shard_map/pallas_call | solution.py:313
  76.0 4.7 %collective-permute-done.6.refs_3_.b3 = bf16[32,2176]{1,0:T(8,128)(2,1)S(1)} collective-permute-done((bf16[32,2176]{1,0:T(8,128)(2,1)S(1)}, bf16[32,2176]{1,0:T(8,128)(2,1)S(1)}, u32[]{:S(2)}, u32[]{:S(2)}) %collective-permute-start.6) | collective-permute-done | bytes 139296 | tf_op jit(solution)/shard_map/ppermute | solution.py:326
  80.7 5.6 %collective-permute-done.7.refs_4_.b2 = bf16[32,2176]{1,0:T(8,128)(2,1)S(1)} collective-permute-done((bf16[32,2176]{1,0:T(8,128)(2,1)S(1)}, bf16[32,2176]{1,0:T(8,128)(2,1)S(1)}, u32[]{:S(2)}, u32[]{:S(2)}) %collective-permute-start.7) | collective-permute-done | bytes 139296 | tf_op jit(solution)/shard_map/ppermute | solution.py:326
  86.4 0.0 collective-permute-done.8.refs_5_.b1
  86.4 0.0 collective-permute-done.16.refs_2_.far_ref
  86.4 0.0 collective-permute-done.18.refs_0_
  86.4 1.6 %collective-permute-start.20 = (bf16[288,1152]{1,0:T(8,128)(2,1)S(1)}, bf16[288,1152]{1,0:T(8,128)(2,1)S(1)}, u32[]{:S(2)}, u32[]{:S(2)}) collective-permute-start(bf16[288,1152]{1,0:T(8,128)(2,1)S(1)} %shard_map.104.refs_2_), channel_id=1, source_target_pairs={{0,1},{1,0},{2,3},{3,2},{4,5},{5,4},{6,7},{7,6},{8,9},{9,8},{10,11... | collective-permute-start | bytes 1990664 | tf_op jit(solution)/shard_map/ppermute | solution.py:326
  87.9 2.3 %shard_map.105 = (bf16[64,2048]{1,0:T(8,128)(2,1)}, bf16[4,64]{1,0:T(4,128)(2,1)}, f32[512,768]{1,0:T(8,128)S(1)}, f32[512,384]{1,0:T(8,128)S(1)}) custom-call(s32[8]{0:T(128)S(1)} %iota_xor_fusion.1.peer_ref, s32[4,64]{1,0:T(4,128)S(1)} %bitcast.8, f32[8,64]{1,0:T(8,128)S(1)} %get-tuple-element.39.w_ref, bf16[32,2176]{1,0:T(8,128)(2,1)S(1)} %get-tuple-element.49.b0, ...), custom_call_target="tpu_custom_call" | custom-call | flops 377487360 | bytes 7392768 | tf_op jit(solution)/shard_map/pallas_call | solution.py:313
  90.2 0.0 collective-permute-done.20.mid_ref
  90.2 1.8 %shard_map.106 = (f32[512,768]{1,0:T(8,128)}, f32[512,384]{1,0:T(8,128)}) custom-call(bf16[288,3200]{1,0:T(8,128)(2,1)S(1)} %collective-permute-done.19.near_ref, bf16[288,1152]{1,0:T(8,128)(2,1)S(1)} %collective-permute-done.20.mid_ref, f32[512,768]{1,0:T(8,128)S(1)} %get-tuple-element.70.in_part, f32[512,384]{1,0:T(8,128)S(1)} %get-tuple-element.71.out_part), custom_call_target="tpu_custom_call" | custom-call | flops 339738624 | bytes 4866048 | tf_op jit(solution)/shard_map/pallas_call | solution.py:313
  (3 shorter events, 0.0 us)
Async XLA Ops:
  0.6 3.6 %copy-start.3 = (bf16[64,4]{0,1:T(4,128)(2,1)S(1)}, bf16[64,4]{0,1:T(4,128)(2,1)}, u32[]{:S(2)}) copy-start(bf16[64,4]{0,1:T(4,128)(2,1)} %param.9) | copy-start | bytes 1540
  0.6 3.5 %copy-start.2 = (s32[64,4]{0,1:T(4,128)S(1)}, s32[64,4]{0,1:T(4,128)}, u32[]{:S(2)}) copy-start(s32[64,4]{0,1:T(4,128)} %param.8) | copy-start | bytes 3076
  0.7 3.5 %copy-start.1 = (bf16[64,2048]{1,0:T(8,128)(2,1)S(1)}, bf16[64,2048]{1,0:T(8,128)(2,1)}, u32[]{:S(2)}) copy-start(bf16[64,2048]{1,0:T(8,128)(2,1)} %dy_ref.1) | copy-start | bytes 786436
  0.7 3.5 %copy-start = (bf16[64,2048]{1,0:T(8,128)(2,1)S(1)}, bf16[64,2048]{1,0:T(8,128)(2,1)}, u32[]{:S(2)}) copy-start(bf16[64,2048]{1,0:T(8,128)(2,1)} %x_ref.1) | copy-start | bytes 786436
  2.1 32.7 %collective-permute-start.4 = (bf16[512,1152]{1,0:T(8,128)(2,1)S(1)}, bf16[512,1152]{1,0:T(8,128)(2,1)S(1)}, u32[]{:S(2)}, u32[]{:S(2)}) collective-permute-start(bf16[512,1152]{1,0:T(8,128)(2,1)S(1)} %pad_maximum_fusion.own_ref), channel_id=1, source_target_pairs={{0,2},{1,3},{2,0},{3,1},{4,6},{5,7},{6,4},{7,5},{8,10},{9,11},{10,... | collective-permute-start | bytes 3538952 | tf_op jit(solution)/shard_map/ppermute | solution.py:326
  4.8 28.4 %collective-permute-start.3 = (bf16[64,4224]{1,0:T(8,128)(2,1)S(1)}, bf16[64,4224]{1,0:T(8,128)(2,1)S(1)}, u32[]{:S(2)}, u32[]{:S(2)}) collective-permute-start(bf16[64,4224]{1,0:T(8,128)(2,1)S(1)} %get-tuple-element.40.joint_ref.refs_0_), channel_id=1, source_target_pairs={{0,16},{4,20},{8,24},{12,28},{16,0},{20,4},{24,8},{28,12},{1,17},{... | collective-permute-start | bytes 1622024 | tf_op jit(solution)/shard_map/ppermute | solution.py:326
  8.6 7.2 %collective-permute-start = (bf16[64,2176]{1,0:T(8,128)(2,1)}, bf16[64,2176]{1,0:T(8,128)(2,1)}, u32[]{:S(2)}, u32[]{:S(2)}) collective-permute-start(bf16[64,2176]{1,0:T(8,128)(2,1)} %get-tuple-element.41), channel_id=1, source_target_pairs={{0,4},{4,0},{8,12},{12,8},{16,20},{20,16},{24,28},{28,24},{1,5},{5... | collective-permute-start | bytes 835592 | tf_op jit(solution)/shard_map/ppermute | solution.py:326
  9.8 14.1 %collective-permute-start.1 = (bf16[64,2176]{1,0:T(8,128)(2,1)}, bf16[64,2176]{1,0:T(8,128)(2,1)}, u32[]{:S(2)}, u32[]{:S(2)}) collective-permute-start(bf16[64,2176]{1,0:T(8,128)(2,1)} %get-tuple-element.42), channel_id=1, source_target_pairs={{0,8},{4,12},{8,0},{12,4},{16,24},{20,28},{24,16},{28,20},{1,9},{5... | collective-permute-start | bytes 835592 | tf_op jit(solution)/shard_map/ppermute | solution.py:326
  11.1 22.0 %collective-permute-start.2 = (bf16[64,2176]{1,0:T(8,128)(2,1)}, bf16[64,2176]{1,0:T(8,128)(2,1)}, u32[]{:S(2)}, u32[]{:S(2)}) collective-permute-start(bf16[64,2176]{1,0:T(8,128)(2,1)} %get-tuple-element.43), channel_id=1, source_target_pairs={{0,12},{4,8},{8,4},{12,0},{16,28},{20,24},{24,20},{28,16},{1,13},{... | collective-permute-start | bytes 835592 | tf_op jit(solution)/shard_map/ppermute | solution.py:326
  35.5 6.7 %collective-permute-start.5 = (bf16[1024,1152]{1,0:T(8,128)(2,1)S(1)}, bf16[1024,1152]{1,0:T(8,128)(2,1)S(1)}, u32[]{:S(2)}, u32[]{:S(2)}) collective-permute-start(bf16[1024,1152]{1,0:T(8,128)(2,1)S(1)} %shard_map.97.refs_0_), channel_id=1, source_target_pairs={{0,1},{1,0},{2,3},{3,2},{4,5},{5,4},{6,7},{7,6},{8,9},{9,8},{10,11... | collective-permute-start | bytes 7077896 | tf_op jit(solution)/shard_map/ppermute | solution.py:326
  38.0 14.9 %collective-permute-start.12 = (bf16[144,2048]{1,0:T(8,128)(2,1)S(1)}, bf16[144,2048]{1,0:T(8,128)(2,1)S(1)}, u32[]{:S(2)}, u32[]{:S(2)}) collective-permute-start(bf16[144,2048]{1,0:T(8,128)(2,1)S(1)} %get-tuple-element.48.refs_4_), channel_id=1, source_target_pairs={{0,2},{1,3},{2,0},{3,1},{4,6},{5,7},{6,4},{7,5},{8,10},{9,11},{10,... | collective-permute-start | bytes 1769480 | tf_op jit(solution)/shard_map/ppermute | solution.py:326
  38.3 14.6 %collective-permute-start.9 = (bf16[64,2176]{1,0:T(8,128)(2,1)S(1)}, bf16[64,2176]{1,0:T(8,128)(2,1)S(1)}, u32[]{:S(2)}, u32[]{:S(2)}) collective-permute-start(bf16[64,2176]{1,0:T(8,128)(2,1)S(1)} %get-tuple-element.53), channel_id=1, source_target_pairs={{0,4},{4,0},{8,12},{12,8},{16,20},{20,16},{24,28},{28,24},{1,5},{5... | collective-permute-start | bytes 835592 | tf_op jit(solution)/shard_map/ppermute | solution.py:326
  39.5 13.5 %collective-permute-start.10 = (bf16[64,2176]{1,0:T(8,128)(2,1)S(1)}, bf16[64,2176]{1,0:T(8,128)(2,1)S(1)}, u32[]{:S(2)}, u32[]{:S(2)}) collective-permute-start(bf16[64,2176]{1,0:T(8,128)(2,1)S(1)} %get-tuple-element.54), channel_id=1, source_target_pairs={{0,8},{4,12},{8,0},{12,4},{16,24},{20,28},{24,16},{28,20},{1,9},{5... | collective-permute-start | bytes 835592 | tf_op jit(solution)/shard_map/ppermute | solution.py:326
  39.5 13.5 %collective-permute-start.11 = (bf16[64,2176]{1,0:T(8,128)(2,1)S(1)}, bf16[64,2176]{1,0:T(8,128)(2,1)S(1)}, u32[]{:S(2)}, u32[]{:S(2)}) collective-permute-start(bf16[64,2176]{1,0:T(8,128)(2,1)S(1)} %get-tuple-element.55), channel_id=1, source_target_pairs={{0,12},{4,8},{8,4},{12,0},{16,28},{20,24},{24,20},{28,16},{1,13},{... | collective-permute-start | bytes 835592 | tf_op jit(solution)/shard_map/ppermute | solution.py:326
  53.7 13.4 %collective-permute-start.17 = (bf16[144,2048]{1,0:T(8,128)(2,1)S(1)}, bf16[144,2048]{1,0:T(8,128)(2,1)S(1)}, u32[]{:S(2)}, u32[]{:S(2)}) collective-permute-start(bf16[144,2048]{1,0:T(8,128)(2,1)S(1)} %get-tuple-element.60.refs_4_), channel_id=1, source_target_pairs={{0,2},{1,3},{2,0},{3,1},{4,6},{5,7},{6,4},{7,5},{8,10},{9,11},{10,... | collective-permute-start | bytes 1769480 | tf_op jit(solution)/shard_map/ppermute | solution.py:326
  57.6 4.9 %collective-permute-start.13 = (bf16[32,2176]{1,0:T(8,128)(2,1)S(1)}, bf16[32,2176]{1,0:T(8,128)(2,1)S(1)}, u32[]{:S(2)}, u32[]{:S(2)}) collective-permute-start(bf16[32,2176]{1,0:T(8,128)(2,1)S(1)} %get-tuple-element.62), channel_id=1, source_target_pairs={{0,12},{4,8},{8,4},{12,0},{16,28},{20,24},{24,20},{28,16},{1,13},{... | collective-permute-start | bytes 417800 | tf_op jit(solution)/shard_map/ppermute | solution.py:326
  59.0 6.1 %collective-permute-start.14 = (bf16[32,2176]{1,0:T(8,128)(2,1)S(1)}, bf16[32,2176]{1,0:T(8,128)(2,1)S(1)}, u32[]{:S(2)}, u32[]{:S(2)}) collective-permute-start(bf16[32,2176]{1,0:T(8,128)(2,1)S(1)} %get-tuple-element.63), channel_id=1, source_target_pairs={{0,8},{4,12},{8,0},{12,4},{16,24},{20,28},{24,16},{28,20},{1,9},{5... | collective-permute-start | bytes 417800 | tf_op jit(solution)/shard_map/ppermute | solution.py:326
  60.1 4.9 %collective-permute-start.15 = (bf16[32,2176]{1,0:T(8,128)(2,1)S(1)}, bf16[32,2176]{1,0:T(8,128)(2,1)S(1)}, u32[]{:S(2)}, u32[]{:S(2)}) collective-permute-start(bf16[32,2176]{1,0:T(8,128)(2,1)S(1)} %get-tuple-element.64), channel_id=1, source_target_pairs={{0,4},{4,0},{8,12},{12,8},{16,20},{20,16},{24,28},{28,24},{1,5},{5... | collective-permute-start | bytes 417800 | tf_op jit(solution)/shard_map/ppermute | solution.py:326
  67.2 7.4 %collective-permute-start.19 = (bf16[288,3200]{1,0:T(8,128)(2,1)S(1)}, bf16[288,3200]{1,0:T(8,128)(2,1)S(1)}, u32[]{:S(2)}, u32[]{:S(2)}) collective-permute-start(bf16[288,3200]{1,0:T(8,128)(2,1)S(1)} %shard_map.102), channel_id=1, source_target_pairs={{0,1},{1,0},{2,3},{3,2},{4,5},{5,4},{6,7},{7,6},{8,9},{9,8},{10,11... | collective-permute-start | bytes 5529608 | tf_op jit(solution)/shard_map/ppermute | solution.py:326
  69.7 16.7 %collective-permute-start.18 = (bf16[288,1152]{1,0:T(8,128)(2,1)S(1)}, bf16[288,1152]{1,0:T(8,128)(2,1)S(1)}, u32[]{:S(2)}, u32[]{:S(2)}) collective-permute-start(bf16[288,1152]{1,0:T(8,128)(2,1)S(1)} %get-tuple-element.65.mid_ref), channel_id=1, source_target_pairs={{0,2},{1,3},{2,0},{3,1},{4,6},{5,7},{6,4},{7,5},{8,10},{9,11},{10,... | collective-permute-start | bytes 1990664 | tf_op jit(solution)/shard_map/ppermute | solution.py:326
  70.9 15.4 %collective-permute-start.16 = (bf16[32,4224]{1,0:T(8,128)(2,1)S(1)}, bf16[32,4224]{1,0:T(8,128)(2,1)S(1)}, u32[]{:S(2)}, u32[]{:S(2)}) collective-permute-start(bf16[32,4224]{1,0:T(8,128)(2,1)S(1)} %shard_map.101.refs_0_), channel_id=1, source_target_pairs={{0,16},{4,20},{8,24},{12,28},{16,0},{20,4},{24,8},{28,12},{1,17},{... | collective-permute-start | bytes 811016 | tf_op jit(solution)/shard_map/ppermute | solution.py:326
  72.2 8.6 %collective-permute-start.6 = (bf16[32,2176]{1,0:T(8,128)(2,1)S(1)}, bf16[32,2176]{1,0:T(8,128)(2,1)S(1)}, u32[]{:S(2)}, u32[]{:S(2)}) collective-permute-start(bf16[32,2176]{1,0:T(8,128)(2,1)S(1)} %get-tuple-element.50), channel_id=1, source_target_pairs={{0,12},{4,8},{8,4},{12,0},{16,28},{20,24},{24,20},{28,16},{1,13},{... | collective-permute-start | bytes 417800 | tf_op jit(solution)/shard_map/ppermute | solution.py:326
  74.3 12.1 %collective-permute-start.7 = (bf16[32,2176]{1,0:T(8,128)(2,1)S(1)}, bf16[32,2176]{1,0:T(8,128)(2,1)S(1)}, u32[]{:S(2)}, u32[]{:S(2)}) collective-permute-start(bf16[32,2176]{1,0:T(8,128)(2,1)S(1)} %get-tuple-element.51), channel_id=1, source_target_pairs={{0,8},{4,12},{8,0},{12,4},{16,24},{20,28},{24,16},{28,20},{1,9},{5... | collective-permute-start | bytes 417800 | tf_op jit(solution)/shard_map/ppermute | solution.py:326
  74.6 11.8 %collective-permute-start.8 = (bf16[32,2176]{1,0:T(8,128)(2,1)S(1)}, bf16[32,2176]{1,0:T(8,128)(2,1)S(1)}, u32[]{:S(2)}, u32[]{:S(2)}) collective-permute-start(bf16[32,2176]{1,0:T(8,128)(2,1)S(1)} %get-tuple-element.52), channel_id=1, source_target_pairs={{0,4},{4,0},{8,12},{12,8},{16,20},{20,16},{24,28},{28,24},{1,5},{5... | collective-permute-start | bytes 417800 | tf_op jit(solution)/shard_map/ppermute | solution.py:326
  86.4 3.8 %collective-permute-start.20 = (bf16[288,1152]{1,0:T(8,128)(2,1)S(1)}, bf16[288,1152]{1,0:T(8,128)(2,1)S(1)}, u32[]{:S(2)}, u32[]{:S(2)}) collective-permute-start(bf16[288,1152]{1,0:T(8,128)(2,1)S(1)} %shard_map.104.refs_2_), channel_id=1, source_target_pairs={{0,1},{1,0},{2,3},{3,2},{4,5},{5,4},{6,7},{7,6},{8,9},{9,8},{10,11... | collective-permute-start | bytes 1990664 | tf_op jit(solution)/shard_map/ppermute | solution.py:326

commit v12 on v11

--- a/solution.py
+++ b/solution.py
@@ -383,7 +383,7 @@
         )
 
     own = [swap(value, "expert", j + 1) for j, value in enumerate(pack(range(half + 1, blocks), joint, []))]
-    *own_slices, own_weight = sliced(half, [joint, *own], [far_joint])
+    *own_slices, own_weight = sliced(half, [joint, *own[::-1]], [far_joint])
     own_far = swap(own_slices[2], "dp", 2)
     far = pack(range(half), far_joint, [own_slices[0], far_weights])
     far = [far[0]] + [swap(far[j], "expert", j) for j in range(1, half)]
@@ -411,8 +411,9 @@
         )
 
     own_mid, *near_back = middle(own_slices, own_weight, [], [])
+    near_back = [near_back[0], *near_back[:0:-1]]
     near_back = near_back[:1] + [swap(near_back[j], "expert", j) for j in range(1, half)]
-    *far_slices, far_weight = sliced(None, far, [own_mid, own_far])
+    *far_slices, far_weight = sliced(None, [far[0], *far[:0:-1]], [own_mid, own_far])
     far_far = swap(far_slices[2], "dp", 2)
     mid, *far_back = middle(far_slices, far_weight, [own_mid], [])
 
@@ -421,6 +422,7 @@
         pltpu.VMEM((half * chunks, LANES), F32),
     ]
     sum_flops = 2 * (half * main + 16) * width * token_count
+    far_back = [far_back[0], *far_back[:0:-1]]
     far_back = far_back[:1] + [swap(far_back[j], "expert", j) for j in range(1, half)]
     (partial,) = call(
         relay_sum_kernel,

time: 92.2 us -> 91.8 us (level)
  starting transfers between devices: 25.7 us -> 23.3 us
  waiting for transfers between devices: 48 us -> 50 us
    ppermute x21, starting transfers between devices: 25.7 us -> 23.3 us  [swap(): lax.ppermute(value, axis, [(i, i ^ mask) for i in range(lax.axis_size(axi...]
    ppermute x21, waiting for transfers between devices: 48 us -> 50 us  [swap(): lax.ppermute(value, axis, [(i, i ^ mask) for i in range(lax.axis_size(axi...]
  transfers between devices with their start and end apart: 21 -> 21, of which waited for: 11 -> 13; matrix products, arithmetic and copies ran while one was open for 0% -> 0% of each run, Pallas kernels for 14% -> 14%
where the time goes in v12:
time: 91.8 us; the launch traced here: 91.6 us
  waiting for transfers between devices  50 us (54%)
  starting transfers between devices  23.3 us (25%)
  Pallas kernels  16.1 us (18%)
  other arithmetic  1.41 us (2%)
    ppermute x21, waiting for transfers between devices, swap(): lax.ppermute(value, axis, [(i, i ^ mask) for i in range(lax.axis_size(axi...  50 us
    ppermute x21, starting transfers between devices, swap(): lax.ppermute(value, axis, [(i, i ^ mask) for i in range(lax.axis_size(axi...  23.3 us
    pallas_call x14, Pallas kernels, call(): pl.pallas_call(kernel, out_shape=tuple(outs), in_specs=[on_smem] * len(sm...  16.1 us
  transfers between devices with their start and end apart: 21, of which 13 were waited for; matrix products, arithmetic and copies ran while one was open for 0% of the time, Pallas kernels for 14%

profile of v12, /device:TPU:1, one launch (start us, length us, event | category | flops | bytes accessed | tf_op | source)
XLA Modules:
  0.0 91.6 jit_solution(7443746312694720332)
XLA Ops:
  0.6 0.0 copy-start.3
  0.6 0.0 copy-start.2
  0.7 0.0 copy-start.1
  0.7 0.0 copy-start
  0.7 1.4 %pad_maximum_fusion.own_ref = bf16[512,1152]{1,0:T(8,128)(2,1)S(1)} fusion(bf16[512,384]{1,0:T(8,128)(2,1)} %bitcast.11, bf16[512,768]{1,0:T(8,128)(2,1)} %bitcast.10), kind=kLoop, calls=%fused_computation | loop fusion | flops 2359296 | bytes 2359296 | tf_op jit(solution)/shard_map/concatenate | solution.py:355
  2.1 2.1 %collective-permute-start.4 = (bf16[512,1152]{1,0:T(8,128)(2,1)S(1)}, bf16[512,1152]{1,0:T(8,128)(2,1)S(1)}, u32[]{:S(2)}, u32[]{:S(2)}) collective-permute-start(bf16[512,1152]{1,0:T(8,128)(2,1)S(1)} %pad_maximum_fusion.own_ref), channel_id=1, source_target_pairs={{0,2},{1,3},{2,0},{3,1},{4,6},{5,7},{6,4},{7,5},{8,10},{9,11},{10,... | collective-permute-start | bytes 3538952 | tf_op jit(solution)/shard_map/ppermute | solution.py:326
  4.2 0.0 copy-done.3
  4.2 0.0 copy-done.2
  4.2 0.0 copy-done.1
  4.2 0.0 copy-done
  4.2 0.6 shard_map.93
  4.8 2.4 %collective-permute-start.3 = (bf16[64,4224]{1,0:T(8,128)(2,1)S(1)}, bf16[64,4224]{1,0:T(8,128)(2,1)S(1)}, u32[]{:S(2)}, u32[]{:S(2)}) collective-permute-start(bf16[64,4224]{1,0:T(8,128)(2,1)S(1)} %get-tuple-element.40.joint_ref.refs_0_), channel_id=1, source_target_pairs={{0,16},{4,20},{8,24},{12,28},{16,0},{20,4},{24,8},{28,12},{1,17},{... | collective-permute-start | bytes 1622024 | tf_op jit(solution)/shard_map/ppermute | solution.py:326
  7.2 1.4 %shard_map.94 = (bf16[64,2176]{1,0:T(8,128)(2,1)}, bf16[64,2176]{1,0:T(8,128)(2,1)}, bf16[64,2176]{1,0:T(8,128)(2,1)}) custom-call(bf16[64,4224]{1,0:T(8,128)(2,1)S(1)} %get-tuple-element.40.joint_ref.refs_0_), custom_call_target="tpu_custom_call" | custom-call | flops 58720256 | bytes 1376256 | tf_op jit(solution)/shard_map/pallas_call | solution.py:313
  8.6 2.3 %collective-permute-start = (bf16[64,2176]{1,0:T(8,128)(2,1)}, bf16[64,2176]{1,0:T(8,128)(2,1)}, u32[]{:S(2)}, u32[]{:S(2)}) collective-permute-start(bf16[64,2176]{1,0:T(8,128)(2,1)} %get-tuple-element.41), channel_id=1, source_target_pairs={{0,12},{4,8},{8,4},{12,0},{16,28},{20,24},{24,20},{28,16},{1,13},{... | collective-permute-start | bytes 835592 | tf_op jit(solution)/shard_map/ppermute | solution.py:326
  10.8 0.2 collective-permute-start.1
  11.0 0.2 collective-permute-start.2
  11.2 12.7 %collective-permute-done.refs_1_ = bf16[64,2176]{1,0:T(8,128)(2,1)} collective-permute-done((bf16[64,2176]{1,0:T(8,128)(2,1)}, bf16[64,2176]{1,0:T(8,128)(2,1)}, u32[]{:S(2)}, u32[]{:S(2)}) %collective-permute-start) | collective-permute-done | bytes 278560 | tf_op jit(solution)/shard_map/ppermute | solution.py:326
  23.9 9.3 %collective-permute-done.1.refs_2_ = bf16[64,2176]{1,0:T(8,128)(2,1)} collective-permute-done((bf16[64,2176]{1,0:T(8,128)(2,1)}, bf16[64,2176]{1,0:T(8,128)(2,1)}, u32[]{:S(2)}, u32[]{:S(2)}) %collective-permute-start.1) | collective-permute-done | bytes 278560 | tf_op jit(solution)/shard_map/ppermute | solution.py:326
  33.3 0.0 collective-permute-done.2.refs_3_
  33.3 0.0 collective-permute-done.3.refs_4_.joint_ref
  33.3 1.6 %shard_map.95 = (bf16[144,1024]{1,0:T(8,128)(2,1)S(1)}, bf16[144,1024]{1,0:T(8,128)(2,1)S(1)}, bf16[144,2048]{1,0:T(8,128)(2,1)S(1)}, f32[144,128]{1,0:T(8,128)S(1)}) custom-call(s32[4]{0:T(128)S(1)} %iota_xor_fusion.place_ref, bf16[64,4224]{1,0:T(8,128)(2,1)S(1)} %get-tuple-element.40.joint_ref.refs_0_, bf16[64,2176]{1,0:T(8,128)(2,1)} %collective-permute-done.refs_1_, ...), custom_call_target="tpu_custom_call" | custom-call | bytes 2629632 | tf_op jit(solution)/shard_map/pallas_call | solution.py:313
  34.9 0.0 collective-permute-done.4.refs_1_.far_ref
  34.9 0.6 shard_map.96
  35.5 0.2 shard_map.97.refs_0_
  35.7 2.2 %collective-permute-start.5 = (bf16[1024,1152]{1,0:T(8,128)(2,1)S(1)}, bf16[1024,1152]{1,0:T(8,128)(2,1)S(1)}, u32[]{:S(2)}, u32[]{:S(2)}) collective-permute-start(bf16[1024,1152]{1,0:T(8,128)(2,1)S(1)} %shard_map.97.refs_0_), channel_id=1, source_target_pairs={{0,1},{1,0},{2,3},{3,2},{4,5},{5,4},{6,7},{7,6},{8,9},{9,8},{10,11... | collective-permute-start | bytes 7077896 | tf_op jit(solution)/shard_map/ppermute | solution.py:326
  37.9 0.2 collective-permute-start.12
  38.1 0.0 collective-permute-start.9
  38.1 1.4 %collective-permute-start.10 = (bf16[64,2176]{1,0:T(8,128)(2,1)S(1)}, bf16[64,2176]{1,0:T(8,128)(2,1)S(1)}, u32[]{:S(2)}, u32[]{:S(2)}) collective-permute-start(bf16[64,2176]{1,0:T(8,128)(2,1)S(1)} %get-tuple-element.54), channel_id=1, source_target_pairs={{0,8},{4,12},{8,0},{12,4},{16,24},{20,28},{24,16},{28,20},{1,9},{5... | collective-permute-start | bytes 835592 | tf_op jit(solution)/shard_map/ppermute | solution.py:326
  39.5 1.2 %collective-permute-start.11 = (bf16[64,2176]{1,0:T(8,128)(2,1)S(1)}, bf16[64,2176]{1,0:T(8,128)(2,1)S(1)}, u32[]{:S(2)}, u32[]{:S(2)}) collective-permute-start(bf16[64,2176]{1,0:T(8,128)(2,1)S(1)} %get-tuple-element.55), channel_id=1, source_target_pairs={{0,4},{4,0},{8,12},{12,8},{16,20},{20,16},{24,28},{28,24},{1,5},{5... | collective-permute-start | bytes 835592 | tf_op jit(solution)/shard_map/ppermute | solution.py:326
  40.7 1.3 %collective-permute-done.5.refs_1_ = bf16[1024,1152]{1,0:T(8,128)(2,1)S(1)} collective-permute-done((bf16[1024,1152]{1,0:T(8,128)(2,1)S(1)}, bf16[1024,1152]{1,0:T(8,128)(2,1)S(1)}, u32[]{:S(2)}, u32[]{:S(2)}) %collective-permute-start.5) | collective-permute-done | bytes 2359328 | tf_op jit(solution)/shard_map/ppermute | solution.py:326
  42.0 2.6 %shard_map.98 = (bf16[144,1152]{1,0:T(8,128)(2,1)S(1)}, bf16[32,2176]{1,0:T(8,128)(2,1)S(1)}, bf16[32,2176]{1,0:T(8,128)(2,1)S(1)}, bf16[32,2176]{1,0:T(8,128)(2,1)S(1)}, bf16[32,2176]{1,0:T(8,128)(2,1)S(1)}) custom-call(s32[4]{0:T(128)S(1)} %iota_xor_fusion.place_ref, f32[144,128]{1,0:T(8,128)S(1)} %get-tuple-element.44.w_ref, ...), custom_call_target="tpu_custom_call" | custom-call | flops 1132462080 | bytes 6860800 | tf_op jit(solution)/shard_map/pallas_call | solution.py:313
  44.7 8.1 %collective-permute-done.12.refs_5_.far_a.refs_0_ = bf16[144,2048]{1,0:T(8,128)(2,1)S(1)} collective-permute-done((bf16[144,2048]{1,0:T(8,128)(2,1)S(1)}, bf16[144,2048]{1,0:T(8,128)(2,1)S(1)}, u32[]{:S(2)}, u32[]{:S(2)}) %collective-permute-start.12) | collective-permute-done | bytes 589856 | tf_op jit(solution)/shard_map/ppermute | solution.py:326
  52.8 0.0 collective-permute-done.9.refs_1_
  52.8 0.0 collective-permute-done.10.refs_2_
  52.8 0.8 collective-permute-done.11.refs_3_
  53.5 0.7 shard_map.99
  54.2 1.3 %collective-permute-start.17 = (bf16[144,2048]{1,0:T(8,128)(2,1)S(1)}, bf16[144,2048]{1,0:T(8,128)(2,1)S(1)}, u32[]{:S(2)}, u32[]{:S(2)}) collective-permute-start(bf16[144,2048]{1,0:T(8,128)(2,1)S(1)} %get-tuple-element.60.refs_4_), channel_id=1, source_target_pairs={{0,2},{1,3},{2,0},{3,1},{4,6},{5,7},{6,4},{7,5},{8,10},{9,11},{10,... | collective-permute-start | bytes 1769480 | tf_op jit(solution)/shard_map/ppermute | solution.py:326
  55.5 2.6 %shard_map.100 = (bf16[288,1152]{1,0:T(8,128)(2,1)S(1)}, bf16[32,2176]{1,0:T(8,128)(2,1)S(1)}, bf16[32,2176]{1,0:T(8,128)(2,1)S(1)}, bf16[32,2176]{1,0:T(8,128)(2,1)S(1)}, bf16[32,2176]{1,0:T(8,128)(2,1)S(1)}) custom-call(s32[4]{0:T(128)S(1)} %iota_xor_fusion.place_ref, f32[144,128]{1,0:T(8,128)S(1)} %get-tuple-element.57.w_ref, ...), custom_call_target="tpu_custom_call" | custom-call | flops 1132462080 | bytes 7524352 | tf_op jit(solution)/shard_map/pallas_call | solution.py:313
  58.2 0.1 collective-permute-start.13
  58.2 1.4 %collective-permute-start.14 = (bf16[32,2176]{1,0:T(8,128)(2,1)S(1)}, bf16[32,2176]{1,0:T(8,128)(2,1)S(1)}, u32[]{:S(2)}, u32[]{:S(2)}) collective-permute-start(bf16[32,2176]{1,0:T(8,128)(2,1)S(1)} %get-tuple-element.63), channel_id=1, source_target_pairs={{0,8},{4,12},{8,0},{12,4},{16,24},{20,28},{24,16},{28,20},{1,9},{5... | collective-permute-start | bytes 417800 | tf_op jit(solution)/shard_map/ppermute | solution.py:326
  59.6 1.2 %collective-permute-start.15 = (bf16[32,2176]{1,0:T(8,128)(2,1)S(1)}, bf16[32,2176]{1,0:T(8,128)(2,1)S(1)}, u32[]{:S(2)}, u32[]{:S(2)}) collective-permute-start(bf16[32,2176]{1,0:T(8,128)(2,1)S(1)} %get-tuple-element.64), channel_id=1, source_target_pairs={{0,4},{4,0},{8,12},{12,8},{16,20},{20,16},{24,28},{28,24},{1,5},{5... | collective-permute-start | bytes 417800 | tf_op jit(solution)/shard_map/ppermute | solution.py:326
  60.9 2.7 %collective-permute-done.13.b3 = bf16[32,2176]{1,0:T(8,128)(2,1)S(1)} collective-permute-done((bf16[32,2176]{1,0:T(8,128)(2,1)S(1)}, bf16[32,2176]{1,0:T(8,128)(2,1)S(1)}, u32[]{:S(2)}, u32[]{:S(2)}) %collective-permute-start.13) | collective-permute-done | bytes 139296 | tf_op jit(solution)/shard_map/ppermute | solution.py:326
  63.6 1.9 %collective-permute-done.14.b2 = bf16[32,2176]{1,0:T(8,128)(2,1)S(1)} collective-permute-done((bf16[32,2176]{1,0:T(8,128)(2,1)S(1)}, bf16[32,2176]{1,0:T(8,128)(2,1)S(1)}, u32[]{:S(2)}, u32[]{:S(2)}) %collective-permute-start.14) | collective-permute-done | bytes 139296 | tf_op jit(solution)/shard_map/ppermute | solution.py:326
  65.5 1.9 %collective-permute-done.15.b1 = bf16[32,2176]{1,0:T(8,128)(2,1)S(1)} collective-permute-done((bf16[32,2176]{1,0:T(8,128)(2,1)S(1)}, bf16[32,2176]{1,0:T(8,128)(2,1)S(1)}, u32[]{:S(2)}, u32[]{:S(2)}) %collective-permute-start.15) | collective-permute-done | bytes 139296 | tf_op jit(solution)/shard_map/ppermute | solution.py:326
  67.4 0.4 shard_map.101.refs_0_
  67.8 0.9 collective-permute-done.17.far_b.refs_1_
  68.7 0.1 shard_map.102
  68.8 1.4 %collective-permute-start.19 = (bf16[288,3200]{1,0:T(8,128)(2,1)S(1)}, bf16[288,3200]{1,0:T(8,128)(2,1)S(1)}, u32[]{:S(2)}, u32[]{:S(2)}) collective-permute-start(bf16[288,3200]{1,0:T(8,128)(2,1)S(1)} %shard_map.102), channel_id=1, source_target_pairs={{0,1},{1,0},{2,3},{3,2},{4,5},{5,4},{6,7},{7,6},{8,9},{9,8},{10,11... | collective-permute-start | bytes 5529608 | tf_op jit(solution)/shard_map/ppermute | solution.py:326
  70.2 1.3 %collective-permute-start.18 = (bf16[288,1152]{1,0:T(8,128)(2,1)S(1)}, bf16[288,1152]{1,0:T(8,128)(2,1)S(1)}, u32[]{:S(2)}, u32[]{:S(2)}) collective-permute-start(bf16[288,1152]{1,0:T(8,128)(2,1)S(1)} %get-tuple-element.65.mid_ref), channel_id=1, source_target_pairs={{0,2},{1,3},{2,0},{3,1},{4,6},{5,7},{6,4},{7,5},{8,10},{9,11},{10,... | collective-permute-start | bytes 1990664 | tf_op jit(solution)/shard_map/ppermute | solution.py:326
  71.5 0.2 collective-permute-start.16
  71.6 2.2 %collective-permute-start.6 = (bf16[32,2176]{1,0:T(8,128)(2,1)S(1)}, bf16[32,2176]{1,0:T(8,128)(2,1)S(1)}, u32[]{:S(2)}, u32[]{:S(2)}) collective-permute-start(bf16[32,2176]{1,0:T(8,128)(2,1)S(1)} %get-tuple-element.50), channel_id=1, source_target_pairs={{0,12},{4,8},{8,4},{12,0},{16,28},{20,24},{24,20},{28,16},{1,13},{... | collective-permute-start | bytes 417800 | tf_op jit(solution)/shard_map/ppermute | solution.py:326
  73.8 0.0 collective-permute-start.7
  73.8 0.0 collective-permute-done.19.near_ref
  73.8 1.2 %collective-permute-start.8 = (bf16[32,2176]{1,0:T(8,128)(2,1)S(1)}, bf16[32,2176]{1,0:T(8,128)(2,1)S(1)}, u32[]{:S(2)}, u32[]{:S(2)}) collective-permute-start(bf16[32,2176]{1,0:T(8,128)(2,1)S(1)} %get-tuple-element.52), channel_id=1, source_target_pairs={{0,4},{4,0},{8,12},{12,8},{16,20},{20,16},{24,28},{28,24},{1,5},{5... | collective-permute-start | bytes 417800 | tf_op jit(solution)/shard_map/ppermute | solution.py:326
  75.0 1.2 %shard_map.103 = (f32[512,768]{1,0:T(8,128)S(1)}, f32[512,384]{1,0:T(8,128)S(1)}) custom-call(bf16[144,1024]{1,0:T(8,128)(2,1)S(1)} %get-tuple-element.45.refs_0_.refs_2_.rows_a, bf16[144,1024]{1,0:T(8,128)(2,1)S(1)} %get-tuple-element.58.refs_2_.rows_b, bf16[288,3200]{1,0:T(8,128)(2,1)S(1)} %collective-permute-done.19.near_ref, ...), custom_call_target="tpu_custom_call" | custom-call | flops 679477248 | bytes 5455872 | tf_op jit(solution)/shard_map/pallas_call | solution.py:313
  76.3 4.0 %collective-permute-done.6.refs_3_.b3 = bf16[32,2176]{1,0:T(8,128)(2,1)S(1)} collective-permute-done((bf16[32,2176]{1,0:T(8,128)(2,1)S(1)}, bf16[32,2176]{1,0:T(8,128)(2,1)S(1)}, u32[]{:S(2)}, u32[]{:S(2)}) %collective-permute-start.6) | collective-permute-done | bytes 139296 | tf_op jit(solution)/shard_map/ppermute | solution.py:326
  80.2 3.0 %collective-permute-done.7.refs_4_.b2 = bf16[32,2176]{1,0:T(8,128)(2,1)S(1)} collective-permute-done((bf16[32,2176]{1,0:T(8,128)(2,1)S(1)}, bf16[32,2176]{1,0:T(8,128)(2,1)S(1)}, u32[]{:S(2)}, u32[]{:S(2)}) %collective-permute-start.7) | collective-permute-done | bytes 139296 | tf_op jit(solution)/shard_map/ppermute | solution.py:326
  83.2 0.0 collective-permute-done.8.refs_5_.b1
  83.2 3.1 %collective-permute-done.16.refs_2_.far_ref = bf16[32,4224]{1,0:T(8,128)(2,1)S(1)} collective-permute-done((bf16[32,4224]{1,0:T(8,128)(2,1)S(1)}, bf16[32,4224]{1,0:T(8,128)(2,1)S(1)}, u32[]{:S(2)}, u32[]{:S(2)}) %collective-permute-start.16) | collective-permute-done | bytes 270368 | tf_op jit(solution)/shard_map/ppermute | solution.py:326
  86.4 0.3 collective-permute-done.18.refs_0_
  86.7 0.8 collective-permute-start.20
  87.5 2.3 %shard_map.105 = (bf16[64,2048]{1,0:T(8,128)(2,1)}, bf16[4,64]{1,0:T(4,128)(2,1)}, f32[512,768]{1,0:T(8,128)S(1)}, f32[512,384]{1,0:T(8,128)S(1)}) custom-call(s32[8]{0:T(128)S(1)} %iota_xor_fusion.1.peer_ref, s32[4,64]{1,0:T(4,128)S(1)} %bitcast.8, f32[8,64]{1,0:T(8,128)S(1)} %get-tuple-element.39.w_ref, bf16[32,2176]{1,0:T(8,128)(2,1)S(1)} %get-tuple-element.49.b0, ...), custom_call_target="tpu_custom_call" | custom-call | flops 377487360 | bytes 7392768 | tf_op jit(solution)/shard_map/pallas_call | solution.py:313
  89.8 0.0 collective-permute-done.20.mid_ref
  89.8 1.8 %shard_map.106 = (f32[512,768]{1,0:T(8,128)}, f32[512,384]{1,0:T(8,128)}) custom-call(bf16[288,3200]{1,0:T(8,128)(2,1)S(1)} %collective-permute-done.19.near_ref, bf16[288,1152]{1,0:T(8,128)(2,1)S(1)} %collective-permute-done.20.mid_ref, f32[512,768]{1,0:T(8,128)S(1)} %get-tuple-element.70.in_part, f32[512,384]{1,0:T(8,128)S(1)} %get-tuple-element.71.out_part), custom_call_target="tpu_custom_call" | custom-call | flops 339738624 | bytes 4866048 | tf_op jit(solution)/shard_map/pallas_call | solution.py:313
  (3 shorter events, 0.0 us)
Async XLA Ops:
  0.6 3.6 %copy-start.3 = (bf16[64,4]{0,1:T(4,128)(2,1)S(1)}, bf16[64,4]{0,1:T(4,128)(2,1)}, u32[]{:S(2)}) copy-start(bf16[64,4]{0,1:T(4,128)(2,1)} %param.9) | copy-start | bytes 1540
  0.6 3.5 %copy-start.2 = (s32[64,4]{0,1:T(4,128)S(1)}, s32[64,4]{0,1:T(4,128)}, u32[]{:S(2)}) copy-start(s32[64,4]{0,1:T(4,128)} %param.8) | copy-start | bytes 3076
  0.7 3.5 %copy-start.1 = (bf16[64,2048]{1,0:T(8,128)(2,1)S(1)}, bf16[64,2048]{1,0:T(8,128)(2,1)}, u32[]{:S(2)}) copy-start(bf16[64,2048]{1,0:T(8,128)(2,1)} %dy_ref.1) | copy-start | bytes 786436
  0.7 3.5 %copy-start = (bf16[64,2048]{1,0:T(8,128)(2,1)S(1)}, bf16[64,2048]{1,0:T(8,128)(2,1)}, u32[]{:S(2)}) copy-start(bf16[64,2048]{1,0:T(8,128)(2,1)} %x_ref.1) | copy-start | bytes 786436
  2.1 32.8 %collective-permute-start.4 = (bf16[512,1152]{1,0:T(8,128)(2,1)S(1)}, bf16[512,1152]{1,0:T(8,128)(2,1)S(1)}, u32[]{:S(2)}, u32[]{:S(2)}) collective-permute-start(bf16[512,1152]{1,0:T(8,128)(2,1)S(1)} %pad_maximum_fusion.own_ref), channel_id=1, source_target_pairs={{0,2},{1,3},{2,0},{3,1},{4,6},{5,7},{6,4},{7,5},{8,10},{9,11},{10,... | collective-permute-start | bytes 3538952 | tf_op jit(solution)/shard_map/ppermute | solution.py:326
  4.8 28.5 %collective-permute-start.3 = (bf16[64,4224]{1,0:T(8,128)(2,1)S(1)}, bf16[64,4224]{1,0:T(8,128)(2,1)S(1)}, u32[]{:S(2)}, u32[]{:S(2)}) collective-permute-start(bf16[64,4224]{1,0:T(8,128)(2,1)S(1)} %get-tuple-element.40.joint_ref.refs_0_), channel_id=1, source_target_pairs={{0,16},{4,20},{8,24},{12,28},{16,0},{20,4},{24,8},{28,12},{1,17},{... | collective-permute-start | bytes 1622024 | tf_op jit(solution)/shard_map/ppermute | solution.py:326
  8.6 15.3 %collective-permute-start = (bf16[64,2176]{1,0:T(8,128)(2,1)}, bf16[64,2176]{1,0:T(8,128)(2,1)}, u32[]{:S(2)}, u32[]{:S(2)}) collective-permute-start(bf16[64,2176]{1,0:T(8,128)(2,1)} %get-tuple-element.41), channel_id=1, source_target_pairs={{0,12},{4,8},{8,4},{12,0},{16,28},{20,24},{24,20},{28,16},{1,13},{... | collective-permute-start | bytes 835592 | tf_op jit(solution)/shard_map/ppermute | solution.py:326
  10.8 22.4 %collective-permute-start.1 = (bf16[64,2176]{1,0:T(8,128)(2,1)}, bf16[64,2176]{1,0:T(8,128)(2,1)}, u32[]{:S(2)}, u32[]{:S(2)}) collective-permute-start(bf16[64,2176]{1,0:T(8,128)(2,1)} %get-tuple-element.42), channel_id=1, source_target_pairs={{0,8},{4,12},{8,0},{12,4},{16,24},{20,28},{24,16},{28,20},{1,9},{5... | collective-permute-start | bytes 835592 | tf_op jit(solution)/shard_map/ppermute | solution.py:326
  11.0 22.3 %collective-permute-start.2 = (bf16[64,2176]{1,0:T(8,128)(2,1)}, bf16[64,2176]{1,0:T(8,128)(2,1)}, u32[]{:S(2)}, u32[]{:S(2)}) collective-permute-start(bf16[64,2176]{1,0:T(8,128)(2,1)} %get-tuple-element.43), channel_id=1, source_target_pairs={{0,4},{4,0},{8,12},{12,8},{16,20},{20,16},{24,28},{28,24},{1,5},{5... | collective-permute-start | bytes 835592 | tf_op jit(solution)/shard_map/ppermute | solution.py:326
  35.7 6.4 %collective-permute-start.5 = (bf16[1024,1152]{1,0:T(8,128)(2,1)S(1)}, bf16[1024,1152]{1,0:T(8,128)(2,1)S(1)}, u32[]{:S(2)}, u32[]{:S(2)}) collective-permute-start(bf16[1024,1152]{1,0:T(8,128)(2,1)S(1)} %shard_map.97.refs_0_), channel_id=1, source_target_pairs={{0,1},{1,0},{2,3},{3,2},{4,5},{5,4},{6,7},{7,6},{8,9},{9,8},{10,11... | collective-permute-start | bytes 7077896 | tf_op jit(solution)/shard_map/ppermute | solution.py:326
  37.9 14.9 %collective-permute-start.12 = (bf16[144,2048]{1,0:T(8,128)(2,1)S(1)}, bf16[144,2048]{1,0:T(8,128)(2,1)S(1)}, u32[]{:S(2)}, u32[]{:S(2)}) collective-permute-start(bf16[144,2048]{1,0:T(8,128)(2,1)S(1)} %get-tuple-element.48.refs_4_), channel_id=1, source_target_pairs={{0,2},{1,3},{2,0},{3,1},{4,6},{5,7},{6,4},{7,5},{8,10},{9,11},{10,... | collective-permute-start | bytes 1769480 | tf_op jit(solution)/shard_map/ppermute | solution.py:326
  38.1 14.7 %collective-permute-start.9 = (bf16[64,2176]{1,0:T(8,128)(2,1)S(1)}, bf16[64,2176]{1,0:T(8,128)(2,1)S(1)}, u32[]{:S(2)}, u32[]{:S(2)}) collective-permute-start(bf16[64,2176]{1,0:T(8,128)(2,1)S(1)} %get-tuple-element.53), channel_id=1, source_target_pairs={{0,12},{4,8},{8,4},{12,0},{16,28},{20,24},{24,20},{28,16},{1,13},{... | collective-permute-start | bytes 835592 | tf_op jit(solution)/shard_map/ppermute | solution.py:326
  38.1 14.7 %collective-permute-start.10 = (bf16[64,2176]{1,0:T(8,128)(2,1)S(1)}, bf16[64,2176]{1,0:T(8,128)(2,1)S(1)}, u32[]{:S(2)}, u32[]{:S(2)}) collective-permute-start(bf16[64,2176]{1,0:T(8,128)(2,1)S(1)} %get-tuple-element.54), channel_id=1, source_target_pairs={{0,8},{4,12},{8,0},{12,4},{16,24},{20,28},{24,16},{28,20},{1,9},{5... | collective-permute-start | bytes 835592 | tf_op jit(solution)/shard_map/ppermute | solution.py:326
  39.5 14.0 %collective-permute-start.11 = (bf16[64,2176]{1,0:T(8,128)(2,1)S(1)}, bf16[64,2176]{1,0:T(8,128)(2,1)S(1)}, u32[]{:S(2)}, u32[]{:S(2)}) collective-permute-start(bf16[64,2176]{1,0:T(8,128)(2,1)S(1)} %get-tuple-element.55), channel_id=1, source_target_pairs={{0,4},{4,0},{8,12},{12,8},{16,20},{20,16},{24,28},{28,24},{1,5},{5... | collective-permute-start | bytes 835592 | tf_op jit(solution)/shard_map/ppermute | solution.py:326
  54.2 14.5 %collective-permute-start.17 = (bf16[144,2048]{1,0:T(8,128)(2,1)S(1)}, bf16[144,2048]{1,0:T(8,128)(2,1)S(1)}, u32[]{:S(2)}, u32[]{:S(2)}) collective-permute-start(bf16[144,2048]{1,0:T(8,128)(2,1)S(1)} %get-tuple-element.60.refs_4_), channel_id=1, source_target_pairs={{0,2},{1,3},{2,0},{3,1},{4,6},{5,7},{6,4},{7,5},{8,10},{9,11},{10,... | collective-permute-start | bytes 1769480 | tf_op jit(solution)/shard_map/ppermute | solution.py:326
  58.2 5.4 %collective-permute-start.13 = (bf16[32,2176]{1,0:T(8,128)(2,1)S(1)}, bf16[32,2176]{1,0:T(8,128)(2,1)S(1)}, u32[]{:S(2)}, u32[]{:S(2)}) collective-permute-start(bf16[32,2176]{1,0:T(8,128)(2,1)S(1)} %get-tuple-element.62), channel_id=1, source_target_pairs={{0,12},{4,8},{8,4},{12,0},{16,28},{20,24},{24,20},{28,16},{1,13},{... | collective-permute-start | bytes 417800 | tf_op jit(solution)/shard_map/ppermute | solution.py:326
  58.2 7.2 %collective-permute-start.14 = (bf16[32,2176]{1,0:T(8,128)(2,1)S(1)}, bf16[32,2176]{1,0:T(8,128)(2,1)S(1)}, u32[]{:S(2)}, u32[]{:S(2)}) collective-permute-start(bf16[32,2176]{1,0:T(8,128)(2,1)S(1)} %get-tuple-element.63), channel_id=1, source_target_pairs={{0,8},{4,12},{8,0},{12,4},{16,24},{20,28},{24,16},{28,20},{1,9},{5... | collective-permute-start | bytes 417800 | tf_op jit(solution)/shard_map/ppermute | solution.py:326
  59.6 7.7 %collective-permute-start.15 = (bf16[32,2176]{1,0:T(8,128)(2,1)S(1)}, bf16[32,2176]{1,0:T(8,128)(2,1)S(1)}, u32[]{:S(2)}, u32[]{:S(2)}) collective-permute-start(bf16[32,2176]{1,0:T(8,128)(2,1)S(1)} %get-tuple-element.64), channel_id=1, source_target_pairs={{0,4},{4,0},{8,12},{12,8},{16,20},{20,16},{24,28},{28,24},{1,5},{5... | collective-permute-start | bytes 417800 | tf_op jit(solution)/shard_map/ppermute | solution.py:326
  68.8 5.0 %collective-permute-start.19 = (bf16[288,3200]{1,0:T(8,128)(2,1)S(1)}, bf16[288,3200]{1,0:T(8,128)(2,1)S(1)}, u32[]{:S(2)}, u32[]{:S(2)}) collective-permute-start(bf16[288,3200]{1,0:T(8,128)(2,1)S(1)} %shard_map.102), channel_id=1, source_target_pairs={{0,1},{1,0},{2,3},{3,2},{4,5},{5,4},{6,7},{7,6},{8,9},{9,8},{10,11... | collective-permute-start | bytes 5529608 | tf_op jit(solution)/shard_map/ppermute | solution.py:326
  70.2 16.5 %collective-permute-start.18 = (bf16[288,1152]{1,0:T(8,128)(2,1)S(1)}, bf16[288,1152]{1,0:T(8,128)(2,1)S(1)}, u32[]{:S(2)}, u32[]{:S(2)}) collective-permute-start(bf16[288,1152]{1,0:T(8,128)(2,1)S(1)} %get-tuple-element.65.mid_ref), channel_id=1, source_target_pairs={{0,2},{1,3},{2,0},{3,1},{4,6},{5,7},{6,4},{7,5},{8,10},{9,11},{10,... | collective-permute-start | bytes 1990664 | tf_op jit(solution)/shard_map/ppermute | solution.py:326
  71.5 14.9 %collective-permute-start.16 = (bf16[32,4224]{1,0:T(8,128)(2,1)S(1)}, bf16[32,4224]{1,0:T(8,128)(2,1)S(1)}, u32[]{:S(2)}, u32[]{:S(2)}) collective-permute-start(bf16[32,4224]{1,0:T(8,128)(2,1)S(1)} %shard_map.101.refs_0_), channel_id=1, source_target_pairs={{0,16},{4,20},{8,24},{12,28},{16,0},{20,4},{24,8},{28,12},{1,17},{... | collective-permute-start | bytes 811016 | tf_op jit(solution)/shard_map/ppermute | solution.py:326
  71.6 8.6 %collective-permute-start.6 = (bf16[32,2176]{1,0:T(8,128)(2,1)S(1)}, bf16[32,2176]{1,0:T(8,128)(2,1)S(1)}, u32[]{:S(2)}, u32[]{:S(2)}) collective-permute-start(bf16[32,2176]{1,0:T(8,128)(2,1)S(1)} %get-tuple-element.50), channel_id=1, source_target_pairs={{0,12},{4,8},{8,4},{12,0},{16,28},{20,24},{24,20},{28,16},{1,13},{... | collective-permute-start | bytes 417800 | tf_op jit(solution)/shard_map/ppermute | solution.py:326
  73.8 9.4 %collective-permute-start.7 = (bf16[32,2176]{1,0:T(8,128)(2,1)S(1)}, bf16[32,2176]{1,0:T(8,128)(2,1)S(1)}, u32[]{:S(2)}, u32[]{:S(2)}) collective-permute-start(bf16[32,2176]{1,0:T(8,128)(2,1)S(1)} %get-tuple-element.51), channel_id=1, source_target_pairs={{0,8},{4,12},{8,0},{12,4},{16,24},{20,28},{24,16},{28,20},{1,9},{5... | collective-permute-start | bytes 417800 | tf_op jit(solution)/shard_map/ppermute | solution.py:326
  73.8 9.4 %collective-permute-start.8 = (bf16[32,2176]{1,0:T(8,128)(2,1)S(1)}, bf16[32,2176]{1,0:T(8,128)(2,1)S(1)}, u32[]{:S(2)}, u32[]{:S(2)}) collective-permute-start(bf16[32,2176]{1,0:T(8,128)(2,1)S(1)} %get-tuple-element.52), channel_id=1, source_target_pairs={{0,4},{4,0},{8,12},{12,8},{16,20},{20,16},{24,28},{28,24},{1,5},{5... | collective-permute-start | bytes 417800 | tf_op jit(solution)/shard_map/ppermute | solution.py:326
  86.7 3.1 %collective-permute-start.20 = (bf16[288,1152]{1,0:T(8,128)(2,1)S(1)}, bf16[288,1152]{1,0:T(8,128)(2,1)S(1)}, u32[]{:S(2)}, u32[]{:S(2)}) collective-permute-start(bf16[288,1152]{1,0:T(8,128)(2,1)S(1)} %shard_map.104.refs_2_), channel_id=1, source_target_pairs={{0,1},{1,0},{2,3},{3,2},{4,5},{5,4},{6,7},{7,6},{8,9},{9,8},{10,11... | collective-permute-start | bytes 1990664 | tf_op jit(solution)/shard_map/ppermute | solution.py:326

commit v13 on v12

--- a/solution.py
+++ b/solution.py
@@ -383,7 +383,8 @@
         )
 
     own = [swap(value, "expert", j + 1) for j, value in enumerate(pack(range(half + 1, blocks), joint, []))]
-    *own_slices, own_weight = sliced(half, [joint, *own[::-1]], [far_joint])
+    (kept,) = pack([half], joint, [own[2]])
+    *own_slices, own_weight = sliced(None, [kept, *own[::-1]], [far_joint])
     own_far = swap(own_slices[2], "dp", 2)
     far = pack(range(half), far_joint, [own_slices[0], far_weights])
     far = [far[0]] + [swap(far[j], "expert", j) for j in range(1, half)]

time: 91.8 us -> 91.4 us (level)
    pallas_call x14 -> x15, Pallas kernels: 16.1 us -> 16.1 us  [call(): pl.pallas_call(kernel, out_shape=tuple(outs), in_specs=[on_smem] * len(sm...]
where the time goes in v13:
time: 91.4 us; the launch traced here: 91.2 us
  waiting for transfers between devices  49.6 us (54%)
  starting transfers between devices  23.3 us (25%)
  Pallas kernels  16.1 us (18%)
  other arithmetic  1.41 us (2%)
    ppermute x21, waiting for transfers between devices, swap(): lax.ppermute(value, axis, [(i, i ^ mask) for i in range(lax.axis_size(axi...  49.6 us
    ppermute x21, starting transfers between devices, swap(): lax.ppermute(value, axis, [(i, i ^ mask) for i in range(lax.axis_size(axi...  23.3 us
    pallas_call x15, Pallas kernels, call(): pl.pallas_call(kernel, out_shape=tuple(outs), in_specs=[on_smem] * len(sm...  16.1 us
  transfers between devices with their start and end apart: 21, of which 13 were waited for; matrix products, arithmetic and copies ran while one was open for 0% of the time, Pallas kernels for 14%

profile of v13, /device:TPU:1, one launch (start us, length us, event | category | flops | bytes accessed | tf_op | source)
XLA Modules:
  0.0 91.2 jit_solution(16524601308455105340)
XLA Ops:
  0.6 0.0 copy-start.3
  0.6 0.0 copy-start.2
  0.7 0.0 copy-start.1
  0.7 0.0 copy-start
  0.7 1.4 %pad_maximum_fusion.own_ref = bf16[512,1152]{1,0:T(8,128)(2,1)S(1)} fusion(bf16[512,384]{1,0:T(8,128)(2,1)} %bitcast.11, bf16[512,768]{1,0:T(8,128)(2,1)} %bitcast.10), kind=kLoop, calls=%fused_computation | loop fusion | flops 2359296 | bytes 2359296 | tf_op jit(solution)/shard_map/concatenate | solution.py:355
  2.1 2.1 %collective-permute-start.4 = (bf16[512,1152]{1,0:T(8,128)(2,1)S(1)}, bf16[512,1152]{1,0:T(8,128)(2,1)S(1)}, u32[]{:S(2)}, u32[]{:S(2)}) collective-permute-start(bf16[512,1152]{1,0:T(8,128)(2,1)S(1)} %pad_maximum_fusion.own_ref), channel_id=1, source_target_pairs={{0,2},{1,3},{2,0},{3,1},{4,6},{5,7},{6,4},{7,5},{8,10},{9,11},{10,... | collective-permute-start | bytes 3538952 | tf_op jit(solution)/shard_map/ppermute | solution.py:326
  4.2 0.0 copy-done.3
  4.2 0.0 copy-done.2
  4.2 0.0 copy-done.1
  4.2 0.6 shard_map.93
  4.8 2.4 %collective-permute-start.3 = (bf16[64,4224]{1,0:T(8,128)(2,1)S(1)}, bf16[64,4224]{1,0:T(8,128)(2,1)S(1)}, u32[]{:S(2)}, u32[]{:S(2)}) collective-permute-start(bf16[64,4224]{1,0:T(8,128)(2,1)S(1)} %get-tuple-element.40.joint_ref), channel_id=1, source_target_pairs={{0,16},{4,20},{8,24},{12,28},{16,0},{20,4},{24,8},{28,12},{1,17},{... | collective-permute-start | bytes 1622024 | tf_op jit(solution)/shard_map/ppermute | solution.py:326
  7.2 1.4 %shard_map.94 = (bf16[64,2176]{1,0:T(8,128)(2,1)}, bf16[64,2176]{1,0:T(8,128)(2,1)}, bf16[64,2176]{1,0:T(8,128)(2,1)}) custom-call(bf16[64,4224]{1,0:T(8,128)(2,1)S(1)} %get-tuple-element.40.joint_ref), custom_call_target="tpu_custom_call" | custom-call | flops 58720256 | bytes 1376256 | tf_op jit(solution)/shard_map/pallas_call | solution.py:313
  8.6 2.3 %collective-permute-start = (bf16[64,2176]{1,0:T(8,128)(2,1)}, bf16[64,2176]{1,0:T(8,128)(2,1)}, u32[]{:S(2)}, u32[]{:S(2)}) collective-permute-start(bf16[64,2176]{1,0:T(8,128)(2,1)} %get-tuple-element.41), channel_id=1, source_target_pairs={{0,12},{4,8},{8,4},{12,0},{16,28},{20,24},{24,20},{28,16},{1,13},{... | collective-permute-start | bytes 835592 | tf_op jit(solution)/shard_map/ppermute | solution.py:326
  10.8 0.2 collective-permute-start.1
  11.0 0.2 collective-permute-start.2
  11.2 12.7 %collective-permute-done.refs_0_.refs_1_ = bf16[64,2176]{1,0:T(8,128)(2,1)} collective-permute-done((bf16[64,2176]{1,0:T(8,128)(2,1)}, bf16[64,2176]{1,0:T(8,128)(2,1)}, u32[]{:S(2)}, u32[]{:S(2)}) %collective-permute-start) | collective-permute-done | bytes 278560 | tf_op jit(solution)/shard_map/ppermute | solution.py:326
  23.9 0.4 shard_map.95.refs_0_
  24.3 9.0 %collective-permute-done.1.refs_2_ = bf16[64,2176]{1,0:T(8,128)(2,1)} collective-permute-done((bf16[64,2176]{1,0:T(8,128)(2,1)}, bf16[64,2176]{1,0:T(8,128)(2,1)}, u32[]{:S(2)}, u32[]{:S(2)}) %collective-permute-start.1) | collective-permute-done | bytes 278560 | tf_op jit(solution)/shard_map/ppermute | solution.py:326
  33.3 0.0 collective-permute-done.2.refs_3_
  33.3 0.0 collective-permute-done.3.refs_4_.joint_ref
  33.3 1.2 %shard_map.96 = (bf16[144,1024]{1,0:T(8,128)(2,1)S(1)}, bf16[144,1024]{1,0:T(8,128)(2,1)S(1)}, bf16[144,2048]{1,0:T(8,128)(2,1)S(1)}, f32[144,128]{1,0:T(8,128)S(1)}) custom-call(s32[4]{0:T(128)S(1)} %iota_xor_fusion.place_ref, bf16[64,2176]{1,0:T(8,128)(2,1)S(1)} %shard_map.95.refs_0_, bf16[64,2176]{1,0:T(8,128)(2,1)} %collective-permute-done.refs_0_.refs_1_, ...), custom_call_target="tpu_custom_call" | custom-call | bytes 2367488 | tf_op jit(solution)/shard_map/pallas_call | solution.py:313
  34.5 0.0 collective-permute-done.4.refs_1_.far_ref
  34.5 0.6 shard_map.97
  35.1 0.2 shard_map.98.refs_0_
  35.3 2.2 %collective-permute-start.5 = (bf16[1024,1152]{1,0:T(8,128)(2,1)S(1)}, bf16[1024,1152]{1,0:T(8,128)(2,1)S(1)}, u32[]{:S(2)}, u32[]{:S(2)}) collective-permute-start(bf16[1024,1152]{1,0:T(8,128)(2,1)S(1)} %shard_map.98.refs_0_), channel_id=1, source_target_pairs={{0,1},{1,0},{2,3},{3,2},{4,5},{5,4},{6,7},{7,6},{8,9},{9,8},{10,11... | collective-permute-start | bytes 7077896 | tf_op jit(solution)/shard_map/ppermute | solution.py:326
  37.5 0.2 collective-permute-start.12
  37.7 0.0 collective-permute-start.9
  37.7 1.5 %collective-permute-start.10 = (bf16[64,2176]{1,0:T(8,128)(2,1)S(1)}, bf16[64,2176]{1,0:T(8,128)(2,1)S(1)}, u32[]{:S(2)}, u32[]{:S(2)}) collective-permute-start(bf16[64,2176]{1,0:T(8,128)(2,1)S(1)} %get-tuple-element.54), channel_id=1, source_target_pairs={{0,8},{4,12},{8,0},{12,4},{16,24},{20,28},{24,16},{28,20},{1,9},{5... | collective-permute-start | bytes 835592 | tf_op jit(solution)/shard_map/ppermute | solution.py:326
  39.2 1.2 %collective-permute-start.11 = (bf16[64,2176]{1,0:T(8,128)(2,1)S(1)}, bf16[64,2176]{1,0:T(8,128)(2,1)S(1)}, u32[]{:S(2)}, u32[]{:S(2)}) collective-permute-start(bf16[64,2176]{1,0:T(8,128)(2,1)S(1)} %get-tuple-element.55), channel_id=1, source_target_pairs={{0,4},{4,0},{8,12},{12,8},{16,20},{20,16},{24,28},{28,24},{1,5},{5... | collective-permute-start | bytes 835592 | tf_op jit(solution)/shard_map/ppermute | solution.py:326
  40.4 1.3 %collective-permute-done.5.refs_1_ = bf16[1024,1152]{1,0:T(8,128)(2,1)S(1)} collective-permute-done((bf16[1024,1152]{1,0:T(8,128)(2,1)S(1)}, bf16[1024,1152]{1,0:T(8,128)(2,1)S(1)}, u32[]{:S(2)}, u32[]{:S(2)}) %collective-permute-start.5) | collective-permute-done | bytes 2359328 | tf_op jit(solution)/shard_map/ppermute | solution.py:326
  41.7 2.6 %shard_map.99 = (bf16[144,1152]{1,0:T(8,128)(2,1)S(1)}, bf16[32,2176]{1,0:T(8,128)(2,1)S(1)}, bf16[32,2176]{1,0:T(8,128)(2,1)S(1)}, bf16[32,2176]{1,0:T(8,128)(2,1)S(1)}, bf16[32,2176]{1,0:T(8,128)(2,1)S(1)}) custom-call(s32[4]{0:T(128)S(1)} %iota_xor_fusion.place_ref, f32[144,128]{1,0:T(8,128)S(1)} %get-tuple-element.44.w_ref, ...), custom_call_target="tpu_custom_call" | custom-call | flops 1132462080 | bytes 6860800 | tf_op jit(solution)/shard_map/pallas_call | solution.py:313
  44.3 8.1 %collective-permute-done.12.refs_5_.far_a.refs_0_ = bf16[144,2048]{1,0:T(8,128)(2,1)S(1)} collective-permute-done((bf16[144,2048]{1,0:T(8,128)(2,1)S(1)}, bf16[144,2048]{1,0:T(8,128)(2,1)S(1)}, u32[]{:S(2)}, u32[]{:S(2)}) %collective-permute-start.12) | collective-permute-done | bytes 589856 | tf_op jit(solution)/shard_map/ppermute | solution.py:326
  52.4 0.0 collective-permute-done.9.refs_1_
  52.4 0.0 collective-permute-done.10.refs_2_
  52.4 0.7 collective-permute-done.11.refs_3_
  53.2 0.7 shard_map.100
  53.8 1.3 %collective-permute-start.17 = (bf16[144,2048]{1,0:T(8,128)(2,1)S(1)}, bf16[144,2048]{1,0:T(8,128)(2,1)S(1)}, u32[]{:S(2)}, u32[]{:S(2)}) collective-permute-start(bf16[144,2048]{1,0:T(8,128)(2,1)S(1)} %get-tuple-element.60.refs_4_), channel_id=1, source_target_pairs={{0,2},{1,3},{2,0},{3,1},{4,6},{5,7},{6,4},{7,5},{8,10},{9,11},{10,... | collective-permute-start | bytes 1769480 | tf_op jit(solution)/shard_map/ppermute | solution.py:326
  55.2 2.6 %shard_map.101 = (bf16[288,1152]{1,0:T(8,128)(2,1)S(1)}, bf16[32,2176]{1,0:T(8,128)(2,1)S(1)}, bf16[32,2176]{1,0:T(8,128)(2,1)S(1)}, bf16[32,2176]{1,0:T(8,128)(2,1)S(1)}, bf16[32,2176]{1,0:T(8,128)(2,1)S(1)}) custom-call(s32[4]{0:T(128)S(1)} %iota_xor_fusion.place_ref, f32[144,128]{1,0:T(8,128)S(1)} %get-tuple-element.57.w_ref, ...), custom_call_target="tpu_custom_call" | custom-call | flops 1132462080 | bytes 7524352 | tf_op jit(solution)/shard_map/pallas_call | solution.py:313
  57.8 0.1 collective-permute-start.13
  57.9 1.4 %collective-permute-start.14 = (bf16[32,2176]{1,0:T(8,128)(2,1)S(1)}, bf16[32,2176]{1,0:T(8,128)(2,1)S(1)}, u32[]{:S(2)}, u32[]{:S(2)}) collective-permute-start(bf16[32,2176]{1,0:T(8,128)(2,1)S(1)} %get-tuple-element.63), channel_id=1, source_target_pairs={{0,8},{4,12},{8,0},{12,4},{16,24},{20,28},{24,16},{28,20},{1,9},{5... | collective-permute-start | bytes 417800 | tf_op jit(solution)/shard_map/ppermute | solution.py:326
  59.3 1.2 %collective-permute-start.15 = (bf16[32,2176]{1,0:T(8,128)(2,1)S(1)}, bf16[32,2176]{1,0:T(8,128)(2,1)S(1)}, u32[]{:S(2)}, u32[]{:S(2)}) collective-permute-start(bf16[32,2176]{1,0:T(8,128)(2,1)S(1)} %get-tuple-element.64), channel_id=1, source_target_pairs={{0,4},{4,0},{8,12},{12,8},{16,20},{20,16},{24,28},{28,24},{1,5},{5... | collective-permute-start | bytes 417800 | tf_op jit(solution)/shard_map/ppermute | solution.py:326
  60.5 2.7 %collective-permute-done.13.b3 = bf16[32,2176]{1,0:T(8,128)(2,1)S(1)} collective-permute-done((bf16[32,2176]{1,0:T(8,128)(2,1)S(1)}, bf16[32,2176]{1,0:T(8,128)(2,1)S(1)}, u32[]{:S(2)}, u32[]{:S(2)}) %collective-permute-start.13) | collective-permute-done | bytes 139296 | tf_op jit(solution)/shard_map/ppermute | solution.py:326
  63.2 1.9 %collective-permute-done.14.b2 = bf16[32,2176]{1,0:T(8,128)(2,1)S(1)} collective-permute-done((bf16[32,2176]{1,0:T(8,128)(2,1)S(1)}, bf16[32,2176]{1,0:T(8,128)(2,1)S(1)}, u32[]{:S(2)}, u32[]{:S(2)}) %collective-permute-start.14) | collective-permute-done | bytes 139296 | tf_op jit(solution)/shard_map/ppermute | solution.py:326
  65.1 2.0 %collective-permute-done.15.b1 = bf16[32,2176]{1,0:T(8,128)(2,1)S(1)} collective-permute-done((bf16[32,2176]{1,0:T(8,128)(2,1)S(1)}, bf16[32,2176]{1,0:T(8,128)(2,1)S(1)}, u32[]{:S(2)}, u32[]{:S(2)}) %collective-permute-start.15) | collective-permute-done | bytes 139296 | tf_op jit(solution)/shard_map/ppermute | solution.py:326
  67.1 0.4 shard_map.102.refs_0_
  67.5 0.8 collective-permute-done.17.far_b.refs_1_
  68.3 0.1 shard_map.103
  68.4 1.4 %collective-permute-start.19 = (bf16[288,3200]{1,0:T(8,128)(2,1)S(1)}, bf16[288,3200]{1,0:T(8,128)(2,1)S(1)}, u32[]{:S(2)}, u32[]{:S(2)}) collective-permute-start(bf16[288,3200]{1,0:T(8,128)(2,1)S(1)} %shard_map.103), channel_id=1, source_target_pairs={{0,1},{1,0},{2,3},{3,2},{4,5},{5,4},{6,7},{7,6},{8,9},{9,8},{10,11... | collective-permute-start | bytes 5529608 | tf_op jit(solution)/shard_map/ppermute | solution.py:326
  69.8 1.3 %collective-permute-start.18 = (bf16[288,1152]{1,0:T(8,128)(2,1)S(1)}, bf16[288,1152]{1,0:T(8,128)(2,1)S(1)}, u32[]{:S(2)}, u32[]{:S(2)}) collective-permute-start(bf16[288,1152]{1,0:T(8,128)(2,1)S(1)} %get-tuple-element.65.mid_ref), channel_id=1, source_target_pairs={{0,2},{1,3},{2,0},{3,1},{4,6},{5,7},{6,4},{7,5},{8,10},{9,11},{10,... | collective-permute-start | bytes 1990664 | tf_op jit(solution)/shard_map/ppermute | solution.py:326
  71.1 0.2 collective-permute-start.16
  71.3 2.2 %collective-permute-start.6 = (bf16[32,2176]{1,0:T(8,128)(2,1)S(1)}, bf16[32,2176]{1,0:T(8,128)(2,1)S(1)}, u32[]{:S(2)}, u32[]{:S(2)}) collective-permute-start(bf16[32,2176]{1,0:T(8,128)(2,1)S(1)} %get-tuple-element.50), channel_id=1, source_target_pairs={{0,12},{4,8},{8,4},{12,0},{16,28},{20,24},{24,20},{28,16},{1,13},{... | collective-permute-start | bytes 417800 | tf_op jit(solution)/shard_map/ppermute | solution.py:326
  73.5 0.0 collective-permute-start.7
  73.5 0.0 collective-permute-done.19.near_ref
  73.5 1.2 %collective-permute-start.8 = (bf16[32,2176]{1,0:T(8,128)(2,1)S(1)}, bf16[32,2176]{1,0:T(8,128)(2,1)S(1)}, u32[]{:S(2)}, u32[]{:S(2)}) collective-permute-start(bf16[32,2176]{1,0:T(8,128)(2,1)S(1)} %get-tuple-element.52), channel_id=1, source_target_pairs={{0,4},{4,0},{8,12},{12,8},{16,20},{20,16},{24,28},{28,24},{1,5},{5... | collective-permute-start | bytes 417800 | tf_op jit(solution)/shard_map/ppermute | solution.py:326
  74.7 1.2 %shard_map.104 = (f32[512,768]{1,0:T(8,128)S(1)}, f32[512,384]{1,0:T(8,128)S(1)}) custom-call(bf16[144,1024]{1,0:T(8,128)(2,1)S(1)} %get-tuple-element.45.refs_0_.refs_2_.rows_a, bf16[144,1024]{1,0:T(8,128)(2,1)S(1)} %get-tuple-element.58.refs_2_.rows_b, bf16[288,3200]{1,0:T(8,128)(2,1)S(1)} %collective-permute-done.19.near_ref, ...), custom_call_target="tpu_custom_call" | custom-call | flops 679477248 | bytes 5455872 | tf_op jit(solution)/shard_map/pallas_call | solution.py:313
  75.9 4.0 %collective-permute-done.6.refs_3_.b3 = bf16[32,2176]{1,0:T(8,128)(2,1)S(1)} collective-permute-done((bf16[32,2176]{1,0:T(8,128)(2,1)S(1)}, bf16[32,2176]{1,0:T(8,128)(2,1)S(1)}, u32[]{:S(2)}, u32[]{:S(2)}) %collective-permute-start.6) | collective-permute-done | bytes 139296 | tf_op jit(solution)/shard_map/ppermute | solution.py:326
  79.9 3.0 %collective-permute-done.7.refs_4_.b2 = bf16[32,2176]{1,0:T(8,128)(2,1)S(1)} collective-permute-done((bf16[32,2176]{1,0:T(8,128)(2,1)S(1)}, bf16[32,2176]{1,0:T(8,128)(2,1)S(1)}, u32[]{:S(2)}, u32[]{:S(2)}) %collective-permute-start.7) | collective-permute-done | bytes 139296 | tf_op jit(solution)/shard_map/ppermute | solution.py:326
  82.9 0.0 collective-permute-done.8.refs_5_.b1
  82.9 3.1 %collective-permute-done.16.refs_2_.far_ref = bf16[32,4224]{1,0:T(8,128)(2,1)S(1)} collective-permute-done((bf16[32,4224]{1,0:T(8,128)(2,1)S(1)}, bf16[32,4224]{1,0:T(8,128)(2,1)S(1)}, u32[]{:S(2)}, u32[]{:S(2)}) %collective-permute-start.16) | collective-permute-done | bytes 270368 | tf_op jit(solution)/shard_map/ppermute | solution.py:326
  86.0 0.3 collective-permute-done.18.refs_0_
  86.3 0.8 collective-permute-start.20
  87.2 2.3 %shard_map.106 = (bf16[64,2048]{1,0:T(8,128)(2,1)}, bf16[4,64]{1,0:T(4,128)(2,1)}, f32[512,768]{1,0:T(8,128)S(1)}, f32[512,384]{1,0:T(8,128)S(1)}) custom-call(s32[8]{0:T(128)S(1)} %iota_xor_fusion.1.peer_ref, s32[4,64]{1,0:T(4,128)S(1)} %bitcast.8, f32[8,64]{1,0:T(8,128)S(1)} %get-tuple-element.39.w_ref, bf16[32,2176]{1,0:T(8,128)(2,1)S(1)} %get-tuple-element.49.b0, ...), custom_call_target="tpu_custom_call" | custom-call | flops 377487360 | bytes 7392768 | tf_op jit(solution)/shard_map/pallas_call | solution.py:313
  89.5 0.0 collective-permute-done.20.mid_ref
  89.5 1.8 %shard_map.107 = (f32[512,768]{1,0:T(8,128)}, f32[512,384]{1,0:T(8,128)}) custom-call(bf16[288,3200]{1,0:T(8,128)(2,1)S(1)} %collective-permute-done.19.near_ref, bf16[288,1152]{1,0:T(8,128)(2,1)S(1)} %collective-permute-done.20.mid_ref, f32[512,768]{1,0:T(8,128)S(1)} %get-tuple-element.70.in_part, f32[512,384]{1,0:T(8,128)S(1)} %get-tuple-element.71.out_part), custom_call_target="tpu_custom_call" | custom-call | flops 339738624 | bytes 4866048 | tf_op jit(solution)/shard_map/pallas_call | solution.py:313
  (4 shorter events, 0.0 us)
Async XLA Ops:
  0.6 3.6 %copy-start.3 = (bf16[64,4]{0,1:T(4,128)(2,1)S(1)}, bf16[64,4]{0,1:T(4,128)(2,1)}, u32[]{:S(2)}) copy-start(bf16[64,4]{0,1:T(4,128)(2,1)} %param.9) | copy-start | bytes 1540
  0.6 3.5 %copy-start.2 = (s32[64,4]{0,1:T(4,128)S(1)}, s32[64,4]{0,1:T(4,128)}, u32[]{:S(2)}) copy-start(s32[64,4]{0,1:T(4,128)} %param.8) | copy-start | bytes 3076
  0.7 3.5 %copy-start.1 = (bf16[64,2048]{1,0:T(8,128)(2,1)S(1)}, bf16[64,2048]{1,0:T(8,128)(2,1)}, u32[]{:S(2)}) copy-start(bf16[64,2048]{1,0:T(8,128)(2,1)} %dy_ref.1) | copy-start | bytes 786436
  0.7 3.5 %copy-start = (bf16[64,2048]{1,0:T(8,128)(2,1)S(1)}, bf16[64,2048]{1,0:T(8,128)(2,1)}, u32[]{:S(2)}) copy-start(bf16[64,2048]{1,0:T(8,128)(2,1)} %x_ref.1) | copy-start | bytes 786436
  2.1 32.4 %collective-permute-start.4 = (bf16[512,1152]{1,0:T(8,128)(2,1)S(1)}, bf16[512,1152]{1,0:T(8,128)(2,1)S(1)}, u32[]{:S(2)}, u32[]{:S(2)}) collective-permute-start(bf16[512,1152]{1,0:T(8,128)(2,1)S(1)} %pad_maximum_fusion.own_ref), channel_id=1, source_target_pairs={{0,2},{1,3},{2,0},{3,1},{4,6},{5,7},{6,4},{7,5},{8,10},{9,11},{10,... | collective-permute-start | bytes 3538952 | tf_op jit(solution)/shard_map/ppermute | solution.py:326
  4.8 28.5 %collective-permute-start.3 = (bf16[64,4224]{1,0:T(8,128)(2,1)S(1)}, bf16[64,4224]{1,0:T(8,128)(2,1)S(1)}, u32[]{:S(2)}, u32[]{:S(2)}) collective-permute-start(bf16[64,4224]{1,0:T(8,128)(2,1)S(1)} %get-tuple-element.40.joint_ref), channel_id=1, source_target_pairs={{0,16},{4,20},{8,24},{12,28},{16,0},{20,4},{24,8},{28,12},{1,17},{... | collective-permute-start | bytes 1622024 | tf_op jit(solution)/shard_map/ppermute | solution.py:326
  8.6 15.3 %collective-permute-start = (bf16[64,2176]{1,0:T(8,128)(2,1)}, bf16[64,2176]{1,0:T(8,128)(2,1)}, u32[]{:S(2)}, u32[]{:S(2)}) collective-permute-start(bf16[64,2176]{1,0:T(8,128)(2,1)} %get-tuple-element.41), channel_id=1, source_target_pairs={{0,12},{4,8},{8,4},{12,0},{16,28},{20,24},{24,20},{28,16},{1,13},{... | collective-permute-start | bytes 835592 | tf_op jit(solution)/shard_map/ppermute | solution.py:326
  10.8 22.4 %collective-permute-start.1 = (bf16[64,2176]{1,0:T(8,128)(2,1)}, bf16[64,2176]{1,0:T(8,128)(2,1)}, u32[]{:S(2)}, u32[]{:S(2)}) collective-permute-start(bf16[64,2176]{1,0:T(8,128)(2,1)} %get-tuple-element.42), channel_id=1, source_target_pairs={{0,8},{4,12},{8,0},{12,4},{16,24},{20,28},{24,16},{28,20},{1,9},{5... | collective-permute-start | bytes 835592 | tf_op jit(solution)/shard_map/ppermute | solution.py:326
  11.0 22.3 %collective-permute-start.2 = (bf16[64,2176]{1,0:T(8,128)(2,1)}, bf16[64,2176]{1,0:T(8,128)(2,1)}, u32[]{:S(2)}, u32[]{:S(2)}) collective-permute-start(bf16[64,2176]{1,0:T(8,128)(2,1)} %get-tuple-element.43), channel_id=1, source_target_pairs={{0,4},{4,0},{8,12},{12,8},{16,20},{20,16},{24,28},{28,24},{1,5},{5... | collective-permute-start | bytes 835592 | tf_op jit(solution)/shard_map/ppermute | solution.py:326
  35.3 6.4 %collective-permute-start.5 = (bf16[1024,1152]{1,0:T(8,128)(2,1)S(1)}, bf16[1024,1152]{1,0:T(8,128)(2,1)S(1)}, u32[]{:S(2)}, u32[]{:S(2)}) collective-permute-start(bf16[1024,1152]{1,0:T(8,128)(2,1)S(1)} %shard_map.98.refs_0_), channel_id=1, source_target_pairs={{0,1},{1,0},{2,3},{3,2},{4,5},{5,4},{6,7},{7,6},{8,9},{9,8},{10,11... | collective-permute-start | bytes 7077896 | tf_op jit(solution)/shard_map/ppermute | solution.py:326
  37.5 14.9 %collective-permute-start.12 = (bf16[144,2048]{1,0:T(8,128)(2,1)S(1)}, bf16[144,2048]{1,0:T(8,128)(2,1)S(1)}, u32[]{:S(2)}, u32[]{:S(2)}) collective-permute-start(bf16[144,2048]{1,0:T(8,128)(2,1)S(1)} %get-tuple-element.48.refs_4_), channel_id=1, source_target_pairs={{0,2},{1,3},{2,0},{3,1},{4,6},{5,7},{6,4},{7,5},{8,10},{9,11},{10,... | collective-permute-start | bytes 1769480 | tf_op jit(solution)/shard_map/ppermute | solution.py:326
  37.7 14.7 %collective-permute-start.9 = (bf16[64,2176]{1,0:T(8,128)(2,1)S(1)}, bf16[64,2176]{1,0:T(8,128)(2,1)S(1)}, u32[]{:S(2)}, u32[]{:S(2)}) collective-permute-start(bf16[64,2176]{1,0:T(8,128)(2,1)S(1)} %get-tuple-element.53), channel_id=1, source_target_pairs={{0,12},{4,8},{8,4},{12,0},{16,28},{20,24},{24,20},{28,16},{1,13},{... | collective-permute-start | bytes 835592 | tf_op jit(solution)/shard_map/ppermute | solution.py:326
  37.7 14.7 %collective-permute-start.10 = (bf16[64,2176]{1,0:T(8,128)(2,1)S(1)}, bf16[64,2176]{1,0:T(8,128)(2,1)S(1)}, u32[]{:S(2)}, u32[]{:S(2)}) collective-permute-start(bf16[64,2176]{1,0:T(8,128)(2,1)S(1)} %get-tuple-element.54), channel_id=1, source_target_pairs={{0,8},{4,12},{8,0},{12,4},{16,24},{20,28},{24,16},{28,20},{1,9},{5... | collective-permute-start | bytes 835592 | tf_op jit(solution)/shard_map/ppermute | solution.py:326
  39.2 14.0 %collective-permute-start.11 = (bf16[64,2176]{1,0:T(8,128)(2,1)S(1)}, bf16[64,2176]{1,0:T(8,128)(2,1)S(1)}, u32[]{:S(2)}, u32[]{:S(2)}) collective-permute-start(bf16[64,2176]{1,0:T(8,128)(2,1)S(1)} %get-tuple-element.55), channel_id=1, source_target_pairs={{0,4},{4,0},{8,12},{12,8},{16,20},{20,16},{24,28},{28,24},{1,5},{5... | collective-permute-start | bytes 835592 | tf_op jit(solution)/shard_map/ppermute | solution.py:326
  53.8 14.5 %collective-permute-start.17 = (bf16[144,2048]{1,0:T(8,128)(2,1)S(1)}, bf16[144,2048]{1,0:T(8,128)(2,1)S(1)}, u32[]{:S(2)}, u32[]{:S(2)}) collective-permute-start(bf16[144,2048]{1,0:T(8,128)(2,1)S(1)} %get-tuple-element.60.refs_4_), channel_id=1, source_target_pairs={{0,2},{1,3},{2,0},{3,1},{4,6},{5,7},{6,4},{7,5},{8,10},{9,11},{10,... | collective-permute-start | bytes 1769480 | tf_op jit(solution)/shard_map/ppermute | solution.py:326
  57.8 5.4 %collective-permute-start.13 = (bf16[32,2176]{1,0:T(8,128)(2,1)S(1)}, bf16[32,2176]{1,0:T(8,128)(2,1)S(1)}, u32[]{:S(2)}, u32[]{:S(2)}) collective-permute-start(bf16[32,2176]{1,0:T(8,128)(2,1)S(1)} %get-tuple-element.62), channel_id=1, source_target_pairs={{0,12},{4,8},{8,4},{12,0},{16,28},{20,24},{24,20},{28,16},{1,13},{... | collective-permute-start | bytes 417800 | tf_op jit(solution)/shard_map/ppermute | solution.py:326
  57.9 7.2 %collective-permute-start.14 = (bf16[32,2176]{1,0:T(8,128)(2,1)S(1)}, bf16[32,2176]{1,0:T(8,128)(2,1)S(1)}, u32[]{:S(2)}, u32[]{:S(2)}) collective-permute-start(bf16[32,2176]{1,0:T(8,128)(2,1)S(1)} %get-tuple-element.63), channel_id=1, source_target_pairs={{0,8},{4,12},{8,0},{12,4},{16,24},{20,28},{24,16},{28,20},{1,9},{5... | collective-permute-start | bytes 417800 | tf_op jit(solution)/shard_map/ppermute | solution.py:326
  59.3 7.8 %collective-permute-start.15 = (bf16[32,2176]{1,0:T(8,128)(2,1)S(1)}, bf16[32,2176]{1,0:T(8,128)(2,1)S(1)}, u32[]{:S(2)}, u32[]{:S(2)}) collective-permute-start(bf16[32,2176]{1,0:T(8,128)(2,1)S(1)} %get-tuple-element.64), channel_id=1, source_target_pairs={{0,4},{4,0},{8,12},{12,8},{16,20},{20,16},{24,28},{28,24},{1,5},{5... | collective-permute-start | bytes 417800 | tf_op jit(solution)/shard_map/ppermute | solution.py:326
  68.4 5.1 %collective-permute-start.19 = (bf16[288,3200]{1,0:T(8,128)(2,1)S(1)}, bf16[288,3200]{1,0:T(8,128)(2,1)S(1)}, u32[]{:S(2)}, u32[]{:S(2)}) collective-permute-start(bf16[288,3200]{1,0:T(8,128)(2,1)S(1)} %shard_map.103), channel_id=1, source_target_pairs={{0,1},{1,0},{2,3},{3,2},{4,5},{5,4},{6,7},{7,6},{8,9},{9,8},{10,11... | collective-permute-start | bytes 5529608 | tf_op jit(solution)/shard_map/ppermute | solution.py:326
  69.8 16.5 %collective-permute-start.18 = (bf16[288,1152]{1,0:T(8,128)(2,1)S(1)}, bf16[288,1152]{1,0:T(8,128)(2,1)S(1)}, u32[]{:S(2)}, u32[]{:S(2)}) collective-permute-start(bf16[288,1152]{1,0:T(8,128)(2,1)S(1)} %get-tuple-element.65.mid_ref), channel_id=1, source_target_pairs={{0,2},{1,3},{2,0},{3,1},{4,6},{5,7},{6,4},{7,5},{8,10},{9,11},{10,... | collective-permute-start | bytes 1990664 | tf_op jit(solution)/shard_map/ppermute | solution.py:326
  71.1 14.9 %collective-permute-start.16 = (bf16[32,4224]{1,0:T(8,128)(2,1)S(1)}, bf16[32,4224]{1,0:T(8,128)(2,1)S(1)}, u32[]{:S(2)}, u32[]{:S(2)}) collective-permute-start(bf16[32,4224]{1,0:T(8,128)(2,1)S(1)} %shard_map.102.refs_0_), channel_id=1, source_target_pairs={{0,16},{4,20},{8,24},{12,28},{16,0},{20,4},{24,8},{28,12},{1,17},{... | collective-permute-start | bytes 811016 | tf_op jit(solution)/shard_map/ppermute | solution.py:326
  71.3 8.6 %collective-permute-start.6 = (bf16[32,2176]{1,0:T(8,128)(2,1)S(1)}, bf16[32,2176]{1,0:T(8,128)(2,1)S(1)}, u32[]{:S(2)}, u32[]{:S(2)}) collective-permute-start(bf16[32,2176]{1,0:T(8,128)(2,1)S(1)} %get-tuple-element.50), channel_id=1, source_target_pairs={{0,12},{4,8},{8,4},{12,0},{16,28},{20,24},{24,20},{28,16},{1,13},{... | collective-permute-start | bytes 417800 | tf_op jit(solution)/shard_map/ppermute | solution.py:326
  73.5 9.4 %collective-permute-start.7 = (bf16[32,2176]{1,0:T(8,128)(2,1)S(1)}, bf16[32,2176]{1,0:T(8,128)(2,1)S(1)}, u32[]{:S(2)}, u32[]{:S(2)}) collective-permute-start(bf16[32,2176]{1,0:T(8,128)(2,1)S(1)} %get-tuple-element.51), channel_id=1, source_target_pairs={{0,8},{4,12},{8,0},{12,4},{16,24},{20,28},{24,16},{28,20},{1,9},{5... | collective-permute-start | bytes 417800 | tf_op jit(solution)/shard_map/ppermute | solution.py:326
  73.5 9.4 %collective-permute-start.8 = (bf16[32,2176]{1,0:T(8,128)(2,1)S(1)}, bf16[32,2176]{1,0:T(8,128)(2,1)S(1)}, u32[]{:S(2)}, u32[]{:S(2)}) collective-permute-start(bf16[32,2176]{1,0:T(8,128)(2,1)S(1)} %get-tuple-element.52), channel_id=1, source_target_pairs={{0,4},{4,0},{8,12},{12,8},{16,20},{20,16},{24,28},{28,24},{1,5},{5... | collective-permute-start | bytes 417800 | tf_op jit(solution)/shard_map/ppermute | solution.py:326
  86.3 3.1 %collective-permute-start.20 = (bf16[288,1152]{1,0:T(8,128)(2,1)S(1)}, bf16[288,1152]{1,0:T(8,128)(2,1)S(1)}, u32[]{:S(2)}, u32[]{:S(2)}) collective-permute-start(bf16[288,1152]{1,0:T(8,128)(2,1)S(1)} %shard_map.105.refs_2_), channel_id=1, source_target_pairs={{0,1},{1,0},{2,3},{3,2},{4,5},{5,4},{6,7},{7,6},{8,9},{9,8},{10,11... | collective-permute-start | bytes 1990664 | tf_op jit(solution)/shard_map/ppermute | solution.py:326

commit v14 on v13

--- a/solution.py
+++ b/solution.py
@@ -112,13 +112,10 @@
     pack_blocks(experts, joint_ref, refs[-1 - len(experts) : -1], refs[-1])
 
 
-def slice_kernel(own, place_ref, *refs):
+def slice_kernel(place_ref, *refs):
     blocks, parts = 4, 4
-    keep_ref, near_ref, far_ref, weight_ref, fold, kept = refs[-6:]
-    in_refs = list(refs[:blocks])
-    if own:
-        in_refs[0] = kept
-        pack_blocks([own], refs[0], [kept], fold.at[0, pl.ds(0, 16)])
+    keep_ref, near_ref, far_ref, weight_ref, fold = refs[-5:]
+    in_refs = refs[:blocks]
     main = in_refs[0].shape[0] // 2
     depth = keep_ref.shape[1] // 2
     width = parts * depth
@@ -366,9 +363,9 @@
             4 * (len(experts) * main + 16) * token_count * width,
         )
 
-    def sliced(own, packed, after):
+    def sliced(packed, after):
         return call(
-            functools.partial(slice_kernel, own),
+            slice_kernel,
             [
                 ((rows, 2 * depth), BF16),
                 ((rows, 2 * depth), BF16),
@@ -378,13 +375,13 @@
             [places],
             packed,
             after,
-            [pltpu.VMEM((2, half * chunks, LANES), F32), pltpu.VMEM(*packed_shape)],
+            [pltpu.VMEM((2, (half + 1) * chunks, LANES), F32)],
             0,
         )
 
     own = [swap(value, "expert", j + 1) for j, value in enumerate(pack(range(half + 1, blocks), joint, []))]
     (kept,) = pack([half], joint, [own[2]])
-    *own_slices, own_weight = sliced(None, [kept, *own[::-1]], [far_joint])
+    *own_slices, own_weight = sliced([kept, *own[::-1]], [far_joint])
     own_far = swap(own_slices[2], "dp", 2)
     far = pack(range(half), far_joint, [own_slices[0], far_weights])
     far = [far[0]] + [swap(far[j], "expert", j) for j in range(1, half)]
@@ -414,13 +411,13 @@
     own_mid, *near_back = middle(own_slices, own_weight, [], [])
     near_back = [near_back[0], *near_back[:0:-1]]
     near_back = near_back[:1] + [swap(near_back[j], "expert", j) for j in range(1, half)]
-    *far_slices, far_weight = sliced(None, [far[0], *far[:0:-1]], [own_mid, own_far])
+    *far_slices, far_weight = sliced([far[0], *far[:0:-1]], [own_mid, own_far])
     far_far = swap(far_slices[2], "dp", 2)
     mid, *far_back = middle(far_slices, far_weight, [own_mid], [])
 
     sum_scratch = [
         pltpu.VMEM((half * main + 16, width), BF16),
-        pltpu.VMEM((half * chunks, LANES), F32),
+        pltpu.VMEM(((half + 1) * chunks, LANES), F32),
     ]
     sum_flops = 2 * (half * main + 16) * width * token_count
     far_back = [far_back[0], *far_back[:0:-1]]

time: 91.4 us -> 91.4 us (level)
  no operation moved by 1% of the time
where the time goes in v14:
time: 91.4 us; the launch traced here: 91.2 us
  waiting for transfers between devices  49.6 us (54%)
  starting transfers between devices  23.3 us (25%)
  Pallas kernels  16.1 us (18%)
  other arithmetic  1.41 us (2%)
    ppermute x21, waiting for transfers between devices, swap(): lax.ppermute(value, axis, [(i, i ^ mask) for i in range(lax.axis_size(axi...  49.6 us
    ppermute x21, starting transfers between devices, swap(): lax.ppermute(value, axis, [(i, i ^ mask) for i in range(lax.axis_size(axi...  23.3 us
    pallas_call x15, Pallas kernels, call(): pl.pallas_call(kernel, out_shape=tuple(outs), in_specs=[on_smem] * len(sm...  16.1 us
  transfers between devices with their start and end apart: 21, of which 13 were waited for; matrix products, arithmetic and copies ran while one was open for 0% of the time, Pallas kernels for 14%

profile of v14, /device:TPU:1, one launch (start us, length us, event | category | flops | bytes accessed | tf_op | source)
XLA Modules:
  0.0 91.2 jit_solution(10451179489024576096)
XLA Ops:
  0.6 0.0 copy-start.3
  0.6 0.0 copy-start.2
  0.7 0.0 copy-start.1
  0.7 0.0 copy-start
  0.7 1.4 %pad_maximum_fusion.own_ref = bf16[512,1152]{1,0:T(8,128)(2,1)S(1)} fusion(bf16[512,384]{1,0:T(8,128)(2,1)} %bitcast.11, bf16[512,768]{1,0:T(8,128)(2,1)} %bitcast.10), kind=kLoop, calls=%fused_computation | loop fusion | flops 2359296 | bytes 2359296 | tf_op jit(solution)/shard_map/concatenate | solution.py:352
  2.1 2.1 %collective-permute-start.4 = (bf16[512,1152]{1,0:T(8,128)(2,1)S(1)}, bf16[512,1152]{1,0:T(8,128)(2,1)S(1)}, u32[]{:S(2)}, u32[]{:S(2)}) collective-permute-start(bf16[512,1152]{1,0:T(8,128)(2,1)S(1)} %pad_maximum_fusion.own_ref), channel_id=1, source_target_pairs={{0,2},{1,3},{2,0},{3,1},{4,6},{5,7},{6,4},{7,5},{8,10},{9,11},{10,... | collective-permute-start | bytes 3538952 | tf_op jit(solution)/shard_map/ppermute | solution.py:323
  4.2 0.0 copy-done.2
  4.2 0.0 copy-done.1
  4.2 0.0 copy-done
  4.2 0.6 shard_map.93
  4.8 2.4 %collective-permute-start.3 = (bf16[64,4224]{1,0:T(8,128)(2,1)S(1)}, bf16[64,4224]{1,0:T(8,128)(2,1)S(1)}, u32[]{:S(2)}, u32[]{:S(2)}) collective-permute-start(bf16[64,4224]{1,0:T(8,128)(2,1)S(1)} %get-tuple-element.40.joint_ref), channel_id=1, source_target_pairs={{0,16},{4,20},{8,24},{12,28},{16,0},{20,4},{24,8},{28,12},{1,17},{... | collective-permute-start | bytes 1622024 | tf_op jit(solution)/shard_map/ppermute | solution.py:323
  7.2 1.4 %shard_map.94 = (bf16[64,2176]{1,0:T(8,128)(2,1)}, bf16[64,2176]{1,0:T(8,128)(2,1)}, bf16[64,2176]{1,0:T(8,128)(2,1)}) custom-call(bf16[64,4224]{1,0:T(8,128)(2,1)S(1)} %get-tuple-element.40.joint_ref), custom_call_target="tpu_custom_call" | custom-call | flops 58720256 | bytes 1376256 | tf_op jit(solution)/shard_map/pallas_call | solution.py:310
  8.6 2.3 %collective-permute-start = (bf16[64,2176]{1,0:T(8,128)(2,1)}, bf16[64,2176]{1,0:T(8,128)(2,1)}, u32[]{:S(2)}, u32[]{:S(2)}) collective-permute-start(bf16[64,2176]{1,0:T(8,128)(2,1)} %get-tuple-element.41), channel_id=1, source_target_pairs={{0,12},{4,8},{8,4},{12,0},{16,28},{20,24},{24,20},{28,16},{1,13},{... | collective-permute-start | bytes 835592 | tf_op jit(solution)/shard_map/ppermute | solution.py:323
  10.8 0.2 collective-permute-start.1
  11.0 0.2 collective-permute-start.2
  11.2 12.7 %collective-permute-done.refs_0_.refs_1_ = bf16[64,2176]{1,0:T(8,128)(2,1)} collective-permute-done((bf16[64,2176]{1,0:T(8,128)(2,1)}, bf16[64,2176]{1,0:T(8,128)(2,1)}, u32[]{:S(2)}, u32[]{:S(2)}) %collective-permute-start) | collective-permute-done | bytes 278560 | tf_op jit(solution)/shard_map/ppermute | solution.py:323
  23.9 0.4 shard_map.95.refs_0_
  24.3 9.0 %collective-permute-done.1.refs_2_ = bf16[64,2176]{1,0:T(8,128)(2,1)} collective-permute-done((bf16[64,2176]{1,0:T(8,128)(2,1)}, bf16[64,2176]{1,0:T(8,128)(2,1)}, u32[]{:S(2)}, u32[]{:S(2)}) %collective-permute-start.1) | collective-permute-done | bytes 278560 | tf_op jit(solution)/shard_map/ppermute | solution.py:323
  33.3 0.0 collective-permute-done.2.refs_3_
  33.3 0.0 collective-permute-done.3.refs_4_.joint_ref
  33.3 1.2 %shard_map.96 = (bf16[144,1024]{1,0:T(8,128)(2,1)S(1)}, bf16[144,1024]{1,0:T(8,128)(2,1)S(1)}, bf16[144,2048]{1,0:T(8,128)(2,1)S(1)}, f32[144,128]{1,0:T(8,128)S(1)}) custom-call(s32[4]{0:T(128)S(1)} %iota_xor_fusion.place_ref, bf16[64,2176]{1,0:T(8,128)(2,1)S(1)} %shard_map.95.refs_0_, bf16[64,2176]{1,0:T(8,128)(2,1)} %collective-permute-done.refs_0_.refs_1_, ...), custom_call_target="tpu_custom_call" | custom-call | bytes 2367488 | tf_op jit(solution)/shard_map/pallas_call | solution.py:310
  34.5 0.0 collective-permute-done.4.refs_1_.far_ref
  34.5 0.6 shard_map.97
  35.1 0.2 shard_map.98.refs_0_
  35.3 2.2 %collective-permute-start.5 = (bf16[1024,1152]{1,0:T(8,128)(2,1)S(1)}, bf16[1024,1152]{1,0:T(8,128)(2,1)S(1)}, u32[]{:S(2)}, u32[]{:S(2)}) collective-permute-start(bf16[1024,1152]{1,0:T(8,128)(2,1)S(1)} %shard_map.98.refs_0_), channel_id=1, source_target_pairs={{0,1},{1,0},{2,3},{3,2},{4,5},{5,4},{6,7},{7,6},{8,9},{9,8},{10,11... | collective-permute-start | bytes 7077896 | tf_op jit(solution)/shard_map/ppermute | solution.py:323
  37.5 0.2 collective-permute-start.12
  37.7 0.0 collective-permute-start.9
  37.7 1.5 %collective-permute-start.10 = (bf16[64,2176]{1,0:T(8,128)(2,1)S(1)}, bf16[64,2176]{1,0:T(8,128)(2,1)S(1)}, u32[]{:S(2)}, u32[]{:S(2)}) collective-permute-start(bf16[64,2176]{1,0:T(8,128)(2,1)S(1)} %get-tuple-element.54), channel_id=1, source_target_pairs={{0,8},{4,12},{8,0},{12,4},{16,24},{20,28},{24,16},{28,20},{1,9},{5... | collective-permute-start | bytes 835592 | tf_op jit(solution)/shard_map/ppermute | solution.py:323
  39.2 1.2 %collective-permute-start.11 = (bf16[64,2176]{1,0:T(8,128)(2,1)S(1)}, bf16[64,2176]{1,0:T(8,128)(2,1)S(1)}, u32[]{:S(2)}, u32[]{:S(2)}) collective-permute-start(bf16[64,2176]{1,0:T(8,128)(2,1)S(1)} %get-tuple-element.55), channel_id=1, source_target_pairs={{0,4},{4,0},{8,12},{12,8},{16,20},{20,16},{24,28},{28,24},{1,5},{5... | collective-permute-start | bytes 835592 | tf_op jit(solution)/shard_map/ppermute | solution.py:323
  40.4 1.3 %collective-permute-done.5.refs_1_ = bf16[1024,1152]{1,0:T(8,128)(2,1)S(1)} collective-permute-done((bf16[1024,1152]{1,0:T(8,128)(2,1)S(1)}, bf16[1024,1152]{1,0:T(8,128)(2,1)S(1)}, u32[]{:S(2)}, u32[]{:S(2)}) %collective-permute-start.5) | collective-permute-done | bytes 2359328 | tf_op jit(solution)/shard_map/ppermute | solution.py:323
  41.7 2.6 %shard_map.99 = (bf16[144,1152]{1,0:T(8,128)(2,1)S(1)}, bf16[32,2176]{1,0:T(8,128)(2,1)S(1)}, bf16[32,2176]{1,0:T(8,128)(2,1)S(1)}, bf16[32,2176]{1,0:T(8,128)(2,1)S(1)}, bf16[32,2176]{1,0:T(8,128)(2,1)S(1)}) custom-call(s32[4]{0:T(128)S(1)} %iota_xor_fusion.place_ref, f32[144,128]{1,0:T(8,128)S(1)} %get-tuple-element.44.w_ref, ...), custom_call_target="tpu_custom_call" | custom-call | flops 1132462080 | bytes 6860800 | tf_op jit(solution)/shard_map/pallas_call | solution.py:310
  44.3 8.1 %collective-permute-done.12.refs_5_.far_a.refs_0_ = bf16[144,2048]{1,0:T(8,128)(2,1)S(1)} collective-permute-done((bf16[144,2048]{1,0:T(8,128)(2,1)S(1)}, bf16[144,2048]{1,0:T(8,128)(2,1)S(1)}, u32[]{:S(2)}, u32[]{:S(2)}) %collective-permute-start.12) | collective-permute-done | bytes 589856 | tf_op jit(solution)/shard_map/ppermute | solution.py:323
  52.4 0.0 collective-permute-done.9.refs_1_
  52.4 0.0 collective-permute-done.10.refs_2_
  52.4 0.7 collective-permute-done.11.refs_3_
  53.2 0.7 shard_map.100
  53.8 1.3 %collective-permute-start.17 = (bf16[144,2048]{1,0:T(8,128)(2,1)S(1)}, bf16[144,2048]{1,0:T(8,128)(2,1)S(1)}, u32[]{:S(2)}, u32[]{:S(2)}) collective-permute-start(bf16[144,2048]{1,0:T(8,128)(2,1)S(1)} %get-tuple-element.60.refs_4_), channel_id=1, source_target_pairs={{0,2},{1,3},{2,0},{3,1},{4,6},{5,7},{6,4},{7,5},{8,10},{9,11},{10,... | collective-permute-start | bytes 1769480 | tf_op jit(solution)/shard_map/ppermute | solution.py:323
  55.2 2.6 %shard_map.101 = (bf16[288,1152]{1,0:T(8,128)(2,1)S(1)}, bf16[32,2176]{1,0:T(8,128)(2,1)S(1)}, bf16[32,2176]{1,0:T(8,128)(2,1)S(1)}, bf16[32,2176]{1,0:T(8,128)(2,1)S(1)}, bf16[32,2176]{1,0:T(8,128)(2,1)S(1)}) custom-call(s32[4]{0:T(128)S(1)} %iota_xor_fusion.place_ref, f32[144,128]{1,0:T(8,128)S(1)} %get-tuple-element.57.w_ref, ...), custom_call_target="tpu_custom_call" | custom-call | flops 1132462080 | bytes 7524352 | tf_op jit(solution)/shard_map/pallas_call | solution.py:310
  57.8 0.1 collective-permute-start.13
  57.9 1.4 %collective-permute-start.14 = (bf16[32,2176]{1,0:T(8,128)(2,1)S(1)}, bf16[32,2176]{1,0:T(8,128)(2,1)S(1)}, u32[]{:S(2)}, u32[]{:S(2)}) collective-permute-start(bf16[32,2176]{1,0:T(8,128)(2,1)S(1)} %get-tuple-element.63), channel_id=1, source_target_pairs={{0,8},{4,12},{8,0},{12,4},{16,24},{20,28},{24,16},{28,20},{1,9},{5... | collective-permute-start | bytes 417800 | tf_op jit(solution)/shard_map/ppermute | solution.py:323
  59.3 1.2 %collective-permute-start.15 = (bf16[32,2176]{1,0:T(8,128)(2,1)S(1)}, bf16[32,2176]{1,0:T(8,128)(2,1)S(1)}, u32[]{:S(2)}, u32[]{:S(2)}) collective-permute-start(bf16[32,2176]{1,0:T(8,128)(2,1)S(1)} %get-tuple-element.64), channel_id=1, source_target_pairs={{0,4},{4,0},{8,12},{12,8},{16,20},{20,16},{24,28},{28,24},{1,5},{5... | collective-permute-start | bytes 417800 | tf_op jit(solution)/shard_map/ppermute | solution.py:323
  60.5 2.7 %collective-permute-done.13.b3 = bf16[32,2176]{1,0:T(8,128)(2,1)S(1)} collective-permute-done((bf16[32,2176]{1,0:T(8,128)(2,1)S(1)}, bf16[32,2176]{1,0:T(8,128)(2,1)S(1)}, u32[]{:S(2)}, u32[]{:S(2)}) %collective-permute-start.13) | collective-permute-done | bytes 139296 | tf_op jit(solution)/shard_map/ppermute | solution.py:323
  63.2 1.9 %collective-permute-done.14.b2 = bf16[32,2176]{1,0:T(8,128)(2,1)S(1)} collective-permute-done((bf16[32,2176]{1,0:T(8,128)(2,1)S(1)}, bf16[32,2176]{1,0:T(8,128)(2,1)S(1)}, u32[]{:S(2)}, u32[]{:S(2)}) %collective-permute-start.14) | collective-permute-done | bytes 139296 | tf_op jit(solution)/shard_map/ppermute | solution.py:323
  65.1 2.0 %collective-permute-done.15.b1 = bf16[32,2176]{1,0:T(8,128)(2,1)S(1)} collective-permute-done((bf16[32,2176]{1,0:T(8,128)(2,1)S(1)}, bf16[32,2176]{1,0:T(8,128)(2,1)S(1)}, u32[]{:S(2)}, u32[]{:S(2)}) %collective-permute-start.15) | collective-permute-done | bytes 139296 | tf_op jit(solution)/shard_map/ppermute | solution.py:323
  67.1 0.4 shard_map.102.refs_0_
  67.5 0.8 collective-permute-done.17.far_b.refs_1_
  68.3 0.1 shard_map.103
  68.4 1.4 %collective-permute-start.19 = (bf16[288,3200]{1,0:T(8,128)(2,1)S(1)}, bf16[288,3200]{1,0:T(8,128)(2,1)S(1)}, u32[]{:S(2)}, u32[]{:S(2)}) collective-permute-start(bf16[288,3200]{1,0:T(8,128)(2,1)S(1)} %shard_map.103), channel_id=1, source_target_pairs={{0,1},{1,0},{2,3},{3,2},{4,5},{5,4},{6,7},{7,6},{8,9},{9,8},{10,11... | collective-permute-start | bytes 5529608 | tf_op jit(solution)/shard_map/ppermute | solution.py:323
  69.8 1.3 %collective-permute-start.18 = (bf16[288,1152]{1,0:T(8,128)(2,1)S(1)}, bf16[288,1152]{1,0:T(8,128)(2,1)S(1)}, u32[]{:S(2)}, u32[]{:S(2)}) collective-permute-start(bf16[288,1152]{1,0:T(8,128)(2,1)S(1)} %get-tuple-element.65.mid_ref), channel_id=1, source_target_pairs={{0,2},{1,3},{2,0},{3,1},{4,6},{5,7},{6,4},{7,5},{8,10},{9,11},{10,... | collective-permute-start | bytes 1990664 | tf_op jit(solution)/shard_map/ppermute | solution.py:323
  71.1 0.2 collective-permute-start.16
  71.3 2.2 %collective-permute-start.6 = (bf16[32,2176]{1,0:T(8,128)(2,1)S(1)}, bf16[32,2176]{1,0:T(8,128)(2,1)S(1)}, u32[]{:S(2)}, u32[]{:S(2)}) collective-permute-start(bf16[32,2176]{1,0:T(8,128)(2,1)S(1)} %get-tuple-element.50), channel_id=1, source_target_pairs={{0,12},{4,8},{8,4},{12,0},{16,28},{20,24},{24,20},{28,16},{1,13},{... | collective-permute-start | bytes 417800 | tf_op jit(solution)/shard_map/ppermute | solution.py:323
  73.5 0.0 collective-permute-start.7
  73.5 0.0 collective-permute-done.19.near_ref
  73.5 1.2 %collective-permute-start.8 = (bf16[32,2176]{1,0:T(8,128)(2,1)S(1)}, bf16[32,2176]{1,0:T(8,128)(2,1)S(1)}, u32[]{:S(2)}, u32[]{:S(2)}) collective-permute-start(bf16[32,2176]{1,0:T(8,128)(2,1)S(1)} %get-tuple-element.52), channel_id=1, source_target_pairs={{0,4},{4,0},{8,12},{12,8},{16,20},{20,16},{24,28},{28,24},{1,5},{5... | collective-permute-start | bytes 417800 | tf_op jit(solution)/shard_map/ppermute | solution.py:323
  74.7 1.2 %shard_map.104 = (f32[512,768]{1,0:T(8,128)S(1)}, f32[512,384]{1,0:T(8,128)S(1)}) custom-call(bf16[144,1024]{1,0:T(8,128)(2,1)S(1)} %get-tuple-element.45.refs_0_.refs_2_.rows_a, bf16[144,1024]{1,0:T(8,128)(2,1)S(1)} %get-tuple-element.58.refs_2_.rows_b, bf16[288,3200]{1,0:T(8,128)(2,1)S(1)} %collective-permute-done.19.near_ref, ...), custom_call_target="tpu_custom_call" | custom-call | flops 679477248 | bytes 5455872 | tf_op jit(solution)/shard_map/pallas_call | solution.py:310
  75.9 4.0 %collective-permute-done.6.refs_3_.b3 = bf16[32,2176]{1,0:T(8,128)(2,1)S(1)} collective-permute-done((bf16[32,2176]{1,0:T(8,128)(2,1)S(1)}, bf16[32,2176]{1,0:T(8,128)(2,1)S(1)}, u32[]{:S(2)}, u32[]{:S(2)}) %collective-permute-start.6) | collective-permute-done | bytes 139296 | tf_op jit(solution)/shard_map/ppermute | solution.py:323
  79.9 3.0 %collective-permute-done.7.refs_4_.b2 = bf16[32,2176]{1,0:T(8,128)(2,1)S(1)} collective-permute-done((bf16[32,2176]{1,0:T(8,128)(2,1)S(1)}, bf16[32,2176]{1,0:T(8,128)(2,1)S(1)}, u32[]{:S(2)}, u32[]{:S(2)}) %collective-permute-start.7) | collective-permute-done | bytes 139296 | tf_op jit(solution)/shard_map/ppermute | solution.py:323
  82.9 0.0 collective-permute-done.8.refs_5_.b1
  82.9 3.1 %collective-permute-done.16.refs_2_.far_ref = bf16[32,4224]{1,0:T(8,128)(2,1)S(1)} collective-permute-done((bf16[32,4224]{1,0:T(8,128)(2,1)S(1)}, bf16[32,4224]{1,0:T(8,128)(2,1)S(1)}, u32[]{:S(2)}, u32[]{:S(2)}) %collective-permute-start.16) | collective-permute-done | bytes 270368 | tf_op jit(solution)/shard_map/ppermute | solution.py:323
  86.0 0.3 collective-permute-done.18.refs_0_
  86.3 0.8 collective-permute-start.20
  87.2 2.3 %shard_map.106 = (bf16[64,2048]{1,0:T(8,128)(2,1)}, bf16[4,64]{1,0:T(4,128)(2,1)}, f32[512,768]{1,0:T(8,128)S(1)}, f32[512,384]{1,0:T(8,128)S(1)}) custom-call(s32[8]{0:T(128)S(1)} %iota_xor_fusion.1.peer_ref, s32[4,64]{1,0:T(4,128)S(1)} %bitcast.8, f32[8,64]{1,0:T(8,128)S(1)} %get-tuple-element.39.w_ref, bf16[32,2176]{1,0:T(8,128)(2,1)S(1)} %get-tuple-element.49.b0, ...), custom_call_target="tpu_custom_call" | custom-call | flops 377487360 | bytes 7392768 | tf_op jit(solution)/shard_map/pallas_call | solution.py:310
  89.5 0.0 collective-permute-done.20.mid_ref
  89.5 1.8 %shard_map.107 = (f32[512,768]{1,0:T(8,128)}, f32[512,384]{1,0:T(8,128)}) custom-call(bf16[288,3200]{1,0:T(8,128)(2,1)S(1)} %collective-permute-done.19.near_ref, bf16[288,1152]{1,0:T(8,128)(2,1)S(1)} %collective-permute-done.20.mid_ref, f32[512,768]{1,0:T(8,128)S(1)} %get-tuple-element.70.in_part, f32[512,384]{1,0:T(8,128)S(1)} %get-tuple-element.71.out_part), custom_call_target="tpu_custom_call" | custom-call | flops 339738624 | bytes 4866048 | tf_op jit(solution)/shard_map/pallas_call | solution.py:310
  (4 shorter events, 0.0 us)
Async XLA Ops:
  0.6 3.6 %copy-start.3 = (bf16[64,4]{0,1:T(4,128)(2,1)S(1)}, bf16[64,4]{0,1:T(4,128)(2,1)}, u32[]{:S(2)}) copy-start(bf16[64,4]{0,1:T(4,128)(2,1)} %param.9) | copy-start | bytes 1540
  0.6 3.5 %copy-start.2 = (s32[64,4]{0,1:T(4,128)S(1)}, s32[64,4]{0,1:T(4,128)}, u32[]{:S(2)}) copy-start(s32[64,4]{0,1:T(4,128)} %param.8) | copy-start | bytes 3076
  0.7 3.5 %copy-start.1 = (bf16[64,2048]{1,0:T(8,128)(2,1)S(1)}, bf16[64,2048]{1,0:T(8,128)(2,1)}, u32[]{:S(2)}) copy-start(bf16[64,2048]{1,0:T(8,128)(2,1)} %dy_ref.1) | copy-start | bytes 786436
  0.7 3.5 %copy-start = (bf16[64,2048]{1,0:T(8,128)(2,1)S(1)}, bf16[64,2048]{1,0:T(8,128)(2,1)}, u32[]{:S(2)}) copy-start(bf16[64,2048]{1,0:T(8,128)(2,1)} %x_ref.1) | copy-start | bytes 786436
  2.1 32.4 %collective-permute-start.4 = (bf16[512,1152]{1,0:T(8,128)(2,1)S(1)}, bf16[512,1152]{1,0:T(8,128)(2,1)S(1)}, u32[]{:S(2)}, u32[]{:S(2)}) collective-permute-start(bf16[512,1152]{1,0:T(8,128)(2,1)S(1)} %pad_maximum_fusion.own_ref), channel_id=1, source_target_pairs={{0,2},{1,3},{2,0},{3,1},{4,6},{5,7},{6,4},{7,5},{8,10},{9,11},{10,... | collective-permute-start | bytes 3538952 | tf_op jit(solution)/shard_map/ppermute | solution.py:323
  4.8 28.5 %collective-permute-start.3 = (bf16[64,4224]{1,0:T(8,128)(2,1)S(1)}, bf16[64,4224]{1,0:T(8,128)(2,1)S(1)}, u32[]{:S(2)}, u32[]{:S(2)}) collective-permute-start(bf16[64,4224]{1,0:T(8,128)(2,1)S(1)} %get-tuple-element.40.joint_ref), channel_id=1, source_target_pairs={{0,16},{4,20},{8,24},{12,28},{16,0},{20,4},{24,8},{28,12},{1,17},{... | collective-permute-start | bytes 1622024 | tf_op jit(solution)/shard_map/ppermute | solution.py:323
  8.6 15.3 %collective-permute-start = (bf16[64,2176]{1,0:T(8,128)(2,1)}, bf16[64,2176]{1,0:T(8,128)(2,1)}, u32[]{:S(2)}, u32[]{:S(2)}) collective-permute-start(bf16[64,2176]{1,0:T(8,128)(2,1)} %get-tuple-element.41), channel_id=1, source_target_pairs={{0,12},{4,8},{8,4},{12,0},{16,28},{20,24},{24,20},{28,16},{1,13},{... | collective-permute-start | bytes 835592 | tf_op jit(solution)/shard_map/ppermute | solution.py:323
  10.8 22.4 %collective-permute-start.1 = (bf16[64,2176]{1,0:T(8,128)(2,1)}, bf16[64,2176]{1,0:T(8,128)(2,1)}, u32[]{:S(2)}, u32[]{:S(2)}) collective-permute-start(bf16[64,2176]{1,0:T(8,128)(2,1)} %get-tuple-element.42), channel_id=1, source_target_pairs={{0,8},{4,12},{8,0},{12,4},{16,24},{20,28},{24,16},{28,20},{1,9},{5... | collective-permute-start | bytes 835592 | tf_op jit(solution)/shard_map/ppermute | solution.py:323
  11.0 22.3 %collective-permute-start.2 = (bf16[64,2176]{1,0:T(8,128)(2,1)}, bf16[64,2176]{1,0:T(8,128)(2,1)}, u32[]{:S(2)}, u32[]{:S(2)}) collective-permute-start(bf16[64,2176]{1,0:T(8,128)(2,1)} %get-tuple-element.43), channel_id=1, source_target_pairs={{0,4},{4,0},{8,12},{12,8},{16,20},{20,16},{24,28},{28,24},{1,5},{5... | collective-permute-start | bytes 835592 | tf_op jit(solution)/shard_map/ppermute | solution.py:323
  35.3 6.4 %collective-permute-start.5 = (bf16[1024,1152]{1,0:T(8,128)(2,1)S(1)}, bf16[1024,1152]{1,0:T(8,128)(2,1)S(1)}, u32[]{:S(2)}, u32[]{:S(2)}) collective-permute-start(bf16[1024,1152]{1,0:T(8,128)(2,1)S(1)} %shard_map.98.refs_0_), channel_id=1, source_target_pairs={{0,1},{1,0},{2,3},{3,2},{4,5},{5,4},{6,7},{7,6},{8,9},{9,8},{10,11... | collective-permute-start | bytes 7077896 | tf_op jit(solution)/shard_map/ppermute | solution.py:323
  37.5 14.9 %collective-permute-start.12 = (bf16[144,2048]{1,0:T(8,128)(2,1)S(1)}, bf16[144,2048]{1,0:T(8,128)(2,1)S(1)}, u32[]{:S(2)}, u32[]{:S(2)}) collective-permute-start(bf16[144,2048]{1,0:T(8,128)(2,1)S(1)} %get-tuple-element.48.refs_4_), channel_id=1, source_target_pairs={{0,2},{1,3},{2,0},{3,1},{4,6},{5,7},{6,4},{7,5},{8,10},{9,11},{10,... | collective-permute-start | bytes 1769480 | tf_op jit(solution)/shard_map/ppermute | solution.py:323
  37.7 14.7 %collective-permute-start.9 = (bf16[64,2176]{1,0:T(8,128)(2,1)S(1)}, bf16[64,2176]{1,0:T(8,128)(2,1)S(1)}, u32[]{:S(2)}, u32[]{:S(2)}) collective-permute-start(bf16[64,2176]{1,0:T(8,128)(2,1)S(1)} %get-tuple-element.53), channel_id=1, source_target_pairs={{0,12},{4,8},{8,4},{12,0},{16,28},{20,24},{24,20},{28,16},{1,13},{... | collective-permute-start | bytes 835592 | tf_op jit(solution)/shard_map/ppermute | solution.py:323
  37.7 14.7 %collective-permute-start.10 = (bf16[64,2176]{1,0:T(8,128)(2,1)S(1)}, bf16[64,2176]{1,0:T(8,128)(2,1)S(1)}, u32[]{:S(2)}, u32[]{:S(2)}) collective-permute-start(bf16[64,2176]{1,0:T(8,128)(2,1)S(1)} %get-tuple-element.54), channel_id=1, source_target_pairs={{0,8},{4,12},{8,0},{12,4},{16,24},{20,28},{24,16},{28,20},{1,9},{5... | collective-permute-start | bytes 835592 | tf_op jit(solution)/shard_map/ppermute | solution.py:323
  39.2 14.0 %collective-permute-start.11 = (bf16[64,2176]{1,0:T(8,128)(2,1)S(1)}, bf16[64,2176]{1,0:T(8,128)(2,1)S(1)}, u32[]{:S(2)}, u32[]{:S(2)}) collective-permute-start(bf16[64,2176]{1,0:T(8,128)(2,1)S(1)} %get-tuple-element.55), channel_id=1, source_target_pairs={{0,4},{4,0},{8,12},{12,8},{16,20},{20,16},{24,28},{28,24},{1,5},{5... | collective-permute-start | bytes 835592 | tf_op jit(solution)/shard_map/ppermute | solution.py:323
  53.8 14.5 %collective-permute-start.17 = (bf16[144,2048]{1,0:T(8,128)(2,1)S(1)}, bf16[144,2048]{1,0:T(8,128)(2,1)S(1)}, u32[]{:S(2)}, u32[]{:S(2)}) collective-permute-start(bf16[144,2048]{1,0:T(8,128)(2,1)S(1)} %get-tuple-element.60.refs_4_), channel_id=1, source_target_pairs={{0,2},{1,3},{2,0},{3,1},{4,6},{5,7},{6,4},{7,5},{8,10},{9,11},{10,... | collective-permute-start | bytes 1769480 | tf_op jit(solution)/shard_map/ppermute | solution.py:323
  57.8 5.4 %collective-permute-start.13 = (bf16[32,2176]{1,0:T(8,128)(2,1)S(1)}, bf16[32,2176]{1,0:T(8,128)(2,1)S(1)}, u32[]{:S(2)}, u32[]{:S(2)}) collective-permute-start(bf16[32,2176]{1,0:T(8,128)(2,1)S(1)} %get-tuple-element.62), channel_id=1, source_target_pairs={{0,12},{4,8},{8,4},{12,0},{16,28},{20,24},{24,20},{28,16},{1,13},{... | collective-permute-start | bytes 417800 | tf_op jit(solution)/shard_map/ppermute | solution.py:323
  57.9 7.2 %collective-permute-start.14 = (bf16[32,2176]{1,0:T(8,128)(2,1)S(1)}, bf16[32,2176]{1,0:T(8,128)(2,1)S(1)}, u32[]{:S(2)}, u32[]{:S(2)}) collective-permute-start(bf16[32,2176]{1,0:T(8,128)(2,1)S(1)} %get-tuple-element.63), channel_id=1, source_target_pairs={{0,8},{4,12},{8,0},{12,4},{16,24},{20,28},{24,16},{28,20},{1,9},{5... | collective-permute-start | bytes 417800 | tf_op jit(solution)/shard_map/ppermute | solution.py:323
  59.3 7.8 %collective-permute-start.15 = (bf16[32,2176]{1,0:T(8,128)(2,1)S(1)}, bf16[32,2176]{1,0:T(8,128)(2,1)S(1)}, u32[]{:S(2)}, u32[]{:S(2)}) collective-permute-start(bf16[32,2176]{1,0:T(8,128)(2,1)S(1)} %get-tuple-element.64), channel_id=1, source_target_pairs={{0,4},{4,0},{8,12},{12,8},{16,20},{20,16},{24,28},{28,24},{1,5},{5... | collective-permute-start | bytes 417800 | tf_op jit(solution)/shard_map/ppermute | solution.py:323
  68.4 5.1 %collective-permute-start.19 = (bf16[288,3200]{1,0:T(8,128)(2,1)S(1)}, bf16[288,3200]{1,0:T(8,128)(2,1)S(1)}, u32[]{:S(2)}, u32[]{:S(2)}) collective-permute-start(bf16[288,3200]{1,0:T(8,128)(2,1)S(1)} %shard_map.103), channel_id=1, source_target_pairs={{0,1},{1,0},{2,3},{3,2},{4,5},{5,4},{6,7},{7,6},{8,9},{9,8},{10,11... | collective-permute-start | bytes 5529608 | tf_op jit(solution)/shard_map/ppermute | solution.py:323
  69.8 16.5 %collective-permute-start.18 = (bf16[288,1152]{1,0:T(8,128)(2,1)S(1)}, bf16[288,1152]{1,0:T(8,128)(2,1)S(1)}, u32[]{:S(2)}, u32[]{:S(2)}) collective-permute-start(bf16[288,1152]{1,0:T(8,128)(2,1)S(1)} %get-tuple-element.65.mid_ref), channel_id=1, source_target_pairs={{0,2},{1,3},{2,0},{3,1},{4,6},{5,7},{6,4},{7,5},{8,10},{9,11},{10,... | collective-permute-start | bytes 1990664 | tf_op jit(solution)/shard_map/ppermute | solution.py:323
  71.1 14.9 %collective-permute-start.16 = (bf16[32,4224]{1,0:T(8,128)(2,1)S(1)}, bf16[32,4224]{1,0:T(8,128)(2,1)S(1)}, u32[]{:S(2)}, u32[]{:S(2)}) collective-permute-start(bf16[32,4224]{1,0:T(8,128)(2,1)S(1)} %shard_map.102.refs_0_), channel_id=1, source_target_pairs={{0,16},{4,20},{8,24},{12,28},{16,0},{20,4},{24,8},{28,12},{1,17},{... | collective-permute-start | bytes 811016 | tf_op jit(solution)/shard_map/ppermute | solution.py:323
  71.3 8.6 %collective-permute-start.6 = (bf16[32,2176]{1,0:T(8,128)(2,1)S(1)}, bf16[32,2176]{1,0:T(8,128)(2,1)S(1)}, u32[]{:S(2)}, u32[]{:S(2)}) collective-permute-start(bf16[32,2176]{1,0:T(8,128)(2,1)S(1)} %get-tuple-element.50), channel_id=1, source_target_pairs={{0,12},{4,8},{8,4},{12,0},{16,28},{20,24},{24,20},{28,16},{1,13},{... | collective-permute-start | bytes 417800 | tf_op jit(solution)/shard_map/ppermute | solution.py:323
  73.5 9.4 %collective-permute-start.7 = (bf16[32,2176]{1,0:T(8,128)(2,1)S(1)}, bf16[32,2176]{1,0:T(8,128)(2,1)S(1)}, u32[]{:S(2)}, u32[]{:S(2)}) collective-permute-start(bf16[32,2176]{1,0:T(8,128)(2,1)S(1)} %get-tuple-element.51), channel_id=1, source_target_pairs={{0,8},{4,12},{8,0},{12,4},{16,24},{20,28},{24,16},{28,20},{1,9},{5... | collective-permute-start | bytes 417800 | tf_op jit(solution)/shard_map/ppermute | solution.py:323
  73.5 9.4 %collective-permute-start.8 = (bf16[32,2176]{1,0:T(8,128)(2,1)S(1)}, bf16[32,2176]{1,0:T(8,128)(2,1)S(1)}, u32[]{:S(2)}, u32[]{:S(2)}) collective-permute-start(bf16[32,2176]{1,0:T(8,128)(2,1)S(1)} %get-tuple-element.52), channel_id=1, source_target_pairs={{0,4},{4,0},{8,12},{12,8},{16,20},{20,16},{24,28},{28,24},{1,5},{5... | collective-permute-start | bytes 417800 | tf_op jit(solution)/shard_map/ppermute | solution.py:323
  86.3 3.1 %collective-permute-start.20 = (bf16[288,1152]{1,0:T(8,128)(2,1)S(1)}, bf16[288,1152]{1,0:T(8,128)(2,1)S(1)}, u32[]{:S(2)}, u32[]{:S(2)}) collective-permute-start(bf16[288,1152]{1,0:T(8,128)(2,1)S(1)} %shard_map.105.refs_2_), channel_id=1, source_target_pairs={{0,1},{1,0},{2,3},{3,2},{4,5},{5,4},{6,7},{7,6},{8,9},{9,8},{10,11... | collective-permute-start | bytes 1990664 | tf_op jit(solution)/shard_map/ppermute | solution.py:323

commit v15 on v14

--- a/solution.py
+++ b/solution.py
@@ -110,6 +110,11 @@
 
 def pack_kernel(experts, joint_ref, *refs):
     pack_blocks(experts, joint_ref, refs[-1 - len(experts) : -1], refs[-1])
+
+
+def keep_kernel(expert, joint_ref, block_ref, kept_ref, held_ref, fold):
+    pack_blocks([expert], joint_ref, [kept_ref], fold)
+    held_ref[...] = block_ref[...]
 
 
 def slice_kernel(place_ref, *refs):
@@ -380,7 +385,15 @@
         )
 
     own = [swap(value, "expert", j + 1) for j, value in enumerate(pack(range(half + 1, blocks), joint, []))]
-    (kept,) = pack([half], joint, [own[2]])
+    kept, own[2] = call(
+        functools.partial(keep_kernel, half),
+        [packed_shape] * 2,
+        [],
+        [joint, own[2]],
+        [],
+        [pltpu.VMEM((chunks, LANES), F32)],
+        4 * (main + 16) * token_count * width,
+    )
     *own_slices, own_weight = sliced([kept, *own[::-1]], [far_joint])
     own_far = swap(own_slices[2], "dp", 2)
     far = pack(range(half), far_joint, [own_slices[0], far_weights])

time: 91.4 us -> 91.3 us (level)
  waiting for transfers between devices: 49.6 us -> 48.6 us
    ppermute x21, waiting for transfers between devices: 49.6 us -> 48.6 us  [swap(): lax.ppermute(value, axis, [(i, i ^ mask) for i in range(lax.axis_size(axi...]
  transfers between devices with their start and end apart: 21 -> 21, of which waited for: 13 -> 13; matrix products, arithmetic and copies ran while one was open for 0% -> 0% of each run, Pallas kernels for 14% -> 15%
where the time goes in v15:
time: 91.3 us; the launch traced here: 91.2 us
  waiting for transfers between devices  48.6 us (53%)
  starting transfers between devices  23.3 us (26%)
  Pallas kernels  17 us (19%)
  other arithmetic  1.41 us (2%)
    ppermute x21, waiting for transfers between devices, swap(): lax.ppermute(value, axis, [(i, i ^ mask) for i in range(lax.axis_size(axi...  48.6 us
    ppermute x21, starting transfers between devices, swap(): lax.ppermute(value, axis, [(i, i ^ mask) for i in range(lax.axis_size(axi...  23.3 us
    pallas_call x15, Pallas kernels, call(): pl.pallas_call(kernel, out_shape=tuple(outs), in_specs=[on_smem] * len(sm...  17 us
  transfers between devices with their start and end apart: 21, of which 13 were waited for; matrix products, arithmetic and copies ran while one was open for 0% of the time, Pallas kernels for 15%

profile of v15, /device:TPU:1, one launch (start us, length us, event | category | flops | bytes accessed | tf_op | source)
XLA Modules:
  0.0 91.2 jit_solution(10563452601421886280)
XLA Ops:
  0.6 0.0 copy-start.3
  0.6 0.0 copy-start.2
  0.7 0.0 copy-start.1
  0.7 0.0 copy-start
  0.7 1.4 %pad_maximum_fusion.own_ref = bf16[512,1152]{1,0:T(8,128)(2,1)S(1)} fusion(bf16[512,384]{1,0:T(8,128)(2,1)} %bitcast.11, bf16[512,768]{1,0:T(8,128)(2,1)} %bitcast.10), kind=kLoop, calls=%fused_computation | loop fusion | flops 2359296 | bytes 2359296 | tf_op jit(solution)/shard_map/concatenate | solution.py:357
  2.1 2.1 %collective-permute-start.4 = (bf16[512,1152]{1,0:T(8,128)(2,1)S(1)}, bf16[512,1152]{1,0:T(8,128)(2,1)S(1)}, u32[]{:S(2)}, u32[]{:S(2)}) collective-permute-start(bf16[512,1152]{1,0:T(8,128)(2,1)S(1)} %pad_maximum_fusion.own_ref), channel_id=1, source_target_pairs={{0,2},{1,3},{2,0},{3,1},{4,6},{5,7},{6,4},{7,5},{8,10},{9,11},{10,... | collective-permute-start | bytes 3538952 | tf_op jit(solution)/shard_map/ppermute | solution.py:328
  4.2 0.0 copy-done.3
  4.2 0.0 copy-done.2
  4.2 0.0 copy-done.1
  4.2 0.6 shard_map.93
  4.8 2.4 %collective-permute-start.3 = (bf16[64,4224]{1,0:T(8,128)(2,1)S(1)}, bf16[64,4224]{1,0:T(8,128)(2,1)S(1)}, u32[]{:S(2)}, u32[]{:S(2)}) collective-permute-start(bf16[64,4224]{1,0:T(8,128)(2,1)S(1)} %get-tuple-element.42.joint_ref), channel_id=1, source_target_pairs={{0,16},{4,20},{8,24},{12,28},{16,0},{20,4},{24,8},{28,12},{1,17},{... | collective-permute-start | bytes 1622024 | tf_op jit(solution)/shard_map/ppermute | solution.py:328
  7.2 1.4 %shard_map.94 = (bf16[64,2176]{1,0:T(8,128)(2,1)}, bf16[64,2176]{1,0:T(8,128)(2,1)}, bf16[64,2176]{1,0:T(8,128)(2,1)}) custom-call(bf16[64,4224]{1,0:T(8,128)(2,1)S(1)} %get-tuple-element.42.joint_ref), custom_call_target="tpu_custom_call" | custom-call | flops 58720256 | bytes 1376256 | tf_op jit(solution)/shard_map/pallas_call | solution.py:315
  8.6 2.3 %collective-permute-start = (bf16[64,2176]{1,0:T(8,128)(2,1)}, bf16[64,2176]{1,0:T(8,128)(2,1)}, u32[]{:S(2)}, u32[]{:S(2)}) collective-permute-start(bf16[64,2176]{1,0:T(8,128)(2,1)} %get-tuple-element.43), channel_id=1, source_target_pairs={{0,12},{4,8},{8,4},{12,0},{16,28},{20,24},{24,20},{28,16},{1,13},{... | collective-permute-start | bytes 835592 | tf_op jit(solution)/shard_map/ppermute | solution.py:328
  10.8 0.2 collective-permute-start.1
  11.0 0.2 collective-permute-start.2
  11.2 12.7 %collective-permute-done.block_ref = bf16[64,2176]{1,0:T(8,128)(2,1)} collective-permute-done((bf16[64,2176]{1,0:T(8,128)(2,1)}, bf16[64,2176]{1,0:T(8,128)(2,1)}, u32[]{:S(2)}, u32[]{:S(2)}) %collective-permute-start) | collective-permute-done | bytes 278560 | tf_op jit(solution)/shard_map/ppermute | solution.py:328
  23.9 1.3 %shard_map.95 = (bf16[64,2176]{1,0:T(8,128)(2,1)S(1)}, bf16[64,2176]{1,0:T(8,128)(2,1)S(1)}) custom-call(bf16[64,4224]{1,0:T(8,128)(2,1)S(1)} %get-tuple-element.42.joint_ref, bf16[64,2176]{1,0:T(8,128)(2,1)} %collective-permute-done.block_ref), custom_call_target="tpu_custom_call" | custom-call | flops 25165824 | bytes 1376256 | tf_op jit(solution)/shard_map/pallas_call | solution.py:315
  25.3 8.0 %collective-permute-done.1.refs_2_ = bf16[64,2176]{1,0:T(8,128)(2,1)} collective-permute-done((bf16[64,2176]{1,0:T(8,128)(2,1)}, bf16[64,2176]{1,0:T(8,128)(2,1)}, u32[]{:S(2)}, u32[]{:S(2)}) %collective-permute-start.1) | collective-permute-done | bytes 278560 | tf_op jit(solution)/shard_map/ppermute | solution.py:328
  33.3 0.0 collective-permute-done.2.refs_3_
  33.3 0.0 collective-permute-done.3.refs_4_.joint_ref
  33.3 1.2 %shard_map.96 = (bf16[144,1024]{1,0:T(8,128)(2,1)S(1)}, bf16[144,1024]{1,0:T(8,128)(2,1)S(1)}, bf16[144,2048]{1,0:T(8,128)(2,1)S(1)}, f32[144,128]{1,0:T(8,128)S(1)}) custom-call(s32[4]{0:T(128)S(1)} %iota_xor_fusion.place_ref, bf16[64,2176]{1,0:T(8,128)(2,1)S(1)} %get-tuple-element.44.refs_0_, bf16[64,2176]{1,0:T(8,128)(2,1)S(1)} %get-tuple-element.45.refs_1_, ...), custom_call_target="tpu_custom_call" | custom-call | bytes 2367488 | tf_op jit(solution)/shard_map/pallas_call | solution.py:315
  34.4 0.0 collective-permute-done.4.refs_1_.far_ref
  34.4 0.6 shard_map.97
  35.0 0.2 shard_map.98.refs_0_
  35.2 2.2 %collective-permute-start.5 = (bf16[1024,1152]{1,0:T(8,128)(2,1)S(1)}, bf16[1024,1152]{1,0:T(8,128)(2,1)S(1)}, u32[]{:S(2)}, u32[]{:S(2)}) collective-permute-start(bf16[1024,1152]{1,0:T(8,128)(2,1)S(1)} %shard_map.98.refs_0_), channel_id=1, source_target_pairs={{0,1},{1,0},{2,3},{3,2},{4,5},{5,4},{6,7},{7,6},{8,9},{9,8},{10,11... | collective-permute-start | bytes 7077896 | tf_op jit(solution)/shard_map/ppermute | solution.py:328
  37.4 0.2 collective-permute-start.12
  37.7 0.0 collective-permute-start.9
  37.7 1.5 %collective-permute-start.10 = (bf16[64,2176]{1,0:T(8,128)(2,1)S(1)}, bf16[64,2176]{1,0:T(8,128)(2,1)S(1)}, u32[]{:S(2)}, u32[]{:S(2)}) collective-permute-start(bf16[64,2176]{1,0:T(8,128)(2,1)S(1)} %get-tuple-element.58), channel_id=1, source_target_pairs={{0,8},{4,12},{8,0},{12,4},{16,24},{20,28},{24,16},{28,20},{1,9},{5... | collective-permute-start | bytes 835592 | tf_op jit(solution)/shard_map/ppermute | solution.py:328
  39.1 1.2 %collective-permute-start.11 = (bf16[64,2176]{1,0:T(8,128)(2,1)S(1)}, bf16[64,2176]{1,0:T(8,128)(2,1)S(1)}, u32[]{:S(2)}, u32[]{:S(2)}) collective-permute-start(bf16[64,2176]{1,0:T(8,128)(2,1)S(1)} %get-tuple-element.59), channel_id=1, source_target_pairs={{0,4},{4,0},{8,12},{12,8},{16,20},{20,16},{24,28},{28,24},{1,5},{5... | collective-permute-start | bytes 835592 | tf_op jit(solution)/shard_map/ppermute | solution.py:328
  40.3 1.3 %collective-permute-done.5.refs_1_ = bf16[1024,1152]{1,0:T(8,128)(2,1)S(1)} collective-permute-done((bf16[1024,1152]{1,0:T(8,128)(2,1)S(1)}, bf16[1024,1152]{1,0:T(8,128)(2,1)S(1)}, u32[]{:S(2)}, u32[]{:S(2)}) %collective-permute-start.5) | collective-permute-done | bytes 2359328 | tf_op jit(solution)/shard_map/ppermute | solution.py:328
  41.6 2.6 %shard_map.99 = (bf16[144,1152]{1,0:T(8,128)(2,1)S(1)}, bf16[32,2176]{1,0:T(8,128)(2,1)S(1)}, bf16[32,2176]{1,0:T(8,128)(2,1)S(1)}, bf16[32,2176]{1,0:T(8,128)(2,1)S(1)}, bf16[32,2176]{1,0:T(8,128)(2,1)S(1)}) custom-call(s32[4]{0:T(128)S(1)} %iota_xor_fusion.place_ref, f32[144,128]{1,0:T(8,128)S(1)} %get-tuple-element.48.w_ref, ...), custom_call_target="tpu_custom_call" | custom-call | flops 1132462080 | bytes 6860800 | tf_op jit(solution)/shard_map/pallas_call | solution.py:315
  44.2 8.1 %collective-permute-done.12.refs_5_.far_a.refs_0_ = bf16[144,2048]{1,0:T(8,128)(2,1)S(1)} collective-permute-done((bf16[144,2048]{1,0:T(8,128)(2,1)S(1)}, bf16[144,2048]{1,0:T(8,128)(2,1)S(1)}, u32[]{:S(2)}, u32[]{:S(2)}) %collective-permute-start.12) | collective-permute-done | bytes 589856 | tf_op jit(solution)/shard_map/ppermute | solution.py:328
  52.3 0.0 collective-permute-done.9.refs_1_
  52.4 0.0 collective-permute-done.10.refs_2_
  52.4 0.8 collective-permute-done.11.refs_3_
  53.1 0.7 shard_map.100
  53.8 1.3 %collective-permute-start.17 = (bf16[144,2048]{1,0:T(8,128)(2,1)S(1)}, bf16[144,2048]{1,0:T(8,128)(2,1)S(1)}, u32[]{:S(2)}, u32[]{:S(2)}) collective-permute-start(bf16[144,2048]{1,0:T(8,128)(2,1)S(1)} %get-tuple-element.64.refs_4_), channel_id=1, source_target_pairs={{0,2},{1,3},{2,0},{3,1},{4,6},{5,7},{6,4},{7,5},{8,10},{9,11},{10,... | collective-permute-start | bytes 1769480 | tf_op jit(solution)/shard_map/ppermute | solution.py:328
  55.1 2.6 %shard_map.101 = (bf16[288,1152]{1,0:T(8,128)(2,1)S(1)}, bf16[32,2176]{1,0:T(8,128)(2,1)S(1)}, bf16[32,2176]{1,0:T(8,128)(2,1)S(1)}, bf16[32,2176]{1,0:T(8,128)(2,1)S(1)}, bf16[32,2176]{1,0:T(8,128)(2,1)S(1)}) custom-call(s32[4]{0:T(128)S(1)} %iota_xor_fusion.place_ref, f32[144,128]{1,0:T(8,128)S(1)} %get-tuple-element.61.w_ref, ...), custom_call_target="tpu_custom_call" | custom-call | flops 1132462080 | bytes 7524352 | tf_op jit(solution)/shard_map/pallas_call | solution.py:315
  57.7 0.1 collective-permute-start.13
  57.8 1.4 %collective-permute-start.14 = (bf16[32,2176]{1,0:T(8,128)(2,1)S(1)}, bf16[32,2176]{1,0:T(8,128)(2,1)S(1)}, u32[]{:S(2)}, u32[]{:S(2)}) collective-permute-start(bf16[32,2176]{1,0:T(8,128)(2,1)S(1)} %get-tuple-element.67), channel_id=1, source_target_pairs={{0,8},{4,12},{8,0},{12,4},{16,24},{20,28},{24,16},{28,20},{1,9},{5... | collective-permute-start | bytes 417800 | tf_op jit(solution)/shard_map/ppermute | solution.py:328
  59.2 1.2 %collective-permute-start.15 = (bf16[32,2176]{1,0:T(8,128)(2,1)S(1)}, bf16[32,2176]{1,0:T(8,128)(2,1)S(1)}, u32[]{:S(2)}, u32[]{:S(2)}) collective-permute-start(bf16[32,2176]{1,0:T(8,128)(2,1)S(1)} %get-tuple-element.68), channel_id=1, source_target_pairs={{0,4},{4,0},{8,12},{12,8},{16,20},{20,16},{24,28},{28,24},{1,5},{5... | collective-permute-start | bytes 417800 | tf_op jit(solution)/shard_map/ppermute | solution.py:328
  60.5 2.7 %collective-permute-done.13.b3 = bf16[32,2176]{1,0:T(8,128)(2,1)S(1)} collective-permute-done((bf16[32,2176]{1,0:T(8,128)(2,1)S(1)}, bf16[32,2176]{1,0:T(8,128)(2,1)S(1)}, u32[]{:S(2)}, u32[]{:S(2)}) %collective-permute-start.13) | collective-permute-done | bytes 139296 | tf_op jit(solution)/shard_map/ppermute | solution.py:328
  63.1 1.9 %collective-permute-done.14.b2 = bf16[32,2176]{1,0:T(8,128)(2,1)S(1)} collective-permute-done((bf16[32,2176]{1,0:T(8,128)(2,1)S(1)}, bf16[32,2176]{1,0:T(8,128)(2,1)S(1)}, u32[]{:S(2)}, u32[]{:S(2)}) %collective-permute-start.14) | collective-permute-done | bytes 139296 | tf_op jit(solution)/shard_map/ppermute | solution.py:328
  65.0 1.9 %collective-permute-done.15.b1 = bf16[32,2176]{1,0:T(8,128)(2,1)S(1)} collective-permute-done((bf16[32,2176]{1,0:T(8,128)(2,1)S(1)}, bf16[32,2176]{1,0:T(8,128)(2,1)S(1)}, u32[]{:S(2)}, u32[]{:S(2)}) %collective-permute-start.15) | collective-permute-done | bytes 139296 | tf_op jit(solution)/shard_map/ppermute | solution.py:328
  67.0 0.4 shard_map.102.refs_0_
  67.4 0.9 collective-permute-done.17.far_b.refs_1_
  68.2 0.1 shard_map.103
  68.4 1.4 %collective-permute-start.19 = (bf16[288,3200]{1,0:T(8,128)(2,1)S(1)}, bf16[288,3200]{1,0:T(8,128)(2,1)S(1)}, u32[]{:S(2)}, u32[]{:S(2)}) collective-permute-start(bf16[288,3200]{1,0:T(8,128)(2,1)S(1)} %shard_map.103), channel_id=1, source_target_pairs={{0,1},{1,0},{2,3},{3,2},{4,5},{5,4},{6,7},{7,6},{8,9},{9,8},{10,11... | collective-permute-start | bytes 5529608 | tf_op jit(solution)/shard_map/ppermute | solution.py:328
  69.8 1.3 %collective-permute-start.18 = (bf16[288,1152]{1,0:T(8,128)(2,1)S(1)}, bf16[288,1152]{1,0:T(8,128)(2,1)S(1)}, u32[]{:S(2)}, u32[]{:S(2)}) collective-permute-start(bf16[288,1152]{1,0:T(8,128)(2,1)S(1)} %get-tuple-element.69.mid_ref), channel_id=1, source_target_pairs={{0,2},{1,3},{2,0},{3,1},{4,6},{5,7},{6,4},{7,5},{8,10},{9,11},{10,... | collective-permute-start | bytes 1990664 | tf_op jit(solution)/shard_map/ppermute | solution.py:328
  71.0 0.2 collective-permute-start.16
  71.2 2.2 %collective-permute-start.6 = (bf16[32,2176]{1,0:T(8,128)(2,1)S(1)}, bf16[32,2176]{1,0:T(8,128)(2,1)S(1)}, u32[]{:S(2)}, u32[]{:S(2)}) collective-permute-start(bf16[32,2176]{1,0:T(8,128)(2,1)S(1)} %get-tuple-element.54), channel_id=1, source_target_pairs={{0,12},{4,8},{8,4},{12,0},{16,28},{20,24},{24,20},{28,16},{1,13},{... | collective-permute-start | bytes 417800 | tf_op jit(solution)/shard_map/ppermute | solution.py:328
  73.4 0.0 collective-permute-start.7
  73.4 0.0 collective-permute-done.19.near_ref
  73.4 1.2 %collective-permute-start.8 = (bf16[32,2176]{1,0:T(8,128)(2,1)S(1)}, bf16[32,2176]{1,0:T(8,128)(2,1)S(1)}, u32[]{:S(2)}, u32[]{:S(2)}) collective-permute-start(bf16[32,2176]{1,0:T(8,128)(2,1)S(1)} %get-tuple-element.56), channel_id=1, source_target_pairs={{0,4},{4,0},{8,12},{12,8},{16,20},{20,16},{24,28},{28,24},{1,5},{5... | collective-permute-start | bytes 417800 | tf_op jit(solution)/shard_map/ppermute | solution.py:328
  74.6 1.2 %shard_map.104 = (f32[512,768]{1,0:T(8,128)S(1)}, f32[512,384]{1,0:T(8,128)S(1)}) custom-call(bf16[144,1024]{1,0:T(8,128)(2,1)S(1)} %get-tuple-element.49.refs_0_.refs_2_.rows_a, bf16[144,1024]{1,0:T(8,128)(2,1)S(1)} %get-tuple-element.62.refs_2_.rows_b, bf16[288,3200]{1,0:T(8,128)(2,1)S(1)} %collective-permute-done.19.near_ref, ...), custom_call_target="tpu_custom_call" | custom-call | flops 679477248 | bytes 5455872 | tf_op jit(solution)/shard_map/pallas_call | solution.py:315
  75.8 4.0 %collective-permute-done.6.refs_3_.b3 = bf16[32,2176]{1,0:T(8,128)(2,1)S(1)} collective-permute-done((bf16[32,2176]{1,0:T(8,128)(2,1)S(1)}, bf16[32,2176]{1,0:T(8,128)(2,1)S(1)}, u32[]{:S(2)}, u32[]{:S(2)}) %collective-permute-start.6) | collective-permute-done | bytes 139296 | tf_op jit(solution)/shard_map/ppermute | solution.py:328
  79.8 3.0 %collective-permute-done.7.refs_4_.b2 = bf16[32,2176]{1,0:T(8,128)(2,1)S(1)} collective-permute-done((bf16[32,2176]{1,0:T(8,128)(2,1)S(1)}, bf16[32,2176]{1,0:T(8,128)(2,1)S(1)}, u32[]{:S(2)}, u32[]{:S(2)}) %collective-permute-start.7) | collective-permute-done | bytes 139296 | tf_op jit(solution)/shard_map/ppermute | solution.py:328
  82.8 0.0 collective-permute-done.8.refs_5_.b1
  82.8 3.1 %collective-permute-done.16.refs_2_.far_ref = bf16[32,4224]{1,0:T(8,128)(2,1)S(1)} collective-permute-done((bf16[32,4224]{1,0:T(8,128)(2,1)S(1)}, bf16[32,4224]{1,0:T(8,128)(2,1)S(1)}, u32[]{:S(2)}, u32[]{:S(2)}) %collective-permute-start.16) | collective-permute-done | bytes 270368 | tf_op jit(solution)/shard_map/ppermute | solution.py:328
  85.9 0.3 collective-permute-done.18.refs_0_
  86.3 0.8 collective-permute-start.20
  87.1 2.3 %shard_map.106 = (bf16[64,2048]{1,0:T(8,128)(2,1)}, bf16[4,64]{1,0:T(4,128)(2,1)}, f32[512,768]{1,0:T(8,128)S(1)}, f32[512,384]{1,0:T(8,128)S(1)}) custom-call(s32[8]{0:T(128)S(1)} %iota_xor_fusion.1.peer_ref, s32[4,64]{1,0:T(4,128)S(1)} %bitcast.8, f32[8,64]{1,0:T(8,128)S(1)} %get-tuple-element.41.w_ref, bf16[32,2176]{1,0:T(8,128)(2,1)S(1)} %get-tuple-element.53.b0, ...), custom_call_target="tpu_custom_call" | custom-call | flops 377487360 | bytes 7392768 | tf_op jit(solution)/shard_map/pallas_call | solution.py:315
  89.4 0.0 collective-permute-done.20.mid_ref
  89.4 1.8 %shard_map.107 = (f32[512,768]{1,0:T(8,128)}, f32[512,384]{1,0:T(8,128)}) custom-call(bf16[288,3200]{1,0:T(8,128)(2,1)S(1)} %collective-permute-done.19.near_ref, bf16[288,1152]{1,0:T(8,128)(2,1)S(1)} %collective-permute-done.20.mid_ref, f32[512,768]{1,0:T(8,128)S(1)} %get-tuple-element.74.in_part, f32[512,384]{1,0:T(8,128)S(1)} %get-tuple-element.75.out_part), custom_call_target="tpu_custom_call" | custom-call | flops 339738624 | bytes 4866048 | tf_op jit(solution)/shard_map/pallas_call | solution.py:315
  (4 shorter events, 0.0 us)
Async XLA Ops:
  0.6 3.6 %copy-start.3 = (bf16[64,4]{0,1:T(4,128)(2,1)S(1)}, bf16[64,4]{0,1:T(4,128)(2,1)}, u32[]{:S(2)}) copy-start(bf16[64,4]{0,1:T(4,128)(2,1)} %param.9) | copy-start | bytes 1540
  0.6 3.5 %copy-start.2 = (s32[64,4]{0,1:T(4,128)S(1)}, s32[64,4]{0,1:T(4,128)}, u32[]{:S(2)}) copy-start(s32[64,4]{0,1:T(4,128)} %param.8) | copy-start | bytes 3076
  0.7 3.5 %copy-start.1 = (bf16[64,2048]{1,0:T(8,128)(2,1)S(1)}, bf16[64,2048]{1,0:T(8,128)(2,1)}, u32[]{:S(2)}) copy-start(bf16[64,2048]{1,0:T(8,128)(2,1)} %dy_ref.1) | copy-start | bytes 786436
  0.7 3.5 %copy-start = (bf16[64,2048]{1,0:T(8,128)(2,1)S(1)}, bf16[64,2048]{1,0:T(8,128)(2,1)}, u32[]{:S(2)}) copy-start(bf16[64,2048]{1,0:T(8,128)(2,1)} %x_ref.1) | copy-start | bytes 786436
  2.1 32.4 %collective-permute-start.4 = (bf16[512,1152]{1,0:T(8,128)(2,1)S(1)}, bf16[512,1152]{1,0:T(8,128)(2,1)S(1)}, u32[]{:S(2)}, u32[]{:S(2)}) collective-permute-start(bf16[512,1152]{1,0:T(8,128)(2,1)S(1)} %pad_maximum_fusion.own_ref), channel_id=1, source_target_pairs={{0,2},{1,3},{2,0},{3,1},{4,6},{5,7},{6,4},{7,5},{8,10},{9,11},{10,... | collective-permute-start | bytes 3538952 | tf_op jit(solution)/shard_map/ppermute | solution.py:328
  4.8 28.5 %collective-permute-start.3 = (bf16[64,4224]{1,0:T(8,128)(2,1)S(1)}, bf16[64,4224]{1,0:T(8,128)(2,1)S(1)}, u32[]{:S(2)}, u32[]{:S(2)}) collective-permute-start(bf16[64,4224]{1,0:T(8,128)(2,1)S(1)} %get-tuple-element.42.joint_ref), channel_id=1, source_target_pairs={{0,16},{4,20},{8,24},{12,28},{16,0},{20,4},{24,8},{28,12},{1,17},{... | collective-permute-start | bytes 1622024 | tf_op jit(solution)/shard_map/ppermute | solution.py:328
  8.6 15.3 %collective-permute-start = (bf16[64,2176]{1,0:T(8,128)(2,1)}, bf16[64,2176]{1,0:T(8,128)(2,1)}, u32[]{:S(2)}, u32[]{:S(2)}) collective-permute-start(bf16[64,2176]{1,0:T(8,128)(2,1)} %get-tuple-element.43), channel_id=1, source_target_pairs={{0,12},{4,8},{8,4},{12,0},{16,28},{20,24},{24,20},{28,16},{1,13},{... | collective-permute-start | bytes 835592 | tf_op jit(solution)/shard_map/ppermute | solution.py:328
  10.8 22.4 %collective-permute-start.1 = (bf16[64,2176]{1,0:T(8,128)(2,1)}, bf16[64,2176]{1,0:T(8,128)(2,1)}, u32[]{:S(2)}, u32[]{:S(2)}) collective-permute-start(bf16[64,2176]{1,0:T(8,128)(2,1)} %get-tuple-element.46), channel_id=1, source_target_pairs={{0,8},{4,12},{8,0},{12,4},{16,24},{20,28},{24,16},{28,20},{1,9},{5... | collective-permute-start | bytes 835592 | tf_op jit(solution)/shard_map/ppermute | solution.py:328
  11.0 22.3 %collective-permute-start.2 = (bf16[64,2176]{1,0:T(8,128)(2,1)}, bf16[64,2176]{1,0:T(8,128)(2,1)}, u32[]{:S(2)}, u32[]{:S(2)}) collective-permute-start(bf16[64,2176]{1,0:T(8,128)(2,1)} %get-tuple-element.47), channel_id=1, source_target_pairs={{0,4},{4,0},{8,12},{12,8},{16,20},{20,16},{24,28},{28,24},{1,5},{5... | collective-permute-start | bytes 835592 | tf_op jit(solution)/shard_map/ppermute | solution.py:328
  35.2 6.4 %collective-permute-start.5 = (bf16[1024,1152]{1,0:T(8,128)(2,1)S(1)}, bf16[1024,1152]{1,0:T(8,128)(2,1)S(1)}, u32[]{:S(2)}, u32[]{:S(2)}) collective-permute-start(bf16[1024,1152]{1,0:T(8,128)(2,1)S(1)} %shard_map.98.refs_0_), channel_id=1, source_target_pairs={{0,1},{1,0},{2,3},{3,2},{4,5},{5,4},{6,7},{7,6},{8,9},{9,8},{10,11... | collective-permute-start | bytes 7077896 | tf_op jit(solution)/shard_map/ppermute | solution.py:328
  37.4 14.9 %collective-permute-start.12 = (bf16[144,2048]{1,0:T(8,128)(2,1)S(1)}, bf16[144,2048]{1,0:T(8,128)(2,1)S(1)}, u32[]{:S(2)}, u32[]{:S(2)}) collective-permute-start(bf16[144,2048]{1,0:T(8,128)(2,1)S(1)} %get-tuple-element.52.refs_4_), channel_id=1, source_target_pairs={{0,2},{1,3},{2,0},{3,1},{4,6},{5,7},{6,4},{7,5},{8,10},{9,11},{10,... | collective-permute-start | bytes 1769480 | tf_op jit(solution)/shard_map/ppermute | solution.py:328
  37.7 14.7 %collective-permute-start.9 = (bf16[64,2176]{1,0:T(8,128)(2,1)S(1)}, bf16[64,2176]{1,0:T(8,128)(2,1)S(1)}, u32[]{:S(2)}, u32[]{:S(2)}) collective-permute-start(bf16[64,2176]{1,0:T(8,128)(2,1)S(1)} %get-tuple-element.57), channel_id=1, source_target_pairs={{0,12},{4,8},{8,4},{12,0},{16,28},{20,24},{24,20},{28,16},{1,13},{... | collective-permute-start | bytes 835592 | tf_op jit(solution)/shard_map/ppermute | solution.py:328
  37.7 14.7 %collective-permute-start.10 = (bf16[64,2176]{1,0:T(8,128)(2,1)S(1)}, bf16[64,2176]{1,0:T(8,128)(2,1)S(1)}, u32[]{:S(2)}, u32[]{:S(2)}) collective-permute-start(bf16[64,2176]{1,0:T(8,128)(2,1)S(1)} %get-tuple-element.58), channel_id=1, source_target_pairs={{0,8},{4,12},{8,0},{12,4},{16,24},{20,28},{24,16},{28,20},{1,9},{5... | collective-permute-start | bytes 835592 | tf_op jit(solution)/shard_map/ppermute | solution.py:328
  39.1 14.0 %collective-permute-start.11 = (bf16[64,2176]{1,0:T(8,128)(2,1)S(1)}, bf16[64,2176]{1,0:T(8,128)(2,1)S(1)}, u32[]{:S(2)}, u32[]{:S(2)}) collective-permute-start(bf16[64,2176]{1,0:T(8,128)(2,1)S(1)} %get-tuple-element.59), channel_id=1, source_target_pairs={{0,4},{4,0},{8,12},{12,8},{16,20},{20,16},{24,28},{28,24},{1,5},{5... | collective-permute-start | bytes 835592 | tf_op jit(solution)/shard_map/ppermute | solution.py:328
  53.8 14.5 %collective-permute-start.17 = (bf16[144,2048]{1,0:T(8,128)(2,1)S(1)}, bf16[144,2048]{1,0:T(8,128)(2,1)S(1)}, u32[]{:S(2)}, u32[]{:S(2)}) collective-permute-start(bf16[144,2048]{1,0:T(8,128)(2,1)S(1)} %get-tuple-element.64.refs_4_), channel_id=1, source_target_pairs={{0,2},{1,3},{2,0},{3,1},{4,6},{5,7},{6,4},{7,5},{8,10},{9,11},{10,... | collective-permute-start | bytes 1769480 | tf_op jit(solution)/shard_map/ppermute | solution.py:328
  57.7 5.4 %collective-permute-start.13 = (bf16[32,2176]{1,0:T(8,128)(2,1)S(1)}, bf16[32,2176]{1,0:T(8,128)(2,1)S(1)}, u32[]{:S(2)}, u32[]{:S(2)}) collective-permute-start(bf16[32,2176]{1,0:T(8,128)(2,1)S(1)} %get-tuple-element.66), channel_id=1, source_target_pairs={{0,12},{4,8},{8,4},{12,0},{16,28},{20,24},{24,20},{28,16},{1,13},{... | collective-permute-start | bytes 417800 | tf_op jit(solution)/shard_map/ppermute | solution.py:328
  57.8 7.2 %collective-permute-start.14 = (bf16[32,2176]{1,0:T(8,128)(2,1)S(1)}, bf16[32,2176]{1,0:T(8,128)(2,1)S(1)}, u32[]{:S(2)}, u32[]{:S(2)}) collective-permute-start(bf16[32,2176]{1,0:T(8,128)(2,1)S(1)} %get-tuple-element.67), channel_id=1, source_target_pairs={{0,8},{4,12},{8,0},{12,4},{16,24},{20,28},{24,16},{28,20},{1,9},{5... | collective-permute-start | bytes 417800 | tf_op jit(solution)/shard_map/ppermute | solution.py:328
  59.2 7.7 %collective-permute-start.15 = (bf16[32,2176]{1,0:T(8,128)(2,1)S(1)}, bf16[32,2176]{1,0:T(8,128)(2,1)S(1)}, u32[]{:S(2)}, u32[]{:S(2)}) collective-permute-start(bf16[32,2176]{1,0:T(8,128)(2,1)S(1)} %get-tuple-element.68), channel_id=1, source_target_pairs={{0,4},{4,0},{8,12},{12,8},{16,20},{20,16},{24,28},{28,24},{1,5},{5... | collective-permute-start | bytes 417800 | tf_op jit(solution)/shard_map/ppermute | solution.py:328
  68.4 5.1 %collective-permute-start.19 = (bf16[288,3200]{1,0:T(8,128)(2,1)S(1)}, bf16[288,3200]{1,0:T(8,128)(2,1)S(1)}, u32[]{:S(2)}, u32[]{:S(2)}) collective-permute-start(bf16[288,3200]{1,0:T(8,128)(2,1)S(1)} %shard_map.103), channel_id=1, source_target_pairs={{0,1},{1,0},{2,3},{3,2},{4,5},{5,4},{6,7},{7,6},{8,9},{9,8},{10,11... | collective-permute-start | bytes 5529608 | tf_op jit(solution)/shard_map/ppermute | solution.py:328
  69.8 16.5 %collective-permute-start.18 = (bf16[288,1152]{1,0:T(8,128)(2,1)S(1)}, bf16[288,1152]{1,0:T(8,128)(2,1)S(1)}, u32[]{:S(2)}, u32[]{:S(2)}) collective-permute-start(bf16[288,1152]{1,0:T(8,128)(2,1)S(1)} %get-tuple-element.69.mid_ref), channel_id=1, source_target_pairs={{0,2},{1,3},{2,0},{3,1},{4,6},{5,7},{6,4},{7,5},{8,10},{9,11},{10,... | collective-permute-start | bytes 1990664 | tf_op jit(solution)/shard_map/ppermute | solution.py:328
  71.0 14.9 %collective-permute-start.16 = (bf16[32,4224]{1,0:T(8,128)(2,1)S(1)}, bf16[32,4224]{1,0:T(8,128)(2,1)S(1)}, u32[]{:S(2)}, u32[]{:S(2)}) collective-permute-start(bf16[32,4224]{1,0:T(8,128)(2,1)S(1)} %shard_map.102.refs_0_), channel_id=1, source_target_pairs={{0,16},{4,20},{8,24},{12,28},{16,0},{20,4},{24,8},{28,12},{1,17},{... | collective-permute-start | bytes 811016 | tf_op jit(solution)/shard_map/ppermute | solution.py:328
  71.2 8.6 %collective-permute-start.6 = (bf16[32,2176]{1,0:T(8,128)(2,1)S(1)}, bf16[32,2176]{1,0:T(8,128)(2,1)S(1)}, u32[]{:S(2)}, u32[]{:S(2)}) collective-permute-start(bf16[32,2176]{1,0:T(8,128)(2,1)S(1)} %get-tuple-element.54), channel_id=1, source_target_pairs={{0,12},{4,8},{8,4},{12,0},{16,28},{20,24},{24,20},{28,16},{1,13},{... | collective-permute-start | bytes 417800 | tf_op jit(solution)/shard_map/ppermute | solution.py:328
  73.4 9.4 %collective-permute-start.7 = (bf16[32,2176]{1,0:T(8,128)(2,1)S(1)}, bf16[32,2176]{1,0:T(8,128)(2,1)S(1)}, u32[]{:S(2)}, u32[]{:S(2)}) collective-permute-start(bf16[32,2176]{1,0:T(8,128)(2,1)S(1)} %get-tuple-element.55), channel_id=1, source_target_pairs={{0,8},{4,12},{8,0},{12,4},{16,24},{20,28},{24,16},{28,20},{1,9},{5... | collective-permute-start | bytes 417800 | tf_op jit(solution)/shard_map/ppermute | solution.py:328
  73.4 9.4 %collective-permute-start.8 = (bf16[32,2176]{1,0:T(8,128)(2,1)S(1)}, bf16[32,2176]{1,0:T(8,128)(2,1)S(1)}, u32[]{:S(2)}, u32[]{:S(2)}) collective-permute-start(bf16[32,2176]{1,0:T(8,128)(2,1)S(1)} %get-tuple-element.56), channel_id=1, source_target_pairs={{0,4},{4,0},{8,12},{12,8},{16,20},{20,16},{24,28},{28,24},{1,5},{5... | collective-permute-start | bytes 417800 | tf_op jit(solution)/shard_map/ppermute | solution.py:328
  86.3 3.1 %collective-permute-start.20 = (bf16[288,1152]{1,0:T(8,128)(2,1)S(1)}, bf16[288,1152]{1,0:T(8,128)(2,1)S(1)}, u32[]{:S(2)}, u32[]{:S(2)}) collective-permute-start(bf16[288,1152]{1,0:T(8,128)(2,1)S(1)} %shard_map.105.refs_2_), channel_id=1, source_target_pairs={{0,1},{1,0},{2,3},{3,2},{4,5},{5,4},{6,7},{7,6},{8,9},{9,8},{10,11... | collective-permute-start | bytes 1990664 | tf_op jit(solution)/shard_map/ppermute | solution.py:328
